TPU v7x, 32 devices: a whole 2x2x4 slice. The times are simulated.
32 devices in a mesh: page: 4 (over z), blk: 8 (over y, x, core).
Axes of the slice: x: 2, y: 2, z: 4, core: 2. Of those that a mesh axis runs over, the one named last changes fastest.
Arguments:
- queries: bfloat16 [64, 2, 32, 128], P(None, None, 'blk'), may hold values from -192 to 192
- prompt_kv: bfloat16 [64, 64, 32, 256], P('page', None, 'blk'), may hold values from -36 to 36
- tail_kv: bfloat16 [64, 256, 32, 256], P('page', None, 'blk'), may hold values from -36 to 36
- page_table: int32 [4, 16], replicated, may hold values from 0 to 63, as said below
- prompt_len: int32 [4], replicated, may hold values from 1 to 1024, 2560 in all
- tail_len: int32 [64], replicated, may hold values from 0 to 254, as said below
- sample_prompt: int32 [64], replicated, may hold values from 0 to 3, as said below
- stream_in: bfloat16 [64, 2, 7168], P(None, None, 'blk'), may hold values from -6 to 6
- w_out: bfloat16 [4096, 7168], P('blk'), may hold values from -0.09375 to 0.09375
- b_out: bfloat16 [7168], replicated, may hold values from -3 to 3
- ln_gain: bfloat16 [7168], P('page'), may hold values from 0.25 to 1.75
- ln_bias: bfloat16 [7168], P('page'), may hold values from -3 to 3
- w_up: bfloat16 [7168, 28672], P('page', 'blk'), may hold values from -0.0625 to 0.0625
- b_up: bfloat16 [28672], P('blk'), may hold values from -3 to 3
- w_down: bfloat16 [28672, 7168], P('blk', 'page'), may hold values from -0.046875 to 0.046875
- b_down: bfloat16 [7168], P(('page', 'blk')), may hold values from -3 to 3
- w_score: bfloat16 [7168], P(('page', 'blk')), may hold values from -0.0625 to 0.0625
Outputs:
- layer_output: bfloat16 [64, 2, 7168], P(None, None, ('page', 'blk'))
- sample_score: float32 [64, 2], replicated
Inputs may be any that keep to these rules, and one draw needn't show every extreme that they name: `page_table`: every slot number appears exactly once in the table. `tail_len`: some sample reaches the largest value. `sample_prompt`: each prompt has exactly 16 samples.
All inputs are finite; a program needn't handle non-finite values.
Results may differ from a plain program's by a relative error of at most 0.03.
Values may be sent and summed in bfloat16 or wider, within the bound.
No kernel may reach another device: no remote copies, remote signals or barrier semaphores. Data moves between devices by JAX's collectives and lax.ppermute only.
A program may use at most 128 MiB of HBM per device.

v0:
```python
import math

import jax
import jax.numpy as jnp
from jax import lax
from jax.sharding import PartitionSpec as P

NEGATIVE = -1e30


def combined_all(value, axis, join):
    pieces = jax.tree.map(lambda part: lax.all_gather(part, axis), value)
    head = jax.tree.map(lambda part: part[0], pieces)
    tail = jax.tree.map(lambda part: part[1:], pieces)
    subtotal, _ = lax.scan(lambda subtotal, share: (join(subtotal, share), None), head, tail)
    return subtotal


def join_partials(earlier, later):
    highest = jnp.maximum(earlier[0], later[0])
    left_scale = jnp.exp(earlier[0] - highest)
    right_scale = jnp.exp(later[0] - highest)
    return (
        highest,
        earlier[1] * left_scale + later[1] * right_scale,
        earlier[2] * left_scale[..., None] + later[2] * right_scale[..., None],
    )


def softmax_part(scores, visible):
    masked = jnp.where(visible, scores, NEGATIVE)
    highest = jnp.max(masked, axis=-1)
    weights = jnp.where(visible, jnp.exp(scores - highest[..., None]), 0.0)
    return (highest, jnp.sum(weights, axis=-1), weights.astype(jnp.bfloat16))


def body(
    queries,
    prompt_kv,
    tail_kv,
    page_table,
    prompt_len,
    tail_len,
    sample_prompt,
    stream_in,
    w_out,
    b_out,
    ln_gain,
    ln_bias,
    w_up,
    b_up,
    w_down,
    b_down,
    w_score,
):
    samples, new_count, heads_dev, head_dim = queries.shape
    slots_dev, page_len = (prompt_kv.shape[0], prompt_kv.shape[1])
    own_count, tail_max = (tail_kv.shape[0], tail_kv.shape[1])
    prompts, pages_max = page_table.shape
    page_pos = lax.axis_index("page")
    blk_pos = lax.axis_index("blk")
    inv_sqrt = 1.0 / math.sqrt(head_dim)
    entries = page_table.reshape(-1)
    slot_ids = page_pos * slots_dev + jnp.arange(slots_dev, dtype=jnp.int32)
    matched = (entries[:, None] == slot_ids[None, :]).astype(jnp.int32)
    owner_index = jnp.sum(matched * jnp.arange(entries.shape[0], dtype=jnp.int32)[:, None], axis=0)
    slot_prompt = owner_index // pages_max
    slot_page = owner_index % pages_max
    prompt_pick = (slot_prompt[:, None] == jnp.arange(prompts, dtype=jnp.int32)[None, :]).astype(
        jnp.int32
    )
    slot_limit = jnp.sum(prompt_pick * prompt_len[None, :], axis=1)
    key_pos = slot_page[:, None] * page_len + jnp.arange(page_len, dtype=jnp.int32)[None, :]
    key_live = (key_pos < slot_limit[:, None]).reshape(-1)
    key_prompt = jnp.repeat(slot_prompt, page_len)
    prompt_visible = ((sample_prompt[:, None] == key_prompt[None, :]) & key_live[None, :])[
        :, None, None, :
    ]
    cache_rows = prompt_kv.reshape(slots_dev * page_len, heads_dev, 2 * head_dim)
    prompt_scores = (
        jnp.einsum(
            "snhd,khd->snhk",
            queries,
            cache_rows[:, :, :head_dim],
            preferred_element_type=jnp.float32,
        )
        * inv_sqrt
    )
    high_p, sum_p, weights_p = softmax_part(prompt_scores, prompt_visible)
    mixed_p = jnp.einsum(
        "snhk,khd->snhd", weights_p, cache_rows[:, :, head_dim:], preferred_element_type=jnp.float32
    )
    first_row = page_pos * own_count
    own_queries = lax.dynamic_slice_in_dim(queries, first_row, own_count, 0)
    own_lengths = lax.dynamic_slice_in_dim(tail_len, first_row, own_count, 0)
    tail_scores = (
        jnp.einsum(
            "snhd,sthd->snht",
            own_queries,
            tail_kv[..., :head_dim],
            preferred_element_type=jnp.float32,
        )
        * inv_sqrt
    )
    reach_pos = own_lengths[:, None] + jnp.arange(new_count, dtype=jnp.int32)[None, :]
    tail_visible = (
        jnp.arange(tail_max, dtype=jnp.int32)[None, None, None, :] <= reach_pos[:, :, None, None]
    )
    high_t, sum_t, weights_t = softmax_part(tail_scores, tail_visible)
    mixed_t = jnp.einsum(
        "snht,sthd->snhd", weights_t, tail_kv[..., head_dim:], preferred_element_type=jnp.float32
    )
    high_t = lax.dynamic_update_slice_in_dim(
        jnp.full(high_p.shape, NEGATIVE, jnp.float32), high_t, first_row, 0
    )
    sum_t = lax.dynamic_update_slice_in_dim(
        jnp.zeros(sum_p.shape, jnp.float32), sum_t, first_row, 0
    )
    mixed_t = lax.dynamic_update_slice_in_dim(
        jnp.zeros(mixed_p.shape, jnp.float32), mixed_t, first_row, 0
    )
    partial_value = join_partials((high_p, sum_p, mixed_p), (high_t, sum_t, mixed_t))
    merged = combined_all(partial_value, "page", join_partials)
    weight_sum, weighted = (merged[1], merged[2])
    attention = (
        (weighted / weight_sum[..., None])
        .astype(jnp.bfloat16)
        .reshape(samples * new_count, heads_dev * head_dim)
    )
    contrib = jnp.dot(attention, w_out, preferred_element_type=jnp.float32)
    slice_width = stream_in.shape[2]
    column = blk_pos * slice_width
    own_stream = stream_in.reshape(samples * new_count, slice_width).astype(jnp.float32)
    contrib = lax.dynamic_update_slice_in_dim(
        contrib, lax.dynamic_slice_in_dim(contrib, column, slice_width, 1) + own_stream, column, 1
    )
    summed = lax.psum(contrib, "blk")
    residual = (summed + b_out.astype(jnp.float32)).astype(jnp.bfloat16)
    residual_f = residual.astype(jnp.float32)
    row_mean = jnp.mean(residual_f, axis=-1, keepdims=True)
    centred = residual_f - row_mean
    inverse_std = lax.rsqrt(jnp.mean(centred * centred, axis=-1, keepdims=True) + 1e-05)
    feature_count = ln_gain.shape[0]
    first_col = page_pos * feature_count
    normed = (
        lax.dynamic_slice_in_dim(centred, first_col, feature_count, 1)
        * inverse_std
        * ln_gain.astype(jnp.float32)
        + ln_bias.astype(jnp.float32)
    ).astype(jnp.bfloat16)
    up_part = jnp.dot(normed, w_up, preferred_element_type=jnp.float32).astype(jnp.bfloat16)
    hidden_sum = lax.psum(up_part, "page").astype(jnp.float32)
    hidden = jnp.maximum(hidden_sum + b_up.astype(jnp.float32), 0.0).astype(jnp.bfloat16)
    projected = jnp.dot(hidden, w_down, preferred_element_type=jnp.float32)
    out_share = lax.psum_scatter(projected, "blk", scatter_dimension=1, tiled=True)
    piece_width = b_down.shape[0]
    out_column = first_col + blk_pos * piece_width
    output = (
        out_share
        + lax.dynamic_slice_in_dim(residual_f, out_column, piece_width, 1)
        + b_down.astype(jnp.float32)
    ).astype(jnp.bfloat16)
    score_part = jnp.sum(output.astype(jnp.float32) * w_score.astype(jnp.float32), axis=-1)
    row_score = lax.psum(score_part, ("page", "blk"))
    return (output.reshape(samples, new_count, piece_width), row_score.reshape(samples, new_count))


def solution(mesh):
    placed = (
        P(None, None, "blk", None),
        P("page", None, "blk", None),
        P("page", None, "blk", None),
        P(),
        P(),
        P(),
        P(),
        P(None, None, "blk"),
        P("blk", None),
        P(),
        P("page"),
        P("page"),
        P("page", "blk"),
        P("blk"),
        P("blk", "page"),
        P(("page", "blk")),
        P(("page", "blk")),
    )
    return jax.shard_map(
        body,
        mesh=mesh,
        in_specs=placed,
        out_specs=(P(None, None, ("page", "blk")), P()),
        check_vma=False,
    )
```

profile of v0, /device:TPU:0, one launch (start us, length us, event | category | flops | bytes accessed | tf_op | source)
XLA Modules:
  0.0 309.0 jit_solution(13106944653056281447)
XLA Ops:
  7.2 0.7 dynamic_slice.26
  8.2 7.0 %fusion.49 = (bf16[16,256,4,128]{3,2,1,0:T(4,128)(2,1)}, bf16[16,256,4,128]{3,2,1,0:T(4,128)(2,1)S(1)}) fusion(bf16[16,256,4,256]{3,2,1,0:T(4,128)(2,1)} %param.21), kind=kLoop, calls=%fused_computation.86 | loop fusion | bytes 16777216 | tf_op jit(solution)/shard_map/slice | solution.py:111
  15.2 1.3 select_reduce_fusion
  17.7 1.7 copy.80
  19.4 1.2 copy-done.3
  20.7 0.7 fusion.4
  22.4 1.3 copy-done.6
  23.7 0.7 fusion.13
  24.6 3.0 fusion.15
  27.8 17.6 %all-gather = f32[256,2,4]{2,1,0:T(2,128)S(1)} all-gather(f32[64,2,4]{2,1,0:T(2,128)S(1)} %copy.85), channel_id=2, replica_groups=mesh['page'=4,'blk'=8] {'page'}, dimensions={0}, use_global_device_ids=true | all-gather | bytes 10240 | tf_op jit(solution)/shard_map/all_gather | solution.py:12
  45.5 16.7 %all-gather.1 = f32[256,2,4]{2,1,0:T(2,128)S(1)} all-gather(f32[64,2,4]{2,1,0:T(2,128)S(1)} %copy.87), channel_id=3, replica_groups=mesh['page'=4,'blk'=8] {'page'}, dimensions={0}, use_global_device_ids=true | all-gather | bytes 10240 | tf_op jit(solution)/shard_map/all_gather | solution.py:12
  62.8 1.6 all-gather.5.cloned.1.call-done
  64.4 1.0 slice.50
  65.6 1.2 slice.53
  66.8 3.3 %while.14 = (s32[]{:T(128)}, f32[64,2,4]{0,2,1:T(4,128)S(1)}, f32[64,2,4]{0,2,1:T(4,128)S(1)}, f32[64,2,4,128]{3,2,1,0:T(4,128)S(1)}, f32[3,64,2,4]{1,3,2,0:T(4,...) while((s32[]{:T(128)}, f32[64,2,4]{0,2,1:T(4,128)S(1)}, ...), condition=%wide.region_7.8_spmd, body=%wide.region_6.7_spmd.sunk | while | flops 199682 | bytes 1339485 | solution.py:15
  67.1 0.8 fusion.56
  68.2 0.8 fusion.56
  69.3 0.8 fusion.56
  70.4 6.0 %fusion.33 = f32[128,7168]{1,0:T(8,128)} fusion(bf16[512,7168]{1,0:T(8,128)(2,1)} %param.27, bf16[16,8,4,128]{3,2,1,0:T(4,128)(2,1)S(1)} %bitcast.85), kind=kOutput, calls=%fused_computation.49 | convolution fusion | flops 939524096 | bytes 11141120 | tf_op jit(solution)/shard_map/dot_general | solution.py:130
  76.5 1.9 add_dynamic-update-slice_fusion
  78.5 75.1 %all-reduce.3.cloned.1.call-done = f32[128,7168]{1,0:T(8,128)} async-done(((f32[128,7168]{1,0:T(8,128)}), f32[128,7168]{1,0:T(8,128)}) %all-reduce.3.cloned.1.call-update) | async-done | bytes 3670032 | tf_op jit(solution)/shard_map/psum | solution.py:137
  153.6 2.5 fusion.47
  156.2 0.8 multiply_reduce_fusion
  157.0 1.0 copy-done.2
  158.0 7.5 %convolution_convert_fusion = bf16[128,3584]{1,0:T(8,128)(2,1)} fusion(bf16[1792,3584]{1,0:T(8,128)(2,1)} %param.31, f32[128,7168]{1,0:T(8,128)S(1)} %get-tuple-element.99, s32[]{:T(128)S(6)} %select_n.59, f32[1792]{0:T(1024)S(1)} %convert_element_type.68, f32[1792]{0:T(1024)S(1)} %convert_element_type.67, f32[128]{0:T(128)S(1)} %add_rsqrt_fusion), kind=kOutput, calls=%fused_computation.10 | convolution fusion | flops 1645543424 | bytes 14696964 | tf_op jit(solution)/shard_map/dot_general | solution.py:151
  165.8 47.7 %all-reduce.5.cloned.1.call-done = bf16[128,3584]{1,0:T(8,128)(2,1)} async-done(((bf16[128,3584]{1,0:T(8,128)(2,1)}), bf16[128,3584]{1,0:T(8,128)(2,1)}) %all-reduce.5.cloned.1.call-update) | async-done | bytes 917520 | tf_op jit(solution)/shard_map/psum | solution.py:152
  213.5 11.0 %convolution_bitcast_fusion = f32[1792,128]{1,0:T(8,128)} fusion(bf16[3584,1792]{1,0:T(8,128)(2,1)} %param.33, bf16[128,3584]{1,0:T(8,128)(2,1)} %all-reduce.5.cloned.1.call-done, f32[3584]{0:T(1024)S(1)} %convert_element_type.72), kind=kOutput, calls=%fused_computation.17 | convolution fusion | flops 1646002176 | bytes 14694400
  224.6 34.8 %reduce-scatter.4.cloned.1.call-done = f32[224,128]{1,0:T(8,128)} async-done(((f32[1792,128]{1,0:T(8,128)}), f32[224,128]{1,0:T(8,128)}) %reduce-scatter.4.cloned.1.call-update) | async-done | bytes 114704
  259.4 1.0 copy.109
  260.4 1.1 multiply_reduce_fusion.1
  261.6 39.5 %psum.23 = f32[64,2]{1,0:T(8,128)S(1)} all-reduce(f32[64,2]{1,0:T(8,128)S(1)} %reshape.174), channel_id=1, replica_groups=mesh['page'=4,'blk'=8] {'page','blk'}, use_global_device_ids=true, to_apply=%region_14.15 | all-reduce | flops 128 | bytes 1024 | tf_op jit(solution)/shard_map/psum | solution.py:164
  301.8 0.7 reshape.173
  (99 shorter events, 5.9 us)
Async XLA Ops:
  7.2 1.0 copy-start
  7.2 57.3 %all-gather.5.cloned.1.call-start = ((), (), s32[]{:S(2)}) async-start(), calls=%async_computation.3 | async-start | bytes 1310720 | tf_op jit(solution)/shard_map/all_gather | solution.py:12
  15.2 1.8 copy-start.12
  15.2 2.1 copy-start.14
  15.2 2.5 copy-start.4
  17.7 2.9 copy-start.3
  17.7 3.9 %copy-start.13 = (s32[64]{0:T(128)S(1)}, s32[64]{0:T(128)}, u32[]{:S(2)}) copy-start(s32[64]{0:T(128)} %param.25) | copy-start | bytes 772
  19.4 2.3 copy-start.5
  22.3 1.4 copy-start.6
  24.6 38.1 %copy-start.7 = (bf16[64,2,896]{2,1,0:T(2,128)(2,1)S(1)}, bf16[64,2,896]{2,1,0:T(2,128)(2,1)}, u32[]{:S(2)}) copy-start(bf16[64,2,896]{2,1,0:T(2,128)(2,1)} %param.26) | copy-start | bytes 688132
  27.6 126.0 %all-reduce.3.cloned.1.call-start = ((), (), s32[]{:S(2)}) async-start(), calls=%async_computation.1 | async-start | bytes 7340032 | tf_op jit(solution)/shard_map/psum | solution.py:137
  76.5 2.0 copy-start.8
  76.5 2.0 copy-start.10
  76.5 2.0 copy-start.11
  78.4 135.1 %all-reduce.5.cloned.1.call-start = ((), (), s32[]{:S(2)}) async-start(), calls=%async_computation.2 | async-start | bytes 1835008 | tf_op jit(solution)/shard_map/psum | solution.py:152
  156.2 1.8 copy-start.2
  158.0 7.8 %copy-start.9 = (bf16[3584]{0:T(1024)(128)(2,1)S(1)}, bf16[3584]{0:T(1024)(128)(2,1)}, u32[]{:S(2)}) copy-start(bf16[3584]{0:T(1024)(128)(2,1)} %param.32) | copy-start | bytes 21508
  165.5 93.8 %reduce-scatter.4.cloned.1.call-start = ((), (), s32[]{:S(2)}) async-start(), calls=%async_computation.4 | async-start | bytes 1032192
  165.8 58.8 %copy-start.15 = (bf16[224]{0:T(256)(128)(2,1)S(1)}, bf16[224]{0:T(256)(128)(2,1)}, u32[]{:S(2)}) copy-start(bf16[224]{0:T(256)(128)(2,1)} %param.34) | copy-start | bytes 1348
  165.8 58.8 %copy-start.16 = (bf16[224]{0:T(256)(128)(2,1)S(1)}, bf16[224]{0:T(256)(128)(2,1)}, u32[]{:S(2)}) copy-start(bf16[224]{0:T(256)(128)(2,1)} %param.35) | copy-start | bytes 1348
  213.5 89.0 %copy-start.1 = (bf16[64,2,4,128]{3,2,1,0:T(4,128)(2,1)S(1)}, bf16[64,2,4,128]{3,2,1,0:T(4,128)(2,1)}, u32[]{:S(2)}) copy-start(bf16[64,2,4,128]{3,2,1,0:T(4,128)(2,1)} %param.19) | copy-start | bytes 393220
Sparse Core Ops, SparseCore 0:
  27.8 36.6 all-gather.4
  78.5 75.0 all-reduce.2
  165.6 47.7 all-reduce.4
  224.7 34.6 reduce-scatter.3
where the time goes:
time: 309 us
  waiting for transfers between devices  159 us (51%)
  blocking collectives  73.8 us (24%)
  matrix products  30.2 us (10%)
  local copies, waits for them, and re-layouts  20.5 us (7%)
  between operations  14.2 us (5%)
  other arithmetic  10.6 us (3%)
    psum x1, waiting for transfers between devices, body(): summed = lax.psum(contrib, 'blk')  75.1 us
    psum x1, waiting for transfers between devices, body(): hidden_sum = lax.psum(up_part, 'page').astype(jnp.float32)  47.7 us
    psum x1, blocking collectives, body(): row_score = lax.psum(score_part, ('page', 'blk'))  39.5 us
    unnamed x5, waiting for transfers between devices  34.8 us
    all_gather x2, blocking collectives, combined_all(): pieces = jax.tree.map(lambda part: lax.all_gather(part, axis), value)  34.3 us
    unnamed x1, matrix products  11 us
    dot_general x1, matrix products, body(): jnp.dot(normed, w_up, preferred_element_type=jnp.float32)  7.54 us
    slice x1, local copies, waits for them, and re-layouts, body(): tail_kv[..., head_dim:]  7.01 us
  transfers between devices with their start and end apart: 4, of which 4 were waited for; matrix products, arithmetic and copies ran while one was open for 0% of the time, Pallas kernels for 0%

commit v1 on v0

--- a/solution.py
+++ b/solution.py
@@ -6,6 +6,7 @@
 from jax.sharding import PartitionSpec as P
 
 NEGATIVE = -1e30
+EPS = 1e-05
 
 
 def combined_all(value, axis, join):
@@ -34,7 +35,255 @@
     return (highest, jnp.sum(weights, axis=-1), weights.astype(jnp.bfloat16))
 
 
+def send_xor(value, axis, distance):
+    size = lax.axis_size(axis)
+    return lax.ppermute(value, axis, [(i, i ^ distance) for i in range(size)])
+
+
+def pick(pieces, index):
+    return lax.dynamic_index_in_dim(pieces, index, 0, keepdims=False)
+
+
+def in_order(pieces, position):
+    stacked = jnp.stack(pieces)
+    out = jnp.zeros_like(stacked)
+    for k, piece in enumerate(pieces):
+        out = lax.dynamic_update_index_in_dim(out, piece, position ^ k, 0)
+    return out
+
+
+def gather_xor(value, axis, distances):
+    return [value] + [send_xor(value, axis, k) for k in distances]
+
+
+def pair_sum(pieces):
+    return (pieces[0] + pieces[1]) + (pieces[2] + pieces[3])
+
+
+def scatter_blk(pieces, blk_pos):
+    pair = pieces.reshape((4, 2) + pieces.shape[1:])
+    core, chip = blk_pos % 2, blk_pos // 2
+    keep = lax.dynamic_index_in_dim(pair, core, 1, keepdims=False)
+    give = lax.dynamic_index_in_dim(pair, 1 - core, 1, keepdims=False)
+    got = send_xor(give.astype(jnp.bfloat16), "blk", 1)
+    both = keep + got.astype(jnp.float32)
+    rounded = both.astype(jnp.bfloat16)
+    arrived = [send_xor(pick(rounded, chip ^ k), "blk", 2 * k) for k in (1, 2, 3)]
+    total = pick(both, chip)
+    for piece in arrived:
+        total = total + piece.astype(jnp.float32)
+    return total
+
+
+def gather_blk(value, blk_pos):
+    core, chip = blk_pos % 2, blk_pos // 2
+    mine = in_order(gather_xor(value, "blk", (2, 4, 6)), chip)
+    other = send_xor(mine, "blk", 1)
+    both = in_order([mine, other], core)
+    return jnp.moveaxis(both, 0, 1).reshape((8,) + value.shape)
+
+
+def prompt_partial(queries, prompt_kv, page_table, prompt_len, sample_prompt):
+    heads_dev, head_dim = queries.shape[2:]
+    slots_dev, page_len = prompt_kv.shape[:2]
+    prompts, pages_max = page_table.shape
+    page_pos = lax.axis_index("page")
+    inv_sqrt = 1.0 / math.sqrt(head_dim)
+    entries = page_table.reshape(-1)
+    slot_ids = page_pos * slots_dev + jnp.arange(slots_dev, dtype=jnp.int32)
+    matched = (entries[:, None] == slot_ids[None, :]).astype(jnp.int32)
+    owner_index = jnp.sum(matched * jnp.arange(entries.shape[0], dtype=jnp.int32)[:, None], axis=0)
+    slot_prompt = owner_index // pages_max
+    slot_page = owner_index % pages_max
+    prompt_pick = (slot_prompt[:, None] == jnp.arange(prompts, dtype=jnp.int32)[None, :]).astype(
+        jnp.int32
+    )
+    slot_limit = jnp.sum(prompt_pick * prompt_len[None, :], axis=1)
+    key_pos = slot_page[:, None] * page_len + jnp.arange(page_len, dtype=jnp.int32)[None, :]
+    key_live = (key_pos < slot_limit[:, None]).reshape(-1)
+    key_prompt = jnp.repeat(slot_prompt, page_len)
+    prompt_visible = ((sample_prompt[:, None] == key_prompt[None, :]) & key_live[None, :])[
+        :, None, None, :
+    ]
+    cache_rows = prompt_kv.reshape(slots_dev * page_len, heads_dev, 2 * head_dim)
+    prompt_scores = (
+        jnp.einsum(
+            "snhd,khd->snhk",
+            queries,
+            cache_rows[:, :, :head_dim],
+            preferred_element_type=jnp.float32,
+        )
+        * inv_sqrt
+    )
+    high_p, sum_p, weights_p = softmax_part(prompt_scores, prompt_visible)
+    mixed_p = jnp.einsum(
+        "snhk,khd->snhd", weights_p, cache_rows[:, :, head_dim:], preferred_element_type=jnp.float32
+    )
+    return high_p, sum_p, mixed_p
+
+
+def tail_partial(queries, tail_kv, tail_len):
+    new_count, heads_dev, head_dim = queries.shape[1:]
+    own_count, tail_max = (tail_kv.shape[0], tail_kv.shape[1])
+    inv_sqrt = 1.0 / math.sqrt(head_dim)
+    first_row = lax.axis_index("page") * own_count
+    own_queries = lax.dynamic_slice_in_dim(queries, first_row, own_count, 0)
+    own_lengths = lax.dynamic_slice_in_dim(tail_len, first_row, own_count, 0)
+    tail_scores = (
+        jnp.einsum(
+            "snhd,sthd->snht",
+            own_queries,
+            tail_kv[..., :head_dim],
+            preferred_element_type=jnp.float32,
+        )
+        * inv_sqrt
+    )
+    reach_pos = own_lengths[:, None] + jnp.arange(new_count, dtype=jnp.int32)[None, :]
+    tail_visible = (
+        jnp.arange(tail_max, dtype=jnp.int32)[None, None, None, :] <= reach_pos[:, :, None, None]
+    )
+    high_t, sum_t, weights_t = softmax_part(tail_scores, tail_visible)
+    mixed_t = jnp.einsum(
+        "snht,sthd->snhd", weights_t, tail_kv[..., head_dim:], preferred_element_type=jnp.float32
+    )
+    return high_t, sum_t, mixed_t
+
+
 def body(
+    queries,
+    prompt_kv,
+    tail_kv,
+    page_table,
+    prompt_len,
+    tail_len,
+    sample_prompt,
+    stream_in,
+    w_out,
+    b_out,
+    ln_gain,
+    ln_bias,
+    w_up,
+    b_up,
+    w_down,
+    b_down,
+    w_score,
+):
+    bf16, f32 = jnp.bfloat16, jnp.float32
+    samples, new_count, heads_dev, head_dim = queries.shape
+    own_count = tail_kv.shape[0]
+    rows = samples * new_count
+    own_rows = own_count * new_count
+    group = ln_gain.shape[0]
+    page_pos = lax.axis_index("page")
+    blk_pos = lax.axis_index("blk")
+    score_group = gather_blk(w_score, blk_pos).reshape(group)
+    image = jnp.dot(w_down, score_group[:, None], preferred_element_type=f32)[:, 0]
+    image = image + send_xor(image, "page", 1)
+    image = image + send_xor(image, "page", 2)
+    high_p, sum_p, mixed_p = prompt_partial(
+        queries, prompt_kv, page_table, prompt_len, sample_prompt
+    )
+    lines = own_rows * heads_dev
+    packed = jnp.concatenate(
+        [
+            mixed_p.reshape(4, lines, head_dim),
+            high_p.reshape(4, lines // head_dim, head_dim),
+            sum_p.reshape(4, lines // head_dim, head_dim),
+        ],
+        axis=1,
+    )
+    shares = [pick(packed, page_pos)] + [
+        send_xor(pick(packed, page_pos ^ k), "page", k) for k in (1, 2, 3)
+    ]
+    merged = tail_partial(queries, tail_kv, tail_len)
+    small = (own_count, new_count, heads_dev)
+    for share in shares:
+        merged = join_partials(
+            merged,
+            (
+                share[lines : lines + lines // head_dim].reshape(small),
+                share[lines + lines // head_dim :].reshape(small),
+                share[:lines].reshape(small + (head_dim,)),
+            ),
+        )
+    own_attention = (
+        (merged[2] / merged[1][..., None]).astype(bf16).reshape(own_rows, heads_dev * head_dim)
+    )
+    attention = in_order(gather_xor(own_attention, "page", (1, 2, 3)), page_pos).reshape(
+        rows, heads_dev * head_dim
+    )
+    first_col = page_pos * group
+    contrib = jnp.dot(
+        attention,
+        lax.dynamic_slice_in_dim(w_out, first_col, group, 1),
+        preferred_element_type=f32,
+    )
+    width = stream_in.shape[2]
+    per_group = group // width
+    own_stream = stream_in.reshape(rows, width).astype(f32)
+    spread = jnp.concatenate(
+        [
+            jnp.where(blk_pos == page_pos * per_group + part, own_stream, 0.0)
+            for part in range(per_group)
+        ],
+        axis=1,
+    )
+    contrib = contrib + spread
+    own_sum = scatter_blk(contrib.reshape(8, rows // 8, group), blk_pos)
+    own_bias = lax.dynamic_slice_in_dim(b_out, first_col, group, 0).astype(f32)
+    residual = gather_blk((own_sum + own_bias).astype(bf16), blk_pos).reshape(rows, group)
+    residual_f = residual.astype(f32)
+    group_mean = jnp.mean(residual_f, axis=1, keepdims=True)
+    centred = residual_f - group_mean
+    group_square = jnp.sum(centred * centred, axis=1, keepdims=True)
+    piece = b_down.shape[0]
+    own_residual = lax.dynamic_slice_in_dim(residual_f, blk_pos * piece, piece, 1)
+    own_base = own_residual + b_down.astype(f32)
+    base_score = jnp.sum(own_base * w_score.astype(f32), axis=1, keepdims=True)
+    gain = ln_gain.astype(f32)
+    lhs = jnp.concatenate(
+        [
+            (centred * gain).astype(bf16),
+            ln_gain[None],
+            ln_bias[None],
+            jnp.zeros((14, group), bf16),
+        ],
+        axis=0,
+    )
+    up_part = jnp.dot(lhs, w_up, preferred_element_type=f32).astype(bf16)
+    units = w_up.shape[1] // 4
+    parts = jnp.stack([up_part[:, j * units : (j + 1) * units] for j in range(4)])
+    up_shares = [pick(parts, page_pos)] + [
+        send_xor(pick(parts, page_pos ^ k), "page", k) for k in (1, 2, 3)
+    ]
+    stats = jnp.concatenate([group_mean, group_square, base_score], axis=1).T
+    all_stats = gather_xor(stats, "page", (1, 2, 3))
+    means = [s[0] for s in all_stats]
+    row_mean = pair_sum(means) * 0.25
+    spread_sq = sum(s[1] + group * (s[0] - row_mean) ** 2 for s in all_stats)
+    inverse_std = lax.rsqrt(spread_sq / (4 * group) + EPS)
+    base_total = pair_sum([s[2] for s in all_stats])
+    total = jnp.zeros((rows, units), f32)
+    shift = jnp.zeros((1, units), f32)
+    for share, mean in zip(up_shares, means):
+        share_f = share.astype(f32)
+        total = total + share_f[:rows] + (mean - row_mean)[:, None] * share_f[rows : rows + 1]
+        shift = shift + share_f[rows + 1 : rows + 2]
+    own_up = lax.dynamic_slice_in_dim(b_up, page_pos * units, units, 0).astype(f32)
+    own_hidden = jnp.maximum(total * inverse_std[:, None] + shift + own_up, 0.0).astype(bf16)
+    hidden_parts = in_order(gather_xor(own_hidden, "page", (1, 2, 3)), page_pos)
+    hidden = jnp.concatenate([hidden_parts[j] for j in range(4)], axis=1)
+    projected = jnp.dot(hidden, w_down, preferred_element_type=f32)
+    out_pieces = jnp.stack([projected[:, j * piece : (j + 1) * piece] for j in range(8)])
+    score = jnp.sum(hidden.astype(f32) * image[None], axis=1) + base_total
+    score = score.reshape(1, rows)
+    score = score + send_xor(score, "blk", 1)
+    output = (scatter_blk(out_pieces, blk_pos) + own_base).astype(bf16)
+    score = pair_sum(gather_xor(score, "blk", (2, 4, 6)))
+    return (output.reshape(samples, new_count, piece), score.reshape(samples, new_count))
+
+
+def general_body(
     queries,
     prompt_kv,
     tail_kv,
@@ -166,6 +415,8 @@
 
 
 def solution(mesh):
+    compute = body if (mesh.shape["page"], mesh.shape["blk"]) == (4, 8) else general_body
+
     placed = (
         P(None, None, "blk", None),
         P("page", None, "blk", None),
@@ -186,7 +437,7 @@
         P(("page", "blk")),
     )
     return jax.shard_map(
-        body,
+        compute,
         mesh=mesh,
         in_specs=placed,
         out_specs=(P(None, None, ("page", "blk")), P()),

time: 309 us -> 148 us (0.48)
  waiting for transfers between devices: 159 us -> 58.3 us
  blocking collectives: 73.8 us -> 0 us
  starting transfers between devices: 0.34 us -> 44 us
  between operations: 14.2 us -> 1.6 us
  matrix products: 30.2 us -> 19.8 us
  other arithmetic: 10.6 us -> 6.71 us
  local copies, waits for them, and re-layouts: 20.5 us -> 17.1 us
    psum x2 -> x0, waiting for transfers between devices: 123 us -> none  [the longest x1 75.1 us: body(): summed = lax.psum(contrib, 'blk')]
    ppermute x0 -> x37, waiting for transfers between devices: none -> 58.3 us  [send_xor(): return lax.ppermute(value, axis, [(i, i ^ distance) for i in range(size)])]
    ppermute x0 -> x37, starting transfers between devices: none -> 44 us  [send_xor(): return lax.ppermute(value, axis, [(i, i ^ distance) for i in range(size)])]
    psum x1 -> x0, blocking collectives: 39.5 us -> none  [body(): row_score = lax.psum(score_part, ('page', 'blk'))]
    unnamed x5 -> x0, waiting for transfers between devices: 34.8 us -> none
    all_gather x2 -> x0, blocking collectives: 34.3 us -> none  [combined_all(): pieces = jax.tree.map(lambda part: lax.all_gather(part, axis), value)]
    unnamed x1 -> x0, matrix products: 11 us -> none
    unnamed x37 -> x36, local copies, waits for them, and re-layouts: 6.98 us -> 3.21 us
  transfers between devices with their start and end apart: 4 -> 37, of which waited for: 4 -> 15; matrix products, arithmetic and copies ran while one was open for 0% -> 20% of each run, Pallas kernels for 0% -> 0%
where the time goes in v1:
time: 148 us; the launch traced here: 147 us
  waiting for transfers between devices  58.3 us (39%)
  starting transfers between devices  44 us (30%)
  matrix products  19.8 us (13%)
  local copies, waits for them, and re-layouts  17.1 us (12%)
  other arithmetic  6.71 us (5%)
  between operations  1.6 us (1%)
    ppermute x37, waiting for transfers between devices, send_xor(): return lax.ppermute(value, axis, [(i, i ^ distance) for i in range(size)])  58.3 us
    ppermute x37, starting transfers between devices, send_xor(): return lax.ppermute(value, axis, [(i, i ^ distance) for i in range(size)])  44 us
    slice x1, local copies, waits for them, and re-layouts, tail_partial(): tail_kv[..., :head_dim]  7.01 us
    dot_general x1, matrix products, body(): up_part = jnp.dot(lhs, w_up, preferred_element_type=f32).astype(bf16)  6.96 us
    dot_general x1, matrix products, body(): jnp.dot(w_down, score_group[:, None], preferred_element_type=f32)[:, 0]  3.42 us
    unnamed x36, local copies, waits for them, and re-layouts  3.21 us
    dot_general x1, matrix products, tail_partial(): jnp.einsum('snht,sthd->snhd', weights_t, tail_kv[..., head_dim:], preferr...  2.96 us
  transfers between devices with their start and end apart: 37, of which 15 were waited for; matrix products, arithmetic and copies ran while one was open for 20% of the time, Pallas kernels for 0%

profile of v1, /device:TPU:0, one launch (start us, length us, event | category | flops | bytes accessed | tf_op | source)
XLA Modules:
  0.0 147.4 jit_solution(6379611934315505875)
XLA Ops:
  2.7 2.0 %copy.190 = bf16[16,64,4,256]{3,1,0,2:T(8,128)(2,1)S(1)} copy(bf16[16,64,4,256]{3,2,1,0:T(4,128)(2,1)} %param.18) | data formatting | bytes 4194304 | tf_op args[1]
  7.6 3.1 %collective-permute-start = (f32[130,128]{1,0:T(8,128)S(1)}, f32[130,128]{1,0:T(8,128)S(1)}, u32[]{:S(2)}, u32[]{:S(2)}) collective-permute-start(f32[130,128]{1,0:T(8,128)S(1)} %get-tuple-element.64), channel_id=1, source_target_pairs={{0,8},{8,0},{16,24},{24,16},{1,9},{9,1},{17,25},{25,17},{2,10},{10... | collective-permute-start | bytes 199688 | tf_op jit(solution)/shard_map/ppermute | solution.py:40
  10.7 2.6 %collective-permute-start.1 = (f32[130,128]{1,0:T(8,128)S(1)}, f32[130,128]{1,0:T(8,128)S(1)}, u32[]{:S(2)}, u32[]{:S(2)}) collective-permute-start(f32[130,128]{1,0:T(8,128)S(1)} %get-tuple-element.66), channel_id=1, source_target_pairs={{0,16},{8,24},{16,0},{24,8},{1,17},{9,25},{17,1},{25,9},{2,18},{10... | collective-permute-start | bytes 199688 | tf_op jit(solution)/shard_map/ppermute | solution.py:40
  14.0 7.0 %fusion.96 = (bf16[16,256,4,128]{3,2,1,0:T(4,128)(2,1)S(1)}, bf16[16,256,4,128]{3,2,1,0:T(4,128)(2,1)}) fusion(bf16[16,256,4,256]{3,2,1,0:T(4,128)(2,1)} %param.19), kind=kLoop, calls=%fused_computation.225 | loop fusion | bytes 16777216 | tf_op jit(solution)/shard_map/slice | solution.py:136
  22.8 3.0 %fusion = f32[16,4,2,128]{3,2,1,0:T(2,128)S(1)} fusion(bf16[16,256,4,128]{3,2,1,0:T(4,128)(2,1)} %get-tuple-element.51, f32[16,2,4,256]{3,1,2,0:T(2,128)S(1)} %get-tuple-element.80, pred[16,2,256]{2,1,0:T(4,128)(4,1)S(1)} %iota_compare_fusion, f32[16,2,4]{1,2,0:T(4,128)S(1)} %get-tuple-element.79), kind=kOutput, calls=%fused_computation.1 | convolution fusion | flops 8486912 | bytes 4399616 | tf_op jit(solution)/shard_map/snht,sthd->snhd/dot_general | solution.py:146
  29.5 3.5 %collective-permute-start.4 = (bf16[32,512]{1,0:T(8,128)(2,1)S(1)}, bf16[32,512]{1,0:T(8,128)(2,1)S(1)}, u32[]{:S(2)}, u32[]{:S(2)}) collective-permute-start(bf16[32,512]{1,0:T(8,128)(2,1)S(1)} %bitcast.320), channel_id=1, source_target_pairs={{0,16},{8,24},{16,0},{24,8},{1,17},{9,25},{17,1},{25,9},{2,18},{10... | collective-permute-start | bytes 98312 | tf_op jit(solution)/shard_map/ppermute | solution.py:40
  33.0 2.2 %collective-permute-done.4 = bf16[32,512]{1,0:T(8,128)(2,1)S(1)} collective-permute-done((bf16[32,512]{1,0:T(8,128)(2,1)S(1)}, bf16[32,512]{1,0:T(8,128)(2,1)S(1)}, u32[]{:S(2)}, u32[]{:S(2)}) %collective-permute-start.4) | collective-permute-done | bytes 32800 | tf_op jit(solution)/shard_map/ppermute | solution.py:40
  35.2 3.5 %collective-permute-done.5 = bf16[32,512]{1,0:T(8,128)(2,1)S(1)} collective-permute-done((bf16[32,512]{1,0:T(8,128)(2,1)S(1)}, bf16[32,512]{1,0:T(8,128)(2,1)S(1)}, u32[]{:S(2)}, u32[]{:S(2)}) %collective-permute-start.5) | collective-permute-done | bytes 32800 | tf_op jit(solution)/shard_map/ppermute | solution.py:40
  38.7 1.9 %convolution_add_fusion = f32[128,1792]{1,0:T(8,128)S(1)} fusion(bf16[128,512]{1,0:T(8,128)(2,1)S(1)} %bitcast.313, bf16[512,7168]{1,0:T(8,128)(2,1)} %param.25, s32[]{:T(128)S(6)} %select_n.174, f32[128,896]{1,0:T(8,128)S(1)} %select_n.180, f32[128,896]{1,0:T(8,128)S(1)} %select_n.177), kind=kOutput, calls=%fused_computation.5 | convolution fusion | flops 235339776 | bytes 3801092 | tf_op jit(solution)/shard_map/dot_general | solution.py:216
  40.8 1.6 %collective-permute-start.27 = (bf16[224]{0:T(256)(128)(2,1)S(1)}, bf16[224]{0:T(256)(128)(2,1)S(1)}, u32[]{:S(2)}, u32[]{:S(2)}) collective-permute-start(bf16[224]{0:T(256)(128)(2,1)S(1)} %copy-done.7), channel_id=1, source_target_pairs={{0,2},{1,3},{2,0},{3,1},{4,6},{5,7},{6,4},{7,5},{8,10},{9,11},{10,... | collective-permute-start | bytes 1352 | tf_op jit(solution)/shard_map/ppermute | solution.py:40
  42.4 1.5 %collective-permute-start.28 = (bf16[224]{0:T(256)(128)(2,1)S(1)}, bf16[224]{0:T(256)(128)(2,1)S(1)}, u32[]{:S(2)}, u32[]{:S(2)}) collective-permute-start(bf16[224]{0:T(256)(128)(2,1)S(1)} %copy-done.7), channel_id=1, source_target_pairs={{0,4},{1,5},{2,6},{3,7},{4,0},{5,1},{6,2},{7,3},{8,12},{9,13},{10,... | collective-permute-start | bytes 1352 | tf_op jit(solution)/shard_map/ppermute | solution.py:40
  45.5 2.1 %collective-permute-start.9 = (bf16[16,1792]{1,0:T(8,128)(2,1)S(1)}, bf16[16,1792]{1,0:T(8,128)(2,1)S(1)}, u32[]{:S(2)}, u32[]{:S(2)}) collective-permute-start(bf16[16,1792]{1,0:T(8,128)(2,1)S(1)} %get-tuple-element.71), channel_id=1, source_target_pairs={{0,6},{1,7},{2,4},{3,5},{4,2},{5,3},{6,0},{7,1},{8,14},{9,15},{10,... | collective-permute-start | bytes 172040 | tf_op jit(solution)/shard_map/ppermute | solution.py:40
  49.3 3.5 %collective-permute-done.29 = bf16[224]{0:T(256)(128)(2,1)S(1)} collective-permute-done((bf16[224]{0:T(256)(128)(2,1)S(1)}, bf16[224]{0:T(256)(128)(2,1)S(1)}, u32[]{:S(2)}, u32[]{:S(2)}) %collective-permute-start.29) | collective-permute-done | bytes 480 | tf_op jit(solution)/shard_map/ppermute | solution.py:40
  55.9 2.1 %collective-permute-start.12 = (bf16[16,1792]{1,0:T(8,128)(2,1)S(1)}, bf16[16,1792]{1,0:T(8,128)(2,1)S(1)}, u32[]{:S(2)}, u32[]{:S(2)}) collective-permute-start(bf16[16,1792]{1,0:T(8,128)(2,1)S(1)} %get-tuple-element.38), channel_id=1, source_target_pairs={{0,6},{1,7},{2,4},{3,5},{4,2},{5,3},{6,0},{7,1},{8,14},{9,15},{10,... | collective-permute-start | bytes 172040 | tf_op jit(solution)/shard_map/ppermute | solution.py:40
  59.2 1.8 %collective-permute-done.12 = bf16[16,1792]{1,0:T(8,128)(2,1)S(1)} collective-permute-done((bf16[16,1792]{1,0:T(8,128)(2,1)S(1)}, bf16[16,1792]{1,0:T(8,128)(2,1)S(1)}, u32[]{:S(2)}, u32[]{:S(2)}) %collective-permute-start.12) | collective-permute-done | bytes 57376 | tf_op jit(solution)/shard_map/ppermute | solution.py:40
  61.1 1.4 collective-permute-done.13
  64.4 3.5 %collective-permute-start.16 = (f32[3,128]{1,0:T(4,128)S(1)}, f32[3,128]{1,0:T(4,128)S(1)}, u32[]{:S(2)}, u32[]{:S(2)}) collective-permute-start(f32[3,128]{1,0:T(4,128)S(1)} %maximum_bitcast_fusion), channel_id=1, source_target_pairs={{0,24},{8,16},{16,8},{24,0},{1,25},{9,17},{17,9},{25,1},{2,26},{10... | collective-permute-start | bytes 4616 | tf_op jit(solution)/shard_map/ppermute | solution.py:40
  68.2 7.0 %convolution_convert_fusion = bf16[144,3584]{1,0:T(8,128)(2,1)S(1)} fusion(bf16[1792,3584]{1,0:T(8,128)(2,1)} %param.29, bf16[1,1792]{1,0:T(2,128)(2,1)S(1)} %broadcast_in_dim.205, bf16[1,1792]{1,0:T(2,128)(2,1)S(1)} %broadcast_in_dim.204, bf16[128,1792]{1,0:T(8,128)(2,1)S(1)} %multiply_convert_fusion, bf16[144]{0:T(256)(128)(2,1)S(1)} %pad.14.clone), kind=kOutput, calls=%fused_computation | convolution fusion | flops 1852268544 | bytes 14343456 | tf_op jit(solution)/shard_map/dot_general | solution.py:253
  76.5 3.5 %collective-permute-start.19 = (bf16[144,896]{1,0:T(8,128)(2,1)S(1)}, bf16[144,896]{1,0:T(8,128)(2,1)S(1)}, u32[]{:S(2)}, u32[]{:S(2)}) collective-permute-start(bf16[144,896]{1,0:T(8,128)(2,1)S(1)} %get-tuple-element.53), channel_id=1, source_target_pairs={{0,24},{8,16},{16,8},{24,0},{1,25},{9,17},{17,9},{25,1},{2,26},{10... | collective-permute-start | bytes 774152 | tf_op jit(solution)/shard_map/ppermute | solution.py:40
  80.0 6.8 %collective-permute-done.17 = bf16[144,896]{1,0:T(8,128)(2,1)S(1)} collective-permute-done((bf16[144,896]{1,0:T(8,128)(2,1)S(1)}, bf16[144,896]{1,0:T(8,128)(2,1)S(1)}, u32[]{:S(2)}, u32[]{:S(2)}) %collective-permute-start.17) | collective-permute-done | bytes 258080 | tf_op jit(solution)/shard_map/ppermute | solution.py:40
  86.9 9.9 %collective-permute-done.18 = bf16[144,896]{1,0:T(8,128)(2,1)S(1)} collective-permute-done((bf16[144,896]{1,0:T(8,128)(2,1)S(1)}, bf16[144,896]{1,0:T(8,128)(2,1)S(1)}, u32[]{:S(2)}, u32[]{:S(2)}) %collective-permute-start.18) | collective-permute-done | bytes 258080 | tf_op jit(solution)/shard_map/ppermute | solution.py:40
  97.4 4.4 %collective-permute-start.20 = (bf16[128,896]{1,0:T(8,128)(2,1)S(1)}, bf16[128,896]{1,0:T(8,128)(2,1)S(1)}, u32[]{:S(2)}, u32[]{:S(2)}) collective-permute-start(bf16[128,896]{1,0:T(8,128)(2,1)S(1)} %get-tuple-element.31), channel_id=1, source_target_pairs={{0,8},{8,0},{16,24},{24,16},{1,9},{9,1},{17,25},{25,17},{2,10},{10... | collective-permute-start | bytes 688136 | tf_op jit(solution)/shard_map/ppermute | solution.py:40
  101.8 3.4 %convolution_reduce_fusion = f32[3584]{0:T(1024)S(1)} fusion(bf16[1792,1]{0,1:T(2,128)(2,1)S(1)} %reshape.574, bf16[3584,1792]{1,0:T(8,128)(2,1)S(1)} %bitcast.303), kind=kOutput, calls=%fused_computation.18 | convolution fusion | flops 12845056 | bytes 12862976 | tf_op jit(solution)/shard_map/dot_general | solution.py:180
  105.4 3.7 %collective-permute-done.31 = f32[3584]{0:T(1024)S(1)} collective-permute-done((f32[3584]{0:T(1024)S(1)}, f32[3584]{0:T(1024)S(1)}, u32[]{:S(2)}, u32[]{:S(2)}) %collective-permute-start.31) | collective-permute-done | bytes 14368 | tf_op jit(solution)/shard_map/ppermute | solution.py:40
  109.1 9.5 %collective-permute-done.32 = f32[3584]{0:T(1024)S(1)} collective-permute-done((f32[3584]{0:T(1024)S(1)}, f32[3584]{0:T(1024)S(1)}, u32[]{:S(2)}, u32[]{:S(2)}) %collective-permute-start.32) | collective-permute-done | bytes 14368 | tf_op jit(solution)/shard_map/ppermute | solution.py:40
  118.6 1.5 collective-permute-start.22
  120.1 10.5 %collective-permute-done.21 = bf16[128,896]{1,0:T(8,128)(2,1)S(1)} collective-permute-done((bf16[128,896]{1,0:T(8,128)(2,1)S(1)}, bf16[128,896]{1,0:T(8,128)(2,1)S(1)}, u32[]{:S(2)}, u32[]{:S(2)}) %collective-permute-start.21) | collective-permute-done | bytes 229408 | tf_op jit(solution)/shard_map/ppermute | solution.py:40
  130.7 2.0 %fusion.42 = f32[128,1792]{1,0:T(8,128)S(1)} fusion(bf16[3584,1792]{1,0:T(8,128)(2,1)S(1)} %bitcast.303, bf16[128,896]{1,0:T(8,128)(2,1)S(1)} %get-tuple-element.61, bf16[128,896]{1,0:T(8,128)(2,1)S(1)} %get-tuple-element.62, bf16[128,896]{1,0:T(8,128)(2,1)S(1)} %get-tuple-element.63, bf16[128,896]{1,0:T(8,128)(2,1)S(1)} %get-tuple-element.60), kind=kOutput, calls=%fused_computation.81 | convolution fusion | flops 1647837184 | bytes 14680064 | tf_op jit(solution)/shard_map/dot_general | solution.py:276
  136.3 1.5 %collective-permute-start.35 = (f32[1,128]{1,0:T(1,128)S(1)}, f32[1,128]{1,0:T(1,128)S(1)}, u32[]{:S(2)}, u32[]{:S(2)}) collective-permute-start(f32[1,128]{1,0:T(1,128)S(1)} %add.527), channel_id=1, source_target_pairs={{0,4},{1,5},{2,6},{3,7},{4,0},{5,1},{6,2},{7,3},{8,12},{9,13},{10,... | collective-permute-start | bytes 1544 | tf_op jit(solution)/shard_map/ppermute | solution.py:40
  140.0 1.5 %collective-permute-start.25 = (bf16[128,224]{1,0:T(8,128)(2,1)S(1)}, bf16[128,224]{1,0:T(8,128)(2,1)S(1)}, u32[]{:S(2)}, u32[]{:S(2)}) collective-permute-start(bf16[128,224]{1,0:T(8,128)(2,1)S(1)} %get-tuple-element.69), channel_id=1, source_target_pairs={{0,4},{1,5},{2,6},{3,7},{4,0},{5,1},{6,2},{7,3},{8,12},{9,13},{10,... | collective-permute-start | bytes 172040 | tf_op jit(solution)/shard_map/ppermute | solution.py:40
  143.3 1.6 %collective-permute-done.25 = bf16[128,224]{1,0:T(8,128)(2,1)S(1)} collective-permute-done((bf16[128,224]{1,0:T(8,128)(2,1)S(1)}, bf16[128,224]{1,0:T(8,128)(2,1)S(1)}, u32[]{:S(2)}, u32[]{:S(2)}) %collective-permute-start.25) | collective-permute-done | bytes 57376 | tf_op jit(solution)/shard_map/ppermute | solution.py:40
  144.9 1.7 %collective-permute-done.26 = bf16[128,224]{1,0:T(8,128)(2,1)S(1)} collective-permute-done((bf16[128,224]{1,0:T(8,128)(2,1)S(1)}, bf16[128,224]{1,0:T(8,128)(2,1)S(1)}, u32[]{:S(2)}, u32[]{:S(2)}) %collective-permute-start.26) | collective-permute-done | bytes 57376 | tf_op jit(solution)/shard_map/ppermute | solution.py:40
  (221 shorter events, 31.3 us)
Async XLA Ops:
  7.6 19.2 %collective-permute-start = (f32[130,128]{1,0:T(8,128)S(1)}, f32[130,128]{1,0:T(8,128)S(1)}, u32[]{:S(2)}, u32[]{:S(2)}) collective-permute-start(f32[130,128]{1,0:T(8,128)S(1)} %get-tuple-element.64), channel_id=1, source_target_pairs={{0,8},{8,0},{16,24},{24,16},{1,9},{9,1},{17,25},{25,17},{2,10},{10... | collective-permute-start | bytes 199688 | tf_op jit(solution)/shard_map/ppermute | solution.py:40
  10.7 16.1 %collective-permute-start.1 = (f32[130,128]{1,0:T(8,128)S(1)}, f32[130,128]{1,0:T(8,128)S(1)}, u32[]{:S(2)}, u32[]{:S(2)}) collective-permute-start(f32[130,128]{1,0:T(8,128)S(1)} %get-tuple-element.66), channel_id=1, source_target_pairs={{0,16},{8,24},{16,0},{24,8},{1,17},{9,25},{17,1},{25,9},{2,18},{10... | collective-permute-start | bytes 199688 | tf_op jit(solution)/shard_map/ppermute | solution.py:40
  13.2 14.5 %collective-permute-start.2 = (f32[130,128]{1,0:T(8,128)S(1)}, f32[130,128]{1,0:T(8,128)S(1)}, u32[]{:S(2)}, u32[]{:S(2)}) collective-permute-start(f32[130,128]{1,0:T(8,128)S(1)} %get-tuple-element.65), channel_id=1, source_target_pairs={{0,24},{8,16},{16,8},{24,0},{1,25},{9,17},{17,9},{25,1},{2,26},{10... | collective-permute-start | bytes 199688 | tf_op jit(solution)/shard_map/ppermute | solution.py:40
  28.5 4.5 %collective-permute-start.3 = (bf16[32,512]{1,0:T(8,128)(2,1)S(1)}, bf16[32,512]{1,0:T(8,128)(2,1)S(1)}, u32[]{:S(2)}, u32[]{:S(2)}) collective-permute-start(bf16[32,512]{1,0:T(8,128)(2,1)S(1)} %bitcast.319), channel_id=1, source_target_pairs={{0,8},{8,0},{16,24},{24,16},{1,9},{9,1},{17,25},{25,17},{2,10},{10... | collective-permute-start | bytes 98312 | tf_op jit(solution)/shard_map/ppermute | solution.py:40
  29.5 5.7 %collective-permute-start.4 = (bf16[32,512]{1,0:T(8,128)(2,1)S(1)}, bf16[32,512]{1,0:T(8,128)(2,1)S(1)}, u32[]{:S(2)}, u32[]{:S(2)}) collective-permute-start(bf16[32,512]{1,0:T(8,128)(2,1)S(1)} %bitcast.320), channel_id=1, source_target_pairs={{0,16},{8,24},{16,0},{24,8},{1,17},{9,25},{17,1},{25,9},{2,18},{10... | collective-permute-start | bytes 98312 | tf_op jit(solution)/shard_map/ppermute | solution.py:40
  33.0 5.7 %collective-permute-start.5 = (bf16[32,512]{1,0:T(8,128)(2,1)S(1)}, bf16[32,512]{1,0:T(8,128)(2,1)S(1)}, u32[]{:S(2)}, u32[]{:S(2)}) collective-permute-start(bf16[32,512]{1,0:T(8,128)(2,1)S(1)} %bitcast.321), channel_id=1, source_target_pairs={{0,24},{8,16},{16,8},{24,0},{1,25},{9,17},{17,9},{25,1},{2,26},{10... | collective-permute-start | bytes 98312 | tf_op jit(solution)/shard_map/ppermute | solution.py:40
  40.8 7.5 %collective-permute-start.27 = (bf16[224]{0:T(256)(128)(2,1)S(1)}, bf16[224]{0:T(256)(128)(2,1)S(1)}, u32[]{:S(2)}, u32[]{:S(2)}) collective-permute-start(bf16[224]{0:T(256)(128)(2,1)S(1)} %copy-done.7), channel_id=1, source_target_pairs={{0,2},{1,3},{2,0},{3,1},{4,6},{5,7},{6,4},{7,5},{8,10},{9,11},{10,... | collective-permute-start | bytes 1352 | tf_op jit(solution)/shard_map/ppermute | solution.py:40
  42.4 6.9 %collective-permute-start.28 = (bf16[224]{0:T(256)(128)(2,1)S(1)}, bf16[224]{0:T(256)(128)(2,1)S(1)}, u32[]{:S(2)}, u32[]{:S(2)}) collective-permute-start(bf16[224]{0:T(256)(128)(2,1)S(1)} %copy-done.7), channel_id=1, source_target_pairs={{0,4},{1,5},{2,6},{3,7},{4,0},{5,1},{6,2},{7,3},{8,12},{9,13},{10,... | collective-permute-start | bytes 1352 | tf_op jit(solution)/shard_map/ppermute | solution.py:40
  44.0 8.9 %collective-permute-start.7 = (bf16[16,1792]{1,0:T(8,128)(2,1)S(1)}, bf16[16,1792]{1,0:T(8,128)(2,1)S(1)}, u32[]{:S(2)}, u32[]{:S(2)}) collective-permute-start(bf16[16,1792]{1,0:T(8,128)(2,1)S(1)} %get-tuple-element.70), channel_id=1, source_target_pairs={{0,2},{1,3},{2,0},{3,1},{4,6},{5,7},{6,4},{7,5},{8,10},{9,11},{10,... | collective-permute-start | bytes 172040 | tf_op jit(solution)/shard_map/ppermute | solution.py:40
  44.6 8.3 %collective-permute-start.8 = (bf16[16,1792]{1,0:T(8,128)(2,1)S(1)}, bf16[16,1792]{1,0:T(8,128)(2,1)S(1)}, u32[]{:S(2)}, u32[]{:S(2)}) collective-permute-start(bf16[16,1792]{1,0:T(8,128)(2,1)S(1)} %get-tuple-element.72), channel_id=1, source_target_pairs={{0,4},{1,5},{2,6},{3,7},{4,0},{5,1},{6,2},{7,3},{8,12},{9,13},{10,... | collective-permute-start | bytes 172040 | tf_op jit(solution)/shard_map/ppermute | solution.py:40
  45.5 7.5 %collective-permute-start.9 = (bf16[16,1792]{1,0:T(8,128)(2,1)S(1)}, bf16[16,1792]{1,0:T(8,128)(2,1)S(1)}, u32[]{:S(2)}, u32[]{:S(2)}) collective-permute-start(bf16[16,1792]{1,0:T(8,128)(2,1)S(1)} %get-tuple-element.71), channel_id=1, source_target_pairs={{0,6},{1,7},{2,4},{3,5},{4,2},{5,3},{6,0},{7,1},{8,14},{9,15},{10,... | collective-permute-start | bytes 172040 | tf_op jit(solution)/shard_map/ppermute | solution.py:40
  48.3 4.5 %collective-permute-start.29 = (bf16[224]{0:T(256)(128)(2,1)S(1)}, bf16[224]{0:T(256)(128)(2,1)S(1)}, u32[]{:S(2)}, u32[]{:S(2)}) collective-permute-start(bf16[224]{0:T(256)(128)(2,1)S(1)} %copy-done.7), channel_id=1, source_target_pairs={{0,6},{1,7},{2,4},{3,5},{4,2},{5,3},{6,0},{7,1},{8,14},{9,15},{10,... | collective-permute-start | bytes 1352 | tf_op jit(solution)/shard_map/ppermute | solution.py:40
  53.0 4.9 %collective-permute-start.10 = (bf16[16,1792]{1,0:T(8,128)(2,1)S(1)}, bf16[16,1792]{1,0:T(8,128)(2,1)S(1)}, u32[]{:S(2)}, u32[]{:S(2)}) collective-permute-start(bf16[16,1792]{1,0:T(8,128)(2,1)S(1)} %get-tuple-element.38), channel_id=1, source_target_pairs={{0,2},{1,3},{2,0},{3,1},{4,6},{5,7},{6,4},{7,5},{8,10},{9,11},{10,... | collective-permute-start | bytes 172040 | tf_op jit(solution)/shard_map/ppermute | solution.py:40
  54.9 4.2 %collective-permute-start.11 = (bf16[16,1792]{1,0:T(8,128)(2,1)S(1)}, bf16[16,1792]{1,0:T(8,128)(2,1)S(1)}, u32[]{:S(2)}, u32[]{:S(2)}) collective-permute-start(bf16[16,1792]{1,0:T(8,128)(2,1)S(1)} %get-tuple-element.38), channel_id=1, source_target_pairs={{0,4},{1,5},{2,6},{3,7},{4,0},{5,1},{6,2},{7,3},{8,12},{9,13},{10,... | collective-permute-start | bytes 172040 | tf_op jit(solution)/shard_map/ppermute | solution.py:40
  55.9 5.1 %collective-permute-start.12 = (bf16[16,1792]{1,0:T(8,128)(2,1)S(1)}, bf16[16,1792]{1,0:T(8,128)(2,1)S(1)}, u32[]{:S(2)}, u32[]{:S(2)}) collective-permute-start(bf16[16,1792]{1,0:T(8,128)(2,1)S(1)} %get-tuple-element.38), channel_id=1, source_target_pairs={{0,6},{1,7},{2,4},{3,5},{4,2},{5,3},{6,0},{7,1},{8,14},{9,15},{10,... | collective-permute-start | bytes 172040 | tf_op jit(solution)/shard_map/ppermute | solution.py:40
  63.4 13.1 %collective-permute-start.14 = (f32[3,128]{1,0:T(4,128)S(1)}, f32[3,128]{1,0:T(4,128)S(1)}, u32[]{:S(2)}, u32[]{:S(2)}) collective-permute-start(f32[3,128]{1,0:T(4,128)S(1)} %maximum_bitcast_fusion), channel_id=1, source_target_pairs={{0,8},{8,0},{16,24},{24,16},{1,9},{9,1},{17,25},{25,17},{2,10},{10... | collective-permute-start | bytes 4616 | tf_op jit(solution)/shard_map/ppermute | solution.py:40
  63.5 16.5 %collective-permute-start.15 = (f32[3,128]{1,0:T(4,128)S(1)}, f32[3,128]{1,0:T(4,128)S(1)}, u32[]{:S(2)}, u32[]{:S(2)}) collective-permute-start(f32[3,128]{1,0:T(4,128)S(1)} %maximum_bitcast_fusion), channel_id=1, source_target_pairs={{0,16},{8,24},{16,0},{24,8},{1,17},{9,25},{17,1},{25,9},{2,18},{10... | collective-permute-start | bytes 4616 | tf_op jit(solution)/shard_map/ppermute | solution.py:40
  64.4 15.6 %collective-permute-start.16 = (f32[3,128]{1,0:T(4,128)S(1)}, f32[3,128]{1,0:T(4,128)S(1)}, u32[]{:S(2)}, u32[]{:S(2)}) collective-permute-start(f32[3,128]{1,0:T(4,128)S(1)} %maximum_bitcast_fusion), channel_id=1, source_target_pairs={{0,24},{8,16},{16,8},{24,0},{1,25},{9,17},{17,9},{25,1},{2,26},{10... | collective-permute-start | bytes 4616 | tf_op jit(solution)/shard_map/ppermute | solution.py:40
  75.5 11.3 %collective-permute-start.17 = (bf16[144,896]{1,0:T(8,128)(2,1)S(1)}, bf16[144,896]{1,0:T(8,128)(2,1)S(1)}, u32[]{:S(2)}, u32[]{:S(2)}) collective-permute-start(bf16[144,896]{1,0:T(8,128)(2,1)S(1)} %get-tuple-element.55), channel_id=1, source_target_pairs={{0,8},{8,0},{16,24},{24,16},{1,9},{9,1},{17,25},{25,17},{2,10},{10... | collective-permute-start | bytes 774152 | tf_op jit(solution)/shard_map/ppermute | solution.py:40
  75.6 21.2 %collective-permute-start.18 = (bf16[144,896]{1,0:T(8,128)(2,1)S(1)}, bf16[144,896]{1,0:T(8,128)(2,1)S(1)}, u32[]{:S(2)}, u32[]{:S(2)}) collective-permute-start(bf16[144,896]{1,0:T(8,128)(2,1)S(1)} %get-tuple-element.54), channel_id=1, source_target_pairs={{0,16},{8,24},{16,0},{24,8},{1,17},{9,25},{17,1},{25,9},{2,18},{10... | collective-permute-start | bytes 774152 | tf_op jit(solution)/shard_map/ppermute | solution.py:40
  76.5 20.3 %collective-permute-start.19 = (bf16[144,896]{1,0:T(8,128)(2,1)S(1)}, bf16[144,896]{1,0:T(8,128)(2,1)S(1)}, u32[]{:S(2)}, u32[]{:S(2)}) collective-permute-start(bf16[144,896]{1,0:T(8,128)(2,1)S(1)} %get-tuple-element.53), channel_id=1, source_target_pairs={{0,24},{8,16},{16,8},{24,0},{1,25},{9,17},{17,9},{25,1},{2,26},{10... | collective-permute-start | bytes 774152 | tf_op jit(solution)/shard_map/ppermute | solution.py:40
  97.4 22.6 %collective-permute-start.20 = (bf16[128,896]{1,0:T(8,128)(2,1)S(1)}, bf16[128,896]{1,0:T(8,128)(2,1)S(1)}, u32[]{:S(2)}, u32[]{:S(2)}) collective-permute-start(bf16[128,896]{1,0:T(8,128)(2,1)S(1)} %get-tuple-element.31), channel_id=1, source_target_pairs={{0,8},{8,0},{16,24},{24,16},{1,9},{9,1},{17,25},{25,17},{2,10},{10... | collective-permute-start | bytes 688136 | tf_op jit(solution)/shard_map/ppermute | solution.py:40
  109.1 9.5 %collective-permute-start.32 = (f32[3584]{0:T(1024)S(1)}, f32[3584]{0:T(1024)S(1)}, u32[]{:S(2)}, u32[]{:S(2)}) collective-permute-start(f32[3584]{0:T(1024)S(1)} %add.521), channel_id=1, source_target_pairs={{0,16},{8,24},{16,0},{24,8},{1,17},{9,25},{17,1},{25,9},{2,18},{10... | collective-permute-start | bytes 43016 | tf_op jit(solution)/shard_map/ppermute | solution.py:40
  118.6 12.0 %collective-permute-start.21 = (bf16[128,896]{1,0:T(8,128)(2,1)S(1)}, bf16[128,896]{1,0:T(8,128)(2,1)S(1)}, u32[]{:S(2)}, u32[]{:S(2)}) collective-permute-start(bf16[128,896]{1,0:T(8,128)(2,1)S(1)} %get-tuple-element.31), channel_id=1, source_target_pairs={{0,16},{8,24},{16,0},{24,8},{1,17},{9,25},{17,1},{25,9},{2,18},{10... | collective-permute-start | bytes 688136 | tf_op jit(solution)/shard_map/ppermute | solution.py:40
  118.6 12.0 %collective-permute-start.22 = (bf16[128,896]{1,0:T(8,128)(2,1)S(1)}, bf16[128,896]{1,0:T(8,128)(2,1)S(1)}, u32[]{:S(2)}, u32[]{:S(2)}) collective-permute-start(bf16[128,896]{1,0:T(8,128)(2,1)S(1)} %get-tuple-element.31), channel_id=1, source_target_pairs={{0,24},{8,16},{16,8},{24,0},{1,25},{9,17},{17,9},{25,1},{2,26},{10... | collective-permute-start | bytes 688136 | tf_op jit(solution)/shard_map/ppermute | solution.py:40
  133.4 5.2 %collective-permute-start.23 = (bf16[4,128,224]{2,1,0:T(8,128)(2,1)S(1)}, bf16[4,128,224]{2,1,0:T(8,128)(2,1)S(1)}, u32[]{:S(2)}, u32[]{:S(2)}) collective-permute-start(bf16[4,128,224]{2,1,0:T(8,128)(2,1)S(1)} %fusion.39), channel_id=1, source_target_pairs={{0,1},{1,0},{2,3},{3,2},{4,5},{5,4},{6,7},{7,6},{8,9},{9,8},{10,11... | collective-permute-start | bytes 688136 | tf_op jit(solution)/shard_map/ppermute | solution.py:40
  135.1 6.3 %collective-permute-start.34 = (f32[1,128]{1,0:T(1,128)S(1)}, f32[1,128]{1,0:T(1,128)S(1)}, u32[]{:S(2)}, u32[]{:S(2)}) collective-permute-start(f32[1,128]{1,0:T(1,128)S(1)} %add.527), channel_id=1, source_target_pairs={{0,2},{1,3},{2,0},{3,1},{4,6},{5,7},{6,4},{7,5},{8,10},{9,11},{10,... | collective-permute-start | bytes 1544 | tf_op jit(solution)/shard_map/ppermute | solution.py:40
  136.3 6.0 %collective-permute-start.35 = (f32[1,128]{1,0:T(1,128)S(1)}, f32[1,128]{1,0:T(1,128)S(1)}, u32[]{:S(2)}, u32[]{:S(2)}) collective-permute-start(f32[1,128]{1,0:T(1,128)S(1)} %add.527), channel_id=1, source_target_pairs={{0,4},{1,5},{2,6},{3,7},{4,0},{5,1},{6,2},{7,3},{8,12},{9,13},{10,... | collective-permute-start | bytes 1544 | tf_op jit(solution)/shard_map/ppermute | solution.py:40
  137.8 4.5 %collective-permute-start.36 = (f32[1,128]{1,0:T(1,128)S(1)}, f32[1,128]{1,0:T(1,128)S(1)}, u32[]{:S(2)}, u32[]{:S(2)}) collective-permute-start(f32[1,128]{1,0:T(1,128)S(1)} %add.527), channel_id=1, source_target_pairs={{0,6},{1,7},{2,4},{3,5},{4,2},{5,3},{6,0},{7,1},{8,14},{9,15},{10,... | collective-permute-start | bytes 1544 | tf_op jit(solution)/shard_map/ppermute | solution.py:40
  138.8 4.6 %collective-permute-start.24 = (bf16[128,224]{1,0:T(8,128)(2,1)S(1)}, bf16[128,224]{1,0:T(8,128)(2,1)S(1)}, u32[]{:S(2)}, u32[]{:S(2)}) collective-permute-start(bf16[128,224]{1,0:T(8,128)(2,1)S(1)} %get-tuple-element.67), channel_id=1, source_target_pairs={{0,2},{1,3},{2,0},{3,1},{4,6},{5,7},{6,4},{7,5},{8,10},{9,11},{10,... | collective-permute-start | bytes 172040 | tf_op jit(solution)/shard_map/ppermute | solution.py:40
  140.0 5.0 %collective-permute-start.25 = (bf16[128,224]{1,0:T(8,128)(2,1)S(1)}, bf16[128,224]{1,0:T(8,128)(2,1)S(1)}, u32[]{:S(2)}, u32[]{:S(2)}) collective-permute-start(bf16[128,224]{1,0:T(8,128)(2,1)S(1)} %get-tuple-element.69), channel_id=1, source_target_pairs={{0,4},{1,5},{2,6},{3,7},{4,0},{5,1},{6,2},{7,3},{8,12},{9,13},{10,... | collective-permute-start | bytes 172040 | tf_op jit(solution)/shard_map/ppermute | solution.py:40
  141.5 5.2 %collective-permute-start.26 = (bf16[128,224]{1,0:T(8,128)(2,1)S(1)}, bf16[128,224]{1,0:T(8,128)(2,1)S(1)}, u32[]{:S(2)}, u32[]{:S(2)}) collective-permute-start(bf16[128,224]{1,0:T(8,128)(2,1)S(1)} %get-tuple-element.68), channel_id=1, source_target_pairs={{0,6},{1,7},{2,4},{3,5},{4,2},{5,3},{6,0},{7,1},{8,14},{9,15},{10,... | collective-permute-start | bytes 172040 | tf_op jit(solution)/shard_map/ppermute | solution.py:40
  (18 other events, 213.6 us)

commit v2 on v0

--- a/solution.py
+++ b/solution.py
@@ -1,11 +1,17 @@
+import functools
 import math
 
 import jax
 import jax.numpy as jnp
 from jax import lax
+from jax.experimental import pallas as pl
+from jax.experimental.pallas import tpu as pltpu
 from jax.sharding import PartitionSpec as P
 
 NEGATIVE = -1e30
+EPS = 1e-05
+VMEM_LIMIT = 24 * 2**20
+FREE = pl.CostEstimate(flops=0, bytes_accessed=0, transcendentals=0)
 
 
 def combined_all(value, axis, join):
@@ -34,7 +40,761 @@
     return (highest, jnp.sum(weights, axis=-1), weights.astype(jnp.bfloat16))
 
 
+def send_xor(value, axis, distance):
+    size = lax.axis_size(axis)
+    return lax.ppermute(value, axis, [(i, i ^ distance) for i in range(size)])
+
+
+def in_hbm(value):
+    return pltpu.with_memory_space_constraint(value, pltpu.HBM)
+
+
+def in_order(pieces, position):
+    stacked = jnp.stack(pieces)
+    out = jnp.zeros_like(stacked)
+    for k, piece in enumerate(pieces):
+        out = lax.dynamic_update_index_in_dim(out, piece, position ^ k, 0)
+    return out
+
+
+def gather_xor(value, axis, distances):
+    return [value] + [send_xor(value, axis, k) for k in distances]
+
+
+def pair_sum(pieces):
+    return (pieces[0] + pieces[1]) + (pieces[2] + pieces[3])
+
+
+def gather_blk(value, blk_pos):
+    core, chip = blk_pos % 2, blk_pos // 2
+    mine = in_order(gather_xor(value, "blk", (2, 4, 6)), chip)
+    other = send_xor(mine, "blk", 1)
+    both = in_order([mine, other], core)
+    return jnp.moveaxis(both, 0, 1).reshape((8,) + value.shape)
+
+
+def flat_rows(ref_value):
+    shape = ref_value.shape
+    return ref_value.reshape(math.prod(shape[:-1]), shape[-1])
+
+
+def prompt_kernel(scale, table_hbm, len_hbm, prompt_hbm, q_hbm, kv_hbm, *refs):
+    outs, scratch = refs[:4], refs[4:]
+    table_ref, len_ref, prompt_ref, q_ref, kv_ref, where_ref, code_ref, rows_ref, sems = scratch
+    copies = [
+        pltpu.make_async_copy(source, target, sems.at[i])
+        for i, (source, target) in enumerate(
+            (
+                (kv_hbm, kv_ref),
+                (q_hbm, q_ref),
+                (table_hbm, table_ref),
+                (len_hbm, len_ref),
+                (prompt_hbm, prompt_ref),
+            )
+        )
+    ]
+    for copy in copies:
+        copy.start()
+    prompts, pages_max = table_ref.shape
+    slots, page_len, heads, _ = kv_ref.shape
+    samples, new = q_ref.shape[:2]
+    dim = q_ref.shape[3]
+    lines = outs[0].shape[0] - 8
+    bf16, f32 = jnp.bfloat16, jnp.float32
+    page_pos = lax.axis_index("page")
+    first = page_pos * slots
+    for copy in copies[2:]:
+        copy.wait()
+    for p in range(prompts):
+        for g in range(pages_max):
+            slot = table_ref[p, g] - first
+            here = jnp.logical_and(slot >= 0, slot < slots)
+            where_ref[jnp.where(here, slot, slots)] = p * pages_max + g
+    row8 = lax.broadcasted_iota(jnp.int32, (new * heads, dim), 0)
+    lane8 = lax.broadcasted_iota(jnp.int32, (new * heads, dim), 1)
+    target = lane8 - row8 % heads
+    for s in range(samples):
+        code_ref[pl.ds(s * new * heads, new * heads), :] = jnp.where(
+            target == prompt_ref[s] * heads, 1.0, 0.0
+        )
+    per_slot = page_len * heads
+    row = lax.broadcasted_iota(jnp.int32, (per_slot, dim), 0)
+    lane = lax.broadcasted_iota(jnp.int32, (per_slot, dim), 1)
+    lane_code = lane - row % heads
+    penalties = []
+    for j in range(slots):
+        entry = where_ref[j]
+        prompt = entry // pages_max
+        left = (len_ref[prompt] - (entry % pages_max) * page_len) * heads
+        own = jnp.logical_and(lane_code == prompt * heads, row < left)
+        penalties.append(jnp.where(own, 0.0, NEGATIVE).astype(bf16))
+    copies[1].wait()
+    rows_ref[:, :dim] = flat_rows(q_ref[...])
+    rows_ref[:, dim:] = code_ref[...].astype(bf16)
+    copies[0].wait()
+    cache = flat_rows(kv_ref[...])
+    keys = jnp.concatenate([cache[:, :dim], jnp.concatenate(penalties, axis=0)], axis=1)
+    values = cache[:, dim:]
+    for k in (3, 2, 1, 0):
+        start = pl.multiple_of((page_pos ^ k) * lines, lines)
+        scores = lax.dot_general(
+            rows_ref[pl.ds(start, lines), :],
+            keys,
+            (((1,), (1,)), ((), ())),
+            preferred_element_type=f32,
+        )
+        best = jnp.max(scores, axis=1, keepdims=True)
+        weights = jnp.exp2((scores - best) * scale)
+        norm = jnp.sum(weights, axis=1, keepdims=True)
+        outs[k][0:lines, :] = jnp.dot(weights.astype(bf16), values, preferred_element_type=f32)
+        outs[k][lines : lines + 1, :] = jnp.broadcast_to(best, (lines, lines)).T[0:1]
+        outs[k][lines + 1 : lines + 2, :] = jnp.broadcast_to(norm, (lines, lines)).T[0:1]
+
+
+def prompt_partial(queries, prompt_kv, page_table, prompt_len, sample_prompt):
+    samples, new, heads, dim = queries.shape
+    slots = prompt_kv.shape[0]
+    total = samples * new * heads
+    lines = total // 4
+    anywhere = pl.BlockSpec(memory_space=pl.ANY)
+    vmem = pl.BlockSpec(memory_space=pltpu.VMEM)
+    return pl.pallas_call(
+        functools.partial(prompt_kernel, math.log2(math.e) / math.sqrt(dim)),
+        in_specs=[anywhere] * 5,
+        out_specs=[vmem] * 4,
+        out_shape=[jax.ShapeDtypeStruct((lines + 8, dim), jnp.float32)] * 4,
+        scratch_shapes=[
+            pltpu.SMEM(page_table.shape, jnp.int32),
+            pltpu.SMEM(prompt_len.shape, jnp.int32),
+            pltpu.SMEM(sample_prompt.shape, jnp.int32),
+            pltpu.VMEM(queries.shape, queries.dtype),
+            pltpu.VMEM(prompt_kv.shape, prompt_kv.dtype),
+            pltpu.SMEM((slots + 1,), jnp.int32),
+            pltpu.VMEM((total, dim), jnp.float32),
+            pltpu.VMEM((total, 2 * dim), jnp.bfloat16),
+            pltpu.SemaphoreType.DMA((5,)),
+        ],
+        compiler_params=pltpu.CompilerParams(vmem_limit_bytes=VMEM_LIMIT),
+        name="prompt_attention",
+    )(*map(in_hbm, (page_table, prompt_len, sample_prompt, queries, prompt_kv)))
+
+
+def tail_kernel(scale, len_ref, q_ref, kv_ref, out_ref, best_ref, norm_ref):
+    per, length, heads, _ = kv_ref.shape
+    new, dim = q_ref.shape[1], q_ref.shape[3]
+    lines = new * heads
+    bf16, f32 = jnp.bfloat16, jnp.float32
+    step = pl.program_id(0)
+    first = (lax.axis_index("page") * pl.num_programs(0) + step) * per
+    row = lax.broadcasted_iota(jnp.int32, (lines, length * heads), 0)
+    col = lax.broadcasted_iota(jnp.int32, (lines, length * heads), 1)
+    same_head = row % heads == col % heads
+    ahead = jnp.where(same_head, col // heads - row // heads, length + new)
+    for i in range(per):
+        cache = flat_rows(kv_ref[i])
+        scores = lax.dot_general(
+            flat_rows(q_ref[i]),
+            cache[:, :dim],
+            (((1,), (1,)), ((), ())),
+            preferred_element_type=f32,
+        )
+        scores = jnp.where(ahead <= len_ref[first + i], scores, NEGATIVE)
+        best = jnp.max(scores, axis=1, keepdims=True)
+        weights = jnp.exp2((scores - best) * scale)
+        norm = jnp.sum(weights, axis=1, keepdims=True)
+        at = pl.ds(pl.multiple_of((step * per + i) * lines, lines), lines)
+        out_ref[at, :] = jnp.dot(weights.astype(bf16), cache[:, dim:], preferred_element_type=f32)
+        best_ref[at, :] = jnp.broadcast_to(best, (lines, dim))
+        norm_ref[at, :] = jnp.broadcast_to(norm, (lines, dim))
+
+    @pl.when(step == pl.num_programs(0) - 1)
+    def _():
+        total = out_ref.shape[0] - 8
+        out_ref[total : total + 1, :] = best_ref[...].T[0:1]
+        out_ref[total + 1 : total + 2, :] = norm_ref[...].T[0:1]
+
+
+def tail_partial(queries, tail_kv, tail_len):
+    _, new, heads, dim = queries.shape
+    own, length = tail_kv.shape[:2]
+    per = math.gcd(own, 4)
+    steps = own // per
+    lines = own * new * heads
+    return pl.pallas_call(
+        functools.partial(tail_kernel, math.log2(math.e) / math.sqrt(dim)),
+        grid=(steps,),
+        in_specs=[
+            pl.BlockSpec(memory_space=pltpu.SMEM),
+            pl.BlockSpec(
+                (per, new, heads, dim), lambda i: (lax.axis_index("page") * steps + i, 0, 0, 0)
+            ),
+            pl.BlockSpec((per, length, heads, 2 * dim), lambda i: (i, 0, 0, 0)),
+        ],
+        out_specs=pl.BlockSpec((lines + 8, dim), lambda i: (0, 0)),
+        out_shape=jax.ShapeDtypeStruct((lines + 8, dim), jnp.float32),
+        scratch_shapes=[pltpu.VMEM((lines, dim), jnp.float32)] * 2,
+        compiler_params=pltpu.CompilerParams(vmem_limit_bytes=VMEM_LIMIT),
+        cost_estimate=FREE,
+        name="tail_attention",
+    )(*map(in_hbm, (tail_len, queries, tail_kv)))
+
+
+def merge_kernel(scale, *refs):
+    parts, out_ref, held_ref = refs[:-2], refs[-2], refs[-1]
+    lines, dim = held_ref.shape
+    heads = out_ref.shape[1] // dim
+    bests = [part[lines : lines + 1, :] for part in parts]
+    best = functools.reduce(jnp.maximum, bests)
+    scales = [jnp.exp2((one - best) * scale) for one in bests]
+    norm = sum(factor * part[lines + 1 : lines + 2, :] for factor, part in zip(scales, parts))
+    total = jnp.zeros((lines, dim), jnp.float32)
+    for factor, part in zip(scales, parts):
+        share = jnp.broadcast_to(factor / norm, (lines, lines)).T
+        total = total + share * part[0:lines, :]
+    held_ref[...] = total
+    for h in range(heads):
+        out_ref[:, h * dim : (h + 1) * dim] = held_ref[
+            pl.ds(h, lines // heads, stride=heads), :
+        ].astype(out_ref.dtype)
+
+
+def merge_partials(parts, heads):
+    lines, dim = parts[0].shape[0] - 8, parts[0].shape[1]
+    vmem = pl.BlockSpec(memory_space=pltpu.VMEM)
+    return pl.pallas_call(
+        functools.partial(merge_kernel, math.log2(math.e) / math.sqrt(dim)),
+        in_specs=[vmem] * len(parts),
+        out_specs=vmem,
+        out_shape=jax.ShapeDtypeStruct((lines // heads, heads * dim), jnp.bfloat16),
+        scratch_shapes=[pltpu.VMEM((lines, dim), jnp.float32)],
+        compiler_params=pltpu.CompilerParams(vmem_limit_bytes=VMEM_LIMIT),
+        name="merge_partials",
+    )(*parts)
+
+
+def project_kernel(per_group, *refs):
+    blocks, (w_ref, stream_ref, keep_ref, give_ref, lhs_ref, sum_ref) = refs[:4], refs[4:]
+    page_pos, blk_pos = lax.axis_index("page"), lax.axis_index("blk")
+    height = blocks[0].shape[0]
+    rows, group = lhs_ref.shape[0], w_ref.shape[1]
+    width = stream_ref.shape[2]
+    for k, block in enumerate(blocks):
+        start = pl.multiple_of((page_pos ^ k) * height, height)
+        lhs_ref[pl.ds(start, height), :] = block[...]
+    product = jnp.dot(lhs_ref[...], w_ref[...], preferred_element_type=jnp.float32)
+    sum_ref[...] = product.reshape(sum_ref.shape)
+    for part in range(per_group):
+
+        @pl.when(blk_pos == page_pos * per_group + part)
+        def _(part=part):
+            stream = flat_rows(stream_ref[...]).astype(jnp.float32)
+            at = (slice(None), slice(None), slice(part * width, (part + 1) * width))
+            sum_ref[at] = sum_ref[at] + stream.reshape(sum_ref.shape[:2] + (width,))
+
+    core = blk_pos % 2
+    for chip in range(4):
+        keep_ref[chip] = sum_ref[2 * chip + core]
+        give_ref[chip] = sum_ref[2 * chip + 1 - core].astype(give_ref.dtype)
+
+
+def project(blocks, w_out, stream_in, group):
+    height, depth = blocks[0].shape
+    rows = 4 * height
+    vmem = pl.BlockSpec(memory_space=pltpu.VMEM)
+    part = (4, rows // 8, group)
+    return pl.pallas_call(
+        functools.partial(project_kernel, group // stream_in.shape[2]),
+        grid=(1,),
+        in_specs=[vmem] * 4
+        + [pl.BlockSpec((depth, group), lambda i: (0, lax.axis_index("page"))), vmem],
+        out_specs=[vmem] * 2,
+        out_shape=[
+            jax.ShapeDtypeStruct(part, jnp.float32),
+            jax.ShapeDtypeStruct(part, jnp.bfloat16),
+        ],
+        scratch_shapes=[
+            pltpu.VMEM((rows, depth), jnp.bfloat16),
+            pltpu.VMEM((8, rows // 8, group), jnp.float32),
+        ],
+        compiler_params=pltpu.CompilerParams(vmem_limit_bytes=VMEM_LIMIT),
+        name="project_attention",
+    )(*blocks, in_hbm(w_out), stream_in)
+
+
+def pair_kernel(keep_ref, got_ref, own_ref, *out_refs):
+    chip = lax.axis_index("blk") // 2
+    own_ref[...] = keep_ref[chip] + got_ref[chip].astype(jnp.float32)
+    for k, out_ref in enumerate(out_refs, 1):
+        total = keep_ref[chip ^ k] + got_ref[chip ^ k].astype(jnp.float32)
+        out_ref[...] = total.astype(out_ref.dtype)
+
+
+def pair_pieces(keep, got):
+    vmem = pl.BlockSpec(memory_space=pltpu.VMEM)
+    shape = keep.shape[1:]
+    return pl.pallas_call(
+        pair_kernel,
+        in_specs=[vmem] * 2,
+        out_specs=[vmem] * 4,
+        out_shape=[jax.ShapeDtypeStruct(shape, jnp.float32)]
+        + [jax.ShapeDtypeStruct(shape, jnp.bfloat16)] * 3,
+        compiler_params=pltpu.CompilerParams(vmem_limit_bytes=VMEM_LIMIT),
+        name="pair_pieces",
+    )(keep, got)
+
+
+def residual_kernel(own_ref, a_ref, b_ref, c_ref, bias_ref, out_ref):
+    total = own_ref[...] + bias_ref[...].astype(jnp.float32)
+    for ref in (a_ref, b_ref, c_ref):
+        total = total + ref[...].astype(jnp.float32)
+    out_ref[...] = total.astype(out_ref.dtype)
+
+
+def residual_rows(own, arrived, b_out):
+    vmem = pl.BlockSpec(memory_space=pltpu.VMEM)
+    return pl.pallas_call(
+        residual_kernel,
+        grid=(1,),
+        in_specs=[vmem] * 4
+        + [pl.BlockSpec((1, own.shape[1]), lambda i: (0, lax.axis_index("page")))],
+        out_specs=vmem,
+        out_shape=jax.ShapeDtypeStruct(own.shape, jnp.bfloat16),
+        compiler_params=pltpu.CompilerParams(vmem_limit_bytes=VMEM_LIMIT),
+        name="residual_rows",
+    )(own, *arrived, b_out.reshape(1, -1))
+
+
+def split2(value):
+    high = value.astype(jnp.bfloat16)
+    return high, (value - high.astype(jnp.float32)).astype(jnp.bfloat16)
+
+
+def whole2(high, low):
+    return high.astype(jnp.float32) + low.astype(jnp.float32)
+
+
+def start_copies(copies):
+    for copy in copies:
+        copy.start()
+    return copies
+
+
+def shard_copies(w_hbm, w_ref, sems, shards, axis):
+    page_pos = lax.axis_index("page")
+    units = w_ref.shape[1 + axis]
+    copies = []
+    for i, k in enumerate(shards):
+        at = pl.ds(pl.multiple_of((page_pos ^ k) * units, 128), units)
+        source = w_hbm.at[:, at] if axis else w_hbm.at[at, :]
+        copies.append(pltpu.make_async_copy(source, w_ref.at[i], sems.at[i]))
+    return start_copies(copies)
+
+
+def up_first_kernel(*refs):
+    blocks, refs = refs[:8], refs[8:]
+    gain_ref, bias_ref, score_ref, down_ref, w_hbm = refs[:5]
+    out_refs, refs = refs[5:8], refs[8:]
+    lhs_ref, residual_ref, stats_ref, mean_ref, square_ref, base_ref, w_ref, sems = refs
+    copies = shard_copies(w_hbm, w_ref, sems, (3, 2, 1), 1)
+    blk_pos = lax.axis_index("blk")
+    core, chip = blk_pos % 2, blk_pos // 2
+    height, group = blocks[0].shape
+    rows = 8 * height
+    gain = gain_ref[...].astype(jnp.float32)
+    fixed = jnp.sum(down_ref[...] * score_ref[...], axis=1, keepdims=True)
+    for i, block in enumerate(blocks):
+        from_core = core if i < 4 else 1 - core
+        start = pl.multiple_of((2 * (chip ^ (i % 4)) + from_core) * height, height)
+        at = pl.ds(start, height)
+        residual = block[...].astype(jnp.float32)
+        mean = jnp.sum(residual, axis=1, keepdims=True) * (1.0 / group)
+        centred = residual - mean
+        square = jnp.sum(centred * centred, axis=1, keepdims=True)
+        base = jnp.sum(residual * score_ref[...], axis=1, keepdims=True) + fixed
+        residual_ref[at, :] = block[...]
+        lhs_ref[at, :] = (centred * gain).astype(lhs_ref.dtype)
+        mean_ref[at, :] = jnp.broadcast_to(mean, (height, rows))
+        square_ref[at, :] = jnp.broadcast_to(square, (height, rows))
+        base_ref[at, :] = jnp.broadcast_to(base, (height, rows))
+    row = lax.broadcasted_iota(jnp.int32, (lhs_ref.shape[0] - rows, group), 0)
+    bias = bias_ref[...].astype(jnp.float32)
+    lhs_ref[rows:, :] = jnp.where(
+        row == 0, gain, jnp.where(row == 1, bias, 0.0)
+    ).astype(lhs_ref.dtype)
+    pieces = []
+    for ref in (mean_ref, square_ref, base_ref):
+        pieces += split2(ref[...].T[0:1])
+    stats_ref[...] = jnp.concatenate(pieces, axis=0)
+    for i, out_ref in enumerate(out_refs):
+        copies[i].wait()
+        up_product(lhs_ref, w_ref.at[i], stats_ref, out_ref, rows)
+
+
+def up_product(lhs_ref, w_ref, stats_ref, out_ref, rows):
+    product = jnp.dot(lhs_ref[...], w_ref[...], preferred_element_type=jnp.float32)
+    below = product[rows : rows + 8]
+    padded = jnp.concatenate(
+        [
+            jnp.zeros((2, rows), jnp.float32),
+            stats_ref[...].astype(jnp.float32),
+        ],
+        axis=0,
+    )
+    row = lax.broadcasted_iota(jnp.int32, (8, rows), 0)
+    first = jnp.where(row < 2, below[:, :rows], padded)
+    out_ref[0:rows, :] = product[:rows].astype(out_ref.dtype)
+    out_ref[rows : rows + 8, :] = jnp.concatenate([first, below[:, rows:]], axis=1).astype(
+        out_ref.dtype
+    )
+
+
+def up_first(blocks, ln_gain, ln_bias, score_row, down_row, w_up):
+    height, group = blocks[0].shape
+    rows = 8 * height
+    units = w_up.shape[1] // 4
+    bf16, f32 = jnp.bfloat16, jnp.float32
+    vmem = pl.BlockSpec(memory_space=pltpu.VMEM)
+    return pl.pallas_call(
+        up_first_kernel,
+        in_specs=[vmem] * 12 + [pl.BlockSpec(memory_space=pl.ANY)],
+        out_specs=[vmem] * 6,
+        out_shape=[pltpu.VMEM((rows + 8, units), bf16)] * 3
+        + [
+            pltpu.VMEM((rows + 16, group), bf16),
+            jax.ShapeDtypeStruct((rows, group), bf16),
+            pltpu.VMEM((6, rows), bf16),
+        ],
+        scratch_shapes=[pltpu.VMEM((rows, rows), f32)] * 3
+        + [pltpu.VMEM((3, group, units), bf16), pltpu.SemaphoreType.DMA((3,))],
+        compiler_params=pltpu.CompilerParams(vmem_limit_bytes=VMEM_LIMIT),
+        name="norm_and_up",
+    )(
+        *blocks,
+        ln_gain.reshape(1, group),
+        ln_bias.reshape(1, group),
+        score_row,
+        down_row,
+        in_hbm(w_up),
+    )
+
+
+def up_second_kernel(lhs_ref, stats_ref, w_hbm, out_ref, w_ref, sems):
+    copies = shard_copies(w_hbm, w_ref, sems, (0,), 1)
+    copies[0].wait()
+    up_product(lhs_ref, w_ref.at[0], stats_ref, out_ref, stats_ref.shape[1])
+
+
+def up_second(lhs, stats, w_up):
+    group = lhs.shape[1]
+    units = w_up.shape[1] // 4
+    bf16 = jnp.bfloat16
+    vmem = pl.BlockSpec(memory_space=pltpu.VMEM)
+    return pl.pallas_call(
+        up_second_kernel,
+        in_specs=[vmem] * 2 + [pl.BlockSpec(memory_space=pl.ANY)],
+        out_specs=vmem,
+        out_shape=pltpu.VMEM((stats.shape[1] + 8, units), bf16),
+        scratch_shapes=[pltpu.VMEM((1, group, units), bf16), pltpu.SemaphoreType.DMA((1,))],
+        compiler_params=pltpu.CompilerParams(vmem_limit_bytes=VMEM_LIMIT),
+        cost_estimate=FREE,
+        name="up_own",
+    )(lhs, stats, in_hbm(w_up))
+
+
+def image_kernel(score_ref, w_ref, out_ref):
+    image = lax.dot_general(
+        score_ref[...], w_ref[...], (((1,), (1,)), ((), ())), preferred_element_type=jnp.float32
+    )
+    step = pl.program_id(0)
+    high, low = split2(image)
+    out_ref[pl.ds(step, 1), :] = high[0:1].astype(jnp.float32)
+    out_ref[pl.ds(step + pl.num_programs(0), 1), :] = low[0:1].astype(jnp.float32)
+
+
+def image_of(score_group, w_down):
+    depth, group = w_down.shape
+    tile = depth // 4
+    lhs = jnp.broadcast_to(score_group.reshape(1, group), (8, group))
+    return pl.pallas_call(
+        image_kernel,
+        grid=(4,),
+        in_specs=[
+            pl.BlockSpec((8, group), lambda i: (0, 0)),
+            pl.BlockSpec((tile, group), lambda i: (i, 0)),
+        ],
+        out_specs=pl.BlockSpec((8, tile), lambda i: (0, 0)),
+        out_shape=jax.ShapeDtypeStruct((8, tile), jnp.float32),
+        compiler_params=pltpu.CompilerParams(vmem_limit_bytes=VMEM_LIMIT),
+        cost_estimate=FREE,
+        name="score_image",
+    )(lhs, in_hbm(w_down))
+
+
+def hidden_kernel(group, a_ref, b_ref, c_ref, d_ref, bias_ref, image_ref, out_ref, base_ref):
+    parts = (a_ref, b_ref, c_ref, d_ref)
+    rows = a_ref.shape[0] - 8
+    f32 = jnp.float32
+    tails = [part[rows : rows + 8, :].astype(f32) for part in parts]
+    stats = [
+        [tail[2 + i : 3 + i, :rows] + tail[3 + i : 4 + i, :rows] for tail in tails]
+        for i in (0, 2, 4)
+    ]
+    means, squares, bases = stats
+    row_mean = pair_sum(means) * 0.25
+    shifts = [mean - row_mean for mean in means]
+    spread = sum(square + group * shift * shift for square, shift in zip(squares, shifts))
+    inverse = lax.rsqrt(spread * (0.25 / group) + EPS)
+    pad = jnp.zeros((rows - 6, rows), f32)
+    columns = jnp.concatenate([inverse, *shifts, pair_sum(bases), pad], axis=0).T
+    total = parts[0][0:rows, :].astype(f32) + columns[:, 1:2] * tails[0][0:1]
+    for k in (1, 2, 3):
+        total = total + parts[k][0:rows, :].astype(f32) + columns[:, 1 + k : 2 + k] * tails[k][0:1]
+    offset = sum(tail[1:2] for tail in tails) + bias_ref[...].astype(f32)
+    hidden = jnp.maximum(total * columns[:, 0:1] + offset, 0.0)
+    out_ref[0:rows, :] = hidden.astype(out_ref.dtype)
+    out_ref[rows : rows + 8, :] = image_ref[...].astype(out_ref.dtype)
+    base_ref[...] = columns[:, 5:6]
+
+
+def own_hidden_units(parts, b_up, image, group):
+    vmem = pl.BlockSpec(memory_space=pltpu.VMEM)
+    height, units = parts[0].shape
+    return pl.pallas_call(
+        functools.partial(hidden_kernel, group),
+        grid=(1,),
+        in_specs=[vmem] * 4
+        + [pl.BlockSpec((1, units), lambda i: (0, lax.axis_index("page"))), vmem],
+        out_specs=[vmem] * 2,
+        out_shape=[
+            jax.ShapeDtypeStruct((height, units), jnp.bfloat16),
+            jax.ShapeDtypeStruct((height - 8, 1), jnp.float32),
+        ],
+        compiler_params=pltpu.CompilerParams(vmem_limit_bytes=VMEM_LIMIT),
+        name="hidden_units",
+    )(*parts, b_up.reshape(1, -1), image)
+
+
+def down_first_kernel(hidden_ref, w_hbm, sum_ref, held_ref, w_ref, sems, held_sems):
+    rows = sum_ref.shape[0]
+    copies = shard_copies(w_hbm, w_ref, sems, (0,), 0)
+    held = shard_copies(w_hbm, held_ref, held_sems, (1, 2, 3), 0)
+    copies[0].wait()
+    sum_ref[...] = jnp.dot(
+        hidden_ref[0:rows, :], w_ref[0], preferred_element_type=jnp.float32
+    )
+    for copy in held:
+        copy.wait()
+
+
+def down_first(hidden, w_down):
+    rows, units = hidden.shape[0] - 8, hidden.shape[1]
+    group = w_down.shape[1]
+    vmem = pl.BlockSpec(memory_space=pltpu.VMEM)
+    return pl.pallas_call(
+        down_first_kernel,
+        in_specs=[vmem, pl.BlockSpec(memory_space=pl.ANY)],
+        out_specs=[vmem] * 2,
+        out_shape=[
+            pltpu.VMEM((rows, group), jnp.float32),
+            pltpu.VMEM((3, units, group), jnp.bfloat16),
+        ],
+        scratch_shapes=[
+            pltpu.VMEM((1, units, group), jnp.bfloat16),
+            pltpu.SemaphoreType.DMA((1,)),
+            pltpu.SemaphoreType.DMA((3,)),
+        ],
+        compiler_params=pltpu.CompilerParams(vmem_limit_bytes=VMEM_LIMIT),
+        cost_estimate=FREE,
+        name="down_own",
+    )(hidden, in_hbm(w_down))
+
+
+def down_rest_kernel(base_ref, sum_ref, held_ref, *refs):
+    hiddens, (keep_ref, give_ref, score_ref, image_ref) = refs[:4], refs[4:]
+    rows = sum_ref.shape[0]
+    f32 = jnp.float32
+    page_pos = lax.axis_index("page")
+    core = lax.axis_index("blk") % 2
+    piece = keep_ref.shape[2]
+    product = sum_ref[...]
+    for k in (1, 2, 3):
+        product = product + jnp.dot(
+            hiddens[k][0:rows, :], held_ref[k - 1], preferred_element_type=f32
+        )
+    tails = [ref[rows : rows + 8, :].astype(f32) for ref in hiddens]
+    image_ref[...] = pair_sum([tail[0:4] + tail[4:8] for tail in tails])
+    score = base_ref[...]
+    by_owner = []
+    for k, ref in enumerate(hiddens):
+        image = image_ref[pl.ds(page_pos ^ k, 1), :]
+        by_owner.append(jnp.sum(ref[0:rows, :].astype(f32) * image, axis=1, keepdims=True))
+    score = score + pair_sum(by_owner)
+    score_ref[...] = score
+    pieces = split3(score)
+    for chip in range(4):
+        pair = [product[:, (2 * chip + c) * piece : (2 * chip + c + 1) * piece] for c in range(2)]
+        keep_ref[chip] = jnp.where(core == 0, pair[0], pair[1])
+        give_ref[chip, :, :piece] = jnp.where(core == 0, pair[1], pair[0]).astype(give_ref.dtype)
+        give_ref[chip, :, piece:] = pieces
+
+
+def down_rest(base, summed, held, hiddens):
+    rows, group = summed.shape
+    units = hiddens[0].shape[1]
+    vmem = pl.BlockSpec(memory_space=pltpu.VMEM)
+    return pl.pallas_call(
+        down_rest_kernel,
+        in_specs=[vmem] * 7,
+        out_specs=[vmem] * 3,
+        out_shape=[
+            pltpu.VMEM((4, rows, group // 8), jnp.float32),
+            jax.ShapeDtypeStruct((4, rows, group // 8 + 3), jnp.bfloat16),
+            pltpu.VMEM((rows, 1), jnp.float32),
+        ],
+        scratch_shapes=[pltpu.VMEM((4, units), jnp.float32)],
+        compiler_params=pltpu.CompilerParams(vmem_limit_bytes=VMEM_LIMIT),
+        name="down_rest",
+    )(base, summed, held, *hiddens)
+
+
+def split3(value):
+    high = value.astype(jnp.bfloat16)
+    left = value - high.astype(jnp.float32)
+    middle = left.astype(jnp.bfloat16)
+    low = (left - middle.astype(jnp.float32)).astype(jnp.bfloat16)
+    return jnp.concatenate([high, middle, low], axis=1)
+
+
+def whole3(pieces):
+    return jnp.sum(pieces.astype(jnp.float32), axis=1, keepdims=True)
+
+
+def pair_score_kernel(keep_ref, score_ref, got_ref, own_ref, both_ref, *out_refs):
+    chip = lax.axis_index("blk") // 2
+    piece = keep_ref.shape[2]
+    score = whole3(split3(score_ref[...])) + whole3(got_ref[0, :, piece:])
+    both_ref[...] = score
+    pieces = split3(score)
+    own_ref[...] = keep_ref[chip] + got_ref[chip, :, :piece].astype(jnp.float32)
+    for k, out_ref in enumerate(out_refs, 1):
+        total = keep_ref[chip ^ k] + got_ref[chip ^ k, :, :piece].astype(jnp.float32)
+        out_ref[:, :piece] = total.astype(out_ref.dtype)
+        out_ref[:, piece:] = pieces
+
+
+def pair_scores(keep, score, got):
+    vmem = pl.BlockSpec(memory_space=pltpu.VMEM)
+    _, rows, piece = keep.shape
+    return pl.pallas_call(
+        pair_score_kernel,
+        in_specs=[vmem] * 3,
+        out_specs=[vmem] * 5,
+        out_shape=[
+            jax.ShapeDtypeStruct((rows, piece), jnp.float32),
+            jax.ShapeDtypeStruct((rows, 1), jnp.float32),
+        ]
+        + [jax.ShapeDtypeStruct((rows, piece + 3), jnp.bfloat16)] * 3,
+        compiler_params=pltpu.CompilerParams(vmem_limit_bytes=VMEM_LIMIT),
+        name="pair_scores",
+    )(keep, score, got)
+
+
+def finish_kernel(own_ref, base_ref, score_ref, a_ref, b_ref, c_ref, out_ref, total_ref, held_ref):
+    piece = own_ref.shape[1]
+    total = own_ref[...] + base_ref[...]
+    for ref in (a_ref, b_ref, c_ref):
+        total = total + ref[:, :piece].astype(jnp.float32)
+    out_ref[...] = total.astype(out_ref.dtype).reshape(out_ref.shape)
+    scores = [whole3(ref[:, piece:]) for ref in (a_ref, b_ref, c_ref)]
+    own_score = whole3(split3(score_ref[...]))
+    score = (own_score + scores[0]) + (scores[1] + scores[2])
+    new, samples = total_ref.shape
+    held_ref[...] = jnp.broadcast_to(score, held_ref.shape)
+    for n in range(new):
+        total_ref[n : n + 1, :] = held_ref[pl.ds(n, samples, stride=new), :].T[0:1]
+
+
+def finish(own, base, score, arrived, samples):
+    vmem = pl.BlockSpec(memory_space=pltpu.VMEM)
+    rows, piece = own.shape
+    return pl.pallas_call(
+        finish_kernel,
+        in_specs=[vmem] * 6,
+        out_specs=[vmem] * 2,
+        out_shape=[
+            jax.ShapeDtypeStruct((samples, rows // samples, piece), jnp.bfloat16),
+            jax.ShapeDtypeStruct((rows // samples, samples), jnp.float32),
+        ],
+        scratch_shapes=[pltpu.VMEM((rows, 128), jnp.float32)],
+        compiler_params=pltpu.CompilerParams(vmem_limit_bytes=VMEM_LIMIT),
+        name="finish",
+    )(own, base, score, *arrived)
+
+
 def body(
+    queries,
+    prompt_kv,
+    tail_kv,
+    page_table,
+    prompt_len,
+    tail_len,
+    sample_prompt,
+    stream_in,
+    w_out,
+    b_out,
+    ln_gain,
+    ln_bias,
+    w_up,
+    b_up,
+    w_down,
+    b_down,
+    w_score,
+):
+    bf16, f32 = jnp.bfloat16, jnp.float32
+    samples, new_count, heads_dev, head_dim = queries.shape
+    group = ln_gain.shape[0]
+    blk_pos = lax.axis_index("blk")
+    piece = b_down.shape[0]
+    packed = prompt_partial(queries, prompt_kv, page_table, prompt_len, sample_prompt)
+    shares = [packed[0]] + [send_xor(packed[k], "page", k) for k in (1, 2, 3)]
+    tail = tail_partial(queries, tail_kv, tail_len)
+    own_attention = merge_partials(shares + [tail], heads_dev)
+    attention = gather_xor(own_attention, "page", (1, 2, 3))
+    w_score_late, own_attention = lax.optimization_barrier((w_score, own_attention))
+    score_group = gather_blk(w_score_late, blk_pos).reshape(group)
+    keep, give = project(attention, w_out, stream_in, group)
+    own, *pieces = pair_pieces(keep, send_xor(give, "blk", 1))
+    arrived = [send_xor(rounded, "blk", 2 * k) for k, rounded in enumerate(pieces, 1)]
+    same_core = gather_xor(residual_rows(own, arrived, b_out), "blk", (2, 4, 6))
+    blocks = same_core + [send_xor(block, "blk", 1) for block in same_core]
+    score_row, down_row = [
+        lax.dynamic_update_slice_in_dim(
+            jnp.zeros((group,), f32), vector.astype(f32), blk_pos * piece, 0
+        ).reshape(1, group)
+        for vector in (w_score, b_down)
+    ]
+    part3, part2, part1, lhs, residual, stats = up_first(
+        blocks, ln_gain, ln_bias, score_row, down_row, w_up
+    )
+    part0 = up_second(lhs, stats, w_up)
+    image = image_of(score_group, w_down)
+    parts = [part0] + [
+        send_xor(part, "page", k) for k, part in ((1, part1), (2, part2), (3, part3))
+    ]
+    own_hidden, base_score = own_hidden_units(parts, b_up, image, group)
+    hiddens = gather_xor(own_hidden, "page", (1, 2, 3))
+    summed, held = down_first(own_hidden, w_down)
+    keep, give, score = down_rest(base_score, summed, held, hiddens)
+    own_base = lax.dynamic_slice_in_dim(residual, blk_pos * piece, piece, 1).astype(
+        f32
+    ) + b_down.astype(f32)
+    own, score, *pieces = pair_scores(keep, score, send_xor(give, "blk", 1))
+    arrived = [send_xor(piece_k, "blk", 2 * k) for k, piece_k in enumerate(pieces, 1)]
+    output, score = finish(own, own_base, score, arrived, samples)
+    return (output, score.T)
+
+
+def general_body(
     queries,
     prompt_kv,
     tail_kv,
@@ -166,6 +926,8 @@
 
 
 def solution(mesh):
+    compute = body if (mesh.shape["page"], mesh.shape["blk"]) == (4, 8) else general_body
+
     placed = (
         P(None, None, "blk", None),
         P("page", None, "blk", None),
@@ -186,7 +948,7 @@
         P(("page", "blk")),
     )
     return jax.shard_map(
-        body,
+        compute,
         mesh=mesh,
         in_specs=placed,
         out_specs=(P(None, None, ("page", "blk")), P()),

time: 309 us -> 114 us (0.37)
  waiting for transfers between devices: 159 us -> 38.7 us
  blocking collectives: 73.8 us -> 0 us
  Pallas kernels: 0 us -> 39.2 us
  starting transfers between devices: 0.34 us -> 33.8 us
  matrix products: 30.2 us -> 0 us
  local copies, waits for them, and re-layouts: 20.5 us -> 0.96 us
  between operations: 14.2 us -> 1.07 us
  other arithmetic: 10.6 us -> 0.09 us
    psum x2 -> x0, waiting for transfers between devices: 123 us -> none  [the longest x1 75.1 us: body(): summed = lax.psum(contrib, 'blk')]
    psum x1 -> x0, blocking collectives: 39.5 us -> none  [body(): row_score = lax.psum(score_part, ('page', 'blk'))]
    pallas_call x0 -> x14, Pallas kernels: none -> 39.2 us  [the longest x1 7.13 us: tail_partial(): pl.pallas_call(functools.partial(tail_kernel, math.log2(math.e) / math.sq...]
    ppermute x0 -> x31, waiting for transfers between devices: none -> 38.7 us  [send_xor(): return lax.ppermute(value, axis, [(i, i ^ distance) for i in range(size)])]
    unnamed x5 -> x0, waiting for transfers between devices: 34.8 us -> none
    all_gather x2 -> x0, blocking collectives: 34.3 us -> none  [combined_all(): pieces = jax.tree.map(lambda part: lax.all_gather(part, axis), value)]
    ppermute x0 -> x31, starting transfers between devices: none -> 33.8 us  [send_xor(): return lax.ppermute(value, axis, [(i, i ^ distance) for i in range(size)])]
    dot_general x6 -> x0, matrix products: 19.2 us -> none  [the longest x1 7.54 us: body(): jnp.dot(normed, w_up, preferred_element_type=jnp.float32)]
  transfers between devices with their start and end apart: 4 -> 31, of which waited for: 4 -> 19; matrix products, arithmetic and copies ran while one was open for 0% -> 1% of each run, Pallas kernels for 0% -> 19%
where the time goes in v2:
time: 114 us
  Pallas kernels  39.2 us (34%)
  waiting for transfers between devices  38.7 us (34%)
  starting transfers between devices  33.8 us (30%)
    ppermute x31, waiting for transfers between devices, send_xor(): return lax.ppermute(value, axis, [(i, i ^ distance) for i in range(size)])  38.7 us
    ppermute x31, starting transfers between devices, send_xor(): return lax.ppermute(value, axis, [(i, i ^ distance) for i in range(size)])  33.8 us
    pallas_call x1, Pallas kernels, tail_partial(): pl.pallas_call(functools.partial(tail_kernel, math.log2(math.e) / math.sq...  7.13 us
    pallas_call x1, Pallas kernels, image_of(): pl.pallas_call(image_kernel, grid=(4,), in_specs=[pl.BlockSpec((8, group)...  6.96 us
    pallas_call x1, Pallas kernels, prompt_partial(): pl.pallas_call(functools.partial(prompt_kernel, math.log2(math.e) / math....  6.78 us
    pallas_call x1, Pallas kernels, up_first(): pl.pallas_call(up_first_kernel, in_specs=[vmem] * 12 + [pl.BlockSpec(memo...  4.95 us
    pallas_call x1, Pallas kernels, down_first(): pl.pallas_call(down_first_kernel, in_specs=[vmem, pl.BlockSpec(memory_spa...  4.76 us
    pallas_call x1, Pallas kernels, up_second(): pl.pallas_call(up_second_kernel, in_specs=[vmem] * 2 + [pl.BlockSpec(memo...  2.64 us
  transfers between devices with their start and end apart: 31, of which 19 were waited for; matrix products, arithmetic and copies ran while one was open for 1% of the time, Pallas kernels for 19%

profile of v2, /device:TPU:0, one launch (start us, length us, event | category | flops | bytes accessed | tf_op | source)
XLA Modules:
  0.0 113.8 jit_solution(4252576133835103312)
XLA Ops:
  0.7 6.8 %prompt_attention.1 = (f32[136,128]{1,0:T(8,128)S(1)}, f32[136,128]{1,0:T(8,128)S(1)}, f32[136,128]{1,0:T(8,128)S(1)}, f32[136,128]{1,0:T(8,128)S(1)}) custom-call(s32[4,16]{1,0:T(4,128)} %table_hbm.1, s32[4]{0:T(128)} %len_hbm.1, s32[64]{0:T(128)} %prompt_hbm.1, bf16[64,2,4,128]{3,2,1,0:T(4,128)(2,1)} %q_ref.1, bf16[16,64,4,256]{3,2,1,0:T(4,128)(2,1)} %kv_hbm.1), custom_call_target="tpu_custom_call" | custom-call | tf_op jit(solution)/shard_map/prompt_attention/pallas_call | solution.py:161
  7.5 3.1 %collective-permute-start = (f32[136,128]{1,0:T(8,128)S(1)}, f32[136,128]{1,0:T(8,128)S(1)}, u32[]{:S(2)}, u32[]{:S(2)}) collective-permute-start(f32[136,128]{1,0:T(8,128)S(1)} %get-tuple-element.34), channel_id=1, source_target_pairs={{0,8},{8,0},{16,24},{24,16},{1,9},{9,1},{17,25},{25,17},{2,10},{10... | collective-permute-start | bytes 208904 | tf_op jit(solution)/shard_map/ppermute | solution.py:45
  10.6 2.6 %collective-permute-start.1 = (f32[136,128]{1,0:T(8,128)S(1)}, f32[136,128]{1,0:T(8,128)S(1)}, u32[]{:S(2)}, u32[]{:S(2)}) collective-permute-start(f32[136,128]{1,0:T(8,128)S(1)} %get-tuple-element.35), channel_id=1, source_target_pairs={{0,16},{8,24},{16,0},{24,8},{1,17},{9,25},{17,1},{25,9},{2,18},{10... | collective-permute-start | bytes 208904 | tf_op jit(solution)/shard_map/ppermute | solution.py:45
  13.2 7.1 %tail_attention.1.refs_4_ = f32[136,128]{1,0:T(8,128)S(1)} custom-call(s32[64]{0:T(128)} %len_ref.1, bf16[64,2,4,128]{3,2,1,0:T(4,128)(2,1)} %q_ref.1, bf16[16,256,4,256]{3,2,1,0:T(4,128)(2,1)} %kv_ref.1), custom_call_target="tpu_custom_call" | custom-call | tf_op jit(solution)/shard_map/tail_attention/pallas_call | solution.py:223
  20.6 3.9 %collective-permute-start.5 = (bf16[32,512]{1,0:T(8,128)(2,1)S(1)}, bf16[32,512]{1,0:T(8,128)(2,1)S(1)}, u32[]{:S(2)}, u32[]{:S(2)}) collective-permute-start(bf16[32,512]{1,0:T(8,128)(2,1)S(1)} %merge_partials.1.refs_0_), channel_id=1, source_target_pairs={{0,24},{8,16},{16,8},{24,0},{1,25},{9,17},{17,9},{25,1},{2,26},{10... | collective-permute-start | bytes 98312 | tf_op jit(solution)/shard_map/ppermute | solution.py:45
  26.4 2.8 %collective-permute-done.4.refs_2_ = bf16[32,512]{1,0:T(8,128)(2,1)S(1)} collective-permute-done((bf16[32,512]{1,0:T(8,128)(2,1)S(1)}, bf16[32,512]{1,0:T(8,128)(2,1)S(1)}, u32[]{:S(2)}, u32[]{:S(2)}) %collective-permute-start.4) | collective-permute-done | bytes 32800 | tf_op jit(solution)/shard_map/ppermute | solution.py:45
  29.3 2.1 %project_attention.1 = (f32[4,16,1792]{2,1,0:T(8,128)S(1)}, bf16[4,16,1792]{2,1,0:T(8,128)(2,1)S(1)}) custom-call(bf16[32,512]{1,0:T(8,128)(2,1)S(1)} %merge_partials.1.refs_0_, bf16[32,512]{1,0:T(8,128)(2,1)S(1)} %collective-permute-done.3.refs_1_, bf16[32,512]{1,0:T(8,128)(2,1)S(1)} %collective-permute-done.4.refs_2_, ...), custom_call_target="tpu_custom_call" | custom-call | tf_op jit(solution)/shard_map/project_attention/pallas_call | solution.py:305
  31.4 1.5 %collective-permute-done.6.got_ref = bf16[4,16,1792]{2,1,0:T(8,128)(2,1)S(1)} collective-permute-done((bf16[4,16,1792]{2,1,0:T(8,128)(2,1)S(1)}, bf16[4,16,1792]{2,1,0:T(8,128)(2,1)S(1)}, u32[]{:S(2)}, u32[]{:S(2)}) %collective-permute-start.6) | collective-permute-done | bytes 229408 | tf_op jit(solution)/shard_map/ppermute | solution.py:45
  32.9 1.5 %collective-permute-start.7 = (bf16[16,1792]{1,0:T(8,128)(2,1)S(1)}, bf16[16,1792]{1,0:T(8,128)(2,1)S(1)}, u32[]{:S(2)}, u32[]{:S(2)}) collective-permute-start(bf16[16,1792]{1,0:T(8,128)(2,1)S(1)} %get-tuple-element.40), channel_id=1, source_target_pairs={{0,2},{1,3},{2,0},{3,1},{4,6},{5,7},{6,4},{7,5},{8,10},{9,11},{10,... | collective-permute-start | bytes 172040 | tf_op jit(solution)/shard_map/ppermute | solution.py:45
  34.4 1.5 %collective-permute-start.8 = (bf16[16,1792]{1,0:T(8,128)(2,1)S(1)}, bf16[16,1792]{1,0:T(8,128)(2,1)S(1)}, u32[]{:S(2)}, u32[]{:S(2)}) collective-permute-start(bf16[16,1792]{1,0:T(8,128)(2,1)S(1)} %get-tuple-element.41), channel_id=1, source_target_pairs={{0,4},{1,5},{2,6},{3,7},{4,0},{5,1},{6,2},{7,3},{8,12},{9,13},{10,... | collective-permute-start | bytes 172040 | tf_op jit(solution)/shard_map/ppermute | solution.py:45
  38.6 2.4 %collective-permute-done.9.c_ref = bf16[16,1792]{1,0:T(8,128)(2,1)S(1)} collective-permute-done((bf16[16,1792]{1,0:T(8,128)(2,1)S(1)}, bf16[16,1792]{1,0:T(8,128)(2,1)S(1)}, u32[]{:S(2)}, u32[]{:S(2)}) %collective-permute-start.9) | collective-permute-done | bytes 57376 | tf_op jit(solution)/shard_map/ppermute | solution.py:45
  43.1 1.5 %collective-permute-start.10 = (bf16[16,1792]{1,0:T(8,128)(2,1)S(1)}, bf16[16,1792]{1,0:T(8,128)(2,1)S(1)}, u32[]{:S(2)}, u32[]{:S(2)}) collective-permute-start(bf16[16,1792]{1,0:T(8,128)(2,1)S(1)} %residual_rows.1.refs_0_), channel_id=1, source_target_pairs={{0,2},{1,3},{2,0},{3,1},{4,6},{5,7},{6,4},{7,5},{8,10},{9,11},{10,... | collective-permute-start | bytes 172040 | tf_op jit(solution)/shard_map/ppermute | solution.py:45
  44.6 1.7 %collective-permute-done.12.refs_3_ = bf16[16,1792]{1,0:T(8,128)(2,1)S(1)} collective-permute-done((bf16[16,1792]{1,0:T(8,128)(2,1)S(1)}, bf16[16,1792]{1,0:T(8,128)(2,1)S(1)}, u32[]{:S(2)}, u32[]{:S(2)}) %collective-permute-start.12) | collective-permute-done | bytes 57376 | tf_op jit(solution)/shard_map/ppermute | solution.py:45
  48.5 4.9 %norm_and_up.1 = (bf16[136,896]{1,0:T(8,128)(2,1)S(1)}, bf16[136,896]{1,0:T(8,128)(2,1)S(1)}, bf16[136,896]{1,0:T(8,128)(2,1)S(1)}, bf16[144,1792]{1,0:T(8,128)(...) custom-call(bf16[16,1792]{1,0:T(8,128)(2,1)S(1)} %residual_rows.1.refs_0_, ...), custom_call_target="tpu_custom_call" | custom-call | tf_op jit(solution)/shard_map/norm_and_up/pallas_call | solution.py:457
  53.6 2.2 %collective-permute-start.18 = (bf16[136,896]{1,0:T(8,128)(2,1)S(1)}, bf16[136,896]{1,0:T(8,128)(2,1)S(1)}, u32[]{:S(2)}, u32[]{:S(2)}) collective-permute-start(bf16[136,896]{1,0:T(8,128)(2,1)S(1)} %get-tuple-element.46), channel_id=1, source_target_pairs={{0,16},{8,24},{16,0},{24,8},{1,17},{9,25},{17,1},{25,9},{2,18},{10... | collective-permute-start | bytes 731144 | tf_op jit(solution)/shard_map/ppermute | solution.py:45
  55.7 2.2 %collective-permute-start.19 = (bf16[136,896]{1,0:T(8,128)(2,1)S(1)}, bf16[136,896]{1,0:T(8,128)(2,1)S(1)}, u32[]{:S(2)}, u32[]{:S(2)}) collective-permute-start(bf16[136,896]{1,0:T(8,128)(2,1)S(1)} %get-tuple-element.47), channel_id=1, source_target_pairs={{0,24},{8,16},{16,8},{24,0},{1,25},{9,17},{17,9},{25,1},{2,26},{10... | collective-permute-start | bytes 731144 | tf_op jit(solution)/shard_map/ppermute | solution.py:45
  57.9 1.5 %collective-permute-start.20 = (bf16[224]{0:T(256)(128)(2,1)S(1)}, bf16[224]{0:T(256)(128)(2,1)S(1)}, u32[]{:S(2)}, u32[]{:S(2)}) collective-permute-start(bf16[224]{0:T(256)(128)(2,1)S(1)} %copy-done.6), channel_id=1, source_target_pairs={{0,2},{1,3},{2,0},{3,1},{4,6},{5,7},{6,4},{7,5},{8,10},{9,11},{10,... | collective-permute-start | bytes 1352 | tf_op jit(solution)/shard_map/ppermute | solution.py:45
  60.0 1.5 %collective-permute-done.20 = bf16[224]{0:T(256)(128)(2,1)S(1)} collective-permute-done((bf16[224]{0:T(256)(128)(2,1)S(1)}, bf16[224]{0:T(256)(128)(2,1)S(1)}, u32[]{:S(2)}, u32[]{:S(2)}) %collective-permute-start.20) | collective-permute-done | bytes 480 | tf_op jit(solution)/shard_map/ppermute | solution.py:45
  61.5 1.4 %collective-permute-start.22 = (bf16[224]{0:T(256)(128)(2,1)S(1)}, bf16[224]{0:T(256)(128)(2,1)S(1)}, u32[]{:S(2)}, u32[]{:S(2)}) collective-permute-start(bf16[224]{0:T(256)(128)(2,1)S(1)} %copy-done.6), channel_id=1, source_target_pairs={{0,6},{1,7},{2,4},{3,5},{4,2},{5,3},{6,0},{7,1},{8,14},{9,15},{10,... | collective-permute-start | bytes 1352 | tf_op jit(solution)/shard_map/ppermute | solution.py:45
  63.1 2.8 %collective-permute-done.22 = bf16[224]{0:T(256)(128)(2,1)S(1)} collective-permute-done((bf16[224]{0:T(256)(128)(2,1)S(1)}, bf16[224]{0:T(256)(128)(2,1)S(1)}, u32[]{:S(2)}, u32[]{:S(2)}) %collective-permute-start.22) | collective-permute-done | bytes 480 | tf_op jit(solution)/shard_map/ppermute | solution.py:45
  67.5 7.0 %score_image.1.image_ref = f32[8,896]{1,0:T(8,128)S(1)} custom-call(bf16[8,1792]{1,0:T(8,128)(2,1)S(1)} %broadcast_in_dim.43.score_ref, bf16[3584,1792]{1,0:T(8,128)(2,1)} %w_hbm.3), custom_call_target="tpu_custom_call" | custom-call | tf_op jit(solution)/shard_map/score_image/pallas_call | solution.py:518
  74.5 2.6 %up_own.1.a_ref = bf16[136,896]{1,0:T(8,128)(2,1)S(1)} custom-call(bf16[144,1792]{1,0:T(8,128)(2,1)S(1)} %get-tuple-element.43.lhs_ref, bf16[6,128]{1,0:T(8,128)(2,1)S(1)} %get-tuple-element.44.stats_ref, bf16[1792,3584]{1,0:T(8,128)(2,1)} %w_hbm.2), custom_call_target="tpu_custom_call" | custom-call | tf_op jit(solution)/shard_map/up_own/pallas_call | solution.py:492
  77.6 1.7 %collective-permute-start.26 = (bf16[136,896]{1,0:T(8,128)(2,1)S(1)}, bf16[136,896]{1,0:T(8,128)(2,1)S(1)}, u32[]{:S(2)}, u32[]{:S(2)}) collective-permute-start(bf16[136,896]{1,0:T(8,128)(2,1)S(1)} %get-tuple-element.50.hidden_ref.refs_0_), channel_id=1, source_target_pairs={{0,24},{8,16},{16,8},{24,0},{1,25},{9,17},{17,9},{25,1},{2,26},{10... | collective-permute-start | bytes 731144 | tf_op jit(solution)/shard_map/ppermute | solution.py:45
  79.3 1.8 %collective-permute-start.25 = (bf16[136,896]{1,0:T(8,128)(2,1)S(1)}, bf16[136,896]{1,0:T(8,128)(2,1)S(1)}, u32[]{:S(2)}, u32[]{:S(2)}) collective-permute-start(bf16[136,896]{1,0:T(8,128)(2,1)S(1)} %get-tuple-element.50.hidden_ref.refs_0_), channel_id=1, source_target_pairs={{0,16},{8,24},{16,0},{24,8},{1,17},{9,25},{17,1},{25,9},{2,18},{10... | collective-permute-start | bytes 731144 | tf_op jit(solution)/shard_map/ppermute | solution.py:45
  82.1 4.8 %down_own.1 = (f32[128,1792]{1,0:T(8,128)S(1)}, bf16[3,896,1792]{2,1,0:T(8,128)(2,1)S(1)}) custom-call(bf16[136,896]{1,0:T(8,128)(2,1)S(1)} %get-tuple-element.50.hidden_ref.refs_0_, bf16[3584,1792]{1,0:T(8,128)(2,1)} %w_hbm.3), custom_call_target="tpu_custom_call" | custom-call | tf_op jit(solution)/shard_map/down_own/pallas_call | solution.py:593
  86.8 1.5 %collective-permute-done.26.refs_3_ = bf16[136,896]{1,0:T(8,128)(2,1)S(1)} collective-permute-done((bf16[136,896]{1,0:T(8,128)(2,1)S(1)}, bf16[136,896]{1,0:T(8,128)(2,1)S(1)}, u32[]{:S(2)}, u32[]{:S(2)}) %collective-permute-start.26) | collective-permute-done | bytes 243744 | tf_op jit(solution)/shard_map/ppermute | solution.py:45
  88.4 13.5 %collective-permute-done.25.refs_2_ = bf16[136,896]{1,0:T(8,128)(2,1)S(1)} collective-permute-done((bf16[136,896]{1,0:T(8,128)(2,1)S(1)}, bf16[136,896]{1,0:T(8,128)(2,1)S(1)}, u32[]{:S(2)}, u32[]{:S(2)}) %collective-permute-start.25) | collective-permute-done | bytes 243744 | tf_op jit(solution)/shard_map/ppermute | solution.py:45
  101.9 1.8 %down_rest.1 = (f32[4,128,224]{2,1,0:T(8,128)S(1)}, bf16[4,128,227]{2,1,0:T(8,128)(2,1)S(1)}, f32[128,1]{1,0:T(8,128)S(1)}) custom-call(f32[128,1]{1,0:T(8,128)S(1)} %get-tuple-element.49.base_ref, f32[128,1792]{1,0:T(8,128)S(1)} %get-tuple-element.51.sum_ref, bf16[3,896,1792]{2,1,0:T(8,128)(2,1)S(1)} %get-tuple-element.52.held_ref, ...), custom_call_target="tpu_custom_call" | custom-call | tf_op jit(solution)/shard_map/down_rest/pallas_call | solution.py:645
  103.8 1.5 %collective-permute-done.27.got_ref = bf16[4,128,227]{2,1,0:T(8,128)(2,1)S(1)} collective-permute-done((bf16[4,128,227]{2,1,0:T(8,128)(2,1)S(1)}, bf16[4,128,227]{2,1,0:T(8,128)(2,1)S(1)}, u32[]{:S(2)}, u32[]{:S(2)}) %collective-permute-start.27) | collective-permute-done | bytes 232480 | tf_op jit(solution)/shard_map/ppermute | solution.py:45
  105.6 1.5 %collective-permute-start.28 = (bf16[128,227]{1,0:T(8,128)(2,1)S(1)}, bf16[128,227]{1,0:T(8,128)(2,1)S(1)}, u32[]{:S(2)}, u32[]{:S(2)}) collective-permute-start(bf16[128,227]{1,0:T(8,128)(2,1)S(1)} %get-tuple-element.59), channel_id=1, source_target_pairs={{0,2},{1,3},{2,0},{3,1},{4,6},{5,7},{6,4},{7,5},{8,10},{9,11},{10,... | collective-permute-start | bytes 174344 | tf_op jit(solution)/shard_map/ppermute | solution.py:45
  107.6 1.6 %collective-permute-start.30 = (bf16[128,227]{1,0:T(8,128)(2,1)S(1)}, bf16[128,227]{1,0:T(8,128)(2,1)S(1)}, u32[]{:S(2)}, u32[]{:S(2)}) collective-permute-start(bf16[128,227]{1,0:T(8,128)(2,1)S(1)} %get-tuple-element.61), channel_id=1, source_target_pairs={{0,6},{1,7},{2,4},{3,5},{4,2},{5,3},{6,0},{7,1},{8,14},{9,15},{10,... | collective-permute-start | bytes 174344 | tf_op jit(solution)/shard_map/ppermute | solution.py:45
  110.0 2.1 %collective-permute-done.29.b_ref = bf16[128,227]{1,0:T(8,128)(2,1)S(1)} collective-permute-done((bf16[128,227]{1,0:T(8,128)(2,1)S(1)}, bf16[128,227]{1,0:T(8,128)(2,1)S(1)}, u32[]{:S(2)}, u32[]{:S(2)}) %collective-permute-start.29) | collective-permute-done | bytes 58144 | tf_op jit(solution)/shard_map/ppermute | solution.py:45
  (85 shorter events, 16.1 us)
Async XLA Ops:
  0.7 46.7 %copy-start.4 = (bf16[1792]{0:T(1024)(128)(2,1)S(1)}, bf16[1792]{0:T(1024)(128)(2,1)}, u32[]{:S(2)}) copy-start(bf16[1792]{0:T(1024)(128)(2,1)} %param.28) | copy-start | bytes 10756
  7.5 12.8 %collective-permute-start = (f32[136,128]{1,0:T(8,128)S(1)}, f32[136,128]{1,0:T(8,128)S(1)}, u32[]{:S(2)}, u32[]{:S(2)}) collective-permute-start(f32[136,128]{1,0:T(8,128)S(1)} %get-tuple-element.34), channel_id=1, source_target_pairs={{0,8},{8,0},{16,24},{24,16},{1,9},{9,1},{17,25},{25,17},{2,10},{10... | collective-permute-start | bytes 208904 | tf_op jit(solution)/shard_map/ppermute | solution.py:45
  10.6 9.7 %collective-permute-start.1 = (f32[136,128]{1,0:T(8,128)S(1)}, f32[136,128]{1,0:T(8,128)S(1)}, u32[]{:S(2)}, u32[]{:S(2)}) collective-permute-start(f32[136,128]{1,0:T(8,128)S(1)} %get-tuple-element.35), channel_id=1, source_target_pairs={{0,16},{8,24},{16,0},{24,8},{1,17},{9,25},{17,1},{25,9},{2,18},{10... | collective-permute-start | bytes 208904 | tf_op jit(solution)/shard_map/ppermute | solution.py:45
  13.2 7.2 %collective-permute-start.2 = (f32[136,128]{1,0:T(8,128)S(1)}, f32[136,128]{1,0:T(8,128)S(1)}, u32[]{:S(2)}, u32[]{:S(2)}) collective-permute-start(f32[136,128]{1,0:T(8,128)S(1)} %get-tuple-element.36), channel_id=1, source_target_pairs={{0,24},{8,16},{16,8},{24,0},{1,25},{9,17},{17,9},{25,1},{2,26},{10... | collective-permute-start | bytes 208904 | tf_op jit(solution)/shard_map/ppermute | solution.py:45
  20.6 5.9 %collective-permute-start.5 = (bf16[32,512]{1,0:T(8,128)(2,1)S(1)}, bf16[32,512]{1,0:T(8,128)(2,1)S(1)}, u32[]{:S(2)}, u32[]{:S(2)}) collective-permute-start(bf16[32,512]{1,0:T(8,128)(2,1)S(1)} %merge_partials.1.refs_0_), channel_id=1, source_target_pairs={{0,24},{8,16},{16,8},{24,0},{1,25},{9,17},{17,9},{25,1},{2,26},{10... | collective-permute-start | bytes 98312 | tf_op jit(solution)/shard_map/ppermute | solution.py:45
  24.4 4.8 %collective-permute-start.4 = (bf16[32,512]{1,0:T(8,128)(2,1)S(1)}, bf16[32,512]{1,0:T(8,128)(2,1)S(1)}, u32[]{:S(2)}, u32[]{:S(2)}) collective-permute-start(bf16[32,512]{1,0:T(8,128)(2,1)S(1)} %merge_partials.1.refs_0_), channel_id=1, source_target_pairs={{0,16},{8,24},{16,0},{24,8},{1,17},{9,25},{17,1},{25,9},{2,18},{10... | collective-permute-start | bytes 98312 | tf_op jit(solution)/shard_map/ppermute | solution.py:45
  24.4 4.8 %collective-permute-start.3 = (bf16[32,512]{1,0:T(8,128)(2,1)S(1)}, bf16[32,512]{1,0:T(8,128)(2,1)S(1)}, u32[]{:S(2)}, u32[]{:S(2)}) collective-permute-start(bf16[32,512]{1,0:T(8,128)(2,1)S(1)} %merge_partials.1.refs_0_), channel_id=1, source_target_pairs={{0,8},{8,0},{16,24},{24,16},{1,9},{9,1},{17,25},{25,17},{2,10},{10... | collective-permute-start | bytes 98312 | tf_op jit(solution)/shard_map/ppermute | solution.py:45
  31.3 1.6 %collective-permute-start.6 = (bf16[4,16,1792]{2,1,0:T(8,128)(2,1)S(1)}, bf16[4,16,1792]{2,1,0:T(8,128)(2,1)S(1)}, u32[]{:S(2)}, u32[]{:S(2)}) collective-permute-start(bf16[4,16,1792]{2,1,0:T(8,128)(2,1)S(1)} %get-tuple-element.38), channel_id=1, source_target_pairs={{0,1},{1,0},{2,3},{3,2},{4,5},{5,4},{6,7},{7,6},{8,9},{9,8},{10,11... | collective-permute-start | bytes 688136 | tf_op jit(solution)/shard_map/ppermute | solution.py:45
  32.9 4.2 %collective-permute-start.7 = (bf16[16,1792]{1,0:T(8,128)(2,1)S(1)}, bf16[16,1792]{1,0:T(8,128)(2,1)S(1)}, u32[]{:S(2)}, u32[]{:S(2)}) collective-permute-start(bf16[16,1792]{1,0:T(8,128)(2,1)S(1)} %get-tuple-element.40), channel_id=1, source_target_pairs={{0,2},{1,3},{2,0},{3,1},{4,6},{5,7},{6,4},{7,5},{8,10},{9,11},{10,... | collective-permute-start | bytes 172040 | tf_op jit(solution)/shard_map/ppermute | solution.py:45
  34.4 4.2 %collective-permute-start.8 = (bf16[16,1792]{1,0:T(8,128)(2,1)S(1)}, bf16[16,1792]{1,0:T(8,128)(2,1)S(1)}, u32[]{:S(2)}, u32[]{:S(2)}) collective-permute-start(bf16[16,1792]{1,0:T(8,128)(2,1)S(1)} %get-tuple-element.41), channel_id=1, source_target_pairs={{0,4},{1,5},{2,6},{3,7},{4,0},{5,1},{6,2},{7,3},{8,12},{9,13},{10,... | collective-permute-start | bytes 172040 | tf_op jit(solution)/shard_map/ppermute | solution.py:45
  35.9 5.1 %collective-permute-start.9 = (bf16[16,1792]{1,0:T(8,128)(2,1)S(1)}, bf16[16,1792]{1,0:T(8,128)(2,1)S(1)}, u32[]{:S(2)}, u32[]{:S(2)}) collective-permute-start(bf16[16,1792]{1,0:T(8,128)(2,1)S(1)} %get-tuple-element.42), channel_id=1, source_target_pairs={{0,6},{1,7},{2,4},{3,5},{4,2},{5,3},{6,0},{7,1},{8,14},{9,15},{10,... | collective-permute-start | bytes 172040 | tf_op jit(solution)/shard_map/ppermute | solution.py:45
  41.1 5.2 %collective-permute-start.12 = (bf16[16,1792]{1,0:T(8,128)(2,1)S(1)}, bf16[16,1792]{1,0:T(8,128)(2,1)S(1)}, u32[]{:S(2)}, u32[]{:S(2)}) collective-permute-start(bf16[16,1792]{1,0:T(8,128)(2,1)S(1)} %residual_rows.1.refs_0_), channel_id=1, source_target_pairs={{0,6},{1,7},{2,4},{3,5},{4,2},{5,3},{6,0},{7,1},{8,14},{9,15},{10,... | collective-permute-start | bytes 172040 | tf_op jit(solution)/shard_map/ppermute | solution.py:45
  41.7 4.8 %collective-permute-start.11 = (bf16[16,1792]{1,0:T(8,128)(2,1)S(1)}, bf16[16,1792]{1,0:T(8,128)(2,1)S(1)}, u32[]{:S(2)}, u32[]{:S(2)}) collective-permute-start(bf16[16,1792]{1,0:T(8,128)(2,1)S(1)} %residual_rows.1.refs_0_), channel_id=1, source_target_pairs={{0,4},{1,5},{2,6},{3,7},{4,0},{5,1},{6,2},{7,3},{8,12},{9,13},{10,... | collective-permute-start | bytes 172040 | tf_op jit(solution)/shard_map/ppermute | solution.py:45
  43.1 4.2 %collective-permute-start.10 = (bf16[16,1792]{1,0:T(8,128)(2,1)S(1)}, bf16[16,1792]{1,0:T(8,128)(2,1)S(1)}, u32[]{:S(2)}, u32[]{:S(2)}) collective-permute-start(bf16[16,1792]{1,0:T(8,128)(2,1)S(1)} %residual_rows.1.refs_0_), channel_id=1, source_target_pairs={{0,2},{1,3},{2,0},{3,1},{4,6},{5,7},{6,4},{7,5},{8,10},{9,11},{10,... | collective-permute-start | bytes 172040 | tf_op jit(solution)/shard_map/ppermute | solution.py:45
  44.6 3.1 %collective-permute-start.13 = (bf16[16,1792]{1,0:T(8,128)(2,1)S(1)}, bf16[16,1792]{1,0:T(8,128)(2,1)S(1)}, u32[]{:S(2)}, u32[]{:S(2)}) collective-permute-start(bf16[16,1792]{1,0:T(8,128)(2,1)S(1)} %residual_rows.1.refs_0_), channel_id=1, source_target_pairs={{0,1},{1,0},{2,3},{3,2},{4,5},{5,4},{6,7},{7,6},{8,9},{9,8},{10,11... | collective-permute-start | bytes 172040 | tf_op jit(solution)/shard_map/ppermute | solution.py:45
  46.3 1.5 %collective-permute-start.16 = (bf16[16,1792]{1,0:T(8,128)(2,1)S(1)}, bf16[16,1792]{1,0:T(8,128)(2,1)S(1)}, u32[]{:S(2)}, u32[]{:S(2)}) collective-permute-start(bf16[16,1792]{1,0:T(8,128)(2,1)S(1)} %collective-permute-done.12.refs_3_), channel_id=1, source_target_pairs={{0,1},{1,0},{2,3},{3,2},{4,5},{5,4},{6,7},{7,6},{8,9},{9,8},{10,11... | collective-permute-start | bytes 172040 | tf_op jit(solution)/shard_map/ppermute | solution.py:45
  46.5 1.3 %collective-permute-start.15 = (bf16[16,1792]{1,0:T(8,128)(2,1)S(1)}, bf16[16,1792]{1,0:T(8,128)(2,1)S(1)}, u32[]{:S(2)}, u32[]{:S(2)}) collective-permute-start(bf16[16,1792]{1,0:T(8,128)(2,1)S(1)} %collective-permute-done.11.refs_2_), channel_id=1, source_target_pairs={{0,1},{1,0},{2,3},{3,2},{4,5},{5,4},{6,7},{7,6},{8,9},{9,8},{10,11... | collective-permute-start | bytes 172040 | tf_op jit(solution)/shard_map/ppermute | solution.py:45
  47.3 1.2 %collective-permute-start.14 = (bf16[16,1792]{1,0:T(8,128)(2,1)S(1)}, bf16[16,1792]{1,0:T(8,128)(2,1)S(1)}, u32[]{:S(2)}, u32[]{:S(2)}) collective-permute-start(bf16[16,1792]{1,0:T(8,128)(2,1)S(1)} %collective-permute-done.10.refs_1_), channel_id=1, source_target_pairs={{0,1},{1,0},{2,3},{3,2},{4,5},{5,4},{6,7},{7,6},{8,9},{9,8},{10,11... | collective-permute-start | bytes 172040 | tf_op jit(solution)/shard_map/ppermute | solution.py:45
  53.5 23.6 %collective-permute-start.17 = (bf16[136,896]{1,0:T(8,128)(2,1)S(1)}, bf16[136,896]{1,0:T(8,128)(2,1)S(1)}, u32[]{:S(2)}, u32[]{:S(2)}) collective-permute-start(bf16[136,896]{1,0:T(8,128)(2,1)S(1)} %get-tuple-element.45), channel_id=1, source_target_pairs={{0,8},{8,0},{16,24},{24,16},{1,9},{9,1},{17,25},{25,17},{2,10},{10... | collective-permute-start | bytes 731144 | tf_op jit(solution)/shard_map/ppermute | solution.py:45
  53.6 23.6 %collective-permute-start.18 = (bf16[136,896]{1,0:T(8,128)(2,1)S(1)}, bf16[136,896]{1,0:T(8,128)(2,1)S(1)}, u32[]{:S(2)}, u32[]{:S(2)}) collective-permute-start(bf16[136,896]{1,0:T(8,128)(2,1)S(1)} %get-tuple-element.46), channel_id=1, source_target_pairs={{0,16},{8,24},{16,0},{24,8},{1,17},{9,25},{17,1},{25,9},{2,18},{10... | collective-permute-start | bytes 731144 | tf_op jit(solution)/shard_map/ppermute | solution.py:45
  55.7 21.4 %collective-permute-start.19 = (bf16[136,896]{1,0:T(8,128)(2,1)S(1)}, bf16[136,896]{1,0:T(8,128)(2,1)S(1)}, u32[]{:S(2)}, u32[]{:S(2)}) collective-permute-start(bf16[136,896]{1,0:T(8,128)(2,1)S(1)} %get-tuple-element.47), channel_id=1, source_target_pairs={{0,24},{8,16},{16,8},{24,0},{1,25},{9,17},{17,9},{25,1},{2,26},{10... | collective-permute-start | bytes 731144 | tf_op jit(solution)/shard_map/ppermute | solution.py:45
  57.9 3.5 %collective-permute-start.20 = (bf16[224]{0:T(256)(128)(2,1)S(1)}, bf16[224]{0:T(256)(128)(2,1)S(1)}, u32[]{:S(2)}, u32[]{:S(2)}) collective-permute-start(bf16[224]{0:T(256)(128)(2,1)S(1)} %copy-done.6), channel_id=1, source_target_pairs={{0,2},{1,3},{2,0},{3,1},{4,6},{5,7},{6,4},{7,5},{8,10},{9,11},{10,... | collective-permute-start | bytes 1352 | tf_op jit(solution)/shard_map/ppermute | solution.py:45
  59.4 3.6 %collective-permute-start.21 = (bf16[224]{0:T(256)(128)(2,1)S(1)}, bf16[224]{0:T(256)(128)(2,1)S(1)}, u32[]{:S(2)}, u32[]{:S(2)}) collective-permute-start(bf16[224]{0:T(256)(128)(2,1)S(1)} %copy-done.6), channel_id=1, source_target_pairs={{0,4},{1,5},{2,6},{3,7},{4,0},{5,1},{6,2},{7,3},{8,12},{9,13},{10,... | collective-permute-start | bytes 1352 | tf_op jit(solution)/shard_map/ppermute | solution.py:45
  61.5 4.4 %collective-permute-start.22 = (bf16[224]{0:T(256)(128)(2,1)S(1)}, bf16[224]{0:T(256)(128)(2,1)S(1)}, u32[]{:S(2)}, u32[]{:S(2)}) collective-permute-start(bf16[224]{0:T(256)(128)(2,1)S(1)} %copy-done.6), channel_id=1, source_target_pairs={{0,6},{1,7},{2,4},{3,5},{4,2},{5,3},{6,0},{7,1},{8,14},{9,15},{10,... | collective-permute-start | bytes 1352 | tf_op jit(solution)/shard_map/ppermute | solution.py:45
  66.0 1.2 %collective-permute-start.23 = (bf16[4,224]{1,0:T(4,128)(2,1)S(1)}, bf16[4,224]{1,0:T(4,128)(2,1)S(1)}, u32[]{:S(2)}, u32[]{:S(2)}) collective-permute-start(bf16[4,224]{1,0:T(4,128)(2,1)S(1)} %dynamic_update_slice.33), channel_id=1, source_target_pairs={{0,1},{1,0},{2,3},{3,2},{4,5},{5,4},{6,7},{7,6},{8,9},{9,8},{10,11... | collective-permute-start | bytes 5384 | tf_op jit(solution)/shard_map/ppermute | solution.py:45
  77.6 10.8 %collective-permute-start.26 = (bf16[136,896]{1,0:T(8,128)(2,1)S(1)}, bf16[136,896]{1,0:T(8,128)(2,1)S(1)}, u32[]{:S(2)}, u32[]{:S(2)}) collective-permute-start(bf16[136,896]{1,0:T(8,128)(2,1)S(1)} %get-tuple-element.50.hidden_ref.refs_0_), channel_id=1, source_target_pairs={{0,24},{8,16},{16,8},{24,0},{1,25},{9,17},{17,9},{25,1},{2,26},{10... | collective-permute-start | bytes 731144 | tf_op jit(solution)/shard_map/ppermute | solution.py:45
  79.3 22.6 %collective-permute-start.25 = (bf16[136,896]{1,0:T(8,128)(2,1)S(1)}, bf16[136,896]{1,0:T(8,128)(2,1)S(1)}, u32[]{:S(2)}, u32[]{:S(2)}) collective-permute-start(bf16[136,896]{1,0:T(8,128)(2,1)S(1)} %get-tuple-element.50.hidden_ref.refs_0_), channel_id=1, source_target_pairs={{0,16},{8,24},{16,0},{24,8},{1,17},{9,25},{17,1},{25,9},{2,18},{10... | collective-permute-start | bytes 731144 | tf_op jit(solution)/shard_map/ppermute | solution.py:45
  81.2 20.7 %collective-permute-start.24 = (bf16[136,896]{1,0:T(8,128)(2,1)S(1)}, bf16[136,896]{1,0:T(8,128)(2,1)S(1)}, u32[]{:S(2)}, u32[]{:S(2)}) collective-permute-start(bf16[136,896]{1,0:T(8,128)(2,1)S(1)} %get-tuple-element.50.hidden_ref.refs_0_), channel_id=1, source_target_pairs={{0,8},{8,0},{16,24},{24,16},{1,9},{9,1},{17,25},{25,17},{2,10},{10... | collective-permute-start | bytes 731144 | tf_op jit(solution)/shard_map/ppermute | solution.py:45
  103.7 1.6 %collective-permute-start.27 = (bf16[4,128,227]{2,1,0:T(8,128)(2,1)S(1)}, bf16[4,128,227]{2,1,0:T(8,128)(2,1)S(1)}, u32[]{:S(2)}, u32[]{:S(2)}) collective-permute-start(bf16[4,128,227]{2,1,0:T(8,128)(2,1)S(1)} %get-tuple-element.55), channel_id=1, source_target_pairs={{0,1},{1,0},{2,3},{3,2},{4,5},{5,4},{6,7},{7,6},{8,9},{9,8},{10,11... | collective-permute-start | bytes 697352 | tf_op jit(solution)/shard_map/ppermute | solution.py:45
  105.6 4.3 %collective-permute-start.28 = (bf16[128,227]{1,0:T(8,128)(2,1)S(1)}, bf16[128,227]{1,0:T(8,128)(2,1)S(1)}, u32[]{:S(2)}, u32[]{:S(2)}) collective-permute-start(bf16[128,227]{1,0:T(8,128)(2,1)S(1)} %get-tuple-element.59), channel_id=1, source_target_pairs={{0,2},{1,3},{2,0},{3,1},{4,6},{5,7},{6,4},{7,5},{8,10},{9,11},{10,... | collective-permute-start | bytes 174344 | tf_op jit(solution)/shard_map/ppermute | solution.py:45
  107.1 5.0 %collective-permute-start.29 = (bf16[128,227]{1,0:T(8,128)(2,1)S(1)}, bf16[128,227]{1,0:T(8,128)(2,1)S(1)}, u32[]{:S(2)}, u32[]{:S(2)}) collective-permute-start(bf16[128,227]{1,0:T(8,128)(2,1)S(1)} %get-tuple-element.60), channel_id=1, source_target_pairs={{0,4},{1,5},{2,6},{3,7},{4,0},{5,1},{6,2},{7,3},{8,12},{9,13},{10,... | collective-permute-start | bytes 174344 | tf_op jit(solution)/shard_map/ppermute | solution.py:45
  107.6 5.2 %collective-permute-start.30 = (bf16[128,227]{1,0:T(8,128)(2,1)S(1)}, bf16[128,227]{1,0:T(8,128)(2,1)S(1)}, u32[]{:S(2)}, u32[]{:S(2)}) collective-permute-start(bf16[128,227]{1,0:T(8,128)(2,1)S(1)} %get-tuple-element.61), channel_id=1, source_target_pairs={{0,6},{1,7},{2,4},{3,5},{4,2},{5,3},{6,0},{7,1},{8,14},{9,15},{10,... | collective-permute-start | bytes 174344 | tf_op jit(solution)/shard_map/ppermute | solution.py:45
  (6 other events, 249.9 us)

commit v3 on v2

v3 whole, which is shorter than its diff:
```python
import functools
import math

import jax
import jax.numpy as jnp
from jax import lax
from jax.experimental import pallas as pl
from jax.experimental.pallas import tpu as pltpu
from jax.sharding import PartitionSpec as P

NEGATIVE = -1e30
EPS = 1e-05
VMEM_LIMIT = 24 * 2**20
TOP = 64
FREE = pl.CostEstimate(flops=0, bytes_accessed=0, transcendentals=0)


def combined_all(value, axis, join):
    pieces = jax.tree.map(lambda part: lax.all_gather(part, axis), value)
    head = jax.tree.map(lambda part: part[0], pieces)
    tail = jax.tree.map(lambda part: part[1:], pieces)
    subtotal, _ = lax.scan(lambda subtotal, share: (join(subtotal, share), None), head, tail)
    return subtotal


def join_partials(earlier, later):
    highest = jnp.maximum(earlier[0], later[0])
    left_scale = jnp.exp(earlier[0] - highest)
    right_scale = jnp.exp(later[0] - highest)
    return (
        highest,
        earlier[1] * left_scale + later[1] * right_scale,
        earlier[2] * left_scale[..., None] + later[2] * right_scale[..., None],
    )


def softmax_part(scores, visible):
    masked = jnp.where(visible, scores, NEGATIVE)
    highest = jnp.max(masked, axis=-1)
    weights = jnp.where(visible, jnp.exp(scores - highest[..., None]), 0.0)
    return (highest, jnp.sum(weights, axis=-1), weights.astype(jnp.bfloat16))


def send_xor(value, axis, distance):
    size = lax.axis_size(axis)
    return lax.ppermute(value, axis, [(i, i ^ distance) for i in range(size)])


def in_hbm(value):
    return pltpu.with_memory_space_constraint(value, pltpu.HBM)


def gather_xor(value, axis, distances):
    return [value] + [send_xor(value, axis, k) for k in distances]


def pair_sum(pieces):
    return (pieces[0] + pieces[1]) + (pieces[2] + pieces[3])


def start_copies(copies):
    for copy in copies:
        copy.start()
    return copies


def flat_rows(ref_value):
    shape = ref_value.shape
    return ref_value.reshape(math.prod(shape[:-1]), shape[-1])


def prompt_kernel(scale, table_hbm, len_hbm, prompt_hbm, q_hbm, kv_hbm, *refs):
    outs, refs = refs[:4], refs[4:]
    table_ref, len_ref, prompt_ref, q_ref, kv_ref, where_ref, count_ref, place_ref = refs[:8]
    query_ref, rows_ref, score_ref, best_ref, norm_ref, mixed_ref, back_ref, sems = refs[8:]
    copies = start_copies(
        [
            pltpu.make_async_copy(source, target, sems.at[i])
            for i, (source, target) in enumerate(
                (
                    (table_hbm, table_ref),
                    (len_hbm, len_ref),
                    (prompt_hbm, prompt_ref),
                    (q_hbm, q_ref),
                    (kv_hbm, kv_ref),
                )
            )
        ]
    )
    prompts, pages_max = table_ref.shape
    slots, page_len, heads, _ = kv_ref.shape
    samples, new = q_ref.shape[:2]
    dim = q_ref.shape[3]
    lines = outs[0].shape[0] - 8
    small = new * heads
    block = samples // prompts * small
    bf16, f32 = jnp.bfloat16, jnp.float32
    page_pos = lax.axis_index("page")
    first = page_pos * slots
    best_ref[...] = jnp.full(best_ref.shape, NEGATIVE, f32)
    norm_ref[...] = jnp.zeros(norm_ref.shape, f32)
    mixed_ref[...] = jnp.zeros(mixed_ref.shape, f32)
    for copy in copies[:3]:
        copy.wait()
    for p in range(prompts):
        count_ref[p] = p * (samples // prompts)
        for g in range(pages_max):
            slot = table_ref[p, g] - first
            here = jnp.logical_and(slot >= 0, slot < slots)
            where_ref[jnp.where(here, slot, slots)] = p * pages_max + g
    copies[3].wait()
    query_ref[...] = flat_rows(q_ref[...]).astype(f32)
    for s in range(samples):
        prompt = prompt_ref[s]
        place = count_ref[prompt]
        count_ref[prompt] = place + 1
        place_ref[s] = place
        to = pl.ds(pl.multiple_of(place * small, small), small)
        back_ref[to, :] = query_ref[s * small : (s + 1) * small, :]
    rows_ref[...] = back_ref[...].astype(bf16)
    width = page_len * heads
    row = lax.broadcasted_iota(jnp.int32, (block, width), 0)
    col = lax.broadcasted_iota(jnp.int32, (block, width), 1)
    position = jnp.where(row % heads == col % heads, col, page_len * heads * pages_max)
    copies[4].wait()
    cache = flat_rows(kv_ref[...])
    at = []
    for j in range(slots):
        entry = where_ref[j]
        prompt = entry // pages_max
        left = (len_ref[prompt] - (entry % pages_max) * page_len) * heads
        at.append(pl.ds(pl.multiple_of(prompt * block, block), block))
        scores = lax.dot_general(
            rows_ref[at[j], :],
            cache[j * width : (j + 1) * width, :dim],
            (((1,), (1,)), ((), ())),
            preferred_element_type=f32,
        )
        scores = jnp.where(position < jnp.minimum(left, width), scores, NEGATIVE)
        score_ref[j] = scores
        best = jnp.max(scores, axis=1, keepdims=True)
        best_ref[at[j], :] = jnp.maximum(best_ref[at[j], :], best)
    for j in range(slots):
        best = best_ref[at[j], :]
        best = jnp.concatenate([best] * (width // dim), axis=1)
        weights = jnp.exp2((score_ref[j] - best) * scale)
        norm_ref[at[j], :] += jnp.sum(weights, axis=1, keepdims=True)
        mixed_ref[at[j], :] += jnp.dot(
            weights.astype(bf16),
            cache[j * width : (j + 1) * width, dim:],
            preferred_element_type=f32,
        )
    for k, out_ref in enumerate(outs):
        for i in range(lines // small):
            place = place_ref[(page_pos ^ k) * (lines // small) + i]
            source = pl.ds(pl.multiple_of(place * small, small), small)
            to = slice(i * small, (i + 1) * small)
            out_ref[to, :] = mixed_ref[source, :]
            back_ref[k * lines + i * small : k * lines + (i + 1) * small, :] = best_ref[source, :]
            query_ref[k * lines + i * small : k * lines + (i + 1) * small, :] = norm_ref[source, :]
        out_ref[lines : lines + 1, :] = back_ref[k * lines : (k + 1) * lines, :].T[0:1]
        out_ref[lines + 1 : lines + 2, :] = query_ref[k * lines : (k + 1) * lines, :].T[0:1]


def prompt_partial(queries, prompt_kv, page_table, prompt_len, sample_prompt):
    samples, new, heads, dim = queries.shape
    slots, page_len = prompt_kv.shape[:2]
    total = samples * new * heads
    block = total // page_table.shape[0]
    lines = total // 4
    anywhere = pl.BlockSpec(memory_space=pl.ANY)
    vmem = pl.BlockSpec(memory_space=pltpu.VMEM)
    wide = pltpu.VMEM((total, dim), jnp.float32)
    return pl.pallas_call(
        functools.partial(prompt_kernel, math.log2(math.e) / math.sqrt(dim)),
        in_specs=[anywhere] * 5,
        out_specs=[vmem] * 4,
        out_shape=[pltpu.VMEM((lines + 8, dim), jnp.float32)] * 4,
        scratch_shapes=[
            pltpu.SMEM(page_table.shape, jnp.int32),
            pltpu.SMEM(prompt_len.shape, jnp.int32),
            pltpu.SMEM(sample_prompt.shape, jnp.int32),
            pltpu.VMEM(queries.shape, queries.dtype),
            pltpu.VMEM(prompt_kv.shape, prompt_kv.dtype),
            pltpu.SMEM((slots + 1,), jnp.int32),
            pltpu.SMEM(prompt_len.shape, jnp.int32),
            pltpu.SMEM(sample_prompt.shape, jnp.int32),
            wide,
            pltpu.VMEM((total, dim), jnp.bfloat16),
            pltpu.VMEM((slots, block, page_len * heads), jnp.float32),
            wide,
            wide,
            wide,
            wide,
            pltpu.SemaphoreType.DMA((5,)),
        ],
        compiler_params=pltpu.CompilerParams(vmem_limit_bytes=VMEM_LIMIT),
        name="prompt_attention",
    )(*map(in_hbm, (page_table, prompt_len, sample_prompt, queries, prompt_kv)))


def tail_kernel(scale, len_ref, q_ref, kv_hbm, out_ref, kv_ref, best_ref, norm_ref, sems):
    own, length, heads, _ = kv_ref.shape
    new, dim = q_ref.shape[1], q_ref.shape[3]
    lines, half = new * heads, length * heads // 2
    steps = sems.shape[0]
    per = own // steps
    bf16, f32 = jnp.bfloat16, jnp.float32
    copies = start_copies(
        [
            pltpu.make_async_copy(
                kv_hbm.at[pl.ds(i * per, per)], kv_ref.at[pl.ds(i * per, per)], sems.at[i]
            )
            for i in range(steps)
        ]
    )
    first = lax.axis_index("page") * own
    row = lax.broadcasted_iota(jnp.int32, (2 * lines, half), 0)
    col = lax.broadcasted_iota(jnp.int32, (2 * lines, half), 1) + (row // lines) * half
    line = row % lines
    same_head = line % heads == col % heads
    ahead = jnp.where(same_head, col // heads - line // heads, length + new)
    for step in range(steps):
        copies[step].wait()
        scores, values = [], []
        for i in range(step * per, (step + 1) * per):
            cache = flat_rows(kv_ref[i])
            keys = jnp.concatenate([cache[:half, :dim], cache[half:, :dim]], axis=1)
            values.append(jnp.concatenate([cache[:half, dim:], cache[half:, dim:]], axis=1))
            query = flat_rows(q_ref[i])
            blank = jnp.zeros_like(query)
            query = jnp.concatenate(
                [
                    jnp.concatenate([query, blank], axis=1),
                    jnp.concatenate([blank, query], axis=1),
                ],
                axis=0,
            )
            score = lax.dot_general(
                query, keys, (((1,), (1,)), ((), ())), preferred_element_type=f32
            )
            scores.append(jnp.where(ahead <= len_ref[first + i], score, NEGATIVE))
        bests = [jnp.max(score, axis=1, keepdims=True) for score in scores]
        bests = [jnp.maximum(best[:lines], best[lines:]) for best in bests]
        weights = [
            jnp.exp2((score - jnp.concatenate([best, best], axis=0)) * scale)
            for score, best in zip(scores, bests)
        ]
        norms = [jnp.sum(weight, axis=1, keepdims=True) for weight in weights]
        for i in range(per):
            mixed = jnp.dot(weights[i].astype(bf16), values[i], preferred_element_type=f32)
            at = pl.ds((step * per + i) * lines, lines)
            out_ref[at, :] = mixed[:lines, :dim] + mixed[lines:, dim:]
            best_ref[at, :] = jnp.broadcast_to(bests[i], (lines, dim))
            norm_ref[at, :] = jnp.broadcast_to(norms[i][:lines] + norms[i][lines:], (lines, dim))
    total = out_ref.shape[0] - 8
    out_ref[total : total + 1, :] = best_ref[...].T[0:1]
    out_ref[total + 1 : total + 2, :] = norm_ref[...].T[0:1]


def tail_partial(queries, tail_kv, tail_len):
    _, new, heads, dim = queries.shape
    own = tail_kv.shape[0]
    lines = own * new * heads
    return pl.pallas_call(
        functools.partial(tail_kernel, math.log2(math.e) / math.sqrt(dim)),
        grid=(1,),
        in_specs=[
            pl.BlockSpec(memory_space=pltpu.SMEM),
            pl.BlockSpec((own, new, heads, dim), lambda i: (lax.axis_index("page"), 0, 0, 0)),
            pl.BlockSpec(memory_space=pl.ANY),
        ],
        out_specs=pl.BlockSpec(memory_space=pltpu.VMEM),
        out_shape=pltpu.VMEM((lines + 8, dim), jnp.float32),
        scratch_shapes=[pltpu.VMEM(tail_kv.shape, tail_kv.dtype)]
        + [pltpu.VMEM((lines, dim), jnp.float32)] * 2
        + [pltpu.SemaphoreType.DMA((4,))],
        compiler_params=pltpu.CompilerParams(vmem_limit_bytes=VMEM_LIMIT),
        cost_estimate=FREE,
        name="tail_attention",
    )(*map(in_hbm, (tail_len, queries, tail_kv)))


def merge_kernel(scale, *refs):
    parts, out_ref, held_ref = refs[:-2], refs[-2], refs[-1]
    lines, dim = held_ref.shape
    heads = out_ref.shape[1] // dim
    bests = [part[lines : lines + 1, :] for part in parts]
    best = functools.reduce(jnp.maximum, bests)
    scales = [jnp.exp2((one - best) * scale) for one in bests]
    norm = sum(factor * part[lines + 1 : lines + 2, :] for factor, part in zip(scales, parts))
    total = jnp.zeros((lines, dim), jnp.float32)
    for factor, part in zip(scales, parts):
        share = jnp.broadcast_to(factor / norm, (lines, lines)).T
        total = total + share * part[0:lines, :]
    held_ref[...] = total
    for h in range(heads):
        out_ref[:, h * dim : (h + 1) * dim] = held_ref[
            pl.ds(h, lines // heads, stride=heads), :
        ].astype(out_ref.dtype)


def merge_partials(parts, heads):
    lines, dim = parts[0].shape[0] - 8, parts[0].shape[1]
    vmem = pl.BlockSpec(memory_space=pltpu.VMEM)
    return pl.pallas_call(
        functools.partial(merge_kernel, math.log2(math.e) / math.sqrt(dim)),
        in_specs=[vmem] * len(parts),
        out_specs=vmem,
        out_shape=jax.ShapeDtypeStruct((lines // heads, heads * dim), jnp.bfloat16),
        scratch_shapes=[pltpu.VMEM((lines, dim), jnp.float32)],
        compiler_params=pltpu.CompilerParams(vmem_limit_bytes=VMEM_LIMIT),
        name="merge_partials",
    )(*parts)


def shard_copies(w_hbm, w_ref, sems, shards, axis):
    page_pos = lax.axis_index("page")
    units = w_ref.shape[1 + axis]
    copies = []
    for i, k in enumerate(shards):
        at = pl.ds(pl.multiple_of((page_pos ^ k) * units, 128), units)
        source = w_hbm.at[:, at] if axis else w_hbm.at[at, :]
        copies.append(pltpu.make_async_copy(source, w_ref.at[i], sems.at[i]))
    return start_copies(copies)


def hold_kernel(shards, after_ref, w_hbm, out_ref, sems):
    for copy in shard_copies(w_hbm, out_ref, sems, shards, 1):
        copy.wait()


def hold_columns(after, weights, shards, units):
    depth = weights.shape[0]
    return pl.pallas_call(
        functools.partial(hold_kernel, shards),
        in_specs=[pl.BlockSpec(memory_space=pltpu.VMEM), pl.BlockSpec(memory_space=pl.ANY)],
        out_specs=pl.BlockSpec(memory_space=pltpu.VMEM),
        out_shape=pltpu.VMEM((len(shards), depth, units), weights.dtype),
        scratch_shapes=[pltpu.SemaphoreType.DMA((len(shards),))],
        compiler_params=pltpu.CompilerParams(vmem_limit_bytes=VMEM_LIMIT),
        cost_estimate=FREE,
        name="hold_columns",
    )(after, in_hbm(weights))


def project_kernel(per_group, *refs):
    blocks, (w_ref, stream_ref, keep_ref, give_ref, lhs_ref, sum_ref) = refs[:4], refs[4:]
    page_pos, blk_pos = lax.axis_index("page"), lax.axis_index("blk")
    height = blocks[0].shape[0]
    group = w_ref.shape[2]
    width = stream_ref.shape[2]
    for k, block in enumerate(blocks):
        start = pl.multiple_of((page_pos ^ k) * height, height)
        lhs_ref[pl.ds(start, height), :] = block[...]
    product = jnp.dot(lhs_ref[...], w_ref[0], preferred_element_type=jnp.float32)
    sum_ref[...] = product.reshape(sum_ref.shape)
    for part in range(per_group):

        @pl.when(blk_pos == page_pos * per_group + part)
        def _(part=part):
            stream = flat_rows(stream_ref[...]).astype(jnp.float32)
            at = (slice(None), slice(None), slice(part * width, (part + 1) * width))
            sum_ref[at] = sum_ref[at] + stream.reshape(sum_ref.shape[:2] + (width,))

    core = blk_pos % 2
    for chip in range(4):
        keep_ref[chip] = sum_ref[2 * chip + core]
        give_ref[chip] = sum_ref[2 * chip + 1 - core].astype(give_ref.dtype)


def project(blocks, w_out, stream_in, group):
    height, depth = blocks[0].shape
    rows = 4 * height
    vmem = pl.BlockSpec(memory_space=pltpu.VMEM)
    part = (4, rows // 8, group)
    return pl.pallas_call(
        functools.partial(project_kernel, group // stream_in.shape[2]),
        in_specs=[vmem] * 6,
        out_specs=[vmem] * 2,
        out_shape=[
            jax.ShapeDtypeStruct(part, jnp.float32),
            jax.ShapeDtypeStruct(part, jnp.bfloat16),
        ],
        scratch_shapes=[
            pltpu.VMEM((rows, depth), jnp.bfloat16),
            pltpu.VMEM((8, rows // 8, group), jnp.float32),
        ],
        compiler_params=pltpu.CompilerParams(vmem_limit_bytes=VMEM_LIMIT),
        name="project_attention",
    )(*blocks, w_out, stream_in)


def pair_kernel(keep_ref, got_ref, own_ref, *out_refs):
    chip = lax.axis_index("blk") // 2
    own_ref[...] = keep_ref[chip] + got_ref[chip].astype(jnp.float32)
    for k, out_ref in enumerate(out_refs, 1):
        total = keep_ref[chip ^ k] + got_ref[chip ^ k].astype(jnp.float32)
        out_ref[...] = total.astype(out_ref.dtype)


def pair_pieces(keep, got):
    vmem = pl.BlockSpec(memory_space=pltpu.VMEM)
    shape = keep.shape[1:]
    return pl.pallas_call(
        pair_kernel,
        in_specs=[vmem] * 2,
        out_specs=[vmem] * 4,
        out_shape=[jax.ShapeDtypeStruct(shape, jnp.float32)]
        + [jax.ShapeDtypeStruct(shape, jnp.bfloat16)] * 3,
        compiler_params=pltpu.CompilerParams(vmem_limit_bytes=VMEM_LIMIT),
        name="pair_pieces",
    )(keep, got)


def residual_kernel(own_ref, c_ref, b_ref, a_ref, bias_ref, score_ref, out_ref):
    group, piece = own_ref.shape[1], score_ref.shape[0]
    total = own_ref[...] + bias_ref[...].astype(jnp.float32)
    for ref in (a_ref, b_ref, c_ref):
        total = total + ref[...].astype(jnp.float32)
    out_ref[:, :group] = total.astype(out_ref.dtype)
    out_ref[:, group : group + piece] = jnp.broadcast_to(
        as_row(score_ref), (own_ref.shape[0], piece)
    ).astype(out_ref.dtype)


def residual_rows(own, arrived, b_out, w_score):
    vmem = pl.BlockSpec(memory_space=pltpu.VMEM)
    return pl.pallas_call(
        residual_kernel,
        grid=(1,),
        in_specs=[vmem] * 4
        + [pl.BlockSpec((1, own.shape[1]), lambda i: (0, lax.axis_index("page"))), vmem],
        out_specs=vmem,
        out_shape=pltpu.VMEM((own.shape[0], own.shape[1] + 256), jnp.bfloat16),
        compiler_params=pltpu.CompilerParams(vmem_limit_bytes=VMEM_LIMIT),
        name="residual_rows",
    )(own, *arrived, b_out.reshape(1, -1), w_score)


def as_row(ref):
    return ref[...].astype(jnp.float32).reshape(1, ref.shape[0])


def split2(value):
    high = value.astype(jnp.bfloat16)
    return high, (value - high.astype(jnp.float32)).astype(jnp.bfloat16)


def whole2(high, low):
    return high.astype(jnp.float32) + low.astype(jnp.float32)


def up_first_kernel(*refs):
    blocks, refs = refs[:8], refs[8:]
    gain_ref, bias_ref, down_ref, near_ref, w_hbm = refs[:5]
    out_refs, weight_ref, refs = refs[5:8], refs[8], refs[9:]
    lhs_ref, residual_ref, stats_ref, mean_ref, square_ref, base_ref, weights_ref, w_ref, sems = refs
    copies = shard_copies(w_hbm, w_ref, sems, (3, 2), 1)
    blk_pos = lax.axis_index("blk")
    core, chip = blk_pos % 2, blk_pos // 2
    height, group = blocks[0].shape[0], lhs_ref.shape[1]
    rows, piece = 8 * height, group // 8
    gain = as_row(gain_ref)
    places = []
    for i, block in enumerate(blocks):
        from_core = core if i < 4 else 1 - core
        owner = 2 * (chip ^ (i % 4)) + from_core
        places.append(pl.ds(pl.multiple_of(owner * height, height), height))
        weights_ref[pl.ds(owner, 1), :] = block[0:1, group:].astype(jnp.float32)
    weights = [weights_ref[b : b + 1, :piece] for b in range(8)]
    weight_ref[...] = jnp.concatenate(weights, axis=1)
    own_weights = [jnp.where(blk_pos == b, weight, 0.0) for b, weight in enumerate(weights)]
    score_row = jnp.concatenate(own_weights, axis=1)
    own_weight = sum(own_weights)
    fixed = jnp.sum(as_row(down_ref) * own_weight, axis=1, keepdims=True)
    for block, at in zip(blocks, places):
        residual = block[:, :group].astype(jnp.float32)
        mean = jnp.sum(residual, axis=1, keepdims=True) * (1.0 / group)
        centred = residual - mean
        square = jnp.sum(centred * centred, axis=1, keepdims=True)
        base = jnp.sum(residual * score_row, axis=1, keepdims=True) + fixed
        residual_ref[at, :] = block[:, :group]
        lhs_ref[at, :] = (centred * gain).astype(lhs_ref.dtype)
        mean_ref[at, :] = jnp.broadcast_to(mean, (height, rows))
        square_ref[at, :] = jnp.broadcast_to(square, (height, rows))
        base_ref[at, :] = jnp.broadcast_to(base, (height, rows))
    row = lax.broadcasted_iota(jnp.int32, (lhs_ref.shape[0] - rows, group), 0)
    bias = as_row(bias_ref)
    lhs_ref[rows:, :] = jnp.where(
        row == 0, gain, jnp.where(row == 1, bias, 0.0)
    ).astype(lhs_ref.dtype)
    pieces = []
    for ref in (mean_ref, square_ref, base_ref):
        pieces += split2(ref[...].T[0:1])
    stats_ref[...] = jnp.concatenate(pieces, axis=0)
    out_refs[2][...] = up_product(lhs_ref, near_ref.at[0], stats_ref, rows)
    for i in range(2):
        copies[i].wait()
        out_refs[i][...] = up_product(lhs_ref, w_ref.at[i], stats_ref, rows)


def up_product(lhs_ref, w_ref, stats_ref, rows):
    product = jnp.dot(lhs_ref[...], w_ref[...], preferred_element_type=jnp.float32)
    below = product[rows : rows + 8]
    padded = jnp.concatenate(
        [
            jnp.zeros((2, rows), jnp.float32),
            stats_ref[...].astype(jnp.float32),
        ],
        axis=0,
    )
    row = lax.broadcasted_iota(jnp.int32, (8, rows), 0)
    first = jnp.where(row < 2, below[:, :rows], padded)
    below = jnp.concatenate([first, below[:, rows:]], axis=1)
    return jnp.concatenate([product[:rows], below], axis=0).astype(jnp.bfloat16)


def up_first(blocks, ln_gain, ln_bias, b_down, near_up, w_up):
    height = blocks[0].shape[0]
    rows = 8 * height
    _, group, units = near_up.shape
    bf16, f32 = jnp.bfloat16, jnp.float32
    vmem = pl.BlockSpec(memory_space=pltpu.VMEM)
    return pl.pallas_call(
        up_first_kernel,
        in_specs=[vmem] * 12 + [pl.BlockSpec(memory_space=pl.ANY)],
        out_specs=[vmem] * 7,
        out_shape=[pltpu.VMEM((rows + 8, units), bf16)] * 3
        + [
            pltpu.VMEM((1, group), f32),
            pltpu.VMEM((rows + 16, group), bf16),
            jax.ShapeDtypeStruct((rows, group), bf16),
            pltpu.VMEM((6, rows), bf16),
        ],
        scratch_shapes=[pltpu.VMEM((rows, rows), f32)] * 3
        + [
            pltpu.VMEM((8, blocks[0].shape[1] - group), f32),
            pltpu.VMEM((2, group, units), bf16),
            pltpu.SemaphoreType.DMA((2,)),
        ],
        compiler_params=pltpu.CompilerParams(vmem_limit_bytes=VMEM_LIMIT),
        name="norm_and_up",
    )(
        *blocks,
        ln_gain,
        ln_bias,
        b_down,
        near_up,
        in_hbm(w_up),
    )


def up_own_kernel(lhs_ref, stats_ref, w_hbm, out_ref, w_ref, sems):
    copies = shard_copies(w_hbm, w_ref, sems, (0,), 1)
    copies[0].wait()
    out_ref[...] = up_product(lhs_ref, w_ref.at[0], stats_ref, stats_ref.shape[1])


def up_own(lhs, stats, w_up):
    group = lhs.shape[1]
    units = w_up.shape[1] // 4
    bf16 = jnp.bfloat16
    vmem = pl.BlockSpec(memory_space=pltpu.VMEM)
    return pl.pallas_call(
        up_own_kernel,
        in_specs=[vmem] * 2 + [pl.BlockSpec(memory_space=pl.ANY)],
        out_specs=vmem,
        out_shape=pltpu.VMEM((stats.shape[1] + 8, units), bf16),
        scratch_shapes=[pltpu.VMEM((1, group, units), bf16), pltpu.SemaphoreType.DMA((1,))],
        compiler_params=pltpu.CompilerParams(vmem_limit_bytes=VMEM_LIMIT),
        cost_estimate=FREE,
        name="up_own",
    )(lhs, stats, in_hbm(w_up))


def image_kernel(score_ref, w_ref, out_ref, column_ref):
    step = pl.program_id(0)

    @pl.when(step == 0)
    def _():
        wide = jnp.broadcast_to(score_ref[...], column_ref.shape[::-1])
        column_ref[...] = wide.T.astype(column_ref.dtype)

    image = jnp.dot(w_ref[...], column_ref[...], preferred_element_type=jnp.float32).T[0:1]
    high, low = split2(image)
    out_ref[pl.ds(step, 1), :] = high.astype(jnp.float32)
    out_ref[pl.ds(step + pl.num_programs(0), 1), :] = low.astype(jnp.float32)


def image_of(score_group, w_down):
    depth, group = w_down.shape
    tile = depth // 4
    return pl.pallas_call(
        image_kernel,
        grid=(4,),
        in_specs=[
            pl.BlockSpec((1, group), lambda i: (0, 0)),
            pl.BlockSpec((tile, group), lambda i: (i, 0)),
        ],
        out_specs=pl.BlockSpec((8, tile), lambda i: (0, 0)),
        out_shape=pltpu.VMEM((8, tile), jnp.float32),
        scratch_shapes=[pltpu.VMEM((group, 128), jnp.bfloat16)],
        compiler_params=pltpu.CompilerParams(vmem_limit_bytes=VMEM_LIMIT),
        cost_estimate=FREE,
        name="score_image",
    )(score_group, in_hbm(w_down))


def hidden_kernel(group, *refs):
    parts, (bias_ref, image_ref, whole_ref, top_ref, bottom_ref, base_ref) = refs[:4], refs[4:]
    rows, cut = parts[0].shape[0] - 8, top_ref.shape[0]
    f32 = jnp.float32
    tails = [part[rows:, :].astype(f32) for part in parts]
    stats = [
        [tail[2 + i : 3 + i, :rows] + tail[3 + i : 4 + i, :rows] for tail in tails]
        for i in (0, 2, 4)
    ]
    means, squares, bases = stats
    row_mean = pair_sum(means) * 0.25
    shifts = [mean - row_mean for mean in means]
    spread = sum(square + group * shift * shift for square, shift in zip(squares, shifts))
    inverse = lax.rsqrt(spread * (0.25 / group) + EPS)
    pad = jnp.zeros((rows - 6, rows), f32)
    columns = jnp.concatenate([inverse, *shifts, pair_sum(bases), pad], axis=0).T
    offset = sum(tail[1:2] for tail in tails) + bias_ref[...].astype(f32)
    total = sum(part[0:rows, :].astype(f32) for part in parts)
    for k, tail in enumerate(tails):
        total = total + columns[:, 1 + k : 2 + k] * tail[0:1]
    hidden = jnp.maximum(total * columns[:, 0:1] + offset, 0.0)
    below = jnp.concatenate([hidden, image_ref[...]], axis=0).astype(whole_ref.dtype)
    whole_ref[...] = below
    top_ref[...] = below[:cut]
    bottom_ref[...] = below[cut:]
    base_ref[...] = columns[:, 5:6]


def own_hidden_units(parts, b_up, image, group):
    vmem = pl.BlockSpec(memory_space=pltpu.VMEM)
    height, units = parts[0].shape
    bf16 = jnp.bfloat16
    return pl.pallas_call(
        functools.partial(hidden_kernel, group),
        grid=(1,),
        in_specs=[vmem] * 4
        + [pl.BlockSpec((1, units), lambda i: (0, lax.axis_index("page"))), vmem],
        out_specs=[vmem] * 4,
        out_shape=[
            pltpu.VMEM((height, units), bf16),
            pltpu.VMEM((TOP, units), bf16),
            pltpu.VMEM((height - TOP, units), bf16),
            pltpu.VMEM((height - 8, 1), jnp.float32),
        ],
        compiler_params=pltpu.CompilerParams(vmem_limit_bytes=VMEM_LIMIT),
        name="hidden_units",
    )(*parts, b_up.reshape(1, -1), image)


def down_first_kernel(hidden_ref, w_hbm, sum_ref, held_ref, w_ref, sems, held_sems):
    rows = sum_ref.shape[0]
    copies = shard_copies(w_hbm, w_ref, sems, (0,), 0)
    held = shard_copies(w_hbm, held_ref, held_sems, (1, 2, 3), 0)
    copies[0].wait()
    sum_ref[...] = jnp.dot(
        hidden_ref[0:rows, :], w_ref[0], preferred_element_type=jnp.float32
    )
    for copy in held:
        copy.wait()


def down_first(hidden, w_down):
    rows, units = hidden.shape[0] - 8, hidden.shape[1]
    group = w_down.shape[1]
    vmem = pl.BlockSpec(memory_space=pltpu.VMEM)
    return pl.pallas_call(
        down_first_kernel,
        in_specs=[vmem, pl.BlockSpec(memory_space=pl.ANY)],
        out_specs=[vmem] * 2,
        out_shape=[
            pltpu.VMEM((rows, group), jnp.float32),
            pltpu.VMEM((3, units, group), jnp.bfloat16),
        ],
        scratch_shapes=[
            pltpu.VMEM((1, units, group), jnp.bfloat16),
            pltpu.SemaphoreType.DMA((1,)),
            pltpu.SemaphoreType.DMA((3,)),
        ],
        compiler_params=pltpu.CompilerParams(vmem_limit_bytes=VMEM_LIMIT),
        cost_estimate=FREE,
        name="down_own",
    )(hidden, in_hbm(w_down))


def down_rest_kernel(base_ref, sum_ref, held_ref, *refs):
    parts, (keep_ref, give_ref, score_ref, image_ref) = refs[:6], refs[6:]
    rows = sum_ref.shape[0]
    f32 = jnp.float32
    page_pos = lax.axis_index("page")
    core = lax.axis_index("blk") % 2
    piece = keep_ref.shape[2]
    cut = parts[2].shape[0]
    hiddens = [part[0:rows, :] for part in parts[:2]]
    for top, bottom in (parts[2:4], parts[4:6]):
        hiddens.append(jnp.concatenate([top[...], bottom[0 : rows - cut, :]], axis=0))
    product = sum_ref[...]
    for k in (1, 2, 3):
        product = product + jnp.dot(hiddens[k], held_ref[k - 1], preferred_element_type=f32)
    tails = [
        part[part.shape[0] - 8 :, :].astype(f32) for part in (*parts[:2], parts[3], parts[5])
    ]
    image_ref[...] = pair_sum([tail[0:4] + tail[4:8] for tail in tails])
    by_owner = []
    for k, hidden in enumerate(hiddens):
        image = image_ref[pl.ds(page_pos ^ k, 1), :]
        by_owner.append(jnp.sum(hidden.astype(f32) * image, axis=1, keepdims=True))
    score = base_ref[...] + pair_sum(by_owner)
    score_ref[...] = score
    pieces = split3(score)
    for chip in range(4):
        pair = [product[:, (2 * chip + c) * piece : (2 * chip + c + 1) * piece] for c in range(2)]
        keep_ref[chip] = jnp.where(core == 0, pair[0], pair[1])
        give_ref[chip, :, :piece] = jnp.where(core == 0, pair[1], pair[0]).astype(give_ref.dtype)
        give_ref[chip, :, piece:] = pieces


def down_rest(base, summed, held, parts):
    rows, group = summed.shape
    units = parts[0].shape[1]
    vmem = pl.BlockSpec(memory_space=pltpu.VMEM)
    return pl.pallas_call(
        down_rest_kernel,
        in_specs=[vmem] * 9,
        out_specs=[vmem] * 3,
        out_shape=[
            pltpu.VMEM((4, rows, group // 8), jnp.float32),
            pltpu.VMEM((4, rows, group // 8 + 3), jnp.bfloat16),
            pltpu.VMEM((rows, 1), jnp.float32),
        ],
        scratch_shapes=[pltpu.VMEM((4, units), jnp.float32)],
        compiler_params=pltpu.CompilerParams(vmem_limit_bytes=VMEM_LIMIT),
        name="down_rest",
    )(base, summed, held, *parts)


def split3(value):
    high = value.astype(jnp.bfloat16)
    left = value - high.astype(jnp.float32)
    middle = left.astype(jnp.bfloat16)
    low = (left - middle.astype(jnp.float32)).astype(jnp.bfloat16)
    return jnp.concatenate([high, middle, low], axis=1)


def whole3(pieces):
    return jnp.sum(pieces.astype(jnp.float32), axis=1, keepdims=True)


def pair_score_kernel(keep_ref, score_ref, got_ref, own_ref, both_ref, *out_refs):
    chip = lax.axis_index("blk") // 2
    piece = keep_ref.shape[2]
    score = whole3(split3(score_ref[...])) + whole3(got_ref[0, :, piece:])
    both_ref[...] = score
    pieces = split3(score)
    own_ref[...] = keep_ref[chip] + got_ref[chip, :, :piece].astype(jnp.float32)
    for k, out_ref in enumerate(out_refs, 1):
        total = keep_ref[chip ^ k] + got_ref[chip ^ k, :, :piece].astype(jnp.float32)
        out_ref[:, :piece] = total.astype(out_ref.dtype)
        out_ref[:, piece:] = pieces


def pair_scores(keep, score, got):
    vmem = pl.BlockSpec(memory_space=pltpu.VMEM)
    _, rows, piece = keep.shape
    return pl.pallas_call(
        pair_score_kernel,
        in_specs=[vmem] * 3,
        out_specs=[vmem] * 5,
        out_shape=[
            jax.ShapeDtypeStruct((rows, piece), jnp.float32),
            jax.ShapeDtypeStruct((rows, 1), jnp.float32),
        ]
        + [jax.ShapeDtypeStruct((rows, piece + 3), jnp.bfloat16)] * 3,
        compiler_params=pltpu.CompilerParams(vmem_limit_bytes=VMEM_LIMIT),
        name="pair_scores",
    )(keep, score, got)


def finish_kernel(own_ref, base_ref, score_ref, c_ref, b_ref, a_ref, out_ref, total_ref, held_ref):
    piece = own_ref.shape[1]
    total = own_ref[...] + base_ref[...]
    for ref in (a_ref, b_ref, c_ref):
        total = total + ref[:, :piece].astype(jnp.float32)
    out_ref[...] = total.astype(out_ref.dtype).reshape(out_ref.shape)
    scores = [whole3(ref[:, piece:]) for ref in (a_ref, b_ref, c_ref)]
    own_score = whole3(split3(score_ref[...]))
    score = (own_score + scores[0]) + (scores[1] + scores[2])
    new, samples = total_ref.shape
    held_ref[...] = jnp.broadcast_to(score, held_ref.shape)
    for n in range(new):
        total_ref[n : n + 1, :] = held_ref[pl.ds(n, samples, stride=new), :].T[0:1]


def finish(own, base, score, arrived, samples):
    vmem = pl.BlockSpec(memory_space=pltpu.VMEM)
    rows, piece = own.shape
    return pl.pallas_call(
        finish_kernel,
        in_specs=[vmem] * 6,
        out_specs=[vmem] * 2,
        out_shape=[
            jax.ShapeDtypeStruct((samples, rows // samples, piece), jnp.bfloat16),
            jax.ShapeDtypeStruct((rows // samples, samples), jnp.float32),
        ],
        scratch_shapes=[pltpu.VMEM((rows, 128), jnp.float32)],
        compiler_params=pltpu.CompilerParams(vmem_limit_bytes=VMEM_LIMIT),
        name="finish",
    )(own, base, score, *arrived)


def body(
    queries,
    prompt_kv,
    tail_kv,
    page_table,
    prompt_len,
    tail_len,
    sample_prompt,
    stream_in,
    w_out,
    b_out,
    ln_gain,
    ln_bias,
    w_up,
    b_up,
    w_down,
    b_down,
    w_score,
):
    bf16, f32 = jnp.bfloat16, jnp.float32
    samples, new_count, heads_dev, head_dim = queries.shape
    group = ln_gain.shape[0]
    blk_pos = lax.axis_index("blk")
    piece = b_down.shape[0]
    packed = prompt_partial(queries, prompt_kv, page_table, prompt_len, sample_prompt)
    shares = [packed[0]] + [send_xor(packed[k], "page", k) for k in (1, 2, 3)]
    tail = tail_partial(queries, tail_kv, tail_len)
    own_attention = merge_partials(shares + [tail], heads_dev)
    attention = gather_xor(own_attention, "page", (1, 2, 3))
    held_out = hold_columns(own_attention, w_out, (0,), group)
    keep, give = project(attention, held_out, stream_in, group)
    own, *pieces = pair_pieces(keep, send_xor(give, "blk", 1))
    units = w_up.shape[1] // 4
    arrived = [send_xor(pieces[k - 1], "blk", 2 * k) for k in (3, 2, 1)]
    own_rows = residual_rows(own, arrived, b_out, w_score)
    same_core = gather_xor(own_rows, "blk", (2, 4, 6))
    near_up = hold_columns(own_rows, w_up, (1,), units)
    same_core[1], near_up = lax.optimization_barrier((same_core[1], near_up))
    blocks = same_core + [send_xor(block, "blk", 1) for block in same_core]
    part3, part2, part1, score_group, lhs, residual, stats = up_first(
        blocks, ln_gain, ln_bias, b_down, near_up, w_up
    )
    part0 = up_own(lhs, stats, w_up)
    image = image_of(score_group, w_down)
    parts = [part0] + [
        send_xor(part, "page", k) for k, part in ((1, part1), (2, part2), (3, part3))
    ]
    whole, top, bottom, base_score = own_hidden_units(parts, b_up, image, group)
    summed, held = down_first(whole, w_down)
    far_top, summed = lax.optimization_barrier((send_xor(top, "page", 2), summed))
    hiddens = [
        whole,
        send_xor(whole, "page", 1),
        far_top,
        send_xor(bottom, "page", 2),
        send_xor(far_top, "page", 1),
        send_xor(bottom, "page", 3),
    ]
    keep, give, score = down_rest(base_score, summed, held, hiddens)
    own_base = lax.dynamic_slice_in_dim(residual, blk_pos * piece, piece, 1).astype(
        f32
    ) + b_down.astype(f32)
    own, score, *pieces = pair_scores(keep, score, send_xor(give, "blk", 1))
    arrived = [send_xor(pieces[k - 1], "blk", 2 * k) for k in (3, 2, 1)]
    output, score = finish(own, own_base, score, arrived, samples)
    return (output, score.T)


def general_body(
    queries,
    prompt_kv,
    tail_kv,
    page_table,
    prompt_len,
    tail_len,
    sample_prompt,
    stream_in,
    w_out,
    b_out,
    ln_gain,
    ln_bias,
    w_up,
    b_up,
    w_down,
    b_down,
    w_score,
):
    samples, new_count, heads_dev, head_dim = queries.shape
    slots_dev, page_len = (prompt_kv.shape[0], prompt_kv.shape[1])
    own_count, tail_max = (tail_kv.shape[0], tail_kv.shape[1])
    prompts, pages_max = page_table.shape
    page_pos = lax.axis_index("page")
    blk_pos = lax.axis_index("blk")
    inv_sqrt = 1.0 / math.sqrt(head_dim)
    entries = page_table.reshape(-1)
    slot_ids = page_pos * slots_dev + jnp.arange(slots_dev, dtype=jnp.int32)
    matched = (entries[:, None] == slot_ids[None, :]).astype(jnp.int32)
    owner_index = jnp.sum(matched * jnp.arange(entries.shape[0], dtype=jnp.int32)[:, None], axis=0)
    slot_prompt = owner_index // pages_max
    slot_page = owner_index % pages_max
    prompt_pick = (slot_prompt[:, None] == jnp.arange(prompts, dtype=jnp.int32)[None, :]).astype(
        jnp.int32
    )
    slot_limit = jnp.sum(prompt_pick * prompt_len[None, :], axis=1)
    key_pos = slot_page[:, None] * page_len + jnp.arange(page_len, dtype=jnp.int32)[None, :]
    key_live = (key_pos < slot_limit[:, None]).reshape(-1)
    key_prompt = jnp.repeat(slot_prompt, page_len)
    prompt_visible = ((sample_prompt[:, None] == key_prompt[None, :]) & key_live[None, :])[
        :, None, None, :
    ]
    cache_rows = prompt_kv.reshape(slots_dev * page_len, heads_dev, 2 * head_dim)
    prompt_scores = (
        jnp.einsum(
            "snhd,khd->snhk",
            queries,
            cache_rows[:, :, :head_dim],
            preferred_element_type=jnp.float32,
        )
        * inv_sqrt
    )
    high_p, sum_p, weights_p = softmax_part(prompt_scores, prompt_visible)
    mixed_p = jnp.einsum(
        "snhk,khd->snhd", weights_p, cache_rows[:, :, head_dim:], preferred_element_type=jnp.float32
    )
    first_row = page_pos * own_count
    own_queries = lax.dynamic_slice_in_dim(queries, first_row, own_count, 0)
    own_lengths = lax.dynamic_slice_in_dim(tail_len, first_row, own_count, 0)
    tail_scores = (
        jnp.einsum(
            "snhd,sthd->snht",
            own_queries,
            tail_kv[..., :head_dim],
            preferred_element_type=jnp.float32,
        )
        * inv_sqrt
    )
    reach_pos = own_lengths[:, None] + jnp.arange(new_count, dtype=jnp.int32)[None, :]
    tail_visible = (
        jnp.arange(tail_max, dtype=jnp.int32)[None, None, None, :] <= reach_pos[:, :, None, None]
    )
    high_t, sum_t, weights_t = softmax_part(tail_scores, tail_visible)
    mixed_t = jnp.einsum(
        "snht,sthd->snhd", weights_t, tail_kv[..., head_dim:], preferred_element_type=jnp.float32
    )
    high_t = lax.dynamic_update_slice_in_dim(
        jnp.full(high_p.shape, NEGATIVE, jnp.float32), high_t, first_row, 0
    )
    sum_t = lax.dynamic_update_slice_in_dim(
        jnp.zeros(sum_p.shape, jnp.float32), sum_t, first_row, 0
    )
    mixed_t = lax.dynamic_update_slice_in_dim(
        jnp.zeros(mixed_p.shape, jnp.float32), mixed_t, first_row, 0
    )
    partial_value = join_partials((high_p, sum_p, mixed_p), (high_t, sum_t, mixed_t))
    merged = combined_all(partial_value, "page", join_partials)
    weight_sum, weighted = (merged[1], merged[2])
    attention = (
        (weighted / weight_sum[..., None])
        .astype(jnp.bfloat16)
        .reshape(samples * new_count, heads_dev * head_dim)
    )
    contrib = jnp.dot(attention, w_out, preferred_element_type=jnp.float32)
    slice_width = stream_in.shape[2]
    column = blk_pos * slice_width
    own_stream = stream_in.reshape(samples * new_count, slice_width).astype(jnp.float32)
    contrib = lax.dynamic_update_slice_in_dim(
        contrib, lax.dynamic_slice_in_dim(contrib, column, slice_width, 1) + own_stream, column, 1
    )
    summed = lax.psum(contrib, "blk")
    residual = (summed + b_out.astype(jnp.float32)).astype(jnp.bfloat16)
    residual_f = residual.astype(jnp.float32)
    row_mean = jnp.mean(residual_f, axis=-1, keepdims=True)
    centred = residual_f - row_mean
    inverse_std = lax.rsqrt(jnp.mean(centred * centred, axis=-1, keepdims=True) + 1e-05)
    feature_count = ln_gain.shape[0]
    first_col = page_pos * feature_count
    normed = (
        lax.dynamic_slice_in_dim(centred, first_col, feature_count, 1)
        * inverse_std
        * ln_gain.astype(jnp.float32)
        + ln_bias.astype(jnp.float32)
    ).astype(jnp.bfloat16)
    up_part = jnp.dot(normed, w_up, preferred_element_type=jnp.float32).astype(jnp.bfloat16)
    hidden_sum = lax.psum(up_part, "page").astype(jnp.float32)
    hidden = jnp.maximum(hidden_sum + b_up.astype(jnp.float32), 0.0).astype(jnp.bfloat16)
    projected = jnp.dot(hidden, w_down, preferred_element_type=jnp.float32)
    out_share = lax.psum_scatter(projected, "blk", scatter_dimension=1, tiled=True)
    piece_width = b_down.shape[0]
    out_column = first_col + blk_pos * piece_width
    output = (
        out_share
        + lax.dynamic_slice_in_dim(residual_f, out_column, piece_width, 1)
        + b_down.astype(jnp.float32)
    ).astype(jnp.bfloat16)
    score_part = jnp.sum(output.astype(jnp.float32) * w_score.astype(jnp.float32), axis=-1)
    row_score = lax.psum(score_part, ("page", "blk"))
    return (output.reshape(samples, new_count, piece_width), row_score.reshape(samples, new_count))


def solution(mesh):
    compute = body if (mesh.shape["page"], mesh.shape["blk"]) == (4, 8) else general_body

    placed = (
        P(None, None, "blk", None),
        P("page", None, "blk", None),
        P("page", None, "blk", None),
        P(),
        P(),
        P(),
        P(),
        P(None, None, "blk"),
        P("blk", None),
        P(),
        P("page"),
        P("page"),
        P("page", "blk"),
        P("blk"),
        P("blk", "page"),
        P(("page", "blk")),
        P(("page", "blk")),
    )
    return jax.shard_map(
        compute,
        mesh=mesh,
        in_specs=placed,
        out_specs=(P(None, None, ("page", "blk")), P()),
        check_vma=False,
    )
```

time: 114 us -> 103 us (0.904)
  waiting for transfers between devices: 38.7 us -> 26.5 us
  starting transfers between devices: 33.8 us -> 39.6 us
  Pallas kernels: 39.2 us -> 35.7 us
    ppermute x31 -> x29, waiting for transfers between devices: 38.7 us -> 26.5 us  [send_xor(): return lax.ppermute(value, axis, [(i, i ^ distance) for i in range(size)])]
    ppermute x31 -> x29, starting transfers between devices: 33.8 us -> 39.6 us  [send_xor(): return lax.ppermute(value, axis, [(i, i ^ distance) for i in range(size)])]
    pallas_call x3 -> x5, Pallas kernels: 11.4 us -> 15.3 us  [the longest x1 7.37 us: image_of(): pl.pallas_call(image_kernel, grid=(4,), in_specs=[pl.BlockSpec((1, group)...]
    pallas_call x1, Pallas kernels: 6.78 us -> 3.24 us  [prompt_partial(): pl.pallas_call(functools.partial(prompt_kernel, math.log2(math.e) / math....]
    pallas_call x1, Pallas kernels: 7.13 us -> 5.23 us  [tail_partial(): pl.pallas_call(functools.partial(tail_kernel, math.log2(math.e) / math.sq...]
    pallas_call x1, Pallas kernels: 2.05 us -> 0.73 us  [project(): pl.pallas_call(functools.partial(project_kernel, group // stream_in.shape...]
  transfers between devices with their start and end apart: 31 -> 29, of which waited for: 19 -> 17; matrix products, arithmetic and copies ran while one was open for 1% -> 0% of each run, Pallas kernels for 19% -> 23%
where the time goes in v3:
time: 103 us
  starting transfers between devices  39.6 us (38%)
  Pallas kernels  35.7 us (35%)
  waiting for transfers between devices  26.5 us (26%)
    ppermute x29, starting transfers between devices, send_xor(): return lax.ppermute(value, axis, [(i, i ^ distance) for i in range(size)])  39.6 us
    ppermute x29, waiting for transfers between devices, send_xor(): return lax.ppermute(value, axis, [(i, i ^ distance) for i in range(size)])  26.5 us
    pallas_call x1, Pallas kernels, image_of(): pl.pallas_call(image_kernel, grid=(4,), in_specs=[pl.BlockSpec((1, group)...  7.37 us
    pallas_call x1, Pallas kernels, tail_partial(): pl.pallas_call(functools.partial(tail_kernel, math.log2(math.e) / math.sq...  5.23 us
    pallas_call x1, Pallas kernels, down_first(): pl.pallas_call(down_first_kernel, in_specs=[vmem, pl.BlockSpec(memory_spa...  4.76 us
    pallas_call x1, Pallas kernels, up_first(): pl.pallas_call(up_first_kernel, in_specs=[vmem] * 12 + [pl.BlockSpec(memo...  4.49 us
    pallas_call x2, Pallas kernels, hold_columns(): pl.pallas_call(functools.partial(hold_kernel, shards), in_specs=[pl.Block...  3.42 us
    pallas_call x1, Pallas kernels, prompt_partial(): pl.pallas_call(functools.partial(prompt_kernel, math.log2(math.e) / math....  3.24 us
  transfers between devices with their start and end apart: 29, of which 17 were waited for; matrix products, arithmetic and copies ran while one was open for 0% of the time, Pallas kernels for 23%

profile of v3, /device:TPU:0, one launch (start us, length us, event | category | flops | bytes accessed | tf_op | source)
XLA Modules:
  0.0 102.8 jit_solution(15196780951356766573)
XLA Ops:
  0.6 3.2 %prompt_attention.1 = (f32[136,128]{1,0:T(8,128)S(1)}, f32[136,128]{1,0:T(8,128)S(1)}, f32[136,128]{1,0:T(8,128)S(1)}, f32[136,128]{1,0:T(8,128)S(1)}) custom-call(s32[4,16]{1,0:T(4,128)} %table_hbm.1, s32[4]{0:T(128)} %len_hbm.1, s32[64]{0:T(128)} %prompt_hbm.1, bf16[64,2,4,128]{3,2,1,0:T(4,128)(2,1)} %q_ref.1, bf16[16,64,4,256]{3,2,1,0:T(4,128)(2,1)} %kv_hbm.2), custom_call_target="tpu_custom_call" | custom-call | tf_op jit(solution)/shard_map/prompt_attention/pallas_call | solution.py:174
  3.9 3.1 %collective-permute-start = (f32[136,128]{1,0:T(8,128)S(1)}, f32[136,128]{1,0:T(8,128)S(1)}, u32[]{:S(2)}, u32[]{:S(2)}) collective-permute-start(f32[136,128]{1,0:T(8,128)S(1)} %get-tuple-element.40), channel_id=1, source_target_pairs={{0,8},{8,0},{16,24},{24,16},{1,9},{9,1},{17,25},{25,17},{2,10},{10... | collective-permute-start | bytes 208904 | tf_op jit(solution)/shard_map/ppermute | solution.py:46
  7.0 2.6 %collective-permute-start.1 = (f32[136,128]{1,0:T(8,128)S(1)}, f32[136,128]{1,0:T(8,128)S(1)}, u32[]{:S(2)}, u32[]{:S(2)}) collective-permute-start(f32[136,128]{1,0:T(8,128)S(1)} %get-tuple-element.41), channel_id=1, source_target_pairs={{0,16},{8,24},{16,0},{24,8},{1,17},{9,25},{17,1},{25,9},{2,18},{10... | collective-permute-start | bytes 208904 | tf_op jit(solution)/shard_map/ppermute | solution.py:46
  9.6 5.2 %tail_attention.1.refs_4_ = f32[136,128]{1,0:T(8,128)S(1)} custom-call(s32[64]{0:T(128)} %len_ref.1, bf16[64,2,4,128]{3,2,1,0:T(4,128)(2,1)} %q_ref.1, bf16[16,256,4,256]{3,2,1,0:T(4,128)(2,1)} %kv_hbm.3), custom_call_target="tpu_custom_call" | custom-call | tf_op jit(solution)/shard_map/tail_attention/pallas_call | solution.py:265
  16.0 2.9 %collective-permute-start.5 = (bf16[32,512]{1,0:T(8,128)(2,1)S(1)}, bf16[32,512]{1,0:T(8,128)(2,1)S(1)}, u32[]{:S(2)}, u32[]{:S(2)}) collective-permute-start(bf16[32,512]{1,0:T(8,128)(2,1)S(1)} %merge_partials.1.after_ref.refs_0_), channel_id=1, source_target_pairs={{0,24},{8,16},{16,8},{24,0},{1,25},{9,17},{17,9},{25,1},{2,26},{10... | collective-permute-start | bytes 98312 | tf_op jit(solution)/shard_map/ppermute | solution.py:46
  18.9 1.5 %collective-permute-start.3 = (bf16[32,512]{1,0:T(8,128)(2,1)S(1)}, bf16[32,512]{1,0:T(8,128)(2,1)S(1)}, u32[]{:S(2)}, u32[]{:S(2)}) collective-permute-start(bf16[32,512]{1,0:T(8,128)(2,1)S(1)} %merge_partials.1.after_ref.refs_0_), channel_id=1, source_target_pairs={{0,8},{8,0},{16,24},{24,16},{1,9},{9,1},{17,25},{25,17},{2,10},{10... | collective-permute-start | bytes 98312 | tf_op jit(solution)/shard_map/ppermute | solution.py:46
  20.4 1.5 %hold_columns.2.refs_4_ = bf16[1,512,1792]{2,1,0:T(8,128)(2,1)S(1)} custom-call(bf16[32,512]{1,0:T(8,128)(2,1)S(1)} %merge_partials.1.after_ref.refs_0_, bf16[512,7168]{1,0:T(8,128)(2,1)} %w_hbm.4), custom_call_target="tpu_custom_call" | custom-call | tf_op jit(solution)/shard_map/hold_columns/pallas_call | solution.py:335
  22.0 1.8 %collective-permute-done.4.refs_2_ = bf16[32,512]{1,0:T(8,128)(2,1)S(1)} collective-permute-done((bf16[32,512]{1,0:T(8,128)(2,1)S(1)}, bf16[32,512]{1,0:T(8,128)(2,1)S(1)}, u32[]{:S(2)}, u32[]{:S(2)}) %collective-permute-start.4) | collective-permute-done | bytes 32800 | tf_op jit(solution)/shard_map/ppermute | solution.py:46
  24.5 1.5 %collective-permute-done.6.got_ref = bf16[4,16,1792]{2,1,0:T(8,128)(2,1)S(1)} collective-permute-done((bf16[4,16,1792]{2,1,0:T(8,128)(2,1)S(1)}, bf16[4,16,1792]{2,1,0:T(8,128)(2,1)S(1)}, u32[]{:S(2)}, u32[]{:S(2)}) %collective-permute-start.6) | collective-permute-done | bytes 229408 | tf_op jit(solution)/shard_map/ppermute | solution.py:46
  26.1 2.4 %collective-permute-start.7 = (bf16[16,1792]{1,0:T(8,128)(2,1)S(1)}, bf16[16,1792]{1,0:T(8,128)(2,1)S(1)}, u32[]{:S(2)}, u32[]{:S(2)}) collective-permute-start(bf16[16,1792]{1,0:T(8,128)(2,1)S(1)} %get-tuple-element.46), channel_id=1, source_target_pairs={{0,6},{1,7},{2,4},{3,5},{4,2},{5,3},{6,0},{7,1},{8,14},{9,15},{10,... | collective-permute-start | bytes 172040 | tf_op jit(solution)/shard_map/ppermute | solution.py:46
  29.7 1.6 %collective-permute-done.7.c_ref = bf16[16,1792]{1,0:T(8,128)(2,1)S(1)} collective-permute-done((bf16[16,1792]{1,0:T(8,128)(2,1)S(1)}, bf16[16,1792]{1,0:T(8,128)(2,1)S(1)}, u32[]{:S(2)}, u32[]{:S(2)}) %collective-permute-start.7) | collective-permute-done | bytes 57376 | tf_op jit(solution)/shard_map/ppermute | solution.py:46
  31.3 1.4 %collective-permute-done.8.b_ref = bf16[16,1792]{1,0:T(8,128)(2,1)S(1)} collective-permute-done((bf16[16,1792]{1,0:T(8,128)(2,1)S(1)}, bf16[16,1792]{1,0:T(8,128)(2,1)S(1)}, u32[]{:S(2)}, u32[]{:S(2)}) %collective-permute-start.8) | collective-permute-done | bytes 57376 | tf_op jit(solution)/shard_map/ppermute | solution.py:46
  34.0 2.4 %collective-permute-start.12 = (bf16[16,2048]{1,0:T(8,128)(2,1)S(1)}, bf16[16,2048]{1,0:T(8,128)(2,1)S(1)}, u32[]{:S(2)}, u32[]{:S(2)}) collective-permute-start(bf16[16,2048]{1,0:T(8,128)(2,1)S(1)} %residual_rows.1.after_ref.refs_0_), channel_id=1, source_target_pairs={{0,6},{1,7},{2,4},{3,5},{4,2},{5,3},{6,0},{7,1},{8,14},{9,15},{10,... | collective-permute-start | bytes 196616 | tf_op jit(solution)/shard_map/ppermute | solution.py:46
  36.8 1.9 %hold_columns.3.refs_11_ = bf16[1,1792,896]{2,1,0:T(8,128)(2,1)S(1)} custom-call(bf16[16,2048]{1,0:T(8,128)(2,1)S(1)} %residual_rows.1.after_ref.refs_0_, bf16[1792,3584]{1,0:T(8,128)(2,1)} %w_hbm.6), custom_call_target="tpu_custom_call" | custom-call | tf_op jit(solution)/shard_map/hold_columns/pallas_call | solution.py:335
  42.0 4.5 %norm_and_up.1 = (bf16[136,896]{1,0:T(8,128)(2,1)S(1)}, bf16[136,896]{1,0:T(8,128)(2,1)S(1)}, bf16[136,896]{1,0:T(8,128)(2,1)S(1)}, f32[1,1792]{1,0:T(1,128)S(1)...) custom-call(bf16[16,2048]{1,0:T(8,128)(2,1)S(1)} %residual_rows.1.after_ref.refs_0_, ...), custom_call_target="tpu_custom_call" | custom-call | tf_op jit(solution)/shard_map/norm_and_up/pallas_call | solution.py:525
  47.2 1.8 %collective-permute-start.18 = (bf16[136,896]{1,0:T(8,128)(2,1)S(1)}, bf16[136,896]{1,0:T(8,128)(2,1)S(1)}, u32[]{:S(2)}, u32[]{:S(2)}) collective-permute-start(bf16[136,896]{1,0:T(8,128)(2,1)S(1)} %get-tuple-element.54), channel_id=1, source_target_pairs={{0,16},{8,24},{16,0},{24,8},{1,17},{9,25},{17,1},{25,9},{2,18},{10... | collective-permute-start | bytes 731144 | tf_op jit(solution)/shard_map/ppermute | solution.py:46
  49.0 2.0 %collective-permute-start.19 = (bf16[136,896]{1,0:T(8,128)(2,1)S(1)}, bf16[136,896]{1,0:T(8,128)(2,1)S(1)}, u32[]{:S(2)}, u32[]{:S(2)}) collective-permute-start(bf16[136,896]{1,0:T(8,128)(2,1)S(1)} %get-tuple-element.55), channel_id=1, source_target_pairs={{0,24},{8,16},{16,8},{24,0},{1,25},{9,17},{17,9},{25,1},{2,26},{10... | collective-permute-start | bytes 731144 | tf_op jit(solution)/shard_map/ppermute | solution.py:46
  51.0 2.6 %up_own.1.refs_0_ = bf16[136,896]{1,0:T(8,128)(2,1)S(1)} custom-call(bf16[144,1792]{1,0:T(8,128)(2,1)S(1)} %get-tuple-element.51.lhs_ref, bf16[6,128]{1,0:T(8,128)(2,1)S(1)} %get-tuple-element.52.stats_ref, bf16[1792,3584]{1,0:T(8,128)(2,1)} %w_hbm.6), custom_call_target="tpu_custom_call" | custom-call | tf_op jit(solution)/shard_map/up_own/pallas_call | solution.py:565
  53.7 7.4 %score_image.1.refs_5_ = f32[8,896]{1,0:T(8,128)S(1)} custom-call(f32[1,1792]{1,0:T(1,128)S(1)} %get-tuple-element.56.score_ref, bf16[3584,1792]{1,0:T(8,128)(2,1)} %w_hbm.7), custom_call_target="tpu_custom_call" | custom-call | tf_op jit(solution)/shard_map/score_image/pallas_call | solution.py:594
  61.0 6.3 %collective-permute-done.18.refs_2_ = bf16[136,896]{1,0:T(8,128)(2,1)S(1)} collective-permute-done((bf16[136,896]{1,0:T(8,128)(2,1)S(1)}, bf16[136,896]{1,0:T(8,128)(2,1)S(1)}, u32[]{:S(2)}, u32[]{:S(2)}) %collective-permute-start.18) | collective-permute-done | bytes 243744 | tf_op jit(solution)/shard_map/ppermute | solution.py:46
  67.8 5.0 %collective-permute-start.21 = (bf16[136,896]{1,0:T(8,128)(2,1)S(1)}, bf16[136,896]{1,0:T(8,128)(2,1)S(1)}, u32[]{:S(2)}, u32[]{:S(2)}) collective-permute-start(bf16[136,896]{1,0:T(8,128)(2,1)S(1)} %get-tuple-element.59.hidden_ref.refs_0_), channel_id=1, source_target_pairs={{0,8},{8,0},{16,24},{24,16},{1,9},{9,1},{17,25},{25,17},{2,10},{10... | collective-permute-start | bytes 731144 | tf_op jit(solution)/shard_map/ppermute | solution.py:46
  72.8 1.5 %collective-permute-start.20 = (bf16[64,896]{1,0:T(8,128)(2,1)S(1)}, bf16[64,896]{1,0:T(8,128)(2,1)S(1)}, u32[]{:S(2)}, u32[]{:S(2)}) collective-permute-start(bf16[64,896]{1,0:T(8,128)(2,1)S(1)} %get-tuple-element.58), channel_id=1, source_target_pairs={{0,16},{8,24},{16,0},{24,8},{1,17},{9,25},{17,1},{25,9},{2,18},{10... | collective-permute-start | bytes 344072 | tf_op jit(solution)/shard_map/ppermute | solution.py:46
  74.3 1.4 %collective-permute-start.24 = (bf16[72,896]{1,0:T(8,128)(2,1)S(1)}, bf16[72,896]{1,0:T(8,128)(2,1)S(1)}, u32[]{:S(2)}, u32[]{:S(2)}) collective-permute-start(bf16[72,896]{1,0:T(8,128)(2,1)S(1)} %get-tuple-element.64), channel_id=1, source_target_pairs={{0,24},{8,16},{16,8},{24,0},{1,25},{9,17},{17,9},{25,1},{2,26},{10... | collective-permute-start | bytes 387080 | tf_op jit(solution)/shard_map/ppermute | solution.py:46
  75.6 2.0 %collective-permute-start.22 = (bf16[72,896]{1,0:T(8,128)(2,1)S(1)}, bf16[72,896]{1,0:T(8,128)(2,1)S(1)}, u32[]{:S(2)}, u32[]{:S(2)}) collective-permute-start(bf16[72,896]{1,0:T(8,128)(2,1)S(1)} %get-tuple-element.64), channel_id=1, source_target_pairs={{0,16},{8,24},{16,0},{24,8},{1,17},{9,25},{17,1},{25,9},{2,18},{10... | collective-permute-start | bytes 387080 | tf_op jit(solution)/shard_map/ppermute | solution.py:46
  77.7 4.8 %down_own.1 = (f32[128,1792]{1,0:T(8,128)S(1)}, bf16[3,896,1792]{2,1,0:T(8,128)(2,1)S(1)}) custom-call(bf16[136,896]{1,0:T(8,128)(2,1)S(1)} %get-tuple-element.59.hidden_ref.refs_0_, bf16[3584,1792]{1,0:T(8,128)(2,1)} %w_hbm.7), custom_call_target="tpu_custom_call" | custom-call | tf_op jit(solution)/shard_map/down_own/pallas_call | solution.py:675
  82.4 3.7 %collective-permute-start.23 = (bf16[64,896]{1,0:T(8,128)(2,1)S(1)}, bf16[64,896]{1,0:T(8,128)(2,1)S(1)}, u32[]{:S(2)}, u32[]{:S(2)}) collective-permute-start(bf16[64,896]{1,0:T(8,128)(2,1)S(1)} %collective-permute-done.20.refs_2_), channel_id=1, source_target_pairs={{0,8},{8,0},{16,24},{24,16},{1,9},{9,1},{17,25},{25,17},{2,10},{10... | collective-permute-start | bytes 344072 | tf_op jit(solution)/shard_map/ppermute | solution.py:46
  86.1 1.6 %collective-permute-done.24.refs_5_ = bf16[72,896]{1,0:T(8,128)(2,1)S(1)} collective-permute-done((bf16[72,896]{1,0:T(8,128)(2,1)S(1)}, bf16[72,896]{1,0:T(8,128)(2,1)S(1)}, u32[]{:S(2)}, u32[]{:S(2)}) %collective-permute-start.24) | collective-permute-done | bytes 129056 | tf_op jit(solution)/shard_map/ppermute | solution.py:46
  87.7 3.9 %collective-permute-done.22.refs_3_ = bf16[72,896]{1,0:T(8,128)(2,1)S(1)} collective-permute-done((bf16[72,896]{1,0:T(8,128)(2,1)S(1)}, bf16[72,896]{1,0:T(8,128)(2,1)S(1)}, u32[]{:S(2)}, u32[]{:S(2)}) %collective-permute-start.22) | collective-permute-done | bytes 129056 | tf_op jit(solution)/shard_map/ppermute | solution.py:46
  91.6 1.8 %down_rest.1 = (f32[4,128,224]{2,1,0:T(8,128)S(1)}, bf16[4,128,227]{2,1,0:T(8,128)(2,1)S(1)}, f32[128,1]{1,0:T(8,128)S(1)}) custom-call(f32[128,1]{1,0:T(8,128)S(1)} %get-tuple-element.57.base_ref, f32[128,1792]{1,0:T(8,128)S(1)} %get-tuple-element.61.sum_ref, bf16[3,896,1792]{2,1,0:T(8,128)(2,1)S(1)} %get-tuple-element.62.held_ref, ...), custom_call_target="tpu_custom_call" | custom-call | tf_op jit(solution)/shard_map/down_rest/pallas_call | solution.py:730
  93.6 1.5 %collective-permute-done.25.got_ref = bf16[4,128,227]{2,1,0:T(8,128)(2,1)S(1)} collective-permute-done((bf16[4,128,227]{2,1,0:T(8,128)(2,1)S(1)}, bf16[4,128,227]{2,1,0:T(8,128)(2,1)S(1)}, u32[]{:S(2)}, u32[]{:S(2)}) %collective-permute-start.25) | collective-permute-done | bytes 232480 | tf_op jit(solution)/shard_map/ppermute | solution.py:46
  97.6 1.4 %collective-permute-start.28 = (bf16[128,227]{1,0:T(8,128)(2,1)S(1)}, bf16[128,227]{1,0:T(8,128)(2,1)S(1)}, u32[]{:S(2)}, u32[]{:S(2)}) collective-permute-start(bf16[128,227]{1,0:T(8,128)(2,1)S(1)} %get-tuple-element.73), channel_id=1, source_target_pairs={{0,2},{1,3},{2,0},{3,1},{4,6},{5,7},{6,4},{7,5},{8,10},{9,11},{10,... | collective-permute-start | bytes 174344 | tf_op jit(solution)/shard_map/ppermute | solution.py:46
  99.0 2.1 %collective-permute-done.26.c_ref = bf16[128,227]{1,0:T(8,128)(2,1)S(1)} collective-permute-done((bf16[128,227]{1,0:T(8,128)(2,1)S(1)}, bf16[128,227]{1,0:T(8,128)(2,1)S(1)}, u32[]{:S(2)}, u32[]{:S(2)}) %collective-permute-start.26) | collective-permute-done | bytes 58144 | tf_op jit(solution)/shard_map/ppermute | solution.py:46
  (60 shorter events, 13.6 us)
Async XLA Ops:
  3.9 10.9 %collective-permute-start = (f32[136,128]{1,0:T(8,128)S(1)}, f32[136,128]{1,0:T(8,128)S(1)}, u32[]{:S(2)}, u32[]{:S(2)}) collective-permute-start(f32[136,128]{1,0:T(8,128)S(1)} %get-tuple-element.40), channel_id=1, source_target_pairs={{0,8},{8,0},{16,24},{24,16},{1,9},{9,1},{17,25},{25,17},{2,10},{10... | collective-permute-start | bytes 208904 | tf_op jit(solution)/shard_map/ppermute | solution.py:46
  7.0 7.9 %collective-permute-start.1 = (f32[136,128]{1,0:T(8,128)S(1)}, f32[136,128]{1,0:T(8,128)S(1)}, u32[]{:S(2)}, u32[]{:S(2)}) collective-permute-start(f32[136,128]{1,0:T(8,128)S(1)} %get-tuple-element.41), channel_id=1, source_target_pairs={{0,16},{8,24},{16,0},{24,8},{1,17},{9,25},{17,1},{25,9},{2,18},{10... | collective-permute-start | bytes 208904 | tf_op jit(solution)/shard_map/ppermute | solution.py:46
  9.6 6.2 %collective-permute-start.2 = (f32[136,128]{1,0:T(8,128)S(1)}, f32[136,128]{1,0:T(8,128)S(1)}, u32[]{:S(2)}, u32[]{:S(2)}) collective-permute-start(f32[136,128]{1,0:T(8,128)S(1)} %get-tuple-element.42), channel_id=1, source_target_pairs={{0,24},{8,16},{16,8},{24,0},{1,25},{9,17},{17,9},{25,1},{2,26},{10... | collective-permute-start | bytes 208904 | tf_op jit(solution)/shard_map/ppermute | solution.py:46
  14.8 18.4 %copy-start.3 = (bf16[224]{0:T(256)(128)(2,1)S(1)}, bf16[224]{0:T(256)(128)(2,1)}, u32[]{:S(2)}) copy-start(bf16[224]{0:T(256)(128)(2,1)} %score_ref.1) | copy-start | bytes 1348
  16.0 6.0 %collective-permute-start.5 = (bf16[32,512]{1,0:T(8,128)(2,1)S(1)}, bf16[32,512]{1,0:T(8,128)(2,1)S(1)}, u32[]{:S(2)}, u32[]{:S(2)}) collective-permute-start(bf16[32,512]{1,0:T(8,128)(2,1)S(1)} %merge_partials.1.after_ref.refs_0_), channel_id=1, source_target_pairs={{0,24},{8,16},{16,8},{24,0},{1,25},{9,17},{17,9},{25,1},{2,26},{10... | collective-permute-start | bytes 98312 | tf_op jit(solution)/shard_map/ppermute | solution.py:46
  18.9 4.8 %collective-permute-start.4 = (bf16[32,512]{1,0:T(8,128)(2,1)S(1)}, bf16[32,512]{1,0:T(8,128)(2,1)S(1)}, u32[]{:S(2)}, u32[]{:S(2)}) collective-permute-start(bf16[32,512]{1,0:T(8,128)(2,1)S(1)} %merge_partials.1.after_ref.refs_0_), channel_id=1, source_target_pairs={{0,16},{8,24},{16,0},{24,8},{1,17},{9,25},{17,1},{25,9},{2,18},{10... | collective-permute-start | bytes 98312 | tf_op jit(solution)/shard_map/ppermute | solution.py:46
  18.9 4.8 %collective-permute-start.3 = (bf16[32,512]{1,0:T(8,128)(2,1)S(1)}, bf16[32,512]{1,0:T(8,128)(2,1)S(1)}, u32[]{:S(2)}, u32[]{:S(2)}) collective-permute-start(bf16[32,512]{1,0:T(8,128)(2,1)S(1)} %merge_partials.1.after_ref.refs_0_), channel_id=1, source_target_pairs={{0,8},{8,0},{16,24},{24,16},{1,9},{9,1},{17,25},{25,17},{2,10},{10... | collective-permute-start | bytes 98312 | tf_op jit(solution)/shard_map/ppermute | solution.py:46
  24.5 1.6 %collective-permute-start.6 = (bf16[4,16,1792]{2,1,0:T(8,128)(2,1)S(1)}, bf16[4,16,1792]{2,1,0:T(8,128)(2,1)S(1)}, u32[]{:S(2)}, u32[]{:S(2)}) collective-permute-start(bf16[4,16,1792]{2,1,0:T(8,128)(2,1)S(1)} %get-tuple-element.44), channel_id=1, source_target_pairs={{0,1},{1,0},{2,3},{3,2},{4,5},{5,4},{6,7},{7,6},{8,9},{9,8},{10,11... | collective-permute-start | bytes 688136 | tf_op jit(solution)/shard_map/ppermute | solution.py:46
  26.1 15.9 %copy-start.1 = (bf16[1792]{0:T(1024)(128)(2,1)S(1)}, bf16[1792]{0:T(1024)(128)(2,1)}, u32[]{:S(2)}) copy-start(bf16[1792]{0:T(1024)(128)(2,1)} %refs_8_.1) | copy-start | bytes 10756
  26.1 15.9 %copy-start.2 = (bf16[1792]{0:T(1024)(128)(2,1)S(1)}, bf16[1792]{0:T(1024)(128)(2,1)}, u32[]{:S(2)}) copy-start(bf16[1792]{0:T(1024)(128)(2,1)} %refs_9_.1) | copy-start | bytes 10756
  26.1 5.2 %collective-permute-start.7 = (bf16[16,1792]{1,0:T(8,128)(2,1)S(1)}, bf16[16,1792]{1,0:T(8,128)(2,1)S(1)}, u32[]{:S(2)}, u32[]{:S(2)}) collective-permute-start(bf16[16,1792]{1,0:T(8,128)(2,1)S(1)} %get-tuple-element.46), channel_id=1, source_target_pairs={{0,6},{1,7},{2,4},{3,5},{4,2},{5,3},{6,0},{7,1},{8,14},{9,15},{10,... | collective-permute-start | bytes 172040 | tf_op jit(solution)/shard_map/ppermute | solution.py:46
  28.5 4.2 %collective-permute-start.8 = (bf16[16,1792]{1,0:T(8,128)(2,1)S(1)}, bf16[16,1792]{1,0:T(8,128)(2,1)S(1)}, u32[]{:S(2)}, u32[]{:S(2)}) collective-permute-start(bf16[16,1792]{1,0:T(8,128)(2,1)S(1)} %get-tuple-element.47), channel_id=1, source_target_pairs={{0,4},{1,5},{2,6},{3,7},{4,0},{5,1},{6,2},{7,3},{8,12},{9,13},{10,... | collective-permute-start | bytes 172040 | tf_op jit(solution)/shard_map/ppermute | solution.py:46
  29.1 4.2 %collective-permute-start.9 = (bf16[16,1792]{1,0:T(8,128)(2,1)S(1)}, bf16[16,1792]{1,0:T(8,128)(2,1)S(1)}, u32[]{:S(2)}, u32[]{:S(2)}) collective-permute-start(bf16[16,1792]{1,0:T(8,128)(2,1)S(1)} %get-tuple-element.48), channel_id=1, source_target_pairs={{0,2},{1,3},{2,0},{3,1},{4,6},{5,7},{6,4},{7,5},{8,10},{9,11},{10,... | collective-permute-start | bytes 172040 | tf_op jit(solution)/shard_map/ppermute | solution.py:46
  33.3 5.5 %collective-permute-start.10 = (bf16[16,2048]{1,0:T(8,128)(2,1)S(1)}, bf16[16,2048]{1,0:T(8,128)(2,1)S(1)}, u32[]{:S(2)}, u32[]{:S(2)}) collective-permute-start(bf16[16,2048]{1,0:T(8,128)(2,1)S(1)} %residual_rows.1.after_ref.refs_0_), channel_id=1, source_target_pairs={{0,2},{1,3},{2,0},{3,1},{4,6},{5,7},{6,4},{7,5},{8,10},{9,11},{10,... | collective-permute-start | bytes 196616 | tf_op jit(solution)/shard_map/ppermute | solution.py:46
  34.0 5.3 %collective-permute-start.12 = (bf16[16,2048]{1,0:T(8,128)(2,1)S(1)}, bf16[16,2048]{1,0:T(8,128)(2,1)S(1)}, u32[]{:S(2)}, u32[]{:S(2)}) collective-permute-start(bf16[16,2048]{1,0:T(8,128)(2,1)S(1)} %residual_rows.1.after_ref.refs_0_), channel_id=1, source_target_pairs={{0,6},{1,7},{2,4},{3,5},{4,2},{5,3},{6,0},{7,1},{8,14},{9,15},{10,... | collective-permute-start | bytes 196616 | tf_op jit(solution)/shard_map/ppermute | solution.py:46
  36.3 4.3 %collective-permute-start.11 = (bf16[16,2048]{1,0:T(8,128)(2,1)S(1)}, bf16[16,2048]{1,0:T(8,128)(2,1)S(1)}, u32[]{:S(2)}, u32[]{:S(2)}) collective-permute-start(bf16[16,2048]{1,0:T(8,128)(2,1)S(1)} %residual_rows.1.after_ref.refs_0_), channel_id=1, source_target_pairs={{0,4},{1,5},{2,6},{3,7},{4,0},{5,1},{6,2},{7,3},{8,12},{9,13},{10,... | collective-permute-start | bytes 196616 | tf_op jit(solution)/shard_map/ppermute | solution.py:46
  36.8 4.3 %collective-permute-start.13 = (bf16[16,2048]{1,0:T(8,128)(2,1)S(1)}, bf16[16,2048]{1,0:T(8,128)(2,1)S(1)}, u32[]{:S(2)}, u32[]{:S(2)}) collective-permute-start(bf16[16,2048]{1,0:T(8,128)(2,1)S(1)} %residual_rows.1.after_ref.refs_0_), channel_id=1, source_target_pairs={{0,1},{1,0},{2,3},{3,2},{4,5},{5,4},{6,7},{7,6},{8,9},{9,8},{10,11... | collective-permute-start | bytes 196616 | tf_op jit(solution)/shard_map/ppermute | solution.py:46
  39.3 1.8 %collective-permute-start.16 = (bf16[16,2048]{1,0:T(8,128)(2,1)S(1)}, bf16[16,2048]{1,0:T(8,128)(2,1)S(1)}, u32[]{:S(2)}, u32[]{:S(2)}) collective-permute-start(bf16[16,2048]{1,0:T(8,128)(2,1)S(1)} %collective-permute-done.12.refs_3_), channel_id=1, source_target_pairs={{0,1},{1,0},{2,3},{3,2},{4,5},{5,4},{6,7},{7,6},{8,9},{9,8},{10,11... | collective-permute-start | bytes 196616 | tf_op jit(solution)/shard_map/ppermute | solution.py:46
  40.6 1.3 %collective-permute-start.15 = (bf16[16,2048]{1,0:T(8,128)(2,1)S(1)}, bf16[16,2048]{1,0:T(8,128)(2,1)S(1)}, u32[]{:S(2)}, u32[]{:S(2)}) collective-permute-start(bf16[16,2048]{1,0:T(8,128)(2,1)S(1)} %collective-permute-done.11.refs_2_), channel_id=1, source_target_pairs={{0,1},{1,0},{2,3},{3,2},{4,5},{5,4},{6,7},{7,6},{8,9},{9,8},{10,11... | collective-permute-start | bytes 196616 | tf_op jit(solution)/shard_map/ppermute | solution.py:46
  40.6 1.4 %collective-permute-start.14 = (bf16[16,2048]{1,0:T(8,128)(2,1)S(1)}, bf16[16,2048]{1,0:T(8,128)(2,1)S(1)}, u32[]{:S(2)}, u32[]{:S(2)}) collective-permute-start(bf16[16,2048]{1,0:T(8,128)(2,1)S(1)} %collective-permute-done.10.refs_1_), channel_id=1, source_target_pairs={{0,1},{1,0},{2,3},{3,2},{4,5},{5,4},{6,7},{7,6},{8,9},{9,8},{10,11... | collective-permute-start | bytes 196616 | tf_op jit(solution)/shard_map/ppermute | solution.py:46
  46.5 14.5 %collective-permute-start.17 = (bf16[136,896]{1,0:T(8,128)(2,1)S(1)}, bf16[136,896]{1,0:T(8,128)(2,1)S(1)}, u32[]{:S(2)}, u32[]{:S(2)}) collective-permute-start(bf16[136,896]{1,0:T(8,128)(2,1)S(1)} %get-tuple-element.53), channel_id=1, source_target_pairs={{0,8},{8,0},{16,24},{24,16},{1,9},{9,1},{17,25},{25,17},{2,10},{10... | collective-permute-start | bytes 731144 | tf_op jit(solution)/shard_map/ppermute | solution.py:46
  47.2 20.2 %collective-permute-start.18 = (bf16[136,896]{1,0:T(8,128)(2,1)S(1)}, bf16[136,896]{1,0:T(8,128)(2,1)S(1)}, u32[]{:S(2)}, u32[]{:S(2)}) collective-permute-start(bf16[136,896]{1,0:T(8,128)(2,1)S(1)} %get-tuple-element.54), channel_id=1, source_target_pairs={{0,16},{8,24},{16,0},{24,8},{1,17},{9,25},{17,1},{25,9},{2,18},{10... | collective-permute-start | bytes 731144 | tf_op jit(solution)/shard_map/ppermute | solution.py:46
  49.0 18.4 %collective-permute-start.19 = (bf16[136,896]{1,0:T(8,128)(2,1)S(1)}, bf16[136,896]{1,0:T(8,128)(2,1)S(1)}, u32[]{:S(2)}, u32[]{:S(2)}) collective-permute-start(bf16[136,896]{1,0:T(8,128)(2,1)S(1)} %get-tuple-element.55), channel_id=1, source_target_pairs={{0,24},{8,16},{16,8},{24,0},{1,25},{9,17},{17,9},{25,1},{2,26},{10... | collective-permute-start | bytes 731144 | tf_op jit(solution)/shard_map/ppermute | solution.py:46
  67.8 23.8 %collective-permute-start.21 = (bf16[136,896]{1,0:T(8,128)(2,1)S(1)}, bf16[136,896]{1,0:T(8,128)(2,1)S(1)}, u32[]{:S(2)}, u32[]{:S(2)}) collective-permute-start(bf16[136,896]{1,0:T(8,128)(2,1)S(1)} %get-tuple-element.59.hidden_ref.refs_0_), channel_id=1, source_target_pairs={{0,8},{8,0},{16,24},{24,16},{1,9},{9,1},{17,25},{25,17},{2,10},{10... | collective-permute-start | bytes 731144 | tf_op jit(solution)/shard_map/ppermute | solution.py:46
  72.8 9.7 %collective-permute-start.20 = (bf16[64,896]{1,0:T(8,128)(2,1)S(1)}, bf16[64,896]{1,0:T(8,128)(2,1)S(1)}, u32[]{:S(2)}, u32[]{:S(2)}) collective-permute-start(bf16[64,896]{1,0:T(8,128)(2,1)S(1)} %get-tuple-element.58), channel_id=1, source_target_pairs={{0,16},{8,24},{16,0},{24,8},{1,17},{9,25},{17,1},{25,9},{2,18},{10... | collective-permute-start | bytes 344072 | tf_op jit(solution)/shard_map/ppermute | solution.py:46
  74.3 13.5 %collective-permute-start.24 = (bf16[72,896]{1,0:T(8,128)(2,1)S(1)}, bf16[72,896]{1,0:T(8,128)(2,1)S(1)}, u32[]{:S(2)}, u32[]{:S(2)}) collective-permute-start(bf16[72,896]{1,0:T(8,128)(2,1)S(1)} %get-tuple-element.64), channel_id=1, source_target_pairs={{0,24},{8,16},{16,8},{24,0},{1,25},{9,17},{17,9},{25,1},{2,26},{10... | collective-permute-start | bytes 387080 | tf_op jit(solution)/shard_map/ppermute | solution.py:46
  75.6 16.0 %collective-permute-start.22 = (bf16[72,896]{1,0:T(8,128)(2,1)S(1)}, bf16[72,896]{1,0:T(8,128)(2,1)S(1)}, u32[]{:S(2)}, u32[]{:S(2)}) collective-permute-start(bf16[72,896]{1,0:T(8,128)(2,1)S(1)} %get-tuple-element.64), channel_id=1, source_target_pairs={{0,16},{8,24},{16,0},{24,8},{1,17},{9,25},{17,1},{25,9},{2,18},{10... | collective-permute-start | bytes 387080 | tf_op jit(solution)/shard_map/ppermute | solution.py:46
  82.4 9.2 %collective-permute-start.23 = (bf16[64,896]{1,0:T(8,128)(2,1)S(1)}, bf16[64,896]{1,0:T(8,128)(2,1)S(1)}, u32[]{:S(2)}, u32[]{:S(2)}) collective-permute-start(bf16[64,896]{1,0:T(8,128)(2,1)S(1)} %collective-permute-done.20.refs_2_), channel_id=1, source_target_pairs={{0,8},{8,0},{16,24},{24,16},{1,9},{9,1},{17,25},{25,17},{2,10},{10... | collective-permute-start | bytes 344072 | tf_op jit(solution)/shard_map/ppermute | solution.py:46
  93.5 1.6 %collective-permute-start.25 = (bf16[4,128,227]{2,1,0:T(8,128)(2,1)S(1)}, bf16[4,128,227]{2,1,0:T(8,128)(2,1)S(1)}, u32[]{:S(2)}, u32[]{:S(2)}) collective-permute-start(bf16[4,128,227]{2,1,0:T(8,128)(2,1)S(1)} %get-tuple-element.67), channel_id=1, source_target_pairs={{0,1},{1,0},{2,3},{3,2},{4,5},{5,4},{6,7},{7,6},{8,9},{9,8},{10,11... | collective-permute-start | bytes 697352 | tf_op jit(solution)/shard_map/ppermute | solution.py:46
  95.4 5.7 %collective-permute-start.26 = (bf16[128,227]{1,0:T(8,128)(2,1)S(1)}, bf16[128,227]{1,0:T(8,128)(2,1)S(1)}, u32[]{:S(2)}, u32[]{:S(2)}) collective-permute-start(bf16[128,227]{1,0:T(8,128)(2,1)S(1)} %get-tuple-element.71), channel_id=1, source_target_pairs={{0,6},{1,7},{2,4},{3,5},{4,2},{5,3},{6,0},{7,1},{8,14},{9,15},{10,... | collective-permute-start | bytes 174344 | tf_op jit(solution)/shard_map/ppermute | solution.py:46
  96.5 5.3 %collective-permute-start.27 = (bf16[128,227]{1,0:T(8,128)(2,1)S(1)}, bf16[128,227]{1,0:T(8,128)(2,1)S(1)}, u32[]{:S(2)}, u32[]{:S(2)}) collective-permute-start(bf16[128,227]{1,0:T(8,128)(2,1)S(1)} %get-tuple-element.72), channel_id=1, source_target_pairs={{0,4},{1,5},{2,6},{3,7},{4,0},{5,1},{6,2},{7,3},{8,12},{9,13},{10,... | collective-permute-start | bytes 174344 | tf_op jit(solution)/shard_map/ppermute | solution.py:46
  97.6 4.3 %collective-permute-start.28 = (bf16[128,227]{1,0:T(8,128)(2,1)S(1)}, bf16[128,227]{1,0:T(8,128)(2,1)S(1)}, u32[]{:S(2)}, u32[]{:S(2)}) collective-permute-start(bf16[128,227]{1,0:T(8,128)(2,1)S(1)} %get-tuple-element.73), channel_id=1, source_target_pairs={{0,2},{1,3},{2,0},{3,1},{4,6},{5,7},{6,4},{7,5},{8,10},{9,11},{10,... | collective-permute-start | bytes 174344 | tf_op jit(solution)/shard_map/ppermute | solution.py:46
  (4 other events, 57.2 us)

commit v4 on v3

--- a/solution.py
+++ b/solution.py
@@ -11,7 +11,7 @@
 NEGATIVE = -1e30
 EPS = 1e-05
 VMEM_LIMIT = 24 * 2**20
-TOP = 64
+TOP = 48
 FREE = pl.CostEstimate(flops=0, bytes_accessed=0, transcendentals=0)
 
 
@@ -69,10 +69,17 @@
     return ref_value.reshape(math.prod(shape[:-1]), shape[-1])
 
 
-def prompt_kernel(scale, table_hbm, len_hbm, prompt_hbm, q_hbm, kv_hbm, *refs):
-    outs, refs = refs[:4], refs[4:]
+def pieces3(value):
+    high = value.astype(jnp.bfloat16)
+    left = value - high.astype(jnp.float32)
+    middle = left.astype(jnp.bfloat16)
+    return high, middle, (left - middle.astype(jnp.float32)).astype(jnp.bfloat16)
+
+
+def prompt_kernel(scale, table_hbm, len_hbm, prompt_hbm, q_hbm, kv_hbm, tail_hbm, *refs):
+    outs, held_ref, refs = refs[:4], refs[4], refs[5:]
     table_ref, len_ref, prompt_ref, q_ref, kv_ref, where_ref, count_ref, place_ref = refs[:8]
-    query_ref, rows_ref, score_ref, best_ref, norm_ref, mixed_ref, back_ref, sems = refs[8:]
+    query_ref, rows_ref, score_ref, best_ref, norm_ref, mixed_ref, back_ref, sent_ref, sems = refs[8:]
     copies = start_copies(
         [
             pltpu.make_async_copy(source, target, sems.at[i])
@@ -83,6 +90,7 @@
                     (prompt_hbm, prompt_ref),
                     (q_hbm, q_ref),
                     (kv_hbm, kv_ref),
+                    (tail_hbm.at[pl.ds(0, held_ref.shape[0])], held_ref),
                 )
             )
         ]
@@ -155,14 +163,28 @@
             place = place_ref[(page_pos ^ k) * (lines // small) + i]
             source = pl.ds(pl.multiple_of(place * small, small), small)
             to = slice(i * small, (i + 1) * small)
-            out_ref[to, :] = mixed_ref[source, :]
+            if k == 0:
+                out_ref[to, :] = mixed_ref[source, :]
+            else:
+                sent_ref[to, :] = mixed_ref[source, :]
             back_ref[k * lines + i * small : k * lines + (i + 1) * small, :] = best_ref[source, :]
             query_ref[k * lines + i * small : k * lines + (i + 1) * small, :] = norm_ref[source, :]
-        out_ref[lines : lines + 1, :] = back_ref[k * lines : (k + 1) * lines, :].T[0:1]
-        out_ref[lines + 1 : lines + 2, :] = query_ref[k * lines : (k + 1) * lines, :].T[0:1]
-
-
-def prompt_partial(queries, prompt_kv, page_table, prompt_len, sample_prompt):
+        if k > 0:
+            out_ref[0:lines, :] = sent_ref[...].astype(bf16)
+        best = back_ref[k * lines : (k + 1) * lines, :].T[0:1]
+        norm = query_ref[k * lines : (k + 1) * lines, :].T[0:1]
+        if k == 0:
+            out_ref[lines : lines + 1, :] = best
+            out_ref[lines + 1 : lines + 2, :] = norm
+        else:
+            pad = jnp.zeros((2, dim), bf16)
+            out_ref[lines : lines + 8, :] = jnp.concatenate(
+                [*pieces3(best), *pieces3(norm), pad], axis=0
+            )
+    copies[5].wait()
+
+
+def prompt_partial(queries, prompt_kv, tail_kv, page_table, prompt_len, sample_prompt):
     samples, new, heads, dim = queries.shape
     slots, page_len = prompt_kv.shape[:2]
     total = samples * new * heads
@@ -173,9 +195,11 @@
     wide = pltpu.VMEM((total, dim), jnp.float32)
     return pl.pallas_call(
         functools.partial(prompt_kernel, math.log2(math.e) / math.sqrt(dim)),
-        in_specs=[anywhere] * 5,
-        out_specs=[vmem] * 4,
-        out_shape=[pltpu.VMEM((lines + 8, dim), jnp.float32)] * 4,
+        in_specs=[anywhere] * 6,
+        out_specs=[vmem] * 5,
+        out_shape=[pltpu.VMEM((lines + 8, dim), jnp.float32)]
+        + [pltpu.VMEM((lines + 8, dim), jnp.bfloat16)] * 3
+        + [pltpu.VMEM((tail_kv.shape[0] // 2, *tail_kv.shape[1:]), tail_kv.dtype)],
         scratch_shapes=[
             pltpu.SMEM(page_table.shape, jnp.int32),
             pltpu.SMEM(prompt_len.shape, jnp.int32),
@@ -192,26 +216,28 @@
             wide,
             wide,
             wide,
-            pltpu.SemaphoreType.DMA((5,)),
+            pltpu.VMEM((lines, dim), jnp.float32),
+            pltpu.SemaphoreType.DMA((6,)),
         ],
         compiler_params=pltpu.CompilerParams(vmem_limit_bytes=VMEM_LIMIT),
         name="prompt_attention",
-    )(*map(in_hbm, (page_table, prompt_len, sample_prompt, queries, prompt_kv)))
-
-
-def tail_kernel(scale, len_ref, q_ref, kv_hbm, out_ref, kv_ref, best_ref, norm_ref, sems):
-    own, length, heads, _ = kv_ref.shape
+    )(*map(in_hbm, (page_table, prompt_len, sample_prompt, queries, prompt_kv, tail_kv)))
+
+
+def tail_kernel(scale, len_ref, q_ref, held_ref, kv_hbm, out_ref, kv_ref, best_ref, norm_ref, sems):
+    held, length, heads, _ = held_ref.shape
+    own = held + kv_ref.shape[0]
     new, dim = q_ref.shape[1], q_ref.shape[3]
     lines, half = new * heads, length * heads // 2
-    steps = sems.shape[0]
+    steps = 2 * sems.shape[0]
     per = own // steps
     bf16, f32 = jnp.bfloat16, jnp.float32
     copies = start_copies(
         [
             pltpu.make_async_copy(
-                kv_hbm.at[pl.ds(i * per, per)], kv_ref.at[pl.ds(i * per, per)], sems.at[i]
+                kv_hbm.at[pl.ds(held + i * per, per)], kv_ref.at[pl.ds(i * per, per)], sems.at[i]
             )
-            for i in range(steps)
+            for i in range(steps // 2)
         ]
     )
     first = lax.axis_index("page") * own
@@ -221,10 +247,11 @@
     same_head = line % heads == col % heads
     ahead = jnp.where(same_head, col // heads - line // heads, length + new)
     for step in range(steps):
-        copies[step].wait()
+        if step >= steps // 2:
+            copies[step - steps // 2].wait()
         scores, values = [], []
         for i in range(step * per, (step + 1) * per):
-            cache = flat_rows(kv_ref[i])
+            cache = flat_rows(held_ref[i] if i < held else kv_ref[i - held])
             keys = jnp.concatenate([cache[:half, :dim], cache[half:, :dim]], axis=1)
             values.append(jnp.concatenate([cache[:half, dim:], cache[half:, dim:]], axis=1))
             query = flat_rows(q_ref[i])
@@ -258,7 +285,7 @@
     out_ref[total + 1 : total + 2, :] = norm_ref[...].T[0:1]
 
 
-def tail_partial(queries, tail_kv, tail_len):
+def tail_partial(queries, held_tail, tail_kv, tail_len):
     _, new, heads, dim = queries.shape
     own = tail_kv.shape[0]
     lines = own * new * heads
@@ -268,31 +295,40 @@
         in_specs=[
             pl.BlockSpec(memory_space=pltpu.SMEM),
             pl.BlockSpec((own, new, heads, dim), lambda i: (lax.axis_index("page"), 0, 0, 0)),
+            pl.BlockSpec(memory_space=pltpu.VMEM),
             pl.BlockSpec(memory_space=pl.ANY),
         ],
         out_specs=pl.BlockSpec(memory_space=pltpu.VMEM),
         out_shape=pltpu.VMEM((lines + 8, dim), jnp.float32),
-        scratch_shapes=[pltpu.VMEM(tail_kv.shape, tail_kv.dtype)]
+        scratch_shapes=[pltpu.VMEM(held_tail.shape, tail_kv.dtype)]
         + [pltpu.VMEM((lines, dim), jnp.float32)] * 2
-        + [pltpu.SemaphoreType.DMA((4,))],
+        + [pltpu.SemaphoreType.DMA((2,))],
         compiler_params=pltpu.CompilerParams(vmem_limit_bytes=VMEM_LIMIT),
         cost_estimate=FREE,
         name="tail_attention",
-    )(*map(in_hbm, (tail_len, queries, tail_kv)))
+    )(in_hbm(tail_len), in_hbm(queries), held_tail, in_hbm(tail_kv))
 
 
 def merge_kernel(scale, *refs):
     parts, out_ref, held_ref = refs[:-2], refs[-2], refs[-1]
     lines, dim = held_ref.shape
     heads = out_ref.shape[1] // dim
-    bests = [part[lines : lines + 1, :] for part in parts]
+    bests, norms = [], []
+    for part in parts:
+        below = part[lines : lines + 8, :].astype(jnp.float32)
+        if part.dtype == jnp.float32:
+            bests.append(below[0:1])
+            norms.append(below[1:2])
+        else:
+            bests.append((below[0:1] + below[1:2]) + below[2:3])
+            norms.append((below[3:4] + below[4:5]) + below[5:6])
     best = functools.reduce(jnp.maximum, bests)
     scales = [jnp.exp2((one - best) * scale) for one in bests]
-    norm = sum(factor * part[lines + 1 : lines + 2, :] for factor, part in zip(scales, parts))
+    norm = sum(factor * own_norm for factor, own_norm in zip(scales, norms))
     total = jnp.zeros((lines, dim), jnp.float32)
     for factor, part in zip(scales, parts):
         share = jnp.broadcast_to(factor / norm, (lines, lines)).T
-        total = total + share * part[0:lines, :]
+        total = total + share * part[0:lines, :].astype(jnp.float32)
     held_ref[...] = total
     for h in range(heads):
         out_ref[:, h * dim : (h + 1) * dim] = held_ref[
@@ -413,9 +449,20 @@
     )(keep, got)
 
 
+def as_row(ref):
+    return ref[...].astype(jnp.float32).reshape(1, ref.shape[0])
+
+
+def own_part(row, width):
+    page_pos = lax.axis_index("page")
+    parts = [row[:, p * width : (p + 1) * width] for p in range(row.shape[1] // width)]
+    return sum(jnp.where(page_pos == p, part, 0.0) for p, part in enumerate(parts))
+
+
 def residual_kernel(own_ref, c_ref, b_ref, a_ref, bias_ref, score_ref, out_ref):
     group, piece = own_ref.shape[1], score_ref.shape[0]
-    total = own_ref[...] + bias_ref[...].astype(jnp.float32)
+    bias = own_part(as_row(bias_ref), group)
+    total = own_ref[...] + bias
     for ref in (a_ref, b_ref, c_ref):
         total = total + ref[...].astype(jnp.float32)
     out_ref[:, :group] = total.astype(out_ref.dtype)
@@ -428,18 +475,12 @@
     vmem = pl.BlockSpec(memory_space=pltpu.VMEM)
     return pl.pallas_call(
         residual_kernel,
-        grid=(1,),
-        in_specs=[vmem] * 4
-        + [pl.BlockSpec((1, own.shape[1]), lambda i: (0, lax.axis_index("page"))), vmem],
+        in_specs=[vmem] * 6,
         out_specs=vmem,
         out_shape=pltpu.VMEM((own.shape[0], own.shape[1] + 256), jnp.bfloat16),
         compiler_params=pltpu.CompilerParams(vmem_limit_bytes=VMEM_LIMIT),
         name="residual_rows",
-    )(own, *arrived, b_out.reshape(1, -1), w_score)
-
-
-def as_row(ref):
-    return ref[...].astype(jnp.float32).reshape(1, ref.shape[0])
+    )(own, *arrived, b_out, w_score)
 
 
 def split2(value):
@@ -453,10 +494,9 @@
 
 def up_first_kernel(*refs):
     blocks, refs = refs[:8], refs[8:]
-    gain_ref, bias_ref, down_ref, near_ref, w_hbm = refs[:5]
-    out_refs, weight_ref, refs = refs[5:8], refs[8], refs[9:]
-    lhs_ref, residual_ref, stats_ref, mean_ref, square_ref, base_ref, weights_ref, w_ref, sems = refs
-    copies = shard_copies(w_hbm, w_ref, sems, (3, 2), 1)
+    gain_ref, bias_ref, down_ref, far_ref, near_ref = refs[:5]
+    out_refs, weight_ref, refs = refs[5:10], refs[10], refs[11:]
+    lhs_ref, residual_ref, stats_ref, mean_ref, square_ref, base_ref, weights_ref = refs
     blk_pos = lax.axis_index("blk")
     core, chip = blk_pos % 2, blk_pos // 2
     height, group = blocks[0].shape[0], lhs_ref.shape[1]
@@ -494,10 +534,11 @@
     for ref in (mean_ref, square_ref, base_ref):
         pieces += split2(ref[...].T[0:1])
     stats_ref[...] = jnp.concatenate(pieces, axis=0)
-    out_refs[2][...] = up_product(lhs_ref, near_ref.at[0], stats_ref, rows)
-    for i in range(2):
-        copies[i].wait()
-        out_refs[i][...] = up_product(lhs_ref, w_ref.at[i], stats_ref, rows)
+    for i, (top_ref, bottom_ref) in enumerate((out_refs[0:2], out_refs[2:4])):
+        part = up_product(lhs_ref, far_ref.at[i], stats_ref, rows)
+        top_ref[...] = part[:TOP]
+        bottom_ref[...] = part[TOP:]
+    out_refs[4][...] = up_product(lhs_ref, near_ref.at[0], stats_ref, rows)
 
 
 def up_product(lhs_ref, w_ref, stats_ref, rows):
@@ -516,18 +557,19 @@
     return jnp.concatenate([product[:rows], below], axis=0).astype(jnp.bfloat16)
 
 
-def up_first(blocks, ln_gain, ln_bias, b_down, near_up, w_up):
+def up_first(blocks, ln_gain, ln_bias, b_down, held_up, near_up):
     height = blocks[0].shape[0]
     rows = 8 * height
-    _, group, units = near_up.shape
+    _, group, units = held_up.shape
     bf16, f32 = jnp.bfloat16, jnp.float32
     vmem = pl.BlockSpec(memory_space=pltpu.VMEM)
     return pl.pallas_call(
         up_first_kernel,
-        in_specs=[vmem] * 12 + [pl.BlockSpec(memory_space=pl.ANY)],
-        out_specs=[vmem] * 7,
-        out_shape=[pltpu.VMEM((rows + 8, units), bf16)] * 3
+        in_specs=[vmem] * 13,
+        out_specs=[vmem] * 9,
+        out_shape=[pltpu.VMEM((TOP, units), bf16), pltpu.VMEM((rows - TOP + 8, units), bf16)] * 2
         + [
+            pltpu.VMEM((rows + 8, units), bf16),
             pltpu.VMEM((1, group), f32),
             pltpu.VMEM((rows + 16, group), bf16),
             jax.ShapeDtypeStruct((rows, group), bf16),
@@ -536,8 +578,6 @@
         scratch_shapes=[pltpu.VMEM((rows, rows), f32)] * 3
         + [
             pltpu.VMEM((8, blocks[0].shape[1] - group), f32),
-            pltpu.VMEM((2, group, units), bf16),
-            pltpu.SemaphoreType.DMA((2,)),
         ],
         compiler_params=pltpu.CompilerParams(vmem_limit_bytes=VMEM_LIMIT),
         name="norm_and_up",
@@ -546,8 +586,8 @@
         ln_gain,
         ln_bias,
         b_down,
+        held_up,
         near_up,
-        in_hbm(w_up),
     )
 
 
@@ -574,33 +614,61 @@
     )(lhs, stats, in_hbm(w_up))
 
 
-def image_kernel(score_ref, w_ref, out_ref, column_ref):
-    step = pl.program_id(0)
-
-    @pl.when(step == 0)
-    def _():
-        wide = jnp.broadcast_to(score_ref[...], column_ref.shape[::-1])
-        column_ref[...] = wide.T.astype(column_ref.dtype)
-
-    image = jnp.dot(w_ref[...], column_ref[...], preferred_element_type=jnp.float32).T[0:1]
-    high, low = split2(image)
-    out_ref[pl.ds(step, 1), :] = high.astype(jnp.float32)
-    out_ref[pl.ds(step + pl.num_programs(0), 1), :] = low.astype(jnp.float32)
-
-
-def image_of(score_group, w_down):
+def relay_kernel(a_ref, b_ref, out_ref):
+    out_ref[...] = (a_ref[...].astype(jnp.float32) + b_ref[...].astype(jnp.float32)).astype(
+        out_ref.dtype
+    )
+
+
+def relay_sum(part, got):
+    vmem = pl.BlockSpec(memory_space=pltpu.VMEM)
+    return pl.pallas_call(
+        relay_kernel,
+        in_specs=[vmem] * 2,
+        out_specs=vmem,
+        out_shape=pltpu.VMEM(part.shape, part.dtype),
+        compiler_params=pltpu.CompilerParams(vmem_limit_bytes=VMEM_LIMIT),
+        cost_estimate=FREE,
+        name="relay_sum",
+    )(part, got)
+
+
+def image_kernel(first, score_ref, w_hbm, out_ref, w_ref, sems):
+    count, units, group = w_ref.shape
+    copies = start_copies(
+        [
+            pltpu.make_async_copy(
+                w_hbm.at[pl.ds((first + i) * units, units)], w_ref.at[i], sems.at[i]
+            )
+            for i in range(count)
+        ]
+    )
+    lanes = 128
+    for i in range(count):
+        copies[i].wait()
+        for start in range(0, units, lanes):
+            total = jnp.zeros((lanes, lanes), jnp.float32)
+            for col in range(0, group, lanes):
+                weights = w_ref[i, start : start + lanes, col : col + lanes].astype(jnp.float32)
+                total = total + weights * score_ref[:, col : col + lanes]
+            high, low = split2(jnp.sum(total.T, axis=0, keepdims=True))
+            out_ref[i : i + 1, start : start + lanes] = high.astype(jnp.float32)
+            out_ref[count + i : count + i + 1, start : start + lanes] = low.astype(jnp.float32)
+
+
+def image_of(score_group, w_down, first, count):
     depth, group = w_down.shape
     tile = depth // 4
-    return pl.pallas_call(
-        image_kernel,
-        grid=(4,),
-        in_specs=[
-            pl.BlockSpec((1, group), lambda i: (0, 0)),
-            pl.BlockSpec((tile, group), lambda i: (i, 0)),
-        ],
-        out_specs=pl.BlockSpec((8, tile), lambda i: (0, 0)),
-        out_shape=pltpu.VMEM((8, tile), jnp.float32),
-        scratch_shapes=[pltpu.VMEM((group, 128), jnp.bfloat16)],
+    vmem = pl.BlockSpec(memory_space=pltpu.VMEM)
+    return pl.pallas_call(
+        functools.partial(image_kernel, first),
+        in_specs=[vmem, pl.BlockSpec(memory_space=pl.ANY)],
+        out_specs=vmem,
+        out_shape=pltpu.VMEM((2 * count, tile), jnp.float32),
+        scratch_shapes=[
+            pltpu.VMEM((count, tile, group), jnp.bfloat16),
+            pltpu.SemaphoreType.DMA((count,)),
+        ],
         compiler_params=pltpu.CompilerParams(vmem_limit_bytes=VMEM_LIMIT),
         cost_estimate=FREE,
         name="score_image",
@@ -608,10 +676,10 @@
 
 
 def hidden_kernel(group, *refs):
-    parts, (bias_ref, image_ref, whole_ref, top_ref, bottom_ref, base_ref) = refs[:4], refs[4:]
-    rows, cut = parts[0].shape[0] - 8, top_ref.shape[0]
+    parts, (bias_ref, image_a_ref, image_b_ref, out_ref, base_ref) = refs[:5], refs[5:]
+    rows, cut = parts[0].shape[0] - 8, parts[2].shape[0]
     f32 = jnp.float32
-    tails = [part[rows:, :].astype(f32) for part in parts]
+    tails = [part[part.shape[0] - 8 :, :].astype(f32) for part in (*parts[:2], *parts[3:])]
     stats = [
         [tail[2 + i : 3 + i, :rows] + tail[3 + i : 4 + i, :rows] for tail in tails]
         for i in (0, 2, 4)
@@ -623,37 +691,34 @@
     inverse = lax.rsqrt(spread * (0.25 / group) + EPS)
     pad = jnp.zeros((rows - 6, rows), f32)
     columns = jnp.concatenate([inverse, *shifts, pair_sum(bases), pad], axis=0).T
-    offset = sum(tail[1:2] for tail in tails) + bias_ref[...].astype(f32)
-    total = sum(part[0:rows, :].astype(f32) for part in parts)
+    offset = sum(tail[1:2] for tail in tails) + own_part(as_row(bias_ref), bias_ref.shape[0] // 4)
+    upper = parts[2][...].astype(f32)
+    lower = parts[3][0 : rows - cut, :].astype(f32) + parts[4][0 : rows - cut, :].astype(f32)
+    total = jnp.concatenate([upper, lower], axis=0)
+    for part in parts[:2]:
+        total = total + part[0:rows, :].astype(f32)
     for k, tail in enumerate(tails):
         total = total + columns[:, 1 + k : 2 + k] * tail[0:1]
     hidden = jnp.maximum(total * columns[:, 0:1] + offset, 0.0)
-    below = jnp.concatenate([hidden, image_ref[...]], axis=0).astype(whole_ref.dtype)
-    whole_ref[...] = below
-    top_ref[...] = below[:cut]
-    bottom_ref[...] = below[cut:]
+    image = [ref[at, :] for at in (slice(0, 2), slice(2, 4)) for ref in (image_a_ref, image_b_ref)]
+    out_ref[...] = jnp.concatenate([hidden, *image], axis=0).astype(out_ref.dtype)
     base_ref[...] = columns[:, 5:6]
 
 
-def own_hidden_units(parts, b_up, image, group):
+def own_hidden_units(parts, b_up, images, group):
     vmem = pl.BlockSpec(memory_space=pltpu.VMEM)
     height, units = parts[0].shape
-    bf16 = jnp.bfloat16
     return pl.pallas_call(
         functools.partial(hidden_kernel, group),
-        grid=(1,),
-        in_specs=[vmem] * 4
-        + [pl.BlockSpec((1, units), lambda i: (0, lax.axis_index("page"))), vmem],
-        out_specs=[vmem] * 4,
+        in_specs=[vmem] * 8,
+        out_specs=[vmem] * 2,
         out_shape=[
-            pltpu.VMEM((height, units), bf16),
-            pltpu.VMEM((TOP, units), bf16),
-            pltpu.VMEM((height - TOP, units), bf16),
+            pltpu.VMEM((height, units), jnp.bfloat16),
             pltpu.VMEM((height - 8, 1), jnp.float32),
         ],
         compiler_params=pltpu.CompilerParams(vmem_limit_bytes=VMEM_LIMIT),
         name="hidden_units",
-    )(*parts, b_up.reshape(1, -1), image)
+    )(*parts, b_up, *images)
 
 
 def down_first_kernel(hidden_ref, w_hbm, sum_ref, held_ref, w_ref, sems, held_sems):
@@ -691,28 +756,44 @@
     )(hidden, in_hbm(w_down))
 
 
-def down_rest_kernel(base_ref, sum_ref, held_ref, *refs):
-    parts, (keep_ref, give_ref, score_ref, image_ref) = refs[:6], refs[6:]
+def down_middle_kernel(sum_ref, held_ref, near_ref, far_ref, out_ref):
+    rows = sum_ref.shape[0]
+    out_ref[...] = (
+        sum_ref[...]
+        + jnp.dot(near_ref[0:rows, :], held_ref[0], preferred_element_type=jnp.float32)
+        + jnp.dot(far_ref[0:rows, :], held_ref[1], preferred_element_type=jnp.float32)
+    )
+
+
+def down_middle(summed, held, near, far):
+    vmem = pl.BlockSpec(memory_space=pltpu.VMEM)
+    return pl.pallas_call(
+        down_middle_kernel,
+        in_specs=[vmem] * 4,
+        out_specs=vmem,
+        out_shape=pltpu.VMEM(summed.shape, summed.dtype),
+        compiler_params=pltpu.CompilerParams(vmem_limit_bytes=VMEM_LIMIT),
+        cost_estimate=FREE,
+        name="down_middle",
+    )(summed, held, near, far)
+
+
+def down_last_kernel(base_ref, sum_ref, held_ref, *refs):
+    parts, (keep_ref, give_ref, score_ref, image_ref) = refs[:4], refs[4:]
     rows = sum_ref.shape[0]
     f32 = jnp.float32
     page_pos = lax.axis_index("page")
     core = lax.axis_index("blk") % 2
     piece = keep_ref.shape[2]
-    cut = parts[2].shape[0]
-    hiddens = [part[0:rows, :] for part in parts[:2]]
-    for top, bottom in (parts[2:4], parts[4:6]):
-        hiddens.append(jnp.concatenate([top[...], bottom[0 : rows - cut, :]], axis=0))
-    product = sum_ref[...]
-    for k in (1, 2, 3):
-        product = product + jnp.dot(hiddens[k], held_ref[k - 1], preferred_element_type=f32)
-    tails = [
-        part[part.shape[0] - 8 :, :].astype(f32) for part in (*parts[:2], parts[3], parts[5])
-    ]
+    product = sum_ref[...] + jnp.dot(
+        parts[3][0:rows, :], held_ref[2], preferred_element_type=f32
+    )
+    tails = [part[rows:, :].astype(f32) for part in parts]
     image_ref[...] = pair_sum([tail[0:4] + tail[4:8] for tail in tails])
     by_owner = []
-    for k, hidden in enumerate(hiddens):
+    for k, part in enumerate(parts):
         image = image_ref[pl.ds(page_pos ^ k, 1), :]
-        by_owner.append(jnp.sum(hidden.astype(f32) * image, axis=1, keepdims=True))
+        by_owner.append(jnp.sum(part[0:rows, :].astype(f32) * image, axis=1, keepdims=True))
     score = base_ref[...] + pair_sum(by_owner)
     score_ref[...] = score
     pieces = split3(score)
@@ -723,13 +804,13 @@
         give_ref[chip, :, piece:] = pieces
 
 
-def down_rest(base, summed, held, parts):
+def down_last(base, summed, held, parts):
     rows, group = summed.shape
     units = parts[0].shape[1]
     vmem = pl.BlockSpec(memory_space=pltpu.VMEM)
     return pl.pallas_call(
-        down_rest_kernel,
-        in_specs=[vmem] * 9,
+        down_last_kernel,
+        in_specs=[vmem] * 7,
         out_specs=[vmem] * 3,
         out_shape=[
             pltpu.VMEM((4, rows, group // 8), jnp.float32),
@@ -738,16 +819,12 @@
         ],
         scratch_shapes=[pltpu.VMEM((4, units), jnp.float32)],
         compiler_params=pltpu.CompilerParams(vmem_limit_bytes=VMEM_LIMIT),
-        name="down_rest",
+        name="down_last",
     )(base, summed, held, *parts)
 
 
 def split3(value):
-    high = value.astype(jnp.bfloat16)
-    left = value - high.astype(jnp.float32)
-    middle = left.astype(jnp.bfloat16)
-    low = (left - middle.astype(jnp.float32)).astype(jnp.bfloat16)
-    return jnp.concatenate([high, middle, low], axis=1)
+    return jnp.concatenate(pieces3(value), axis=1)
 
 
 def whole3(pieces):
@@ -840,41 +917,48 @@
     group = ln_gain.shape[0]
     blk_pos = lax.axis_index("blk")
     piece = b_down.shape[0]
-    packed = prompt_partial(queries, prompt_kv, page_table, prompt_len, sample_prompt)
-    shares = [packed[0]] + [send_xor(packed[k], "page", k) for k in (1, 2, 3)]
-    tail = tail_partial(queries, tail_kv, tail_len)
+    *packed, held_tail = prompt_partial(
+        queries, prompt_kv, tail_kv, page_table, prompt_len, sample_prompt
+    )
+    sent = {k: send_xor(packed[k], "page", k) for k in (2, 3, 1)}
+    shares = [packed[0], sent[1], sent[2], sent[3]]
+    tail = tail_partial(queries, held_tail, tail_kv, tail_len)
     own_attention = merge_partials(shares + [tail], heads_dev)
-    attention = gather_xor(own_attention, "page", (1, 2, 3))
+    sent = {k: send_xor(own_attention, "page", k) for k in (2, 1, 3)}
+    attention = [own_attention, sent[1], sent[2], sent[3]]
     held_out = hold_columns(own_attention, w_out, (0,), group)
+    near_up = hold_columns(own_attention, w_up, (1,), w_up.shape[1] // 4)
+    held_out, near_up = lax.optimization_barrier((held_out, near_up))
     keep, give = project(attention, held_out, stream_in, group)
     own, *pieces = pair_pieces(keep, send_xor(give, "blk", 1))
     units = w_up.shape[1] // 4
     arrived = [send_xor(pieces[k - 1], "blk", 2 * k) for k in (3, 2, 1)]
+    held_up = hold_columns(own, w_up, (3, 2), units)
+    own, held_up = lax.optimization_barrier((own, held_up))
     own_rows = residual_rows(own, arrived, b_out, w_score)
     same_core = gather_xor(own_rows, "blk", (2, 4, 6))
-    near_up = hold_columns(own_rows, w_up, (1,), units)
-    same_core[1], near_up = lax.optimization_barrier((same_core[1], near_up))
     blocks = same_core + [send_xor(block, "blk", 1) for block in same_core]
-    part3, part2, part1, score_group, lhs, residual, stats = up_first(
-        blocks, ln_gain, ln_bias, b_down, near_up, w_up
-    )
+    top3, bottom3, top2, bottom2, part1, score_group, lhs, residual, stats = up_first(
+        blocks, ln_gain, ln_bias, b_down, held_up, near_up
+    )
+    passing = send_xor(top3, "page", 1)
+    far = send_xor(bottom3, "page", 3)
+    middle = send_xor(bottom2, "page", 2)
+    near = send_xor(part1, "page", 1)
     part0 = up_own(lhs, stats, w_up)
-    image = image_of(score_group, w_down)
-    parts = [part0] + [
-        send_xor(part, "page", k) for k, part in ((1, part1), (2, part2), (3, part3))
-    ]
-    whole, top, bottom, base_score = own_hidden_units(parts, b_up, image, group)
-    summed, held = down_first(whole, w_down)
-    far_top, summed = lax.optimization_barrier((send_xor(top, "page", 2), summed))
-    hiddens = [
-        whole,
-        send_xor(whole, "page", 1),
-        far_top,
-        send_xor(bottom, "page", 2),
-        send_xor(far_top, "page", 1),
-        send_xor(bottom, "page", 3),
-    ]
-    keep, give, score = down_rest(base_score, summed, held, hiddens)
+    image_a = image_of(score_group, w_down, 0, 2)
+    passing, part0, image_a = lax.optimization_barrier((passing, part0, image_a))
+    both, score_group = lax.optimization_barrier((relay_sum(top2, passing), score_group))
+    images = image_a, image_of(score_group, w_down, 2, 2)
+    parts = [part0, near, send_xor(both, "page", 2), middle, far]
+    hidden, base_score = own_hidden_units(parts, b_up, images, group)
+    summed, held = down_first(hidden, w_down)
+    far, near, summed = lax.optimization_barrier(
+        (send_xor(hidden, "page", 2), send_xor(hidden, "page", 1), summed)
+    )
+    summed = down_middle(summed, held, near, far)
+    relayed = send_xor(far, "page", 1)
+    keep, give, score = down_last(base_score, summed, held, [hidden, near, far, relayed])
     own_base = lax.dynamic_slice_in_dim(residual, blk_pos * piece, piece, 1).astype(
         f32
     ) + b_down.astype(f32)

time: 103 us -> 96.7 us (0.939)
  starting transfers between devices: 39.6 us -> 30.8 us
  waiting for transfers between devices: 26.5 us -> 28.6 us
    ppermute x29, starting transfers between devices: 39.6 us -> 30.8 us  [send_xor(): return lax.ppermute(value, axis, [(i, i ^ distance) for i in range(size)])]
    pallas_call x2 -> x3, Pallas kernels: 3.42 us -> 6.44 us  [hold_columns(): pl.pallas_call(functools.partial(hold_kernel, shards), in_specs=[pl.Block...]
    ppermute x29, waiting for transfers between devices: 26.5 us -> 28.6 us  [send_xor(): return lax.ppermute(value, axis, [(i, i ^ distance) for i in range(size)])]
    pallas_call x5 -> x8, Pallas kernels: 14.2 us -> 12.1 us  [the longest x2 7.24 us: image_of(): pl.pallas_call(functools.partial(image_kernel, first), in_specs=[vmem, pl...]
  transfers between devices with their start and end apart: 29 -> 29, of which waited for: 17 -> 20; matrix products, arithmetic and copies ran while one was open for 0% -> 0% of each run, Pallas kernels for 23% -> 28%
where the time goes in v4:
time: 96.7 us; the launch traced here: 96.5 us
  Pallas kernels  36 us (37%)
  starting transfers between devices  30.8 us (32%)
  waiting for transfers between devices  28.6 us (30%)
    ppermute x29, starting transfers between devices, send_xor(): return lax.ppermute(value, axis, [(i, i ^ distance) for i in range(size)])  30.8 us
    ppermute x29, waiting for transfers between devices, send_xor(): return lax.ppermute(value, axis, [(i, i ^ distance) for i in range(size)])  28.6 us
    pallas_call x2, Pallas kernels, image_of(): pl.pallas_call(functools.partial(image_kernel, first), in_specs=[vmem, pl...  7.24 us
    pallas_call x3, Pallas kernels, hold_columns(): pl.pallas_call(functools.partial(hold_kernel, shards), in_specs=[pl.Block...  6.44 us
    pallas_call x1, Pallas kernels, down_first(): pl.pallas_call(down_first_kernel, in_specs=[vmem, pl.BlockSpec(memory_spa...  4.76 us
    pallas_call x1, Pallas kernels, tail_partial(): pl.pallas_call(functools.partial(tail_kernel, math.log2(math.e) / math.sq...  4.6 us
    pallas_call x1, Pallas kernels, prompt_partial(): pl.pallas_call(functools.partial(prompt_kernel, math.log2(math.e) / math....  3.25 us
    pallas_call x1, Pallas kernels, up_own(): pl.pallas_call(up_own_kernel, in_specs=[vmem] * 2 + [pl.BlockSpec(memory_...  2.65 us
  transfers between devices with their start and end apart: 29, of which 20 were waited for; matrix products, arithmetic and copies ran while one was open for 0% of the time, Pallas kernels for 28%

profile of v4, /device:TPU:0, one launch (start us, length us, event | category | flops | bytes accessed | tf_op | source)
XLA Modules:
  0.0 96.5 jit_solution(6185012822894235009)
XLA Ops:
  0.6 3.2 %prompt_attention.1 = (f32[136,128]{1,0:T(8,128)S(1)}, bf16[136,128]{1,0:T(8,128)(2,1)S(1)}, bf16[136,128]{1,0:T(8,128)(2,1)S(1)}, bf16[136,128]{1,0:T(8,128)(2,1)S(1)}, bf16[8,256,4,256]{3,2,1,0:T(4,128)(2,1)S(1)}) custom-call(s32[4,16]{1,0:T(4,128)} %table_hbm.1, s32[4]{0:T(128)} %len_hbm.1, s32[64]{0:T(128)} %prompt_hbm.1, bf16[64,2,4,128]{3,2,1,0:T(4,128)(2,1)} %q_ref.1, ...), custom_call_target="tpu_custom_call" | custom-call | tf_op jit(solution)/shard_map/prompt_attention/pallas_call | solution.py:196
  3.9 3.1 %collective-permute-start = (bf16[136,128]{1,0:T(8,128)(2,1)S(1)}, bf16[136,128]{1,0:T(8,128)(2,1)S(1)}, u32[]{:S(2)}, u32[]{:S(2)}) collective-permute-start(bf16[136,128]{1,0:T(8,128)(2,1)S(1)} %get-tuple-element.49), channel_id=1, source_target_pairs={{0,8},{8,0},{16,24},{24,16},{1,9},{9,1},{17,25},{25,17},{2,10},{10... | collective-permute-start | bytes 104456 | tf_op jit(solution)/shard_map/ppermute | solution.py:46
  7.0 2.6 %collective-permute-start.1 = (bf16[136,128]{1,0:T(8,128)(2,1)S(1)}, bf16[136,128]{1,0:T(8,128)(2,1)S(1)}, u32[]{:S(2)}, u32[]{:S(2)}) collective-permute-start(bf16[136,128]{1,0:T(8,128)(2,1)S(1)} %get-tuple-element.50), channel_id=1, source_target_pairs={{0,16},{8,24},{16,0},{24,8},{1,17},{9,25},{17,1},{25,9},{2,18},{10... | collective-permute-start | bytes 104456 | tf_op jit(solution)/shard_map/ppermute | solution.py:46
  9.6 4.6 %tail_attention.1.refs_4_ = f32[136,128]{1,0:T(8,128)S(1)} custom-call(s32[64]{0:T(128)} %len_ref.1, bf16[64,2,4,128]{3,2,1,0:T(4,128)(2,1)} %q_ref.1, bf16[8,256,4,256]{3,2,1,0:T(4,128)(2,1)S(1)} %get-tuple-element.52.held_ref, bf16[16,256,4,256]{3,2,1,0:T(4,128)(2,1)} %kv_hbm.3), custom_call_target="tpu_custom_call" | custom-call | tf_op jit(solution)/shard_map/tail_attention/pallas_call | solution.py:292
  15.5 2.8 %collective-permute-start.5 = (bf16[32,512]{1,0:T(8,128)(2,1)S(1)}, bf16[32,512]{1,0:T(8,128)(2,1)S(1)}, u32[]{:S(2)}, u32[]{:S(2)}) collective-permute-start(bf16[32,512]{1,0:T(8,128)(2,1)S(1)} %merge_partials.1.after_ref.refs_0_), channel_id=1, source_target_pairs={{0,24},{8,16},{16,8},{24,0},{1,25},{9,17},{17,9},{25,1},{2,26},{10... | collective-permute-start | bytes 98312 | tf_op jit(solution)/shard_map/ppermute | solution.py:46
  18.3 1.7 %collective-permute-start.3 = (bf16[32,512]{1,0:T(8,128)(2,1)S(1)}, bf16[32,512]{1,0:T(8,128)(2,1)S(1)}, u32[]{:S(2)}, u32[]{:S(2)}) collective-permute-start(bf16[32,512]{1,0:T(8,128)(2,1)S(1)} %merge_partials.1.after_ref.refs_0_), channel_id=1, source_target_pairs={{0,8},{8,0},{16,24},{24,16},{1,9},{9,1},{17,25},{25,17},{2,10},{10... | collective-permute-start | bytes 98312 | tf_op jit(solution)/shard_map/ppermute | solution.py:46
  20.0 1.5 %hold_columns.3.refs_4_ = bf16[1,512,1792]{2,1,0:T(8,128)(2,1)S(1)} custom-call(bf16[32,512]{1,0:T(8,128)(2,1)S(1)} %merge_partials.1.after_ref.refs_0_, bf16[512,7168]{1,0:T(8,128)(2,1)} %w_hbm.7), custom_call_target="tpu_custom_call" | custom-call | tf_op jit(solution)/shard_map/hold_columns/pallas_call | solution.py:371
  21.5 2.0 %hold_columns.4.refs_12_ = bf16[1,1792,896]{2,1,0:T(8,128)(2,1)S(1)} custom-call(bf16[32,512]{1,0:T(8,128)(2,1)S(1)} %merge_partials.1.after_ref.refs_0_, bf16[1792,3584]{1,0:T(8,128)(2,1)} %w_hbm.10), custom_call_target="tpu_custom_call" | custom-call | tf_op jit(solution)/shard_map/hold_columns/pallas_call | solution.py:371
  24.3 1.5 %collective-permute-done.6.got_ref = bf16[4,16,1792]{2,1,0:T(8,128)(2,1)S(1)} collective-permute-done((bf16[4,16,1792]{2,1,0:T(8,128)(2,1)S(1)}, bf16[4,16,1792]{2,1,0:T(8,128)(2,1)S(1)}, u32[]{:S(2)}, u32[]{:S(2)}) %collective-permute-start.6) | collective-permute-done | bytes 229408 | tf_op jit(solution)/shard_map/ppermute | solution.py:46
  25.9 2.4 %collective-permute-start.7 = (bf16[16,1792]{1,0:T(8,128)(2,1)S(1)}, bf16[16,1792]{1,0:T(8,128)(2,1)S(1)}, u32[]{:S(2)}, u32[]{:S(2)}) collective-permute-start(bf16[16,1792]{1,0:T(8,128)(2,1)S(1)} %get-tuple-element.58), channel_id=1, source_target_pairs={{0,6},{1,7},{2,4},{3,5},{4,2},{5,3},{6,0},{7,1},{8,14},{9,15},{10,... | collective-permute-start | bytes 172040 | tf_op jit(solution)/shard_map/ppermute | solution.py:46
  29.4 3.0 %hold_columns.5.refs_11_ = bf16[2,1792,896]{2,1,0:T(8,128)(2,1)S(1)} custom-call(f32[16,1792]{1,0:T(8,128)S(1)} %get-tuple-element.57.after_ref.own_ref, bf16[1792,3584]{1,0:T(8,128)(2,1)} %w_hbm.10), custom_call_target="tpu_custom_call" | custom-call | tf_op jit(solution)/shard_map/hold_columns/pallas_call | solution.py:371
  33.1 1.9 %collective-permute-start.12 = (bf16[16,2048]{1,0:T(8,128)(2,1)S(1)}, bf16[16,2048]{1,0:T(8,128)(2,1)S(1)}, u32[]{:S(2)}, u32[]{:S(2)}) collective-permute-start(bf16[16,2048]{1,0:T(8,128)(2,1)S(1)} %residual_rows.1.refs_0_), channel_id=1, source_target_pairs={{0,6},{1,7},{2,4},{3,5},{4,2},{5,3},{6,0},{7,1},{8,14},{9,15},{10,... | collective-permute-start | bytes 196616 | tf_op jit(solution)/shard_map/ppermute | solution.py:46
  36.6 2.2 %collective-permute-done.12.refs_3_ = bf16[16,2048]{1,0:T(8,128)(2,1)S(1)} collective-permute-done((bf16[16,2048]{1,0:T(8,128)(2,1)S(1)}, bf16[16,2048]{1,0:T(8,128)(2,1)S(1)}, u32[]{:S(2)}, u32[]{:S(2)}) %collective-permute-start.12) | collective-permute-done | bytes 65568 | tf_op jit(solution)/shard_map/ppermute | solution.py:46
  41.0 2.1 %norm_and_up.1 = (bf16[48,896]{1,0:T(8,128)(2,1)S(1)}, bf16[88,896]{1,0:T(8,128)(2,1)S(1)}, bf16[48,896]{1,0:T(8,128)(2,1)S(1)}, bf16[88,896]{1,0:T(8,128)(2,1)S...) custom-call(bf16[16,2048]{1,0:T(8,128)(2,1)S(1)} %residual_rows.1.re, ...), custom_call_target="tpu_custom_call" | custom-call | tf_op jit(solution)/shard_map/norm_and_up/pallas_call | solution.py:566
  43.7 1.6 %collective-permute-start.17 = (bf16[48,896]{1,0:T(8,128)(2,1)S(1)}, bf16[48,896]{1,0:T(8,128)(2,1)S(1)}, u32[]{:S(2)}, u32[]{:S(2)}) collective-permute-start(bf16[48,896]{1,0:T(8,128)(2,1)S(1)} %get-tuple-element.63), channel_id=1, source_target_pairs={{0,8},{8,0},{16,24},{24,16},{1,9},{9,1},{17,25},{25,17},{2,10},{10... | collective-permute-start | bytes 258056 | tf_op jit(solution)/shard_map/ppermute | solution.py:46
  45.2 1.6 %collective-permute-start.20 = (bf16[88,896]{1,0:T(8,128)(2,1)S(1)}, bf16[88,896]{1,0:T(8,128)(2,1)S(1)}, u32[]{:S(2)}, u32[]{:S(2)}) collective-permute-start(bf16[88,896]{1,0:T(8,128)(2,1)S(1)} %get-tuple-element.72), channel_id=1, source_target_pairs={{0,16},{8,24},{16,0},{24,8},{1,17},{9,25},{17,1},{25,9},{2,18},{10... | collective-permute-start | bytes 473096 | tf_op jit(solution)/shard_map/ppermute | solution.py:46
  46.9 1.2 %collective-permute-start.21 = (bf16[88,896]{1,0:T(8,128)(2,1)S(1)}, bf16[88,896]{1,0:T(8,128)(2,1)S(1)}, u32[]{:S(2)}, u32[]{:S(2)}) collective-permute-start(bf16[88,896]{1,0:T(8,128)(2,1)S(1)} %get-tuple-element.73), channel_id=1, source_target_pairs={{0,24},{8,16},{16,8},{24,0},{1,25},{9,17},{17,9},{25,1},{2,26},{10... | collective-permute-start | bytes 473096 | tf_op jit(solution)/shard_map/ppermute | solution.py:46
  48.1 3.6 %score_image.2.refs_6_ = f32[4,896]{1,0:T(4,128)S(1)} custom-call(f32[1,1792]{1,0:T(1,128)S(1)} %get-tuple-element.75.score_ref, bf16[3584,1792]{1,0:T(8,128)(2,1)} %w_hbm.13), custom_call_target="tpu_custom_call" | custom-call | tf_op jit(solution)/shard_map/score_image/pallas_call | solution.py:663
  51.7 2.6 %up_own.1.refs_0_ = bf16[136,896]{1,0:T(8,128)(2,1)S(1)} custom-call(bf16[144,1792]{1,0:T(8,128)(2,1)S(1)} %get-tuple-element.64.lhs_ref, bf16[6,128]{1,0:T(8,128)(2,1)S(1)} %get-tuple-element.65.stats_ref, bf16[1792,3584]{1,0:T(8,128)(2,1)} %w_hbm.10), custom_call_target="tpu_custom_call" | custom-call | tf_op jit(solution)/shard_map/up_own/pallas_call | solution.py:605
  54.4 2.1 %collective-permute-done.17.b_ref = bf16[48,896]{1,0:T(8,128)(2,1)S(1)} collective-permute-done((bf16[48,896]{1,0:T(8,128)(2,1)S(1)}, bf16[48,896]{1,0:T(8,128)(2,1)S(1)}, u32[]{:S(2)}, u32[]{:S(2)}) %collective-permute-start.17) | collective-permute-done | bytes 86048 | tf_op jit(solution)/shard_map/ppermute | solution.py:46
  56.4 1.4 %collective-permute-start.19 = (bf16[48,896]{1,0:T(8,128)(2,1)S(1)}, bf16[48,896]{1,0:T(8,128)(2,1)S(1)}, u32[]{:S(2)}, u32[]{:S(2)}) collective-permute-start(bf16[48,896]{1,0:T(8,128)(2,1)S(1)} %relay_sum.1), channel_id=1, source_target_pairs={{0,16},{8,24},{16,0},{24,8},{1,17},{9,25},{17,1},{25,9},{2,18},{10... | collective-permute-start | bytes 258056 | tf_op jit(solution)/shard_map/ppermute | solution.py:46
  57.9 3.6 %score_image.3.refs_7_ = f32[4,896]{1,0:T(4,128)S(1)} custom-call(f32[1,1792]{1,0:T(1,128)S(1)} %get-tuple-element.75.score_ref, bf16[3584,1792]{1,0:T(8,128)(2,1)} %w_hbm.13), custom_call_target="tpu_custom_call" | custom-call | tf_op jit(solution)/shard_map/score_image/pallas_call | solution.py:663
  61.8 3.8 %collective-permute-done.19.refs_2_ = bf16[48,896]{1,0:T(8,128)(2,1)S(1)} collective-permute-done((bf16[48,896]{1,0:T(8,128)(2,1)S(1)}, bf16[48,896]{1,0:T(8,128)(2,1)S(1)}, u32[]{:S(2)}, u32[]{:S(2)}) %collective-permute-start.19) | collective-permute-done | bytes 86048 | tf_op jit(solution)/shard_map/ppermute | solution.py:46
  66.4 3.0 %collective-permute-start.22 = (bf16[136,896]{1,0:T(8,128)(2,1)S(1)}, bf16[136,896]{1,0:T(8,128)(2,1)S(1)}, u32[]{:S(2)}, u32[]{:S(2)}) collective-permute-start(bf16[136,896]{1,0:T(8,128)(2,1)S(1)} %get-tuple-element.77.hidden_ref.refs_0_), channel_id=1, source_target_pairs={{0,16},{8,24},{16,0},{24,8},{1,17},{9,25},{17,1},{25,9},{2,18},{10... | collective-permute-start | bytes 731144 | tf_op jit(solution)/shard_map/ppermute | solution.py:46
  69.4 4.8 %down_own.1 = (f32[128,1792]{1,0:T(8,128)S(1)}, bf16[3,896,1792]{2,1,0:T(8,128)(2,1)S(1)}) custom-call(bf16[136,896]{1,0:T(8,128)(2,1)S(1)} %get-tuple-element.77.hidden_ref.refs_0_, bf16[3584,1792]{1,0:T(8,128)(2,1)} %w_hbm.13), custom_call_target="tpu_custom_call" | custom-call | tf_op jit(solution)/shard_map/down_own/pallas_call | solution.py:740
  74.2 3.5 %collective-permute-done.23.near_ref.refs_1_ = bf16[136,896]{1,0:T(8,128)(2,1)S(1)} collective-permute-done((bf16[136,896]{1,0:T(8,128)(2,1)S(1)}, bf16[136,896]{1,0:T(8,128)(2,1)S(1)}, u32[]{:S(2)}, u32[]{:S(2)}) %collective-permute-start.23) | collective-permute-done | bytes 243744 | tf_op jit(solution)/shard_map/ppermute | solution.py:46
  77.7 1.7 %collective-permute-done.22.far_ref.refs_2_ = bf16[136,896]{1,0:T(8,128)(2,1)S(1)} collective-permute-done((bf16[136,896]{1,0:T(8,128)(2,1)S(1)}, bf16[136,896]{1,0:T(8,128)(2,1)S(1)}, u32[]{:S(2)}, u32[]{:S(2)}) %collective-permute-start.22) | collective-permute-done | bytes 243744 | tf_op jit(solution)/shard_map/ppermute | solution.py:46
  80.5 5.1 %collective-permute-done.24.refs_3_ = bf16[136,896]{1,0:T(8,128)(2,1)S(1)} collective-permute-done((bf16[136,896]{1,0:T(8,128)(2,1)S(1)}, bf16[136,896]{1,0:T(8,128)(2,1)S(1)}, u32[]{:S(2)}, u32[]{:S(2)}) %collective-permute-start.24) | collective-permute-done | bytes 243744 | tf_op jit(solution)/shard_map/ppermute | solution.py:46
  86.8 1.5 %collective-permute-done.25.got_ref = bf16[4,128,227]{2,1,0:T(8,128)(2,1)S(1)} collective-permute-done((bf16[4,128,227]{2,1,0:T(8,128)(2,1)S(1)}, bf16[4,128,227]{2,1,0:T(8,128)(2,1)S(1)}, u32[]{:S(2)}, u32[]{:S(2)}) %collective-permute-start.25) | collective-permute-done | bytes 232480 | tf_op jit(solution)/shard_map/ppermute | solution.py:46
  88.6 2.2 %collective-permute-start.26 = (bf16[128,227]{1,0:T(8,128)(2,1)S(1)}, bf16[128,227]{1,0:T(8,128)(2,1)S(1)}, u32[]{:S(2)}, u32[]{:S(2)}) collective-permute-start(bf16[128,227]{1,0:T(8,128)(2,1)S(1)} %get-tuple-element.89), channel_id=1, source_target_pairs={{0,6},{1,7},{2,4},{3,5},{4,2},{5,3},{6,0},{7,1},{8,14},{9,15},{10,... | collective-permute-start | bytes 174344 | tf_op jit(solution)/shard_map/ppermute | solution.py:46
  92.2 1.6 %collective-permute-done.26.c_ref = bf16[128,227]{1,0:T(8,128)(2,1)S(1)} collective-permute-done((bf16[128,227]{1,0:T(8,128)(2,1)S(1)}, bf16[128,227]{1,0:T(8,128)(2,1)S(1)}, u32[]{:S(2)}, u32[]{:S(2)}) %collective-permute-start.26) | collective-permute-done | bytes 58144 | tf_op jit(solution)/shard_map/ppermute | solution.py:46
  93.8 1.3 %collective-permute-done.27.b_ref = bf16[128,227]{1,0:T(8,128)(2,1)S(1)} collective-permute-done((bf16[128,227]{1,0:T(8,128)(2,1)S(1)}, bf16[128,227]{1,0:T(8,128)(2,1)S(1)}, u32[]{:S(2)}, u32[]{:S(2)}) %collective-permute-start.27) | collective-permute-done | bytes 58144 | tf_op jit(solution)/shard_map/ppermute | solution.py:46
  (62 shorter events, 14.7 us)
Async XLA Ops:
  3.9 10.3 %collective-permute-start = (bf16[136,128]{1,0:T(8,128)(2,1)S(1)}, bf16[136,128]{1,0:T(8,128)(2,1)S(1)}, u32[]{:S(2)}, u32[]{:S(2)}) collective-permute-start(bf16[136,128]{1,0:T(8,128)(2,1)S(1)} %get-tuple-element.49), channel_id=1, source_target_pairs={{0,8},{8,0},{16,24},{24,16},{1,9},{9,1},{17,25},{25,17},{2,10},{10... | collective-permute-start | bytes 104456 | tf_op jit(solution)/shard_map/ppermute | solution.py:46
  7.0 7.2 %collective-permute-start.1 = (bf16[136,128]{1,0:T(8,128)(2,1)S(1)}, bf16[136,128]{1,0:T(8,128)(2,1)S(1)}, u32[]{:S(2)}, u32[]{:S(2)}) collective-permute-start(bf16[136,128]{1,0:T(8,128)(2,1)S(1)} %get-tuple-element.50), channel_id=1, source_target_pairs={{0,16},{8,24},{16,0},{24,8},{1,17},{9,25},{17,1},{25,9},{2,18},{10... | collective-permute-start | bytes 104456 | tf_op jit(solution)/shard_map/ppermute | solution.py:46
  9.6 5.7 %collective-permute-start.2 = (bf16[136,128]{1,0:T(8,128)(2,1)S(1)}, bf16[136,128]{1,0:T(8,128)(2,1)S(1)}, u32[]{:S(2)}, u32[]{:S(2)}) collective-permute-start(bf16[136,128]{1,0:T(8,128)(2,1)S(1)} %get-tuple-element.51), channel_id=1, source_target_pairs={{0,24},{8,16},{16,8},{24,0},{1,25},{9,17},{17,9},{25,1},{2,26},{10... | collective-permute-start | bytes 104456 | tf_op jit(solution)/shard_map/ppermute | solution.py:46
  15.5 8.0 %collective-permute-start.5 = (bf16[32,512]{1,0:T(8,128)(2,1)S(1)}, bf16[32,512]{1,0:T(8,128)(2,1)S(1)}, u32[]{:S(2)}, u32[]{:S(2)}) collective-permute-start(bf16[32,512]{1,0:T(8,128)(2,1)S(1)} %merge_partials.1.after_ref.refs_0_), channel_id=1, source_target_pairs={{0,24},{8,16},{16,8},{24,0},{1,25},{9,17},{17,9},{25,1},{2,26},{10... | collective-permute-start | bytes 98312 | tf_op jit(solution)/shard_map/ppermute | solution.py:46
  18.3 5.2 %collective-permute-start.4 = (bf16[32,512]{1,0:T(8,128)(2,1)S(1)}, bf16[32,512]{1,0:T(8,128)(2,1)S(1)}, u32[]{:S(2)}, u32[]{:S(2)}) collective-permute-start(bf16[32,512]{1,0:T(8,128)(2,1)S(1)} %merge_partials.1.after_ref.refs_0_), channel_id=1, source_target_pairs={{0,16},{8,24},{16,0},{24,8},{1,17},{9,25},{17,1},{25,9},{2,18},{10... | collective-permute-start | bytes 98312 | tf_op jit(solution)/shard_map/ppermute | solution.py:46
  18.3 5.2 %collective-permute-start.3 = (bf16[32,512]{1,0:T(8,128)(2,1)S(1)}, bf16[32,512]{1,0:T(8,128)(2,1)S(1)}, u32[]{:S(2)}, u32[]{:S(2)}) collective-permute-start(bf16[32,512]{1,0:T(8,128)(2,1)S(1)} %merge_partials.1.after_ref.refs_0_), channel_id=1, source_target_pairs={{0,8},{8,0},{16,24},{24,16},{1,9},{9,1},{17,25},{25,17},{2,10},{10... | collective-permute-start | bytes 98312 | tf_op jit(solution)/shard_map/ppermute | solution.py:46
  24.2 1.6 %collective-permute-start.6 = (bf16[4,16,1792]{2,1,0:T(8,128)(2,1)S(1)}, bf16[4,16,1792]{2,1,0:T(8,128)(2,1)S(1)}, u32[]{:S(2)}, u32[]{:S(2)}) collective-permute-start(bf16[4,16,1792]{2,1,0:T(8,128)(2,1)S(1)} %get-tuple-element.55), channel_id=1, source_target_pairs={{0,1},{1,0},{2,3},{3,2},{4,5},{5,4},{6,7},{7,6},{8,9},{9,8},{10,11... | collective-permute-start | bytes 688136 | tf_op jit(solution)/shard_map/ppermute | solution.py:46
  25.9 6.5 %collective-permute-start.7 = (bf16[16,1792]{1,0:T(8,128)(2,1)S(1)}, bf16[16,1792]{1,0:T(8,128)(2,1)S(1)}, u32[]{:S(2)}, u32[]{:S(2)}) collective-permute-start(bf16[16,1792]{1,0:T(8,128)(2,1)S(1)} %get-tuple-element.58), channel_id=1, source_target_pairs={{0,6},{1,7},{2,4},{3,5},{4,2},{5,3},{6,0},{7,1},{8,14},{9,15},{10,... | collective-permute-start | bytes 172040 | tf_op jit(solution)/shard_map/ppermute | solution.py:46
  28.3 4.2 %collective-permute-start.8 = (bf16[16,1792]{1,0:T(8,128)(2,1)S(1)}, bf16[16,1792]{1,0:T(8,128)(2,1)S(1)}, u32[]{:S(2)}, u32[]{:S(2)}) collective-permute-start(bf16[16,1792]{1,0:T(8,128)(2,1)S(1)} %get-tuple-element.59), channel_id=1, source_target_pairs={{0,4},{1,5},{2,6},{3,7},{4,0},{5,1},{6,2},{7,3},{8,12},{9,13},{10,... | collective-permute-start | bytes 172040 | tf_op jit(solution)/shard_map/ppermute | solution.py:46
  28.8 4.2 %collective-permute-start.9 = (bf16[16,1792]{1,0:T(8,128)(2,1)S(1)}, bf16[16,1792]{1,0:T(8,128)(2,1)S(1)}, u32[]{:S(2)}, u32[]{:S(2)}) collective-permute-start(bf16[16,1792]{1,0:T(8,128)(2,1)S(1)} %get-tuple-element.60), channel_id=1, source_target_pairs={{0,2},{1,3},{2,0},{3,1},{4,6},{5,7},{6,4},{7,5},{8,10},{9,11},{10,... | collective-permute-start | bytes 172040 | tf_op jit(solution)/shard_map/ppermute | solution.py:46
  29.4 11.6 %copy-start.3 = (bf16[1792]{0:T(1024)(128)(2,1)S(1)}, bf16[1792]{0:T(1024)(128)(2,1)}, u32[]{:S(2)}) copy-start(bf16[1792]{0:T(1024)(128)(2,1)} %refs_8_.1) | copy-start | bytes 10756
  29.4 11.6 %copy-start.4 = (bf16[1792]{0:T(1024)(128)(2,1)S(1)}, bf16[1792]{0:T(1024)(128)(2,1)}, u32[]{:S(2)}) copy-start(bf16[1792]{0:T(1024)(128)(2,1)} %refs_9_.1) | copy-start | bytes 10756
  29.4 11.6 %copy-start.6 = (bf16[224]{0:T(256)(128)(2,1)S(1)}, bf16[224]{0:T(256)(128)(2,1)}, u32[]{:S(2)}) copy-start(bf16[224]{0:T(256)(128)(2,1)} %refs_10_.1) | copy-start | bytes 1348
  33.1 5.7 %collective-permute-start.12 = (bf16[16,2048]{1,0:T(8,128)(2,1)S(1)}, bf16[16,2048]{1,0:T(8,128)(2,1)S(1)}, u32[]{:S(2)}, u32[]{:S(2)}) collective-permute-start(bf16[16,2048]{1,0:T(8,128)(2,1)S(1)} %residual_rows.1.refs_0_), channel_id=1, source_target_pairs={{0,6},{1,7},{2,4},{3,5},{4,2},{5,3},{6,0},{7,1},{8,14},{9,15},{10,... | collective-permute-start | bytes 196616 | tf_op jit(solution)/shard_map/ppermute | solution.py:46
  35.0 4.4 %collective-permute-start.11 = (bf16[16,2048]{1,0:T(8,128)(2,1)S(1)}, bf16[16,2048]{1,0:T(8,128)(2,1)S(1)}, u32[]{:S(2)}, u32[]{:S(2)}) collective-permute-start(bf16[16,2048]{1,0:T(8,128)(2,1)S(1)} %residual_rows.1.refs_0_), channel_id=1, source_target_pairs={{0,4},{1,5},{2,6},{3,7},{4,0},{5,1},{6,2},{7,3},{8,12},{9,13},{10,... | collective-permute-start | bytes 196616 | tf_op jit(solution)/shard_map/ppermute | solution.py:46
  35.5 4.3 %collective-permute-start.10 = (bf16[16,2048]{1,0:T(8,128)(2,1)S(1)}, bf16[16,2048]{1,0:T(8,128)(2,1)S(1)}, u32[]{:S(2)}, u32[]{:S(2)}) collective-permute-start(bf16[16,2048]{1,0:T(8,128)(2,1)S(1)} %residual_rows.1.refs_0_), channel_id=1, source_target_pairs={{0,2},{1,3},{2,0},{3,1},{4,6},{5,7},{6,4},{7,5},{8,10},{9,11},{10,... | collective-permute-start | bytes 196616 | tf_op jit(solution)/shard_map/ppermute | solution.py:46
  36.6 3.3 %collective-permute-start.13 = (bf16[16,2048]{1,0:T(8,128)(2,1)S(1)}, bf16[16,2048]{1,0:T(8,128)(2,1)S(1)}, u32[]{:S(2)}, u32[]{:S(2)}) collective-permute-start(bf16[16,2048]{1,0:T(8,128)(2,1)S(1)} %residual_rows.1.refs_0_), channel_id=1, source_target_pairs={{0,1},{1,0},{2,3},{3,2},{4,5},{5,4},{6,7},{7,6},{8,9},{9,8},{10,11... | collective-permute-start | bytes 196616 | tf_op jit(solution)/shard_map/ppermute | solution.py:46
  38.8 1.3 %collective-permute-start.16 = (bf16[16,2048]{1,0:T(8,128)(2,1)S(1)}, bf16[16,2048]{1,0:T(8,128)(2,1)S(1)}, u32[]{:S(2)}, u32[]{:S(2)}) collective-permute-start(bf16[16,2048]{1,0:T(8,128)(2,1)S(1)} %collective-permute-done.12.refs_3_), channel_id=1, source_target_pairs={{0,1},{1,0},{2,3},{3,2},{4,5},{5,4},{6,7},{7,6},{8,9},{9,8},{10,11... | collective-permute-start | bytes 196616 | tf_op jit(solution)/shard_map/ppermute | solution.py:46
  39.4 1.3 %collective-permute-start.15 = (bf16[16,2048]{1,0:T(8,128)(2,1)S(1)}, bf16[16,2048]{1,0:T(8,128)(2,1)S(1)}, u32[]{:S(2)}, u32[]{:S(2)}) collective-permute-start(bf16[16,2048]{1,0:T(8,128)(2,1)S(1)} %collective-permute-done.11.refs_2_), channel_id=1, source_target_pairs={{0,1},{1,0},{2,3},{3,2},{4,5},{5,4},{6,7},{7,6},{8,9},{9,8},{10,11... | collective-permute-start | bytes 196616 | tf_op jit(solution)/shard_map/ppermute | solution.py:46
  39.7 1.3 %collective-permute-start.14 = (bf16[16,2048]{1,0:T(8,128)(2,1)S(1)}, bf16[16,2048]{1,0:T(8,128)(2,1)S(1)}, u32[]{:S(2)}, u32[]{:S(2)}) collective-permute-start(bf16[16,2048]{1,0:T(8,128)(2,1)S(1)} %collective-permute-done.10.refs_1_), channel_id=1, source_target_pairs={{0,1},{1,0},{2,3},{3,2},{4,5},{5,4},{6,7},{7,6},{8,9},{9,8},{10,11... | collective-permute-start | bytes 196616 | tf_op jit(solution)/shard_map/ppermute | solution.py:46
  43.2 22.4 %collective-permute-start.18 = (bf16[136,896]{1,0:T(8,128)(2,1)S(1)}, bf16[136,896]{1,0:T(8,128)(2,1)S(1)}, u32[]{:S(2)}, u32[]{:S(2)}) collective-permute-start(bf16[136,896]{1,0:T(8,128)(2,1)S(1)} %get-tuple-element.68), channel_id=1, source_target_pairs={{0,8},{8,0},{16,24},{24,16},{1,9},{9,1},{17,25},{25,17},{2,10},{10... | collective-permute-start | bytes 731144 | tf_op jit(solution)/shard_map/ppermute | solution.py:46
  43.7 12.7 %collective-permute-start.17 = (bf16[48,896]{1,0:T(8,128)(2,1)S(1)}, bf16[48,896]{1,0:T(8,128)(2,1)S(1)}, u32[]{:S(2)}, u32[]{:S(2)}) collective-permute-start(bf16[48,896]{1,0:T(8,128)(2,1)S(1)} %get-tuple-element.63), channel_id=1, source_target_pairs={{0,8},{8,0},{16,24},{24,16},{1,9},{9,1},{17,25},{25,17},{2,10},{10... | collective-permute-start | bytes 258056 | tf_op jit(solution)/shard_map/ppermute | solution.py:46
  45.2 16.2 %collective-permute-start.20 = (bf16[88,896]{1,0:T(8,128)(2,1)S(1)}, bf16[88,896]{1,0:T(8,128)(2,1)S(1)}, u32[]{:S(2)}, u32[]{:S(2)}) collective-permute-start(bf16[88,896]{1,0:T(8,128)(2,1)S(1)} %get-tuple-element.72), channel_id=1, source_target_pairs={{0,16},{8,24},{16,0},{24,8},{1,17},{9,25},{17,1},{25,9},{2,18},{10... | collective-permute-start | bytes 473096 | tf_op jit(solution)/shard_map/ppermute | solution.py:46
  46.9 14.9 %collective-permute-start.21 = (bf16[88,896]{1,0:T(8,128)(2,1)S(1)}, bf16[88,896]{1,0:T(8,128)(2,1)S(1)}, u32[]{:S(2)}, u32[]{:S(2)}) collective-permute-start(bf16[88,896]{1,0:T(8,128)(2,1)S(1)} %get-tuple-element.73), channel_id=1, source_target_pairs={{0,24},{8,16},{16,8},{24,0},{1,25},{9,17},{17,9},{25,1},{2,26},{10... | collective-permute-start | bytes 473096 | tf_op jit(solution)/shard_map/ppermute | solution.py:46
  56.4 9.1 %collective-permute-start.19 = (bf16[48,896]{1,0:T(8,128)(2,1)S(1)}, bf16[48,896]{1,0:T(8,128)(2,1)S(1)}, u32[]{:S(2)}, u32[]{:S(2)}) collective-permute-start(bf16[48,896]{1,0:T(8,128)(2,1)S(1)} %relay_sum.1), channel_id=1, source_target_pairs={{0,16},{8,24},{16,0},{24,8},{1,17},{9,25},{17,1},{25,9},{2,18},{10... | collective-permute-start | bytes 258056 | tf_op jit(solution)/shard_map/ppermute | solution.py:46
  66.0 11.7 %collective-permute-start.23 = (bf16[136,896]{1,0:T(8,128)(2,1)S(1)}, bf16[136,896]{1,0:T(8,128)(2,1)S(1)}, u32[]{:S(2)}, u32[]{:S(2)}) collective-permute-start(bf16[136,896]{1,0:T(8,128)(2,1)S(1)} %get-tuple-element.77.hidden_ref.refs_0_), channel_id=1, source_target_pairs={{0,8},{8,0},{16,24},{24,16},{1,9},{9,1},{17,25},{25,17},{2,10},{10... | collective-permute-start | bytes 731144 | tf_op jit(solution)/shard_map/ppermute | solution.py:46
  66.4 13.0 %collective-permute-start.22 = (bf16[136,896]{1,0:T(8,128)(2,1)S(1)}, bf16[136,896]{1,0:T(8,128)(2,1)S(1)}, u32[]{:S(2)}, u32[]{:S(2)}) collective-permute-start(bf16[136,896]{1,0:T(8,128)(2,1)S(1)} %get-tuple-element.77.hidden_ref.refs_0_), channel_id=1, source_target_pairs={{0,16},{8,24},{16,0},{24,8},{1,17},{9,25},{17,1},{25,9},{2,18},{10... | collective-permute-start | bytes 731144 | tf_op jit(solution)/shard_map/ppermute | solution.py:46
  79.4 6.2 %collective-permute-start.24 = (bf16[136,896]{1,0:T(8,128)(2,1)S(1)}, bf16[136,896]{1,0:T(8,128)(2,1)S(1)}, u32[]{:S(2)}, u32[]{:S(2)}) collective-permute-start(bf16[136,896]{1,0:T(8,128)(2,1)S(1)} %collective-permute-done.22.far_ref.refs_2_), channel_id=1, source_target_pairs={{0,8},{8,0},{16,24},{24,16},{1,9},{9,1},{17,25},{25,17},{2,10},{10... | collective-permute-start | bytes 731144 | tf_op jit(solution)/shard_map/ppermute | solution.py:46
  86.7 1.6 %collective-permute-start.25 = (bf16[4,128,227]{2,1,0:T(8,128)(2,1)S(1)}, bf16[4,128,227]{2,1,0:T(8,128)(2,1)S(1)}, u32[]{:S(2)}, u32[]{:S(2)}) collective-permute-start(bf16[4,128,227]{2,1,0:T(8,128)(2,1)S(1)} %get-tuple-element.85), channel_id=1, source_target_pairs={{0,1},{1,0},{2,3},{3,2},{4,5},{5,4},{6,7},{7,6},{8,9},{9,8},{10,11... | collective-permute-start | bytes 697352 | tf_op jit(solution)/shard_map/ppermute | solution.py:46
  88.6 5.3 %collective-permute-start.26 = (bf16[128,227]{1,0:T(8,128)(2,1)S(1)}, bf16[128,227]{1,0:T(8,128)(2,1)S(1)}, u32[]{:S(2)}, u32[]{:S(2)}) collective-permute-start(bf16[128,227]{1,0:T(8,128)(2,1)S(1)} %get-tuple-element.89), channel_id=1, source_target_pairs={{0,6},{1,7},{2,4},{3,5},{4,2},{5,3},{6,0},{7,1},{8,14},{9,15},{10,... | collective-permute-start | bytes 174344 | tf_op jit(solution)/shard_map/ppermute | solution.py:46
  90.7 4.5 %collective-permute-start.27 = (bf16[128,227]{1,0:T(8,128)(2,1)S(1)}, bf16[128,227]{1,0:T(8,128)(2,1)S(1)}, u32[]{:S(2)}, u32[]{:S(2)}) collective-permute-start(bf16[128,227]{1,0:T(8,128)(2,1)S(1)} %get-tuple-element.90), channel_id=1, source_target_pairs={{0,4},{1,5},{2,6},{3,7},{4,0},{5,1},{6,2},{7,3},{8,12},{9,13},{10,... | collective-permute-start | bytes 174344 | tf_op jit(solution)/shard_map/ppermute | solution.py:46
  91.2 4.3 %collective-permute-start.28 = (bf16[128,227]{1,0:T(8,128)(2,1)S(1)}, bf16[128,227]{1,0:T(8,128)(2,1)S(1)}, u32[]{:S(2)}, u32[]{:S(2)}) collective-permute-start(bf16[128,227]{1,0:T(8,128)(2,1)S(1)} %get-tuple-element.91), channel_id=1, source_target_pairs={{0,2},{1,3},{2,0},{3,1},{4,6},{5,7},{6,4},{7,5},{8,10},{9,11},{10,... | collective-permute-start | bytes 174344 | tf_op jit(solution)/shard_map/ppermute | solution.py:46
  (4 other events, 20.4 us)

commit v5 on v4

--- a/solution.py
+++ b/solution.py
@@ -11,7 +11,7 @@
 NEGATIVE = -1e30
 EPS = 1e-05
 VMEM_LIMIT = 24 * 2**20
-TOP = 48
+TOP = 64
 FREE = pl.CostEstimate(flops=0, bytes_accessed=0, transcendentals=0)
 
 
@@ -76,10 +76,10 @@
     return high, middle, (left - middle.astype(jnp.float32)).astype(jnp.bfloat16)
 
 
-def prompt_kernel(scale, table_hbm, len_hbm, prompt_hbm, q_hbm, kv_hbm, tail_hbm, *refs):
-    outs, held_ref, refs = refs[:4], refs[4], refs[5:]
+def prompt_kernel(scale, table_hbm, len_hbm, prompt_hbm, q_hbm, kv_hbm, tail_hbm, tail_len_hbm, *refs):
+    outs, (held_ref, own_q_ref, own_len_ref), refs = refs[:4], refs[4:7], refs[7:]
     table_ref, len_ref, prompt_ref, q_ref, kv_ref, where_ref, count_ref, place_ref = refs[:8]
-    query_ref, rows_ref, score_ref, best_ref, norm_ref, mixed_ref, back_ref, sent_ref, sems = refs[8:]
+    query_ref, rows_ref, score_ref, best_ref, norm_ref, mixed_ref, back_ref, sent_ref, tail_len_ref, sems = refs[8:]
     copies = start_copies(
         [
             pltpu.make_async_copy(source, target, sems.at[i])
@@ -91,6 +91,7 @@
                     (q_hbm, q_ref),
                     (kv_hbm, kv_ref),
                     (tail_hbm.at[pl.ds(0, held_ref.shape[0])], held_ref),
+                    (tail_len_hbm, tail_len_ref),
                 )
             )
         ]
@@ -146,18 +147,28 @@
         )
         scores = jnp.where(position < jnp.minimum(left, width), scores, NEGATIVE)
         score_ref[j] = scores
-        best = jnp.max(scores, axis=1, keepdims=True)
-        best_ref[at[j], :] = jnp.maximum(best_ref[at[j], :], best)
+        best = best_ref[at[j], :]
+        for start in range(0, width, dim):
+            best = jnp.maximum(best, scores[:, start : start + dim])
+        best_ref[at[j], :] = best
+    best = jnp.max(best_ref[...], axis=1, keepdims=True)
+    best_ref[...] = jnp.broadcast_to(best, best_ref.shape)
     for j in range(slots):
         best = best_ref[at[j], :]
         best = jnp.concatenate([best] * (width // dim), axis=1)
         weights = jnp.exp2((score_ref[j] - best) * scale)
-        norm_ref[at[j], :] += jnp.sum(weights, axis=1, keepdims=True)
+        norm = norm_ref[at[j], :]
+        for start in range(0, width, dim):
+            norm = norm + weights[:, start : start + dim]
+        norm_ref[at[j], :] = norm
         mixed_ref[at[j], :] += jnp.dot(
             weights.astype(bf16),
             cache[j * width : (j + 1) * width, dim:],
             preferred_element_type=f32,
         )
+    norm = jnp.sum(norm_ref[...], axis=1, keepdims=True)
+    lane = lax.broadcasted_iota(jnp.int32, norm_ref.shape, 1)
+    norm_ref[...] = jnp.where(lane == 0, best_ref[...], norm)
     for k, out_ref in enumerate(outs):
         for i in range(lines // small):
             place = place_ref[(page_pos ^ k) * (lines // small) + i]
@@ -167,39 +178,44 @@
                 out_ref[to, :] = mixed_ref[source, :]
             else:
                 sent_ref[to, :] = mixed_ref[source, :]
-            back_ref[k * lines + i * small : k * lines + (i + 1) * small, :] = best_ref[source, :]
-            query_ref[k * lines + i * small : k * lines + (i + 1) * small, :] = norm_ref[source, :]
-        if k > 0:
-            out_ref[0:lines, :] = sent_ref[...].astype(bf16)
-        best = back_ref[k * lines : (k + 1) * lines, :].T[0:1]
-        norm = query_ref[k * lines : (k + 1) * lines, :].T[0:1]
+            back_ref[to, :] = norm_ref[source, :]
+        both = back_ref[0:lines, :].T[0:2]
         if k == 0:
-            out_ref[lines : lines + 1, :] = best
-            out_ref[lines + 1 : lines + 2, :] = norm
+            out_ref[lines : lines + 2, :] = both
         else:
             pad = jnp.zeros((2, dim), bf16)
-            out_ref[lines : lines + 8, :] = jnp.concatenate(
-                [*pieces3(best), *pieces3(norm), pad], axis=0
-            )
+            below = [*pieces3(both[0:1]), *pieces3(both[1:2]), pad]
+            out_ref[0:lines, :] = sent_ref[...].astype(bf16)
+            out_ref[lines : lines + 8, :] = jnp.concatenate(below, axis=0)
+    copies[6].wait()
+    own = own_len_ref.shape[0]
+    for i in range(own):
+        own_q_ref[i] = q_ref[page_pos * own + i]
+        own_len_ref[i] = jnp.full(own_len_ref.shape[1:], tail_len_ref[page_pos * own + i])
     copies[5].wait()
 
 
-def prompt_partial(queries, prompt_kv, tail_kv, page_table, prompt_len, sample_prompt):
+def prompt_partial(queries, prompt_kv, tail_kv, page_table, prompt_len, sample_prompt, tail_len):
     samples, new, heads, dim = queries.shape
     slots, page_len = prompt_kv.shape[:2]
     total = samples * new * heads
     block = total // page_table.shape[0]
     lines = total // 4
+    own = tail_kv.shape[0]
     anywhere = pl.BlockSpec(memory_space=pl.ANY)
     vmem = pl.BlockSpec(memory_space=pltpu.VMEM)
     wide = pltpu.VMEM((total, dim), jnp.float32)
     return pl.pallas_call(
         functools.partial(prompt_kernel, math.log2(math.e) / math.sqrt(dim)),
-        in_specs=[anywhere] * 6,
-        out_specs=[vmem] * 5,
+        in_specs=[anywhere] * 7,
+        out_specs=[vmem] * 7,
         out_shape=[pltpu.VMEM((lines + 8, dim), jnp.float32)]
         + [pltpu.VMEM((lines + 8, dim), jnp.bfloat16)] * 3
-        + [pltpu.VMEM((tail_kv.shape[0] // 2, *tail_kv.shape[1:]), tail_kv.dtype)],
+        + [
+            pltpu.VMEM((own * 1 // 2, *tail_kv.shape[1:]), tail_kv.dtype),
+            pltpu.VMEM((own, new, heads, dim), queries.dtype),
+            pltpu.VMEM((own, new * heads, dim), jnp.int32),
+        ],
         scratch_shapes=[
             pltpu.SMEM(page_table.shape, jnp.int32),
             pltpu.SMEM(prompt_len.shape, jnp.int32),
@@ -217,40 +233,37 @@
             wide,
             wide,
             pltpu.VMEM((lines, dim), jnp.float32),
-            pltpu.SemaphoreType.DMA((6,)),
+            pltpu.SMEM(tail_len.shape, jnp.int32),
+            pltpu.SemaphoreType.DMA((7,)),
         ],
         compiler_params=pltpu.CompilerParams(vmem_limit_bytes=VMEM_LIMIT),
         name="prompt_attention",
-    )(*map(in_hbm, (page_table, prompt_len, sample_prompt, queries, prompt_kv, tail_kv)))
-
-
-def tail_kernel(scale, len_ref, q_ref, held_ref, kv_hbm, out_ref, kv_ref, best_ref, norm_ref, sems):
+    )(
+        *map(
+            in_hbm,
+            (page_table, prompt_len, sample_prompt, queries, prompt_kv, tail_kv, tail_len),
+        )
+    )
+
+
+def tail_kernel(scale, q_ref, len_ref, held_ref, kv_hbm, out_ref, kv_ref, column_ref, sem):
     held, length, heads, _ = held_ref.shape
-    own = held + kv_ref.shape[0]
-    new, dim = q_ref.shape[1], q_ref.shape[3]
+    own, new, _, dim = q_ref.shape
     lines, half = new * heads, length * heads // 2
-    steps = 2 * sems.shape[0]
-    per = own // steps
     bf16, f32 = jnp.bfloat16, jnp.float32
-    copies = start_copies(
-        [
-            pltpu.make_async_copy(
-                kv_hbm.at[pl.ds(held + i * per, per)], kv_ref.at[pl.ds(i * per, per)], sems.at[i]
-            )
-            for i in range(steps // 2)
-        ]
-    )
-    first = lax.axis_index("page") * own
+    copy = pltpu.make_async_copy(kv_hbm.at[pl.ds(held, own - held)], kv_ref, sem)
+    copy.start()
     row = lax.broadcasted_iota(jnp.int32, (2 * lines, half), 0)
     col = lax.broadcasted_iota(jnp.int32, (2 * lines, half), 1) + (row // lines) * half
     line = row % lines
     same_head = line % heads == col % heads
     ahead = jnp.where(same_head, col // heads - line // heads, length + new)
-    for step in range(steps):
-        if step >= steps // 2:
-            copies[step - steps // 2].wait()
+    lane = lax.broadcasted_iota(jnp.int32, (lines, dim), 1)
+    for part in (range(0, own // 2), range(own // 2, own)):
+        if part.stop > held:
+            copy.wait()
         scores, values = [], []
-        for i in range(step * per, (step + 1) * per):
+        for i in part:
             cache = flat_rows(held_ref[i] if i < held else kv_ref[i - held])
             keys = jnp.concatenate([cache[:half, :dim], cache[half:, :dim]], axis=1)
             values.append(jnp.concatenate([cache[:half, dim:], cache[half:, dim:]], axis=1))
@@ -266,7 +279,9 @@
             score = lax.dot_general(
                 query, keys, (((1,), (1,)), ((), ())), preferred_element_type=f32
             )
-            scores.append(jnp.where(ahead <= len_ref[first + i], score, NEGATIVE))
+            limit = jnp.concatenate([len_ref[i]] * 2, axis=0)
+            limit = jnp.concatenate([limit] * (half // dim), axis=1)
+            scores.append(jnp.where(ahead <= limit, score, NEGATIVE))
         bests = [jnp.max(score, axis=1, keepdims=True) for score in scores]
         bests = [jnp.maximum(best[:lines], best[lines:]) for best in bests]
         weights = [
@@ -274,39 +289,31 @@
             for score, best in zip(scores, bests)
         ]
         norms = [jnp.sum(weight, axis=1, keepdims=True) for weight in weights]
-        for i in range(per):
-            mixed = jnp.dot(weights[i].astype(bf16), values[i], preferred_element_type=f32)
-            at = pl.ds((step * per + i) * lines, lines)
+        for i, weight, value, best, norm in zip(part, weights, values, bests, norms):
+            mixed = jnp.dot(weight.astype(bf16), value, preferred_element_type=f32)
+            at = pl.ds(i * lines, lines)
             out_ref[at, :] = mixed[:lines, :dim] + mixed[lines:, dim:]
-            best_ref[at, :] = jnp.broadcast_to(bests[i], (lines, dim))
-            norm_ref[at, :] = jnp.broadcast_to(norms[i][:lines] + norms[i][lines:], (lines, dim))
+            column_ref[at, :] = jnp.where(lane == 0, best, norm[:lines] + norm[lines:])
     total = out_ref.shape[0] - 8
-    out_ref[total : total + 1, :] = best_ref[...].T[0:1]
-    out_ref[total + 1 : total + 2, :] = norm_ref[...].T[0:1]
-
-
-def tail_partial(queries, held_tail, tail_kv, tail_len):
-    _, new, heads, dim = queries.shape
-    own = tail_kv.shape[0]
+    out_ref[total : total + 2, :] = column_ref[...].T[0:2]
+
+
+def tail_partial(own_queries, own_lengths, held_tail, tail_kv):
+    own, new, heads, dim = own_queries.shape
     lines = own * new * heads
+    left = (own - held_tail.shape[0], *tail_kv.shape[1:])
+    vmem = pl.BlockSpec(memory_space=pltpu.VMEM)
     return pl.pallas_call(
         functools.partial(tail_kernel, math.log2(math.e) / math.sqrt(dim)),
-        grid=(1,),
-        in_specs=[
-            pl.BlockSpec(memory_space=pltpu.SMEM),
-            pl.BlockSpec((own, new, heads, dim), lambda i: (lax.axis_index("page"), 0, 0, 0)),
-            pl.BlockSpec(memory_space=pltpu.VMEM),
-            pl.BlockSpec(memory_space=pl.ANY),
-        ],
-        out_specs=pl.BlockSpec(memory_space=pltpu.VMEM),
+        in_specs=[vmem] * 3 + [pl.BlockSpec(memory_space=pl.ANY)],
+        out_specs=vmem,
         out_shape=pltpu.VMEM((lines + 8, dim), jnp.float32),
-        scratch_shapes=[pltpu.VMEM(held_tail.shape, tail_kv.dtype)]
-        + [pltpu.VMEM((lines, dim), jnp.float32)] * 2
-        + [pltpu.SemaphoreType.DMA((2,))],
+        scratch_shapes=[pltpu.VMEM(left, tail_kv.dtype)]
+        + [pltpu.VMEM((lines, dim), jnp.float32), pltpu.SemaphoreType.DMA],
         compiler_params=pltpu.CompilerParams(vmem_limit_bytes=VMEM_LIMIT),
         cost_estimate=FREE,
         name="tail_attention",
-    )(in_hbm(tail_len), in_hbm(queries), held_tail, in_hbm(tail_kv))
+    )(own_queries, own_lengths, held_tail, in_hbm(tail_kv))
 
 
 def merge_kernel(scale, *refs):
@@ -361,23 +368,35 @@
     return start_copies(copies)
 
 
-def hold_kernel(shards, after_ref, w_hbm, out_ref, sems):
-    for copy in shard_copies(w_hbm, out_ref, sems, shards, 1):
+def hold_kernel(plan, after_ref, *refs):
+    weights, held, sems = refs[: len(plan)], refs[len(plan) : -1], refs[-1]
+    copies = []
+    for w_hbm, out_ref, (first, shards) in zip(weights, held, plan):
+        own_sems = sems.at[pl.ds(first, len(shards))]
+        copies += shard_copies(w_hbm, out_ref, own_sems, shards, 1)
+    for copy in copies:
         copy.wait()
 
 
-def hold_columns(after, weights, shards, units):
-    depth = weights.shape[0]
-    return pl.pallas_call(
-        functools.partial(hold_kernel, shards),
-        in_specs=[pl.BlockSpec(memory_space=pltpu.VMEM), pl.BlockSpec(memory_space=pl.ANY)],
-        out_specs=pl.BlockSpec(memory_space=pltpu.VMEM),
-        out_shape=pltpu.VMEM((len(shards), depth, units), weights.dtype),
-        scratch_shapes=[pltpu.SemaphoreType.DMA((len(shards),))],
+def hold_columns(after, wanted):
+    plan, total = [], 0
+    for _, shards, _ in wanted:
+        plan.append((total, shards))
+        total += len(shards)
+    vmem = pl.BlockSpec(memory_space=pltpu.VMEM)
+    return pl.pallas_call(
+        functools.partial(hold_kernel, tuple(plan)),
+        in_specs=[vmem] + [pl.BlockSpec(memory_space=pl.ANY)] * len(wanted),
+        out_specs=[vmem] * len(wanted),
+        out_shape=[
+            pltpu.VMEM((len(shards), weight.shape[0], units), weight.dtype)
+            for weight, shards, units in wanted
+        ],
+        scratch_shapes=[pltpu.SemaphoreType.DMA((total,))],
         compiler_params=pltpu.CompilerParams(vmem_limit_bytes=VMEM_LIMIT),
         cost_estimate=FREE,
         name="hold_columns",
-    )(after, in_hbm(weights))
+    )(after, *[in_hbm(weight) for weight, _, _ in wanted])
 
 
 def project_kernel(per_group, *refs):
@@ -496,7 +515,7 @@
     blocks, refs = refs[:8], refs[8:]
     gain_ref, bias_ref, down_ref, far_ref, near_ref = refs[:5]
     out_refs, weight_ref, refs = refs[5:10], refs[10], refs[11:]
-    lhs_ref, residual_ref, stats_ref, mean_ref, square_ref, base_ref, weights_ref = refs
+    lhs_ref, residual_ref, stats_ref, column_ref, weights_ref = refs
     blk_pos = lax.axis_index("blk")
     core, chip = blk_pos % 2, blk_pos // 2
     height, group = blocks[0].shape[0], lhs_ref.shape[1]
@@ -514,6 +533,7 @@
     score_row = jnp.concatenate(own_weights, axis=1)
     own_weight = sum(own_weights)
     fixed = jnp.sum(as_row(down_ref) * own_weight, axis=1, keepdims=True)
+    lane = lax.broadcasted_iota(jnp.int32, (height, rows), 1)
     for block, at in zip(blocks, places):
         residual = block[:, :group].astype(jnp.float32)
         mean = jnp.sum(residual, axis=1, keepdims=True) * (1.0 / group)
@@ -522,17 +542,16 @@
         base = jnp.sum(residual * score_row, axis=1, keepdims=True) + fixed
         residual_ref[at, :] = block[:, :group]
         lhs_ref[at, :] = (centred * gain).astype(lhs_ref.dtype)
-        mean_ref[at, :] = jnp.broadcast_to(mean, (height, rows))
-        square_ref[at, :] = jnp.broadcast_to(square, (height, rows))
-        base_ref[at, :] = jnp.broadcast_to(base, (height, rows))
+        column_ref[at, :] = jnp.where(lane == 0, mean, jnp.where(lane == 1, square, base))
     row = lax.broadcasted_iota(jnp.int32, (lhs_ref.shape[0] - rows, group), 0)
     bias = as_row(bias_ref)
     lhs_ref[rows:, :] = jnp.where(
         row == 0, gain, jnp.where(row == 1, bias, 0.0)
     ).astype(lhs_ref.dtype)
+    columns = column_ref[...].T
     pieces = []
-    for ref in (mean_ref, square_ref, base_ref):
-        pieces += split2(ref[...].T[0:1])
+    for i in range(3):
+        pieces += split2(columns[i : i + 1])
     stats_ref[...] = jnp.concatenate(pieces, axis=0)
     for i, (top_ref, bottom_ref) in enumerate((out_refs[0:2], out_refs[2:4])):
         part = up_product(lhs_ref, far_ref.at[i], stats_ref, rows)
@@ -575,7 +594,7 @@
             jax.ShapeDtypeStruct((rows, group), bf16),
             pltpu.VMEM((6, rows), bf16),
         ],
-        scratch_shapes=[pltpu.VMEM((rows, rows), f32)] * 3
+        scratch_shapes=[pltpu.VMEM((rows, rows), f32)]
         + [
             pltpu.VMEM((8, blocks[0].shape[1] - group), f32),
         ],
@@ -917,23 +936,23 @@
     group = ln_gain.shape[0]
     blk_pos = lax.axis_index("blk")
     piece = b_down.shape[0]
-    *packed, held_tail = prompt_partial(
-        queries, prompt_kv, tail_kv, page_table, prompt_len, sample_prompt
+    *packed, held_tail, own_queries, own_lengths = prompt_partial(
+        queries, prompt_kv, tail_kv, page_table, prompt_len, sample_prompt, tail_len
     )
     sent = {k: send_xor(packed[k], "page", k) for k in (2, 3, 1)}
     shares = [packed[0], sent[1], sent[2], sent[3]]
-    tail = tail_partial(queries, held_tail, tail_kv, tail_len)
+    tail = tail_partial(own_queries, own_lengths, held_tail, tail_kv)
     own_attention = merge_partials(shares + [tail], heads_dev)
     sent = {k: send_xor(own_attention, "page", k) for k in (2, 1, 3)}
     attention = [own_attention, sent[1], sent[2], sent[3]]
-    held_out = hold_columns(own_attention, w_out, (0,), group)
-    near_up = hold_columns(own_attention, w_up, (1,), w_up.shape[1] // 4)
-    held_out, near_up = lax.optimization_barrier((held_out, near_up))
+    units = w_up.shape[1] // 4
+    held_out, near_up = hold_columns(
+        own_attention, ((w_out, (0,), group), (w_up, (1,), units))
+    )
     keep, give = project(attention, held_out, stream_in, group)
     own, *pieces = pair_pieces(keep, send_xor(give, "blk", 1))
-    units = w_up.shape[1] // 4
     arrived = [send_xor(pieces[k - 1], "blk", 2 * k) for k in (3, 2, 1)]
-    held_up = hold_columns(own, w_up, (3, 2), units)
+    (held_up,) = hold_columns(own, ((w_up, (3, 2), units),))
     own, held_up = lax.optimization_barrier((own, held_up))
     own_rows = residual_rows(own, arrived, b_out, w_score)
     same_core = gather_xor(own_rows, "blk", (2, 4, 6))

time: 96.7 us -> 95.9 us (level)
  Pallas kernels: 36 us -> 33.7 us
  waiting for transfers between devices: 28.6 us -> 30.3 us
    ppermute x29, waiting for transfers between devices: 28.6 us -> 30.3 us  [send_xor(): return lax.ppermute(value, axis, [(i, i ^ distance) for i in range(size)])]
    pallas_call x1, Pallas kernels: 4.6 us -> 3.18 us  [tail_partial(): pl.pallas_call(functools.partial(tail_kernel, math.log2(math.e) / math.sq...]
    pallas_call x3 -> x2, Pallas kernels: 6.44 us -> 5.44 us  [hold_columns(): pl.pallas_call(functools.partial(hold_kernel, tuple(plan)), in_specs=[vme...]
  transfers between devices with their start and end apart: 29 -> 29, of which waited for: 20 -> 20; matrix products, arithmetic and copies ran while one was open for 0% -> 0% of each run, Pallas kernels for 28% -> 25%
where the time goes in v5:
time: 95.9 us; the launch traced here: 95.7 us
  Pallas kernels  33.7 us (35%)
  starting transfers between devices  30.6 us (32%)
  waiting for transfers between devices  30.3 us (32%)
    ppermute x29, starting transfers between devices, send_xor(): return lax.ppermute(value, axis, [(i, i ^ distance) for i in range(size)])  30.6 us
    ppermute x29, waiting for transfers between devices, send_xor(): return lax.ppermute(value, axis, [(i, i ^ distance) for i in range(size)])  30.3 us
    pallas_call x2, Pallas kernels, image_of(): pl.pallas_call(functools.partial(image_kernel, first), in_specs=[vmem, pl...  7.21 us
    pallas_call x2, Pallas kernels, hold_columns(): pl.pallas_call(functools.partial(hold_kernel, tuple(plan)), in_specs=[vme...  5.44 us
    pallas_call x1, Pallas kernels, down_first(): pl.pallas_call(down_first_kernel, in_specs=[vmem, pl.BlockSpec(memory_spa...  4.76 us
    pallas_call x1, Pallas kernels, prompt_partial(): pl.pallas_call(functools.partial(prompt_kernel, math.log2(math.e) / math....  3.29 us
    pallas_call x1, Pallas kernels, tail_partial(): pl.pallas_call(functools.partial(tail_kernel, math.log2(math.e) / math.sq...  3.18 us
    pallas_call x1, Pallas kernels, up_own(): pl.pallas_call(up_own_kernel, in_specs=[vmem] * 2 + [pl.BlockSpec(memory_...  2.65 us
  transfers between devices with their start and end apart: 29, of which 20 were waited for; matrix products, arithmetic and copies ran while one was open for 0% of the time, Pallas kernels for 25%

profile of v5, /device:TPU:0, one launch (start us, length us, event | category | flops | bytes accessed | tf_op | source)
XLA Modules:
  0.0 95.7 jit_solution(4439655930615097763)
XLA Ops:
  0.6 3.3 %prompt_attention.1 = (f32[136,128]{1,0:T(8,128)S(1)}, bf16[136,128]{1,0:T(8,128)(2,1)S(1)}, bf16[136,128]{1,0:T(8,128)(2,1)S(1)}, bf16[136,128]{1,0:T(8,128)(2,...) custom-call(s32[4,16]{1,0:T(4,128)} %table_hbm.1, ...), custom_call_target="tpu_custom_call" | custom-call | tf_op jit(solution)/shard_map/prompt_attention/pallas_call | solution.py:208
  3.9 3.1 %collective-permute-start = (bf16[136,128]{1,0:T(8,128)(2,1)S(1)}, bf16[136,128]{1,0:T(8,128)(2,1)S(1)}, u32[]{:S(2)}, u32[]{:S(2)}) collective-permute-start(bf16[136,128]{1,0:T(8,128)(2,1)S(1)} %get-tuple-element.51), channel_id=1, source_target_pairs={{0,8},{8,0},{16,24},{24,16},{1,9},{9,1},{17,25},{25,17},{2,10},{10... | collective-permute-start | bytes 104456 | tf_op jit(solution)/shard_map/ppermute | solution.py:46
  7.0 2.6 %collective-permute-start.1 = (bf16[136,128]{1,0:T(8,128)(2,1)S(1)}, bf16[136,128]{1,0:T(8,128)(2,1)S(1)}, u32[]{:S(2)}, u32[]{:S(2)}) collective-permute-start(bf16[136,128]{1,0:T(8,128)(2,1)S(1)} %get-tuple-element.52), channel_id=1, source_target_pairs={{0,16},{8,24},{16,0},{24,8},{1,17},{9,25},{17,1},{25,9},{2,18},{10... | collective-permute-start | bytes 104456 | tf_op jit(solution)/shard_map/ppermute | solution.py:46
  9.6 3.2 %tail_attention.1.refs_4_ = f32[136,128]{1,0:T(8,128)S(1)} custom-call(bf16[16,2,4,128]{3,2,1,0:T(4,128)(2,1)S(1)} %get-tuple-element.54.q_ref, s32[16,8,128]{2,1,0:T(8,128)S(1)} %get-tuple-element.55.len_ref, bf16[8,256,4,256]{3,2,1,0:T(4,128)(2,1)S(1)} %get-tuple-element.56.held_ref, bf16[16,256,4,256]{3,2,1,0:T(4,128)(2,1)} %kv_hbm.3), custom_call_target="tpu_custom_call" | custom-call | tf_op jit(solution)/shard_map/tail_attention/pallas_call | solution.py:306
  12.8 2.6 %collective-permute-done.2.refs_3_ = bf16[136,128]{1,0:T(8,128)(2,1)S(1)} collective-permute-done((bf16[136,128]{1,0:T(8,128)(2,1)S(1)}, bf16[136,128]{1,0:T(8,128)(2,1)S(1)}, u32[]{:S(2)}, u32[]{:S(2)}) %collective-permute-start.2) | collective-permute-done | bytes 34848 | tf_op jit(solution)/shard_map/ppermute | solution.py:46
  15.6 1.3 %collective-permute-start.5 = (bf16[32,512]{1,0:T(8,128)(2,1)S(1)}, bf16[32,512]{1,0:T(8,128)(2,1)S(1)}, u32[]{:S(2)}, u32[]{:S(2)}) collective-permute-start(bf16[32,512]{1,0:T(8,128)(2,1)S(1)} %merge_partials.1.after_ref.refs_0_), channel_id=1, source_target_pairs={{0,24},{8,16},{16,8},{24,0},{1,25},{9,17},{17,9},{25,1},{2,26},{10... | collective-permute-start | bytes 98312 | tf_op jit(solution)/shard_map/ppermute | solution.py:46
  16.9 3.1 %collective-permute-start.3 = (bf16[32,512]{1,0:T(8,128)(2,1)S(1)}, bf16[32,512]{1,0:T(8,128)(2,1)S(1)}, u32[]{:S(2)}, u32[]{:S(2)}) collective-permute-start(bf16[32,512]{1,0:T(8,128)(2,1)S(1)} %merge_partials.1.after_ref.refs_0_), channel_id=1, source_target_pairs={{0,8},{8,0},{16,24},{24,16},{1,9},{9,1},{17,25},{25,17},{2,10},{10... | collective-permute-start | bytes 98312 | tf_op jit(solution)/shard_map/ppermute | solution.py:46
  20.1 2.5 %hold_columns.2 = (bf16[1,512,1792]{2,1,0:T(8,128)(2,1)S(1)}, bf16[1,1792,896]{2,1,0:T(8,128)(2,1)S(1)}) custom-call(bf16[32,512]{1,0:T(8,128)(2,1)S(1)} %merge_partials.1.after_ref.refs_0_, bf16[512,7168]{1,0:T(8,128)(2,1)} %refs_0_.2, bf16[1792,3584]{1,0:T(8,128)(2,1)} %w_hbm.4), custom_call_target="tpu_custom_call" | custom-call | tf_op jit(solution)/shard_map/hold_columns/pallas_call | solution.py:387
  23.4 1.5 %collective-permute-done.6.got_ref = bf16[4,16,1792]{2,1,0:T(8,128)(2,1)S(1)} collective-permute-done((bf16[4,16,1792]{2,1,0:T(8,128)(2,1)S(1)}, bf16[4,16,1792]{2,1,0:T(8,128)(2,1)S(1)}, u32[]{:S(2)}, u32[]{:S(2)}) %collective-permute-start.6) | collective-permute-done | bytes 229408 | tf_op jit(solution)/shard_map/ppermute | solution.py:46
  24.9 2.4 %collective-permute-start.7 = (bf16[16,1792]{1,0:T(8,128)(2,1)S(1)}, bf16[16,1792]{1,0:T(8,128)(2,1)S(1)}, u32[]{:S(2)}, u32[]{:S(2)}) collective-permute-start(bf16[16,1792]{1,0:T(8,128)(2,1)S(1)} %get-tuple-element.62), channel_id=1, source_target_pairs={{0,6},{1,7},{2,4},{3,5},{4,2},{5,3},{6,0},{7,1},{8,14},{9,15},{10,... | collective-permute-start | bytes 172040 | tf_op jit(solution)/shard_map/ppermute | solution.py:46
  28.5 3.0 %hold_columns.3.refs_11_ = bf16[2,1792,896]{2,1,0:T(8,128)(2,1)S(1)} custom-call(f32[16,1792]{1,0:T(8,128)S(1)} %get-tuple-element.61.after_ref.own_ref, bf16[1792,3584]{1,0:T(8,128)(2,1)} %w_hbm.4), custom_call_target="tpu_custom_call" | custom-call | tf_op jit(solution)/shard_map/hold_columns/pallas_call | solution.py:387
  32.1 1.9 %collective-permute-start.12 = (bf16[16,2048]{1,0:T(8,128)(2,1)S(1)}, bf16[16,2048]{1,0:T(8,128)(2,1)S(1)}, u32[]{:S(2)}, u32[]{:S(2)}) collective-permute-start(bf16[16,2048]{1,0:T(8,128)(2,1)S(1)} %residual_rows.1.refs_0_), channel_id=1, source_target_pairs={{0,6},{1,7},{2,4},{3,5},{4,2},{5,3},{6,0},{7,1},{8,14},{9,15},{10,... | collective-permute-start | bytes 196616 | tf_op jit(solution)/shard_map/ppermute | solution.py:46
  34.5 1.1 %collective-permute-start.10 = (bf16[16,2048]{1,0:T(8,128)(2,1)S(1)}, bf16[16,2048]{1,0:T(8,128)(2,1)S(1)}, u32[]{:S(2)}, u32[]{:S(2)}) collective-permute-start(bf16[16,2048]{1,0:T(8,128)(2,1)S(1)} %residual_rows.1.refs_0_), channel_id=1, source_target_pairs={{0,2},{1,3},{2,0},{3,1},{4,6},{5,7},{6,4},{7,5},{8,10},{9,11},{10,... | collective-permute-start | bytes 196616 | tf_op jit(solution)/shard_map/ppermute | solution.py:46
  35.7 2.2 %collective-permute-done.12.refs_3_ = bf16[16,2048]{1,0:T(8,128)(2,1)S(1)} collective-permute-done((bf16[16,2048]{1,0:T(8,128)(2,1)S(1)}, bf16[16,2048]{1,0:T(8,128)(2,1)S(1)}, u32[]{:S(2)}, u32[]{:S(2)}) %collective-permute-start.12) | collective-permute-done | bytes 65568 | tf_op jit(solution)/shard_map/ppermute | solution.py:46
  40.1 2.2 %norm_and_up.1 = (bf16[64,896]{1,0:T(8,128)(2,1)S(1)}, bf16[72,896]{1,0:T(8,128)(2,1)S(1)}, bf16[64,896]{1,0:T(8,128)(2,1)S(1)}, bf16[72,896]{1,0:T(8,128)(2,1)S...) custom-call(bf16[16,2048]{1,0:T(8,128)(2,1)S(1)} %residual_rows.1.re, ...), custom_call_target="tpu_custom_call" | custom-call | tf_op jit(solution)/shard_map/norm_and_up/pallas_call | solution.py:585
  42.3 1.5 %collective-permute-start.18 = (bf16[136,896]{1,0:T(8,128)(2,1)S(1)}, bf16[136,896]{1,0:T(8,128)(2,1)S(1)}, u32[]{:S(2)}, u32[]{:S(2)}) collective-permute-start(bf16[136,896]{1,0:T(8,128)(2,1)S(1)} %get-tuple-element.72), channel_id=1, source_target_pairs={{0,8},{8,0},{16,24},{24,16},{1,9},{9,1},{17,25},{25,17},{2,10},{10... | collective-permute-start | bytes 731144 | tf_op jit(solution)/shard_map/ppermute | solution.py:46
  44.4 1.2 %collective-permute-start.20 = (bf16[72,896]{1,0:T(8,128)(2,1)S(1)}, bf16[72,896]{1,0:T(8,128)(2,1)S(1)}, u32[]{:S(2)}, u32[]{:S(2)}) collective-permute-start(bf16[72,896]{1,0:T(8,128)(2,1)S(1)} %get-tuple-element.76), channel_id=1, source_target_pairs={{0,16},{8,24},{16,0},{24,8},{1,17},{9,25},{17,1},{25,9},{2,18},{10... | collective-permute-start | bytes 387080 | tf_op jit(solution)/shard_map/ppermute | solution.py:46
  45.6 2.6 %collective-permute-start.21 = (bf16[72,896]{1,0:T(8,128)(2,1)S(1)}, bf16[72,896]{1,0:T(8,128)(2,1)S(1)}, u32[]{:S(2)}, u32[]{:S(2)}) collective-permute-start(bf16[72,896]{1,0:T(8,128)(2,1)S(1)} %get-tuple-element.77), channel_id=1, source_target_pairs={{0,24},{8,16},{16,8},{24,0},{1,25},{9,17},{17,9},{25,1},{2,26},{10... | collective-permute-start | bytes 387080 | tf_op jit(solution)/shard_map/ppermute | solution.py:46
  48.2 3.6 %score_image.2.refs_6_ = f32[4,896]{1,0:T(4,128)S(1)} custom-call(f32[1,1792]{1,0:T(1,128)S(1)} %get-tuple-element.79.score_ref, bf16[3584,1792]{1,0:T(8,128)(2,1)} %w_hbm.7), custom_call_target="tpu_custom_call" | custom-call | tf_op jit(solution)/shard_map/score_image/pallas_call | solution.py:682
  51.8 2.6 %up_own.1.refs_0_ = bf16[136,896]{1,0:T(8,128)(2,1)S(1)} custom-call(bf16[144,1792]{1,0:T(8,128)(2,1)S(1)} %get-tuple-element.68.lhs_ref, bf16[6,128]{1,0:T(8,128)(2,1)S(1)} %get-tuple-element.69.stats_ref, bf16[1792,3584]{1,0:T(8,128)(2,1)} %w_hbm.4), custom_call_target="tpu_custom_call" | custom-call | tf_op jit(solution)/shard_map/up_own/pallas_call | solution.py:624
  54.5 1.2 %collective-permute-done.17.b_ref = bf16[64,896]{1,0:T(8,128)(2,1)S(1)} collective-permute-done((bf16[64,896]{1,0:T(8,128)(2,1)S(1)}, bf16[64,896]{1,0:T(8,128)(2,1)S(1)}, u32[]{:S(2)}, u32[]{:S(2)}) %collective-permute-start.17) | collective-permute-done | bytes 114720 | tf_op jit(solution)/shard_map/ppermute | solution.py:46
  55.8 3.6 %score_image.3.refs_7_ = f32[4,896]{1,0:T(4,128)S(1)} custom-call(f32[1,1792]{1,0:T(1,128)S(1)} %get-tuple-element.79.score_ref, bf16[3584,1792]{1,0:T(8,128)(2,1)} %w_hbm.7), custom_call_target="tpu_custom_call" | custom-call | tf_op jit(solution)/shard_map/score_image/pallas_call | solution.py:682
  59.8 4.0 %collective-permute-done.19.refs_2_ = bf16[64,896]{1,0:T(8,128)(2,1)S(1)} collective-permute-done((bf16[64,896]{1,0:T(8,128)(2,1)S(1)}, bf16[64,896]{1,0:T(8,128)(2,1)S(1)}, u32[]{:S(2)}, u32[]{:S(2)}) %collective-permute-start.19) | collective-permute-done | bytes 114720 | tf_op jit(solution)/shard_map/ppermute | solution.py:46
  64.4 3.2 %collective-permute-start.22 = (bf16[136,896]{1,0:T(8,128)(2,1)S(1)}, bf16[136,896]{1,0:T(8,128)(2,1)S(1)}, u32[]{:S(2)}, u32[]{:S(2)}) collective-permute-start(bf16[136,896]{1,0:T(8,128)(2,1)S(1)} %get-tuple-element.81.hidden_ref.refs_0_), channel_id=1, source_target_pairs={{0,16},{8,24},{16,0},{24,8},{1,17},{9,25},{17,1},{25,9},{2,18},{10... | collective-permute-start | bytes 731144 | tf_op jit(solution)/shard_map/ppermute | solution.py:46
  67.5 4.8 %down_own.1 = (f32[128,1792]{1,0:T(8,128)S(1)}, bf16[3,896,1792]{2,1,0:T(8,128)(2,1)S(1)}) custom-call(bf16[136,896]{1,0:T(8,128)(2,1)S(1)} %get-tuple-element.81.hidden_ref.refs_0_, bf16[3584,1792]{1,0:T(8,128)(2,1)} %w_hbm.7), custom_call_target="tpu_custom_call" | custom-call | tf_op jit(solution)/shard_map/down_own/pallas_call | solution.py:759
  72.3 4.9 %collective-permute-done.23.near_ref.refs_1_ = bf16[136,896]{1,0:T(8,128)(2,1)S(1)} collective-permute-done((bf16[136,896]{1,0:T(8,128)(2,1)S(1)}, bf16[136,896]{1,0:T(8,128)(2,1)S(1)}, u32[]{:S(2)}, u32[]{:S(2)}) %collective-permute-start.23) | collective-permute-done | bytes 243744 | tf_op jit(solution)/shard_map/ppermute | solution.py:46
  77.2 1.4 %collective-permute-done.22.far_ref.refs_2_ = bf16[136,896]{1,0:T(8,128)(2,1)S(1)} collective-permute-done((bf16[136,896]{1,0:T(8,128)(2,1)S(1)}, bf16[136,896]{1,0:T(8,128)(2,1)S(1)}, u32[]{:S(2)}, u32[]{:S(2)}) %collective-permute-start.22) | collective-permute-done | bytes 243744 | tf_op jit(solution)/shard_map/ppermute | solution.py:46
  80.1 4.7 %collective-permute-done.24.refs_3_ = bf16[136,896]{1,0:T(8,128)(2,1)S(1)} collective-permute-done((bf16[136,896]{1,0:T(8,128)(2,1)S(1)}, bf16[136,896]{1,0:T(8,128)(2,1)S(1)}, u32[]{:S(2)}, u32[]{:S(2)}) %collective-permute-start.24) | collective-permute-done | bytes 243744 | tf_op jit(solution)/shard_map/ppermute | solution.py:46
  86.0 1.5 %collective-permute-done.25.got_ref = bf16[4,128,227]{2,1,0:T(8,128)(2,1)S(1)} collective-permute-done((bf16[4,128,227]{2,1,0:T(8,128)(2,1)S(1)}, bf16[4,128,227]{2,1,0:T(8,128)(2,1)S(1)}, u32[]{:S(2)}, u32[]{:S(2)}) %collective-permute-start.25) | collective-permute-done | bytes 232480 | tf_op jit(solution)/shard_map/ppermute | solution.py:46
  87.7 2.1 %collective-permute-start.26 = (bf16[128,227]{1,0:T(8,128)(2,1)S(1)}, bf16[128,227]{1,0:T(8,128)(2,1)S(1)}, u32[]{:S(2)}, u32[]{:S(2)}) collective-permute-start(bf16[128,227]{1,0:T(8,128)(2,1)S(1)} %get-tuple-element.93), channel_id=1, source_target_pairs={{0,6},{1,7},{2,4},{3,5},{4,2},{5,3},{6,0},{7,1},{8,14},{9,15},{10,... | collective-permute-start | bytes 174344 | tf_op jit(solution)/shard_map/ppermute | solution.py:46
  91.4 1.7 %collective-permute-done.26.c_ref = bf16[128,227]{1,0:T(8,128)(2,1)S(1)} collective-permute-done((bf16[128,227]{1,0:T(8,128)(2,1)S(1)}, bf16[128,227]{1,0:T(8,128)(2,1)S(1)}, u32[]{:S(2)}, u32[]{:S(2)}) %collective-permute-start.26) | collective-permute-done | bytes 58144 | tf_op jit(solution)/shard_map/ppermute | solution.py:46
  93.1 1.3 %collective-permute-done.27.b_ref = bf16[128,227]{1,0:T(8,128)(2,1)S(1)} collective-permute-done((bf16[128,227]{1,0:T(8,128)(2,1)S(1)}, bf16[128,227]{1,0:T(8,128)(2,1)S(1)}, u32[]{:S(2)}, u32[]{:S(2)}) %collective-permute-start.27) | collective-permute-done | bytes 58144 | tf_op jit(solution)/shard_map/ppermute | solution.py:46
  (61 shorter events, 12.8 us)
Async XLA Ops:
  3.9 8.9 %collective-permute-start = (bf16[136,128]{1,0:T(8,128)(2,1)S(1)}, bf16[136,128]{1,0:T(8,128)(2,1)S(1)}, u32[]{:S(2)}, u32[]{:S(2)}) collective-permute-start(bf16[136,128]{1,0:T(8,128)(2,1)S(1)} %get-tuple-element.51), channel_id=1, source_target_pairs={{0,8},{8,0},{16,24},{24,16},{1,9},{9,1},{17,25},{25,17},{2,10},{10... | collective-permute-start | bytes 104456 | tf_op jit(solution)/shard_map/ppermute | solution.py:46
  7.0 5.8 %collective-permute-start.1 = (bf16[136,128]{1,0:T(8,128)(2,1)S(1)}, bf16[136,128]{1,0:T(8,128)(2,1)S(1)}, u32[]{:S(2)}, u32[]{:S(2)}) collective-permute-start(bf16[136,128]{1,0:T(8,128)(2,1)S(1)} %get-tuple-element.52), channel_id=1, source_target_pairs={{0,16},{8,24},{16,0},{24,8},{1,17},{9,25},{17,1},{25,9},{2,18},{10... | collective-permute-start | bytes 104456 | tf_op jit(solution)/shard_map/ppermute | solution.py:46
  9.6 5.8 %collective-permute-start.2 = (bf16[136,128]{1,0:T(8,128)(2,1)S(1)}, bf16[136,128]{1,0:T(8,128)(2,1)S(1)}, u32[]{:S(2)}, u32[]{:S(2)}) collective-permute-start(bf16[136,128]{1,0:T(8,128)(2,1)S(1)} %get-tuple-element.53), channel_id=1, source_target_pairs={{0,24},{8,16},{16,8},{24,0},{1,25},{9,17},{17,9},{25,1},{2,26},{10... | collective-permute-start | bytes 104456 | tf_op jit(solution)/shard_map/ppermute | solution.py:46
  15.6 6.9 %collective-permute-start.5 = (bf16[32,512]{1,0:T(8,128)(2,1)S(1)}, bf16[32,512]{1,0:T(8,128)(2,1)S(1)}, u32[]{:S(2)}, u32[]{:S(2)}) collective-permute-start(bf16[32,512]{1,0:T(8,128)(2,1)S(1)} %merge_partials.1.after_ref.refs_0_), channel_id=1, source_target_pairs={{0,24},{8,16},{16,8},{24,0},{1,25},{9,17},{17,9},{25,1},{2,26},{10... | collective-permute-start | bytes 98312 | tf_op jit(solution)/shard_map/ppermute | solution.py:46
  16.9 5.6 %collective-permute-start.4 = (bf16[32,512]{1,0:T(8,128)(2,1)S(1)}, bf16[32,512]{1,0:T(8,128)(2,1)S(1)}, u32[]{:S(2)}, u32[]{:S(2)}) collective-permute-start(bf16[32,512]{1,0:T(8,128)(2,1)S(1)} %merge_partials.1.after_ref.refs_0_), channel_id=1, source_target_pairs={{0,16},{8,24},{16,0},{24,8},{1,17},{9,25},{17,1},{25,9},{2,18},{10... | collective-permute-start | bytes 98312 | tf_op jit(solution)/shard_map/ppermute | solution.py:46
  16.9 5.6 %collective-permute-start.3 = (bf16[32,512]{1,0:T(8,128)(2,1)S(1)}, bf16[32,512]{1,0:T(8,128)(2,1)S(1)}, u32[]{:S(2)}, u32[]{:S(2)}) collective-permute-start(bf16[32,512]{1,0:T(8,128)(2,1)S(1)} %merge_partials.1.after_ref.refs_0_), channel_id=1, source_target_pairs={{0,8},{8,0},{16,24},{24,16},{1,9},{9,1},{17,25},{25,17},{2,10},{10... | collective-permute-start | bytes 98312 | tf_op jit(solution)/shard_map/ppermute | solution.py:46
  23.3 1.6 %collective-permute-start.6 = (bf16[4,16,1792]{2,1,0:T(8,128)(2,1)S(1)}, bf16[4,16,1792]{2,1,0:T(8,128)(2,1)S(1)}, u32[]{:S(2)}, u32[]{:S(2)}) collective-permute-start(bf16[4,16,1792]{2,1,0:T(8,128)(2,1)S(1)} %get-tuple-element.59), channel_id=1, source_target_pairs={{0,1},{1,0},{2,3},{3,2},{4,5},{5,4},{6,7},{7,6},{8,9},{9,8},{10,11... | collective-permute-start | bytes 688136 | tf_op jit(solution)/shard_map/ppermute | solution.py:46
  24.9 6.5 %collective-permute-start.7 = (bf16[16,1792]{1,0:T(8,128)(2,1)S(1)}, bf16[16,1792]{1,0:T(8,128)(2,1)S(1)}, u32[]{:S(2)}, u32[]{:S(2)}) collective-permute-start(bf16[16,1792]{1,0:T(8,128)(2,1)S(1)} %get-tuple-element.62), channel_id=1, source_target_pairs={{0,6},{1,7},{2,4},{3,5},{4,2},{5,3},{6,0},{7,1},{8,14},{9,15},{10,... | collective-permute-start | bytes 172040 | tf_op jit(solution)/shard_map/ppermute | solution.py:46
  27.4 4.2 %collective-permute-start.8 = (bf16[16,1792]{1,0:T(8,128)(2,1)S(1)}, bf16[16,1792]{1,0:T(8,128)(2,1)S(1)}, u32[]{:S(2)}, u32[]{:S(2)}) collective-permute-start(bf16[16,1792]{1,0:T(8,128)(2,1)S(1)} %get-tuple-element.63), channel_id=1, source_target_pairs={{0,4},{1,5},{2,6},{3,7},{4,0},{5,1},{6,2},{7,3},{8,12},{9,13},{10,... | collective-permute-start | bytes 172040 | tf_op jit(solution)/shard_map/ppermute | solution.py:46
  27.9 4.2 %collective-permute-start.9 = (bf16[16,1792]{1,0:T(8,128)(2,1)S(1)}, bf16[16,1792]{1,0:T(8,128)(2,1)S(1)}, u32[]{:S(2)}, u32[]{:S(2)}) collective-permute-start(bf16[16,1792]{1,0:T(8,128)(2,1)S(1)} %get-tuple-element.64), channel_id=1, source_target_pairs={{0,2},{1,3},{2,0},{3,1},{4,6},{5,7},{6,4},{7,5},{8,10},{9,11},{10,... | collective-permute-start | bytes 172040 | tf_op jit(solution)/shard_map/ppermute | solution.py:46
  28.5 11.6 %copy-start.3 = (bf16[1792]{0:T(1024)(128)(2,1)S(1)}, bf16[1792]{0:T(1024)(128)(2,1)}, u32[]{:S(2)}) copy-start(bf16[1792]{0:T(1024)(128)(2,1)} %refs_8_.1) | copy-start | bytes 10756
  28.5 11.6 %copy-start.4 = (bf16[1792]{0:T(1024)(128)(2,1)S(1)}, bf16[1792]{0:T(1024)(128)(2,1)}, u32[]{:S(2)}) copy-start(bf16[1792]{0:T(1024)(128)(2,1)} %refs_9_.1) | copy-start | bytes 10756
  28.5 11.6 %copy-start.6 = (bf16[224]{0:T(256)(128)(2,1)S(1)}, bf16[224]{0:T(256)(128)(2,1)}, u32[]{:S(2)}) copy-start(bf16[224]{0:T(256)(128)(2,1)} %refs_10_.1) | copy-start | bytes 1348
  32.1 5.8 %collective-permute-start.12 = (bf16[16,2048]{1,0:T(8,128)(2,1)S(1)}, bf16[16,2048]{1,0:T(8,128)(2,1)S(1)}, u32[]{:S(2)}, u32[]{:S(2)}) collective-permute-start(bf16[16,2048]{1,0:T(8,128)(2,1)S(1)} %residual_rows.1.refs_0_), channel_id=1, source_target_pairs={{0,6},{1,7},{2,4},{3,5},{4,2},{5,3},{6,0},{7,1},{8,14},{9,15},{10,... | collective-permute-start | bytes 196616 | tf_op jit(solution)/shard_map/ppermute | solution.py:46
  34.0 4.4 %collective-permute-start.11 = (bf16[16,2048]{1,0:T(8,128)(2,1)S(1)}, bf16[16,2048]{1,0:T(8,128)(2,1)S(1)}, u32[]{:S(2)}, u32[]{:S(2)}) collective-permute-start(bf16[16,2048]{1,0:T(8,128)(2,1)S(1)} %residual_rows.1.refs_0_), channel_id=1, source_target_pairs={{0,4},{1,5},{2,6},{3,7},{4,0},{5,1},{6,2},{7,3},{8,12},{9,13},{10,... | collective-permute-start | bytes 196616 | tf_op jit(solution)/shard_map/ppermute | solution.py:46
  34.5 4.3 %collective-permute-start.10 = (bf16[16,2048]{1,0:T(8,128)(2,1)S(1)}, bf16[16,2048]{1,0:T(8,128)(2,1)S(1)}, u32[]{:S(2)}, u32[]{:S(2)}) collective-permute-start(bf16[16,2048]{1,0:T(8,128)(2,1)S(1)} %residual_rows.1.refs_0_), channel_id=1, source_target_pairs={{0,2},{1,3},{2,0},{3,1},{4,6},{5,7},{6,4},{7,5},{8,10},{9,11},{10,... | collective-permute-start | bytes 196616 | tf_op jit(solution)/shard_map/ppermute | solution.py:46
  35.7 3.3 %collective-permute-start.13 = (bf16[16,2048]{1,0:T(8,128)(2,1)S(1)}, bf16[16,2048]{1,0:T(8,128)(2,1)S(1)}, u32[]{:S(2)}, u32[]{:S(2)}) collective-permute-start(bf16[16,2048]{1,0:T(8,128)(2,1)S(1)} %residual_rows.1.refs_0_), channel_id=1, source_target_pairs={{0,1},{1,0},{2,3},{3,2},{4,5},{5,4},{6,7},{7,6},{8,9},{9,8},{10,11... | collective-permute-start | bytes 196616 | tf_op jit(solution)/shard_map/ppermute | solution.py:46
  37.9 1.3 %collective-permute-start.16 = (bf16[16,2048]{1,0:T(8,128)(2,1)S(1)}, bf16[16,2048]{1,0:T(8,128)(2,1)S(1)}, u32[]{:S(2)}, u32[]{:S(2)}) collective-permute-start(bf16[16,2048]{1,0:T(8,128)(2,1)S(1)} %collective-permute-done.12.refs_3_), channel_id=1, source_target_pairs={{0,1},{1,0},{2,3},{3,2},{4,5},{5,4},{6,7},{7,6},{8,9},{9,8},{10,11... | collective-permute-start | bytes 196616 | tf_op jit(solution)/shard_map/ppermute | solution.py:46
  38.4 1.3 %collective-permute-start.15 = (bf16[16,2048]{1,0:T(8,128)(2,1)S(1)}, bf16[16,2048]{1,0:T(8,128)(2,1)S(1)}, u32[]{:S(2)}, u32[]{:S(2)}) collective-permute-start(bf16[16,2048]{1,0:T(8,128)(2,1)S(1)} %collective-permute-done.11.refs_2_), channel_id=1, source_target_pairs={{0,1},{1,0},{2,3},{3,2},{4,5},{5,4},{6,7},{7,6},{8,9},{9,8},{10,11... | collective-permute-start | bytes 196616 | tf_op jit(solution)/shard_map/ppermute | solution.py:46
  38.8 1.3 %collective-permute-start.14 = (bf16[16,2048]{1,0:T(8,128)(2,1)S(1)}, bf16[16,2048]{1,0:T(8,128)(2,1)S(1)}, u32[]{:S(2)}, u32[]{:S(2)}) collective-permute-start(bf16[16,2048]{1,0:T(8,128)(2,1)S(1)} %collective-permute-done.10.refs_1_), channel_id=1, source_target_pairs={{0,1},{1,0},{2,3},{3,2},{4,5},{5,4},{6,7},{7,6},{8,9},{9,8},{10,11... | collective-permute-start | bytes 196616 | tf_op jit(solution)/shard_map/ppermute | solution.py:46
  42.3 21.6 %collective-permute-start.18 = (bf16[136,896]{1,0:T(8,128)(2,1)S(1)}, bf16[136,896]{1,0:T(8,128)(2,1)S(1)}, u32[]{:S(2)}, u32[]{:S(2)}) collective-permute-start(bf16[136,896]{1,0:T(8,128)(2,1)S(1)} %get-tuple-element.72), channel_id=1, source_target_pairs={{0,8},{8,0},{16,24},{24,16},{1,9},{9,1},{17,25},{25,17},{2,10},{10... | collective-permute-start | bytes 731144 | tf_op jit(solution)/shard_map/ppermute | solution.py:46
  43.8 11.9 %collective-permute-start.17 = (bf16[64,896]{1,0:T(8,128)(2,1)S(1)}, bf16[64,896]{1,0:T(8,128)(2,1)S(1)}, u32[]{:S(2)}, u32[]{:S(2)}) collective-permute-start(bf16[64,896]{1,0:T(8,128)(2,1)S(1)} %get-tuple-element.67), channel_id=1, source_target_pairs={{0,8},{8,0},{16,24},{24,16},{1,9},{9,1},{17,25},{25,17},{2,10},{10... | collective-permute-start | bytes 344072 | tf_op jit(solution)/shard_map/ppermute | solution.py:46
  44.4 15.0 %collective-permute-start.20 = (bf16[72,896]{1,0:T(8,128)(2,1)S(1)}, bf16[72,896]{1,0:T(8,128)(2,1)S(1)}, u32[]{:S(2)}, u32[]{:S(2)}) collective-permute-start(bf16[72,896]{1,0:T(8,128)(2,1)S(1)} %get-tuple-element.76), channel_id=1, source_target_pairs={{0,16},{8,24},{16,0},{24,8},{1,17},{9,25},{17,1},{25,9},{2,18},{10... | collective-permute-start | bytes 387080 | tf_op jit(solution)/shard_map/ppermute | solution.py:46
  45.6 14.2 %collective-permute-start.21 = (bf16[72,896]{1,0:T(8,128)(2,1)S(1)}, bf16[72,896]{1,0:T(8,128)(2,1)S(1)}, u32[]{:S(2)}, u32[]{:S(2)}) collective-permute-start(bf16[72,896]{1,0:T(8,128)(2,1)S(1)} %get-tuple-element.77), channel_id=1, source_target_pairs={{0,24},{8,16},{16,8},{24,0},{1,25},{9,17},{17,9},{25,1},{2,26},{10... | collective-permute-start | bytes 387080 | tf_op jit(solution)/shard_map/ppermute | solution.py:46
  55.7 8.1 %collective-permute-start.19 = (bf16[64,896]{1,0:T(8,128)(2,1)S(1)}, bf16[64,896]{1,0:T(8,128)(2,1)S(1)}, u32[]{:S(2)}, u32[]{:S(2)}) collective-permute-start(bf16[64,896]{1,0:T(8,128)(2,1)S(1)} %relay_sum.1), channel_id=1, source_target_pairs={{0,16},{8,24},{16,0},{24,8},{1,17},{9,25},{17,1},{25,9},{2,18},{10... | collective-permute-start | bytes 344072 | tf_op jit(solution)/shard_map/ppermute | solution.py:46
  64.3 12.9 %collective-permute-start.23 = (bf16[136,896]{1,0:T(8,128)(2,1)S(1)}, bf16[136,896]{1,0:T(8,128)(2,1)S(1)}, u32[]{:S(2)}, u32[]{:S(2)}) collective-permute-start(bf16[136,896]{1,0:T(8,128)(2,1)S(1)} %get-tuple-element.81.hidden_ref.refs_0_), channel_id=1, source_target_pairs={{0,8},{8,0},{16,24},{24,16},{1,9},{9,1},{17,25},{25,17},{2,10},{10... | collective-permute-start | bytes 731144 | tf_op jit(solution)/shard_map/ppermute | solution.py:46
  64.4 14.2 %collective-permute-start.22 = (bf16[136,896]{1,0:T(8,128)(2,1)S(1)}, bf16[136,896]{1,0:T(8,128)(2,1)S(1)}, u32[]{:S(2)}, u32[]{:S(2)}) collective-permute-start(bf16[136,896]{1,0:T(8,128)(2,1)S(1)} %get-tuple-element.81.hidden_ref.refs_0_), channel_id=1, source_target_pairs={{0,16},{8,24},{16,0},{24,8},{1,17},{9,25},{17,1},{25,9},{2,18},{10... | collective-permute-start | bytes 731144 | tf_op jit(solution)/shard_map/ppermute | solution.py:46
  78.6 6.2 %collective-permute-start.24 = (bf16[136,896]{1,0:T(8,128)(2,1)S(1)}, bf16[136,896]{1,0:T(8,128)(2,1)S(1)}, u32[]{:S(2)}, u32[]{:S(2)}) collective-permute-start(bf16[136,896]{1,0:T(8,128)(2,1)S(1)} %collective-permute-done.22.far_ref.refs_2_), channel_id=1, source_target_pairs={{0,8},{8,0},{16,24},{24,16},{1,9},{9,1},{17,25},{25,17},{2,10},{10... | collective-permute-start | bytes 731144 | tf_op jit(solution)/shard_map/ppermute | solution.py:46
  85.9 1.6 %collective-permute-start.25 = (bf16[4,128,227]{2,1,0:T(8,128)(2,1)S(1)}, bf16[4,128,227]{2,1,0:T(8,128)(2,1)S(1)}, u32[]{:S(2)}, u32[]{:S(2)}) collective-permute-start(bf16[4,128,227]{2,1,0:T(8,128)(2,1)S(1)} %get-tuple-element.89), channel_id=1, source_target_pairs={{0,1},{1,0},{2,3},{3,2},{4,5},{5,4},{6,7},{7,6},{8,9},{9,8},{10,11... | collective-permute-start | bytes 697352 | tf_op jit(solution)/shard_map/ppermute | solution.py:46
  87.7 5.3 %collective-permute-start.26 = (bf16[128,227]{1,0:T(8,128)(2,1)S(1)}, bf16[128,227]{1,0:T(8,128)(2,1)S(1)}, u32[]{:S(2)}, u32[]{:S(2)}) collective-permute-start(bf16[128,227]{1,0:T(8,128)(2,1)S(1)} %get-tuple-element.93), channel_id=1, source_target_pairs={{0,6},{1,7},{2,4},{3,5},{4,2},{5,3},{6,0},{7,1},{8,14},{9,15},{10,... | collective-permute-start | bytes 174344 | tf_op jit(solution)/shard_map/ppermute | solution.py:46
  89.8 4.6 %collective-permute-start.27 = (bf16[128,227]{1,0:T(8,128)(2,1)S(1)}, bf16[128,227]{1,0:T(8,128)(2,1)S(1)}, u32[]{:S(2)}, u32[]{:S(2)}) collective-permute-start(bf16[128,227]{1,0:T(8,128)(2,1)S(1)} %get-tuple-element.94), channel_id=1, source_target_pairs={{0,4},{1,5},{2,6},{3,7},{4,0},{5,1},{6,2},{7,3},{8,12},{9,13},{10,... | collective-permute-start | bytes 174344 | tf_op jit(solution)/shard_map/ppermute | solution.py:46
  90.4 4.3 %collective-permute-start.28 = (bf16[128,227]{1,0:T(8,128)(2,1)S(1)}, bf16[128,227]{1,0:T(8,128)(2,1)S(1)}, u32[]{:S(2)}, u32[]{:S(2)}) collective-permute-start(bf16[128,227]{1,0:T(8,128)(2,1)S(1)} %get-tuple-element.95), channel_id=1, source_target_pairs={{0,2},{1,3},{2,0},{3,1},{4,6},{5,7},{6,4},{7,5},{8,10},{9,11},{10,... | collective-permute-start | bytes 174344 | tf_op jit(solution)/shard_map/ppermute | solution.py:46
  (4 other events, 23.5 us)

commit v6 on v5

--- a/solution.py
+++ b/solution.py
@@ -11,7 +11,7 @@
 NEGATIVE = -1e30
 EPS = 1e-05
 VMEM_LIMIT = 24 * 2**20
-TOP = 64
+TOP = 80
 FREE = pl.CostEstimate(flops=0, bytes_accessed=0, transcendentals=0)
 
 
@@ -964,10 +964,10 @@
     far = send_xor(bottom3, "page", 3)
     middle = send_xor(bottom2, "page", 2)
     near = send_xor(part1, "page", 1)
+    image_a = image_of(score_group, w_down, 0, 2)
+    passing, image_a = lax.optimization_barrier((passing, image_a))
+    both, score_group, lhs = lax.optimization_barrier((relay_sum(top2, passing), score_group, lhs))
     part0 = up_own(lhs, stats, w_up)
-    image_a = image_of(score_group, w_down, 0, 2)
-    passing, part0, image_a = lax.optimization_barrier((passing, part0, image_a))
-    both, score_group = lax.optimization_barrier((relay_sum(top2, passing), score_group))
     images = image_a, image_of(score_group, w_down, 2, 2)
     parts = [part0, near, send_xor(both, "page", 2), middle, far]
     hidden, base_score = own_hidden_units(parts, b_up, images, group)

time: 95.9 us -> 95.5 us (level)
  waiting for transfers between devices: 30.3 us -> 29.1 us
    ppermute x29, waiting for transfers between devices: 30.3 us -> 29.1 us  [send_xor(): return lax.ppermute(value, axis, [(i, i ^ distance) for i in range(size)])]
  transfers between devices with their start and end apart: 29 -> 29, of which waited for: 20 -> 19; matrix products, arithmetic and copies ran while one was open for 0% -> 0% of each run, Pallas kernels for 25% -> 26%
where the time goes in v6:
time: 95.5 us; the launch traced here: 95.3 us
  Pallas kernels  33.7 us (35%)
  starting transfers between devices  31.4 us (33%)
  waiting for transfers between devices  29.1 us (30%)
    ppermute x29, starting transfers between devices, send_xor(): return lax.ppermute(value, axis, [(i, i ^ distance) for i in range(size)])  31.4 us
    ppermute x29, waiting for transfers between devices, send_xor(): return lax.ppermute(value, axis, [(i, i ^ distance) for i in range(size)])  29.1 us
    pallas_call x2, Pallas kernels, image_of(): pl.pallas_call(functools.partial(image_kernel, first), in_specs=[vmem, pl...  7.24 us
    pallas_call x2, Pallas kernels, hold_columns(): pl.pallas_call(functools.partial(hold_kernel, tuple(plan)), in_specs=[vme...  5.44 us
    pallas_call x1, Pallas kernels, down_first(): pl.pallas_call(down_first_kernel, in_specs=[vmem, pl.BlockSpec(memory_spa...  4.76 us
    pallas_call x1, Pallas kernels, prompt_partial(): pl.pallas_call(functools.partial(prompt_kernel, math.log2(math.e) / math....  3.29 us
    pallas_call x1, Pallas kernels, tail_partial(): pl.pallas_call(functools.partial(tail_kernel, math.log2(math.e) / math.sq...  3.18 us
    pallas_call x1, Pallas kernels, up_own(): pl.pallas_call(up_own_kernel, in_specs=[vmem] * 2 + [pl.BlockSpec(memory_...  2.66 us
  transfers between devices with their start and end apart: 29, of which 19 were waited for; matrix products, arithmetic and copies ran while one was open for 0% of the time, Pallas kernels for 26%

profile of v6, /device:TPU:0, one launch (start us, length us, event | category | flops | bytes accessed | tf_op | source)
XLA Modules:
  0.0 95.3 jit_solution(1338359702485500460)
XLA Ops:
  0.6 3.3 %prompt_attention.1 = (f32[136,128]{1,0:T(8,128)S(1)}, bf16[136,128]{1,0:T(8,128)(2,1)S(1)}, bf16[136,128]{1,0:T(8,128)(2,1)S(1)}, bf16[136,128]{1,0:T(8,128)(2,...) custom-call(s32[4,16]{1,0:T(4,128)} %table_hbm.1, ...), custom_call_target="tpu_custom_call" | custom-call | tf_op jit(solution)/shard_map/prompt_attention/pallas_call | solution.py:208
  3.9 3.1 %collective-permute-start = (bf16[136,128]{1,0:T(8,128)(2,1)S(1)}, bf16[136,128]{1,0:T(8,128)(2,1)S(1)}, u32[]{:S(2)}, u32[]{:S(2)}) collective-permute-start(bf16[136,128]{1,0:T(8,128)(2,1)S(1)} %get-tuple-element.51), channel_id=1, source_target_pairs={{0,8},{8,0},{16,24},{24,16},{1,9},{9,1},{17,25},{25,17},{2,10},{10... | collective-permute-start | bytes 104456 | tf_op jit(solution)/shard_map/ppermute | solution.py:46
  7.0 2.6 %collective-permute-start.1 = (bf16[136,128]{1,0:T(8,128)(2,1)S(1)}, bf16[136,128]{1,0:T(8,128)(2,1)S(1)}, u32[]{:S(2)}, u32[]{:S(2)}) collective-permute-start(bf16[136,128]{1,0:T(8,128)(2,1)S(1)} %get-tuple-element.52), channel_id=1, source_target_pairs={{0,16},{8,24},{16,0},{24,8},{1,17},{9,25},{17,1},{25,9},{2,18},{10... | collective-permute-start | bytes 104456 | tf_op jit(solution)/shard_map/ppermute | solution.py:46
  9.6 3.2 %tail_attention.1.refs_4_ = f32[136,128]{1,0:T(8,128)S(1)} custom-call(bf16[16,2,4,128]{3,2,1,0:T(4,128)(2,1)S(1)} %get-tuple-element.54.q_ref, s32[16,8,128]{2,1,0:T(8,128)S(1)} %get-tuple-element.55.len_ref, bf16[8,256,4,256]{3,2,1,0:T(4,128)(2,1)S(1)} %get-tuple-element.56.held_ref, bf16[16,256,4,256]{3,2,1,0:T(4,128)(2,1)} %kv_hbm.3), custom_call_target="tpu_custom_call" | custom-call | tf_op jit(solution)/shard_map/tail_attention/pallas_call | solution.py:306
  12.8 2.6 %collective-permute-done.2.refs_3_ = bf16[136,128]{1,0:T(8,128)(2,1)S(1)} collective-permute-done((bf16[136,128]{1,0:T(8,128)(2,1)S(1)}, bf16[136,128]{1,0:T(8,128)(2,1)S(1)}, u32[]{:S(2)}, u32[]{:S(2)}) %collective-permute-start.2) | collective-permute-done | bytes 34848 | tf_op jit(solution)/shard_map/ppermute | solution.py:46
  15.6 1.3 %collective-permute-start.5 = (bf16[32,512]{1,0:T(8,128)(2,1)S(1)}, bf16[32,512]{1,0:T(8,128)(2,1)S(1)}, u32[]{:S(2)}, u32[]{:S(2)}) collective-permute-start(bf16[32,512]{1,0:T(8,128)(2,1)S(1)} %merge_partials.1.after_ref.refs_0_), channel_id=1, source_target_pairs={{0,24},{8,16},{16,8},{24,0},{1,25},{9,17},{17,9},{25,1},{2,26},{10... | collective-permute-start | bytes 98312 | tf_op jit(solution)/shard_map/ppermute | solution.py:46
  16.9 3.1 %collective-permute-start.3 = (bf16[32,512]{1,0:T(8,128)(2,1)S(1)}, bf16[32,512]{1,0:T(8,128)(2,1)S(1)}, u32[]{:S(2)}, u32[]{:S(2)}) collective-permute-start(bf16[32,512]{1,0:T(8,128)(2,1)S(1)} %merge_partials.1.after_ref.refs_0_), channel_id=1, source_target_pairs={{0,8},{8,0},{16,24},{24,16},{1,9},{9,1},{17,25},{25,17},{2,10},{10... | collective-permute-start | bytes 98312 | tf_op jit(solution)/shard_map/ppermute | solution.py:46
  20.1 2.5 %hold_columns.2 = (bf16[1,512,1792]{2,1,0:T(8,128)(2,1)S(1)}, bf16[1,1792,896]{2,1,0:T(8,128)(2,1)S(1)}) custom-call(bf16[32,512]{1,0:T(8,128)(2,1)S(1)} %merge_partials.1.after_ref.refs_0_, bf16[512,7168]{1,0:T(8,128)(2,1)} %refs_0_.2, bf16[1792,3584]{1,0:T(8,128)(2,1)} %w_hbm.5), custom_call_target="tpu_custom_call" | custom-call | tf_op jit(solution)/shard_map/hold_columns/pallas_call | solution.py:387
  23.4 1.5 %collective-permute-done.6.got_ref = bf16[4,16,1792]{2,1,0:T(8,128)(2,1)S(1)} collective-permute-done((bf16[4,16,1792]{2,1,0:T(8,128)(2,1)S(1)}, bf16[4,16,1792]{2,1,0:T(8,128)(2,1)S(1)}, u32[]{:S(2)}, u32[]{:S(2)}) %collective-permute-start.6) | collective-permute-done | bytes 229408 | tf_op jit(solution)/shard_map/ppermute | solution.py:46
  24.9 2.4 %collective-permute-start.7 = (bf16[16,1792]{1,0:T(8,128)(2,1)S(1)}, bf16[16,1792]{1,0:T(8,128)(2,1)S(1)}, u32[]{:S(2)}, u32[]{:S(2)}) collective-permute-start(bf16[16,1792]{1,0:T(8,128)(2,1)S(1)} %get-tuple-element.62), channel_id=1, source_target_pairs={{0,6},{1,7},{2,4},{3,5},{4,2},{5,3},{6,0},{7,1},{8,14},{9,15},{10,... | collective-permute-start | bytes 172040 | tf_op jit(solution)/shard_map/ppermute | solution.py:46
  28.5 3.0 %hold_columns.3.refs_11_ = bf16[2,1792,896]{2,1,0:T(8,128)(2,1)S(1)} custom-call(f32[16,1792]{1,0:T(8,128)S(1)} %get-tuple-element.61.after_ref.own_ref, bf16[1792,3584]{1,0:T(8,128)(2,1)} %w_hbm.5), custom_call_target="tpu_custom_call" | custom-call | tf_op jit(solution)/shard_map/hold_columns/pallas_call | solution.py:387
  32.1 1.9 %collective-permute-start.12 = (bf16[16,2048]{1,0:T(8,128)(2,1)S(1)}, bf16[16,2048]{1,0:T(8,128)(2,1)S(1)}, u32[]{:S(2)}, u32[]{:S(2)}) collective-permute-start(bf16[16,2048]{1,0:T(8,128)(2,1)S(1)} %residual_rows.1.refs_0_), channel_id=1, source_target_pairs={{0,6},{1,7},{2,4},{3,5},{4,2},{5,3},{6,0},{7,1},{8,14},{9,15},{10,... | collective-permute-start | bytes 196616 | tf_op jit(solution)/shard_map/ppermute | solution.py:46
  34.5 1.1 %collective-permute-start.10 = (bf16[16,2048]{1,0:T(8,128)(2,1)S(1)}, bf16[16,2048]{1,0:T(8,128)(2,1)S(1)}, u32[]{:S(2)}, u32[]{:S(2)}) collective-permute-start(bf16[16,2048]{1,0:T(8,128)(2,1)S(1)} %residual_rows.1.refs_0_), channel_id=1, source_target_pairs={{0,2},{1,3},{2,0},{3,1},{4,6},{5,7},{6,4},{7,5},{8,10},{9,11},{10,... | collective-permute-start | bytes 196616 | tf_op jit(solution)/shard_map/ppermute | solution.py:46
  35.7 2.2 %collective-permute-done.12.refs_3_ = bf16[16,2048]{1,0:T(8,128)(2,1)S(1)} collective-permute-done((bf16[16,2048]{1,0:T(8,128)(2,1)S(1)}, bf16[16,2048]{1,0:T(8,128)(2,1)S(1)}, u32[]{:S(2)}, u32[]{:S(2)}) %collective-permute-start.12) | collective-permute-done | bytes 65568 | tf_op jit(solution)/shard_map/ppermute | solution.py:46
  40.1 2.2 %norm_and_up.1 = (bf16[80,896]{1,0:T(8,128)(2,1)S(1)}, bf16[56,896]{1,0:T(8,128)(2,1)S(1)}, bf16[80,896]{1,0:T(8,128)(2,1)S(1)}, bf16[56,896]{1,0:T(8,128)(2,1)S...) custom-call(bf16[16,2048]{1,0:T(8,128)(2,1)S(1)} %residual_rows.1.re, ...), custom_call_target="tpu_custom_call" | custom-call | tf_op jit(solution)/shard_map/norm_and_up/pallas_call | solution.py:585
  42.3 1.5 %collective-permute-start.17 = (bf16[80,896]{1,0:T(8,128)(2,1)S(1)}, bf16[80,896]{1,0:T(8,128)(2,1)S(1)}, u32[]{:S(2)}, u32[]{:S(2)}) collective-permute-start(bf16[80,896]{1,0:T(8,128)(2,1)S(1)} %get-tuple-element.68), channel_id=1, source_target_pairs={{0,8},{8,0},{16,24},{24,16},{1,9},{9,1},{17,25},{25,17},{2,10},{10... | collective-permute-start | bytes 430088 | tf_op jit(solution)/shard_map/ppermute | solution.py:46
  44.4 3.6 %score_image.2.refs_6_ = f32[4,896]{1,0:T(4,128)S(1)} custom-call(f32[1,1792]{1,0:T(1,128)S(1)} %get-tuple-element.79.score_ref, bf16[3584,1792]{1,0:T(8,128)(2,1)} %w_hbm.7), custom_call_target="tpu_custom_call" | custom-call | tf_op jit(solution)/shard_map/score_image/pallas_call | solution.py:682
  49.0 1.3 %collective-permute-start.19 = (bf16[80,896]{1,0:T(8,128)(2,1)S(1)}, bf16[80,896]{1,0:T(8,128)(2,1)S(1)}, u32[]{:S(2)}, u32[]{:S(2)}) collective-permute-start(bf16[80,896]{1,0:T(8,128)(2,1)S(1)} %relay_sum.1), channel_id=1, source_target_pairs={{0,16},{8,24},{16,0},{24,8},{1,17},{9,25},{17,1},{25,9},{2,18},{10... | collective-permute-start | bytes 430088 | tf_op jit(solution)/shard_map/ppermute | solution.py:46
  50.3 1.7 %collective-permute-start.20 = (bf16[56,896]{1,0:T(8,128)(2,1)S(1)}, bf16[56,896]{1,0:T(8,128)(2,1)S(1)}, u32[]{:S(2)}, u32[]{:S(2)}) collective-permute-start(bf16[56,896]{1,0:T(8,128)(2,1)S(1)} %get-tuple-element.76), channel_id=1, source_target_pairs={{0,16},{8,24},{16,0},{24,8},{1,17},{9,25},{17,1},{25,9},{2,18},{10... | collective-permute-start | bytes 301064 | tf_op jit(solution)/shard_map/ppermute | solution.py:46
  52.0 1.7 %collective-permute-start.21 = (bf16[56,896]{1,0:T(8,128)(2,1)S(1)}, bf16[56,896]{1,0:T(8,128)(2,1)S(1)}, u32[]{:S(2)}, u32[]{:S(2)}) collective-permute-start(bf16[56,896]{1,0:T(8,128)(2,1)S(1)} %get-tuple-element.77), channel_id=1, source_target_pairs={{0,24},{8,16},{16,8},{24,0},{1,25},{9,17},{17,9},{25,1},{2,26},{10... | collective-permute-start | bytes 301064 | tf_op jit(solution)/shard_map/ppermute | solution.py:46
  53.7 3.6 %score_image.3.refs_7_ = f32[4,896]{1,0:T(4,128)S(1)} custom-call(f32[1,1792]{1,0:T(1,128)S(1)} %get-tuple-element.79.score_ref, bf16[3584,1792]{1,0:T(8,128)(2,1)} %w_hbm.7), custom_call_target="tpu_custom_call" | custom-call | tf_op jit(solution)/shard_map/score_image/pallas_call | solution.py:682
  57.3 2.7 %up_own.1.refs_0_ = bf16[136,896]{1,0:T(8,128)(2,1)S(1)} custom-call(bf16[144,1792]{1,0:T(8,128)(2,1)S(1)} %get-tuple-element.72.lhs_ref, bf16[6,128]{1,0:T(8,128)(2,1)S(1)} %get-tuple-element.73.stats_ref, bf16[1792,3584]{1,0:T(8,128)(2,1)} %w_hbm.5), custom_call_target="tpu_custom_call" | custom-call | tf_op jit(solution)/shard_map/up_own/pallas_call | solution.py:624
  60.0 4.9 %collective-permute-done.20.refs_3_ = bf16[56,896]{1,0:T(8,128)(2,1)S(1)} collective-permute-done((bf16[56,896]{1,0:T(8,128)(2,1)S(1)}, bf16[56,896]{1,0:T(8,128)(2,1)S(1)}, u32[]{:S(2)}, u32[]{:S(2)}) %collective-permute-start.20) | collective-permute-done | bytes 100384 | tf_op jit(solution)/shard_map/ppermute | solution.py:46
  65.4 1.7 %collective-permute-start.23 = (bf16[136,896]{1,0:T(8,128)(2,1)S(1)}, bf16[136,896]{1,0:T(8,128)(2,1)S(1)}, u32[]{:S(2)}, u32[]{:S(2)}) collective-permute-start(bf16[136,896]{1,0:T(8,128)(2,1)S(1)} %get-tuple-element.81.hidden_ref.refs_0_), channel_id=1, source_target_pairs={{0,8},{8,0},{16,24},{24,16},{1,9},{9,1},{17,25},{25,17},{2,10},{10... | collective-permute-start | bytes 731144 | tf_op jit(solution)/shard_map/ppermute | solution.py:46
  67.9 4.8 %down_own.1 = (f32[128,1792]{1,0:T(8,128)S(1)}, bf16[3,896,1792]{2,1,0:T(8,128)(2,1)S(1)}) custom-call(bf16[136,896]{1,0:T(8,128)(2,1)S(1)} %get-tuple-element.81.hidden_ref.refs_0_, bf16[3584,1792]{1,0:T(8,128)(2,1)} %w_hbm.7), custom_call_target="tpu_custom_call" | custom-call | tf_op jit(solution)/shard_map/down_own/pallas_call | solution.py:759
  72.7 2.9 %collective-permute-done.23.near_ref.refs_1_ = bf16[136,896]{1,0:T(8,128)(2,1)S(1)} collective-permute-done((bf16[136,896]{1,0:T(8,128)(2,1)S(1)}, bf16[136,896]{1,0:T(8,128)(2,1)S(1)}, u32[]{:S(2)}, u32[]{:S(2)}) %collective-permute-start.23) | collective-permute-done | bytes 243744 | tf_op jit(solution)/shard_map/ppermute | solution.py:46
  75.6 2.6 %collective-permute-done.22.far_ref.refs_2_ = bf16[136,896]{1,0:T(8,128)(2,1)S(1)} collective-permute-done((bf16[136,896]{1,0:T(8,128)(2,1)S(1)}, bf16[136,896]{1,0:T(8,128)(2,1)S(1)}, u32[]{:S(2)}, u32[]{:S(2)}) %collective-permute-start.22) | collective-permute-done | bytes 243744 | tf_op jit(solution)/shard_map/ppermute | solution.py:46
  80.3 4.1 %collective-permute-done.24.refs_3_ = bf16[136,896]{1,0:T(8,128)(2,1)S(1)} collective-permute-done((bf16[136,896]{1,0:T(8,128)(2,1)S(1)}, bf16[136,896]{1,0:T(8,128)(2,1)S(1)}, u32[]{:S(2)}, u32[]{:S(2)}) %collective-permute-start.24) | collective-permute-done | bytes 243744 | tf_op jit(solution)/shard_map/ppermute | solution.py:46
  85.6 1.5 %collective-permute-done.25.got_ref = bf16[4,128,227]{2,1,0:T(8,128)(2,1)S(1)} collective-permute-done((bf16[4,128,227]{2,1,0:T(8,128)(2,1)S(1)}, bf16[4,128,227]{2,1,0:T(8,128)(2,1)S(1)}, u32[]{:S(2)}, u32[]{:S(2)}) %collective-permute-start.25) | collective-permute-done | bytes 232480 | tf_op jit(solution)/shard_map/ppermute | solution.py:46
  87.4 2.4 %collective-permute-start.26 = (bf16[128,227]{1,0:T(8,128)(2,1)S(1)}, bf16[128,227]{1,0:T(8,128)(2,1)S(1)}, u32[]{:S(2)}, u32[]{:S(2)}) collective-permute-start(bf16[128,227]{1,0:T(8,128)(2,1)S(1)} %get-tuple-element.93), channel_id=1, source_target_pairs={{0,6},{1,7},{2,4},{3,5},{4,2},{5,3},{6,0},{7,1},{8,14},{9,15},{10,... | collective-permute-start | bytes 174344 | tf_op jit(solution)/shard_map/ppermute | solution.py:46
  91.0 1.6 %collective-permute-done.26.c_ref = bf16[128,227]{1,0:T(8,128)(2,1)S(1)} collective-permute-done((bf16[128,227]{1,0:T(8,128)(2,1)S(1)}, bf16[128,227]{1,0:T(8,128)(2,1)S(1)}, u32[]{:S(2)}, u32[]{:S(2)}) %collective-permute-start.26) | collective-permute-done | bytes 58144 | tf_op jit(solution)/shard_map/ppermute | solution.py:46
  92.6 1.4 %collective-permute-done.27.b_ref = bf16[128,227]{1,0:T(8,128)(2,1)S(1)} collective-permute-done((bf16[128,227]{1,0:T(8,128)(2,1)S(1)}, bf16[128,227]{1,0:T(8,128)(2,1)S(1)}, u32[]{:S(2)}, u32[]{:S(2)}) %collective-permute-start.27) | collective-permute-done | bytes 58144 | tf_op jit(solution)/shard_map/ppermute | solution.py:46
  (61 shorter events, 14.4 us)
Async XLA Ops:
  3.9 8.9 %collective-permute-start = (bf16[136,128]{1,0:T(8,128)(2,1)S(1)}, bf16[136,128]{1,0:T(8,128)(2,1)S(1)}, u32[]{:S(2)}, u32[]{:S(2)}) collective-permute-start(bf16[136,128]{1,0:T(8,128)(2,1)S(1)} %get-tuple-element.51), channel_id=1, source_target_pairs={{0,8},{8,0},{16,24},{24,16},{1,9},{9,1},{17,25},{25,17},{2,10},{10... | collective-permute-start | bytes 104456 | tf_op jit(solution)/shard_map/ppermute | solution.py:46
  7.0 5.8 %collective-permute-start.1 = (bf16[136,128]{1,0:T(8,128)(2,1)S(1)}, bf16[136,128]{1,0:T(8,128)(2,1)S(1)}, u32[]{:S(2)}, u32[]{:S(2)}) collective-permute-start(bf16[136,128]{1,0:T(8,128)(2,1)S(1)} %get-tuple-element.52), channel_id=1, source_target_pairs={{0,16},{8,24},{16,0},{24,8},{1,17},{9,25},{17,1},{25,9},{2,18},{10... | collective-permute-start | bytes 104456 | tf_op jit(solution)/shard_map/ppermute | solution.py:46
  9.6 5.8 %collective-permute-start.2 = (bf16[136,128]{1,0:T(8,128)(2,1)S(1)}, bf16[136,128]{1,0:T(8,128)(2,1)S(1)}, u32[]{:S(2)}, u32[]{:S(2)}) collective-permute-start(bf16[136,128]{1,0:T(8,128)(2,1)S(1)} %get-tuple-element.53), channel_id=1, source_target_pairs={{0,24},{8,16},{16,8},{24,0},{1,25},{9,17},{17,9},{25,1},{2,26},{10... | collective-permute-start | bytes 104456 | tf_op jit(solution)/shard_map/ppermute | solution.py:46
  15.6 6.9 %collective-permute-start.5 = (bf16[32,512]{1,0:T(8,128)(2,1)S(1)}, bf16[32,512]{1,0:T(8,128)(2,1)S(1)}, u32[]{:S(2)}, u32[]{:S(2)}) collective-permute-start(bf16[32,512]{1,0:T(8,128)(2,1)S(1)} %merge_partials.1.after_ref.refs_0_), channel_id=1, source_target_pairs={{0,24},{8,16},{16,8},{24,0},{1,25},{9,17},{17,9},{25,1},{2,26},{10... | collective-permute-start | bytes 98312 | tf_op jit(solution)/shard_map/ppermute | solution.py:46
  16.9 5.6 %collective-permute-start.4 = (bf16[32,512]{1,0:T(8,128)(2,1)S(1)}, bf16[32,512]{1,0:T(8,128)(2,1)S(1)}, u32[]{:S(2)}, u32[]{:S(2)}) collective-permute-start(bf16[32,512]{1,0:T(8,128)(2,1)S(1)} %merge_partials.1.after_ref.refs_0_), channel_id=1, source_target_pairs={{0,16},{8,24},{16,0},{24,8},{1,17},{9,25},{17,1},{25,9},{2,18},{10... | collective-permute-start | bytes 98312 | tf_op jit(solution)/shard_map/ppermute | solution.py:46
  16.9 5.6 %collective-permute-start.3 = (bf16[32,512]{1,0:T(8,128)(2,1)S(1)}, bf16[32,512]{1,0:T(8,128)(2,1)S(1)}, u32[]{:S(2)}, u32[]{:S(2)}) collective-permute-start(bf16[32,512]{1,0:T(8,128)(2,1)S(1)} %merge_partials.1.after_ref.refs_0_), channel_id=1, source_target_pairs={{0,8},{8,0},{16,24},{24,16},{1,9},{9,1},{17,25},{25,17},{2,10},{10... | collective-permute-start | bytes 98312 | tf_op jit(solution)/shard_map/ppermute | solution.py:46
  23.3 1.6 %collective-permute-start.6 = (bf16[4,16,1792]{2,1,0:T(8,128)(2,1)S(1)}, bf16[4,16,1792]{2,1,0:T(8,128)(2,1)S(1)}, u32[]{:S(2)}, u32[]{:S(2)}) collective-permute-start(bf16[4,16,1792]{2,1,0:T(8,128)(2,1)S(1)} %get-tuple-element.59), channel_id=1, source_target_pairs={{0,1},{1,0},{2,3},{3,2},{4,5},{5,4},{6,7},{7,6},{8,9},{9,8},{10,11... | collective-permute-start | bytes 688136 | tf_op jit(solution)/shard_map/ppermute | solution.py:46
  24.9 6.5 %collective-permute-start.7 = (bf16[16,1792]{1,0:T(8,128)(2,1)S(1)}, bf16[16,1792]{1,0:T(8,128)(2,1)S(1)}, u32[]{:S(2)}, u32[]{:S(2)}) collective-permute-start(bf16[16,1792]{1,0:T(8,128)(2,1)S(1)} %get-tuple-element.62), channel_id=1, source_target_pairs={{0,6},{1,7},{2,4},{3,5},{4,2},{5,3},{6,0},{7,1},{8,14},{9,15},{10,... | collective-permute-start | bytes 172040 | tf_op jit(solution)/shard_map/ppermute | solution.py:46
  27.4 4.2 %collective-permute-start.8 = (bf16[16,1792]{1,0:T(8,128)(2,1)S(1)}, bf16[16,1792]{1,0:T(8,128)(2,1)S(1)}, u32[]{:S(2)}, u32[]{:S(2)}) collective-permute-start(bf16[16,1792]{1,0:T(8,128)(2,1)S(1)} %get-tuple-element.63), channel_id=1, source_target_pairs={{0,4},{1,5},{2,6},{3,7},{4,0},{5,1},{6,2},{7,3},{8,12},{9,13},{10,... | collective-permute-start | bytes 172040 | tf_op jit(solution)/shard_map/ppermute | solution.py:46
  27.9 4.2 %collective-permute-start.9 = (bf16[16,1792]{1,0:T(8,128)(2,1)S(1)}, bf16[16,1792]{1,0:T(8,128)(2,1)S(1)}, u32[]{:S(2)}, u32[]{:S(2)}) collective-permute-start(bf16[16,1792]{1,0:T(8,128)(2,1)S(1)} %get-tuple-element.64), channel_id=1, source_target_pairs={{0,2},{1,3},{2,0},{3,1},{4,6},{5,7},{6,4},{7,5},{8,10},{9,11},{10,... | collective-permute-start | bytes 172040 | tf_op jit(solution)/shard_map/ppermute | solution.py:46
  28.5 11.6 %copy-start.3 = (bf16[1792]{0:T(1024)(128)(2,1)S(1)}, bf16[1792]{0:T(1024)(128)(2,1)}, u32[]{:S(2)}) copy-start(bf16[1792]{0:T(1024)(128)(2,1)} %refs_8_.1) | copy-start | bytes 10756
  28.5 11.6 %copy-start.4 = (bf16[1792]{0:T(1024)(128)(2,1)S(1)}, bf16[1792]{0:T(1024)(128)(2,1)}, u32[]{:S(2)}) copy-start(bf16[1792]{0:T(1024)(128)(2,1)} %refs_9_.1) | copy-start | bytes 10756
  28.5 11.6 %copy-start.6 = (bf16[224]{0:T(256)(128)(2,1)S(1)}, bf16[224]{0:T(256)(128)(2,1)}, u32[]{:S(2)}) copy-start(bf16[224]{0:T(256)(128)(2,1)} %refs_10_.1) | copy-start | bytes 1348
  32.1 5.8 %collective-permute-start.12 = (bf16[16,2048]{1,0:T(8,128)(2,1)S(1)}, bf16[16,2048]{1,0:T(8,128)(2,1)S(1)}, u32[]{:S(2)}, u32[]{:S(2)}) collective-permute-start(bf16[16,2048]{1,0:T(8,128)(2,1)S(1)} %residual_rows.1.refs_0_), channel_id=1, source_target_pairs={{0,6},{1,7},{2,4},{3,5},{4,2},{5,3},{6,0},{7,1},{8,14},{9,15},{10,... | collective-permute-start | bytes 196616 | tf_op jit(solution)/shard_map/ppermute | solution.py:46
  34.0 4.4 %collective-permute-start.11 = (bf16[16,2048]{1,0:T(8,128)(2,1)S(1)}, bf16[16,2048]{1,0:T(8,128)(2,1)S(1)}, u32[]{:S(2)}, u32[]{:S(2)}) collective-permute-start(bf16[16,2048]{1,0:T(8,128)(2,1)S(1)} %residual_rows.1.refs_0_), channel_id=1, source_target_pairs={{0,4},{1,5},{2,6},{3,7},{4,0},{5,1},{6,2},{7,3},{8,12},{9,13},{10,... | collective-permute-start | bytes 196616 | tf_op jit(solution)/shard_map/ppermute | solution.py:46
  34.5 4.3 %collective-permute-start.10 = (bf16[16,2048]{1,0:T(8,128)(2,1)S(1)}, bf16[16,2048]{1,0:T(8,128)(2,1)S(1)}, u32[]{:S(2)}, u32[]{:S(2)}) collective-permute-start(bf16[16,2048]{1,0:T(8,128)(2,1)S(1)} %residual_rows.1.refs_0_), channel_id=1, source_target_pairs={{0,2},{1,3},{2,0},{3,1},{4,6},{5,7},{6,4},{7,5},{8,10},{9,11},{10,... | collective-permute-start | bytes 196616 | tf_op jit(solution)/shard_map/ppermute | solution.py:46
  35.7 3.3 %collective-permute-start.13 = (bf16[16,2048]{1,0:T(8,128)(2,1)S(1)}, bf16[16,2048]{1,0:T(8,128)(2,1)S(1)}, u32[]{:S(2)}, u32[]{:S(2)}) collective-permute-start(bf16[16,2048]{1,0:T(8,128)(2,1)S(1)} %residual_rows.1.refs_0_), channel_id=1, source_target_pairs={{0,1},{1,0},{2,3},{3,2},{4,5},{5,4},{6,7},{7,6},{8,9},{9,8},{10,11... | collective-permute-start | bytes 196616 | tf_op jit(solution)/shard_map/ppermute | solution.py:46
  37.9 1.3 %collective-permute-start.16 = (bf16[16,2048]{1,0:T(8,128)(2,1)S(1)}, bf16[16,2048]{1,0:T(8,128)(2,1)S(1)}, u32[]{:S(2)}, u32[]{:S(2)}) collective-permute-start(bf16[16,2048]{1,0:T(8,128)(2,1)S(1)} %collective-permute-done.12.refs_3_), channel_id=1, source_target_pairs={{0,1},{1,0},{2,3},{3,2},{4,5},{5,4},{6,7},{7,6},{8,9},{9,8},{10,11... | collective-permute-start | bytes 196616 | tf_op jit(solution)/shard_map/ppermute | solution.py:46
  38.4 1.3 %collective-permute-start.15 = (bf16[16,2048]{1,0:T(8,128)(2,1)S(1)}, bf16[16,2048]{1,0:T(8,128)(2,1)S(1)}, u32[]{:S(2)}, u32[]{:S(2)}) collective-permute-start(bf16[16,2048]{1,0:T(8,128)(2,1)S(1)} %collective-permute-done.11.refs_2_), channel_id=1, source_target_pairs={{0,1},{1,0},{2,3},{3,2},{4,5},{5,4},{6,7},{7,6},{8,9},{9,8},{10,11... | collective-permute-start | bytes 196616 | tf_op jit(solution)/shard_map/ppermute | solution.py:46
  38.8 1.3 %collective-permute-start.14 = (bf16[16,2048]{1,0:T(8,128)(2,1)S(1)}, bf16[16,2048]{1,0:T(8,128)(2,1)S(1)}, u32[]{:S(2)}, u32[]{:S(2)}) collective-permute-start(bf16[16,2048]{1,0:T(8,128)(2,1)S(1)} %collective-permute-done.10.refs_1_), channel_id=1, source_target_pairs={{0,1},{1,0},{2,3},{3,2},{4,5},{5,4},{6,7},{7,6},{8,9},{9,8},{10,11... | collective-permute-start | bytes 196616 | tf_op jit(solution)/shard_map/ppermute | solution.py:46
  42.3 6.7 %collective-permute-start.17 = (bf16[80,896]{1,0:T(8,128)(2,1)S(1)}, bf16[80,896]{1,0:T(8,128)(2,1)S(1)}, u32[]{:S(2)}, u32[]{:S(2)}) collective-permute-start(bf16[80,896]{1,0:T(8,128)(2,1)S(1)} %get-tuple-element.68), channel_id=1, source_target_pairs={{0,8},{8,0},{16,24},{24,16},{1,9},{9,1},{17,25},{25,17},{2,10},{10... | collective-permute-start | bytes 430088 | tf_op jit(solution)/shard_map/ppermute | solution.py:46
  43.8 21.1 %collective-permute-start.18 = (bf16[136,896]{1,0:T(8,128)(2,1)S(1)}, bf16[136,896]{1,0:T(8,128)(2,1)S(1)}, u32[]{:S(2)}, u32[]{:S(2)}) collective-permute-start(bf16[136,896]{1,0:T(8,128)(2,1)S(1)} %get-tuple-element.74), channel_id=1, source_target_pairs={{0,8},{8,0},{16,24},{24,16},{1,9},{9,1},{17,25},{25,17},{2,10},{10... | collective-permute-start | bytes 731144 | tf_op jit(solution)/shard_map/ppermute | solution.py:46
  49.0 16.0 %collective-permute-start.19 = (bf16[80,896]{1,0:T(8,128)(2,1)S(1)}, bf16[80,896]{1,0:T(8,128)(2,1)S(1)}, u32[]{:S(2)}, u32[]{:S(2)}) collective-permute-start(bf16[80,896]{1,0:T(8,128)(2,1)S(1)} %relay_sum.1), channel_id=1, source_target_pairs={{0,16},{8,24},{16,0},{24,8},{1,17},{9,25},{17,1},{25,9},{2,18},{10... | collective-permute-start | bytes 430088 | tf_op jit(solution)/shard_map/ppermute | solution.py:46
  50.3 14.7 %collective-permute-start.20 = (bf16[56,896]{1,0:T(8,128)(2,1)S(1)}, bf16[56,896]{1,0:T(8,128)(2,1)S(1)}, u32[]{:S(2)}, u32[]{:S(2)}) collective-permute-start(bf16[56,896]{1,0:T(8,128)(2,1)S(1)} %get-tuple-element.76), channel_id=1, source_target_pairs={{0,16},{8,24},{16,0},{24,8},{1,17},{9,25},{17,1},{25,9},{2,18},{10... | collective-permute-start | bytes 301064 | tf_op jit(solution)/shard_map/ppermute | solution.py:46
  52.0 13.0 %collective-permute-start.21 = (bf16[56,896]{1,0:T(8,128)(2,1)S(1)}, bf16[56,896]{1,0:T(8,128)(2,1)S(1)}, u32[]{:S(2)}, u32[]{:S(2)}) collective-permute-start(bf16[56,896]{1,0:T(8,128)(2,1)S(1)} %get-tuple-element.77), channel_id=1, source_target_pairs={{0,24},{8,16},{16,8},{24,0},{1,25},{9,17},{17,9},{25,1},{2,26},{10... | collective-permute-start | bytes 301064 | tf_op jit(solution)/shard_map/ppermute | solution.py:46
  65.4 10.2 %collective-permute-start.23 = (bf16[136,896]{1,0:T(8,128)(2,1)S(1)}, bf16[136,896]{1,0:T(8,128)(2,1)S(1)}, u32[]{:S(2)}, u32[]{:S(2)}) collective-permute-start(bf16[136,896]{1,0:T(8,128)(2,1)S(1)} %get-tuple-element.81.hidden_ref.refs_0_), channel_id=1, source_target_pairs={{0,8},{8,0},{16,24},{24,16},{1,9},{9,1},{17,25},{25,17},{2,10},{10... | collective-permute-start | bytes 731144 | tf_op jit(solution)/shard_map/ppermute | solution.py:46
  67.1 11.1 %collective-permute-start.22 = (bf16[136,896]{1,0:T(8,128)(2,1)S(1)}, bf16[136,896]{1,0:T(8,128)(2,1)S(1)}, u32[]{:S(2)}, u32[]{:S(2)}) collective-permute-start(bf16[136,896]{1,0:T(8,128)(2,1)S(1)} %get-tuple-element.81.hidden_ref.refs_0_), channel_id=1, source_target_pairs={{0,16},{8,24},{16,0},{24,8},{1,17},{9,25},{17,1},{25,9},{2,18},{10... | collective-permute-start | bytes 731144 | tf_op jit(solution)/shard_map/ppermute | solution.py:46
  78.2 6.2 %collective-permute-start.24 = (bf16[136,896]{1,0:T(8,128)(2,1)S(1)}, bf16[136,896]{1,0:T(8,128)(2,1)S(1)}, u32[]{:S(2)}, u32[]{:S(2)}) collective-permute-start(bf16[136,896]{1,0:T(8,128)(2,1)S(1)} %collective-permute-done.22.far_ref.refs_2_), channel_id=1, source_target_pairs={{0,8},{8,0},{16,24},{24,16},{1,9},{9,1},{17,25},{25,17},{2,10},{10... | collective-permute-start | bytes 731144 | tf_op jit(solution)/shard_map/ppermute | solution.py:46
  85.5 1.6 %collective-permute-start.25 = (bf16[4,128,227]{2,1,0:T(8,128)(2,1)S(1)}, bf16[4,128,227]{2,1,0:T(8,128)(2,1)S(1)}, u32[]{:S(2)}, u32[]{:S(2)}) collective-permute-start(bf16[4,128,227]{2,1,0:T(8,128)(2,1)S(1)} %get-tuple-element.89), channel_id=1, source_target_pairs={{0,1},{1,0},{2,3},{3,2},{4,5},{5,4},{6,7},{7,6},{8,9},{9,8},{10,11... | collective-permute-start | bytes 697352 | tf_op jit(solution)/shard_map/ppermute | solution.py:46
  87.4 5.3 %collective-permute-start.26 = (bf16[128,227]{1,0:T(8,128)(2,1)S(1)}, bf16[128,227]{1,0:T(8,128)(2,1)S(1)}, u32[]{:S(2)}, u32[]{:S(2)}) collective-permute-start(bf16[128,227]{1,0:T(8,128)(2,1)S(1)} %get-tuple-element.93), channel_id=1, source_target_pairs={{0,6},{1,7},{2,4},{3,5},{4,2},{5,3},{6,0},{7,1},{8,14},{9,15},{10,... | collective-permute-start | bytes 174344 | tf_op jit(solution)/shard_map/ppermute | solution.py:46
  89.8 4.3 %collective-permute-start.27 = (bf16[128,227]{1,0:T(8,128)(2,1)S(1)}, bf16[128,227]{1,0:T(8,128)(2,1)S(1)}, u32[]{:S(2)}, u32[]{:S(2)}) collective-permute-start(bf16[128,227]{1,0:T(8,128)(2,1)S(1)} %get-tuple-element.94), channel_id=1, source_target_pairs={{0,4},{1,5},{2,6},{3,7},{4,0},{5,1},{6,2},{7,3},{8,12},{9,13},{10,... | collective-permute-start | bytes 174344 | tf_op jit(solution)/shard_map/ppermute | solution.py:46
  90.0 4.3 %collective-permute-start.28 = (bf16[128,227]{1,0:T(8,128)(2,1)S(1)}, bf16[128,227]{1,0:T(8,128)(2,1)S(1)}, u32[]{:S(2)}, u32[]{:S(2)}) collective-permute-start(bf16[128,227]{1,0:T(8,128)(2,1)S(1)} %get-tuple-element.95), channel_id=1, source_target_pairs={{0,2},{1,3},{2,0},{3,1},{4,6},{5,7},{6,4},{7,5},{8,10},{9,11},{10,... | collective-permute-start | bytes 174344 | tf_op jit(solution)/shard_map/ppermute | solution.py:46
  (4 other events, 21.7 us)
